TPU v7x, 32 devices: a whole 2x2x4 slice. The times are simulated.
32 devices in a mesh: dp: 8 (over y, x, core), stream: 4 (over z).
Axes of the slice: x: 2, y: 2, z: 4, core: 2. Of those that a mesh axis runs over, the one named last changes fastest.
Arguments:
- history: bfloat16 [11, 8192, 2048], P(None, 'dp', 'stream'), may hold values from -6 to 6
- mix_in: bfloat16 [2048, 44], replicated, may hold values from -0.125 to 0.125
- mix_out: bfloat16 [44, 44], replicated, may hold values from -0.875 to 0.875
- mix_static: float32 [4, 11], replicated, may hold values from 0.05 to 0.6
- stream_gain: float32 [3, 2048], P(None, 'stream'), may hold values from 0.1 to 1.9
- qkv_weight: bfloat16 [2048, 3, 2048], P(None, None, 'stream'), may hold values from -0.125 to 0.125
- out_weight: bfloat16 [2048, 2048], P(None, 'stream'), may hold values from -2 to 2
- mlp_gain: float32 [2048], replicated, may hold values from 0.1 to 1.9
- up_weight: bfloat16 [2048, 8192], P(None, 'stream'), may hold values from -0.125 to 0.125
- down_weight: bfloat16 [2048, 8192], P(None, 'stream'), may hold values from -0.0625 to 0.0625
- out_grad: bfloat16 [8192, 2048], P('dp', 'stream'), may hold values from -6 to 6
- seq_group: int32 [8], P('dp'), may hold values from 0 to 21
- group_weight: int32 [22], replicated, may hold values from 1 to 4
Outputs:
- output: bfloat16 [8192, 2048], P('dp', 'stream')
- history_grad: bfloat16 [11, 8192, 2048], P(None, 'dp', 'stream')
- mix_in_grad: float32 [2048, 44], P('stream')
- mix_out_grad: float32 [44, 44], replicated
- mix_static_grad: float32 [4, 11], replicated
- stream_gain_grad: float32 [3, 2048], P(None, 'stream')
- qkv_grad: float32 [2048, 3, 2048], P('dp', None, 'stream')
- out_weight_grad: float32 [2048, 2048], P('dp', 'stream')
- mlp_gain_grad: float32 [2048], replicated
- up_grad: float32 [2048, 8192], P('dp', 'stream')
- down_grad: float32 [2048, 8192], P('dp', 'stream')
All inputs are finite; a program needn't handle non-finite values.
Results may differ from a plain program's by a relative error of at most 0.014.
The roundings to bfloat16 on the way count: a program that leaves them out, or rounds other values in their place, can miss the bound.
Values may be sent and summed in bfloat16 or wider, within the bound.
No kernel may reach another device: no remote copies, remote signals or barrier semaphores. Data moves between devices by JAX's collectives and lax.ppermute only.
A program may use at most 320 MiB of HBM per device.

v0:
```python
import jax
import jax.numpy as jnp
from jax import lax
from jax.sharding import PartitionSpec as P

HEAD_DIM = 128
SEQ = 1024


HIGH = lax.Precision.HIGHEST
EPS_NORM = 1e-05
EPS_MIX = 1e-06
COT_SCALE = 0.4


def gelu_exact(values):
    return jax.nn.gelu(values, approximate=False)


def gelu_back(values, incoming):
    return jax.vjp(gelu_exact, values)[1](incoming)[0]


def contract_rows(former, latter):
    return lax.dot_general(
        former, latter, (((0,), (0,)), ((), ())), preferred_element_type=jnp.float32
    )


def contract_rows_high(former, latter):
    return lax.dot_general(
        former, latter, (((0,), (0,)), ((), ())), precision=HIGH, preferred_element_type=jnp.float32
    )


def times_transpose(former, latter):
    return lax.dot_general(
        former, latter, (((1,), (1,)), ((), ())), preferred_element_type=jnp.float32
    )


def times_transpose_high(former, latter):
    return lax.dot_general(
        former, latter, (((1,), (1,)), ((), ())), precision=HIGH, preferred_element_type=jnp.float32
    )


def causal_allowed(row_count, row_begin, key_count):
    row_index = row_begin + lax.broadcasted_iota(jnp.int32, (row_count, key_count), 0)
    key_index = lax.broadcasted_iota(jnp.int32, (row_count, key_count), 1)
    return key_index <= row_index


def attend_forward(operands):
    queries, key_seq, value_seq = operands
    block_rows = min(512, SEQ)
    score_scale = HEAD_DIM ** (-0.5)
    block_outs = []
    lse_list = []
    for block_idx in range(SEQ // block_rows):
        row_begin = block_idx * block_rows
        finish = row_begin + block_rows
        scores = (
            jnp.einsum(
                "qhd,khd->hqk",
                queries[row_begin:finish],
                key_seq[:finish],
                preferred_element_type=jnp.float32,
            )
            * score_scale
        )
        allowed = causal_allowed(block_rows, row_begin, finish)
        scores = jnp.where(allowed[None], scores, -1e30)
        top_score = jnp.max(scores, axis=2, keepdims=True)
        exp_scores = jnp.exp(scores - top_score)
        row_total = jnp.sum(exp_scores, axis=2, keepdims=True)
        attn_probs = (exp_scores / row_total).astype(jnp.bfloat16)
        lse_list.append((top_score + jnp.log(row_total))[:, :, 0])
        block_outs.append(
            jnp.einsum(
                "hqk,khd->qhd", attn_probs, value_seq[:finish], preferred_element_type=jnp.float32
            ).astype(jnp.bfloat16)
        )
    return (jnp.concatenate(block_outs, axis=0), jnp.concatenate(lse_list, axis=1))


def attend_backward(operands):
    queries, key_seq, value_seq, grad_out, lse_seq = operands
    block_rows = min(512, SEQ)
    score_scale = HEAD_DIM ** (-0.5)
    key_grad = jnp.zeros(key_seq.shape, jnp.float32)
    value_grad = jnp.zeros(value_seq.shape, jnp.float32)
    query_grads = []
    for block_idx in range(SEQ // block_rows):
        row_begin = block_idx * block_rows
        finish = row_begin + block_rows
        query_block = queries[row_begin:finish]
        grad_block = grad_out[row_begin:finish]
        scores = (
            jnp.einsum(
                "qhd,khd->hqk", query_block, key_seq[:finish], preferred_element_type=jnp.float32
            )
            * score_scale
        )
        allowed = causal_allowed(block_rows, row_begin, finish)
        attn_probs = jnp.where(
            allowed[None], jnp.exp(scores - lse_seq[:, row_begin:finish, None]), 0.0
        )
        prob_grad = jnp.einsum(
            "qhd,khd->hqk", grad_block, value_seq[:finish], preferred_element_type=jnp.float32
        )
        value_grad = value_grad.at[:finish].add(
            jnp.einsum(
                "hqk,qhd->khd",
                attn_probs.astype(jnp.bfloat16),
                grad_block,
                preferred_element_type=jnp.float32,
            )
        )
        row_dot = jnp.sum(attn_probs * prob_grad, axis=2, keepdims=True)
        score_grad = (attn_probs * (prob_grad - row_dot) * score_scale).astype(jnp.bfloat16)
        query_grads.append(
            jnp.einsum(
                "hqk,khd->qhd", score_grad, key_seq[:finish], preferred_element_type=jnp.float32
            )
        )
        key_grad = key_grad.at[:finish].add(
            jnp.einsum("hqk,qhd->khd", score_grad, query_block, preferred_element_type=jnp.float32)
        )
    return (
        jnp.concatenate(query_grads, axis=0).astype(jnp.bfloat16),
        key_grad.astype(jnp.bfloat16),
        value_grad.astype(jnp.bfloat16),
    )


def local(
    history,
    mix_in,
    mix_out,
    mix_static,
    stream_gain,
    qkv_weight,
    out_weight,
    mlp_gain,
    up_weight,
    down_weight,
    out_grad,
    seq_group,
    group_weight,
):
    n_stream = lax.axis_size("stream")
    member = lax.axis_index("stream")
    n_hist, tokens, local_width = history.shape
    full_width = local_width * n_stream
    local_heads = local_width // HEAD_DIM
    n_seqs = tokens // SEQ
    first_col = member * local_width
    last_layer = history[n_hist - 1]
    mix_in_rows = lax.dynamic_slice_in_dim(mix_in, first_col, local_width, 0)
    square_part = jnp.sum(jnp.square(last_layer.astype(jnp.float32)), axis=1)
    raw_part = jnp.dot(last_layer, mix_in_rows, preferred_element_type=jnp.float32)
    square_total, mix_raw = lax.psum((square_part, raw_part), "stream")
    mix_scale = lax.rsqrt(square_total / full_width + EPS_MIX)[:, None]
    mix_pre = mix_scale * mix_raw
    mix_act = gelu_exact(mix_pre)
    mix_out_float = mix_out.astype(jnp.float32)
    mix_coef = (
        jnp.dot(mix_act, mix_out_float, precision=HIGH, preferred_element_type=jnp.float32)
        + mix_static.reshape(1, -1)
    ).reshape(tokens, 4, n_hist)

    def mix_stream(stream_idx):
        mixed = mix_coef[:, stream_idx, 0][:, None] * history[0].astype(jnp.float32)
        for hist_idx in range(1, n_hist):
            mixed = mixed + mix_coef[:, stream_idx, hist_idx][:, None] * history[hist_idx].astype(
                jnp.float32
            )
        return mixed

    streams = jnp.stack([mix_stream(stream_idx) for stream_idx in range(3)])
    resid_cols = mix_stream(3)
    sum_first = jnp.sum(streams, axis=2)
    sum_second = jnp.sum(jnp.square(streams), axis=2)
    feat_sum, feat_square = lax.psum((sum_first, sum_second), "stream")
    row_mean = feat_sum / full_width
    inv_std = lax.rsqrt(feat_square / full_width - jnp.square(row_mean) + EPS_NORM)
    normed_hat = (streams - row_mean[:, :, None]) * inv_std[:, :, None]
    normed_cols = (normed_hat * stream_gain[:, None, :]).astype(jnp.bfloat16)
    normed = lax.all_gather(normed_cols, "stream", axis=2, tiled=True)
    projected = jnp.einsum(
        "std,dsc->stc", normed, qkv_weight, preferred_element_type=jnp.float32
    ).astype(jnp.bfloat16)
    head_shape = (n_seqs, SEQ, local_heads, HEAD_DIM)
    query_seqs = projected[0].reshape(head_shape)
    key_seqs = projected[1].reshape(head_shape)
    value_seqs = projected[2].reshape(head_shape)
    heads_seq, lse_all = lax.map(attend_forward, (query_seqs, key_seqs, value_seqs))
    heads_out = heads_seq.reshape(tokens, local_width)
    branch_part = times_transpose(heads_out, out_weight)
    own_cols = lax.dynamic_slice_in_dim(branch_part, first_col, local_width, 1) + resid_cols
    branch_part = lax.dynamic_update_slice_in_dim(branch_part, own_cols, first_col, 1)
    residual = lax.psum(branch_part, "stream")
    resid_center = residual - jnp.mean(residual, axis=1, keepdims=True)
    inv_std_mlp = lax.rsqrt(jnp.mean(jnp.square(resid_center), axis=1, keepdims=True) + EPS_NORM)
    hat_mlp = resid_center * inv_std_mlp
    normed_mlp = (hat_mlp * mlp_gain[None, :]).astype(jnp.bfloat16)
    hidden_pre = jnp.dot(normed_mlp, up_weight, preferred_element_type=jnp.float32)
    hidden = gelu_exact(hidden_pre).astype(jnp.bfloat16)
    mlp_part = times_transpose(hidden, down_weight)
    mlp_cols = lax.psum_scatter(mlp_part, "stream", scatter_dimension=1, tiled=True)
    output_cols = (lax.dynamic_slice_in_dim(residual, first_col, local_width, 1) + mlp_cols).astype(
        jnp.bfloat16
    )
    group_pick = (
        seq_group[:, None] == jnp.arange(group_weight.shape[0], dtype=jnp.int32)[None, :]
    ).astype(jnp.float32)
    seq_weight = jnp.sum(group_pick * group_weight.astype(jnp.float32)[None, :], axis=1) * COT_SCALE
    tok_weight = (seq_weight[:, None] * jnp.ones((1, SEQ), jnp.float32)).reshape(tokens, 1)
    cot_rows = lax.all_gather(out_grad, "stream", axis=1, tiled=True)
    cotangent = cot_rows.astype(jnp.float32) * tok_weight
    cot_low = cotangent.astype(jnp.bfloat16)
    d_hidden = jnp.dot(cot_low, down_weight, preferred_element_type=jnp.float32)
    d_hpre = gelu_back(hidden_pre, d_hidden).astype(jnp.bfloat16)
    down_grad = contract_rows(cot_low, hidden)
    up_grad = contract_rows(normed_mlp, d_hpre)
    d_normed_mlp = lax.psum(times_transpose(d_hpre, up_weight), "stream")
    gain_mlp_grad = jnp.sum(d_normed_mlp * hat_mlp, axis=0)
    gain_scaled = d_normed_mlp * mlp_gain[None, :]
    d_residual = cotangent + inv_std_mlp * (
        gain_scaled
        - jnp.mean(gain_scaled, axis=1, keepdims=True)
        - hat_mlp * jnp.mean(gain_scaled * hat_mlp, axis=1, keepdims=True)
    )
    d_branch = d_residual.astype(jnp.bfloat16)
    out_weight_grad = contract_rows(d_branch, heads_out)
    d_heads = jnp.dot(d_branch, out_weight, preferred_element_type=jnp.float32).astype(jnp.bfloat16)
    grad_query, grad_key, grad_value = lax.map(
        attend_backward, (query_seqs, key_seqs, value_seqs, d_heads.reshape(head_shape), lse_all)
    )
    d_proj = jnp.stack(
        [
            grad_query.reshape(tokens, local_width),
            grad_key.reshape(tokens, local_width),
            grad_value.reshape(tokens, local_width),
        ]
    )
    qkv_grad = jnp.einsum("std,stc->dsc", normed, d_proj, preferred_element_type=jnp.float32)
    norm_part = jnp.einsum("stc,dsc->std", d_proj, qkv_weight, preferred_element_type=jnp.float32)
    d_normed = lax.psum_scatter(norm_part, "stream", scatter_dimension=2, tiled=True)
    stream_gain_grad = jnp.sum(d_normed * normed_hat, axis=1)
    grad_norm = d_normed * stream_gain[:, None, :]
    grad_sum = jnp.sum(grad_norm, axis=2)
    grad_hat_sum = jnp.sum(grad_norm * normed_hat, axis=2)
    resid_grad_cols = lax.dynamic_slice_in_dim(d_residual, first_col, local_width, 1)
    part_first, part_second, part_third, part_resid = ([], [], [], [])
    for hist_idx in range(n_hist):
        layer_value = history[hist_idx].astype(jnp.float32)
        part_first.append(jnp.sum(grad_norm * layer_value[None], axis=2))
        part_second.append(jnp.sum(layer_value, axis=1))
        part_third.append(jnp.sum(normed_hat * layer_value[None], axis=2))
        part_resid.append(jnp.sum(resid_grad_cols * layer_value, axis=1))
    grad_sum, grad_hat_sum, sums_first, sums_second, sums_third, sums_resid = lax.psum(
        (
            grad_sum,
            grad_hat_sum,
            jnp.stack(part_first, axis=2),
            jnp.stack(part_second, axis=1),
            jnp.stack(part_third, axis=2),
            jnp.stack(part_resid, axis=1),
        ),
        "stream",
    )
    mean_grad = grad_sum / full_width
    mean_grad_hat = grad_hat_sum / full_width
    coef_qkv = inv_std[:, :, None] * (
        sums_first
        - mean_grad[:, :, None] * sums_second[None]
        - mean_grad_hat[:, :, None] * sums_third
    )
    d_coef = jnp.concatenate(
        [jnp.transpose(coef_qkv, (1, 0, 2)), sums_resid[:, None, :]], axis=1
    ).reshape(tokens, 4 * n_hist)
    d_streams = inv_std[:, :, None] * (
        grad_norm - mean_grad[:, :, None] - normed_hat * mean_grad_hat[:, :, None]
    )
    mix_static_grad = jnp.sum(d_coef, axis=0).reshape(4, n_hist)
    mix_out_grad = contract_rows_high(mix_act, d_coef)
    d_act = times_transpose_high(d_coef, mix_out_float)
    d_mix_pre = gelu_back(mix_pre, d_act)
    d_raw = d_mix_pre * mix_scale
    mix_in_rows_grad = contract_rows_high(last_layer.astype(jnp.float32), d_raw)
    scale_term = (
        jnp.power(mix_scale, 3) / full_width * jnp.sum(d_mix_pre * mix_raw, axis=1, keepdims=True)
    )
    mix_back = times_transpose_high(
        d_raw, mix_in_rows.astype(jnp.float32)
    ) - scale_term * last_layer.astype(jnp.float32)
    grad_layers = []
    for hist_idx in range(n_hist):
        layer_grad = mix_coef[:, 3, hist_idx][:, None] * resid_grad_cols
        for stream_idx in range(3):
            layer_grad = (
                layer_grad + mix_coef[:, stream_idx, hist_idx][:, None] * d_streams[stream_idx]
            )
        if hist_idx == n_hist - 1:
            layer_grad = layer_grad + mix_back
        grad_layers.append(layer_grad.astype(jnp.bfloat16))
    history_grad = jnp.stack(grad_layers)
    qkv_summed, out_weight_summed, up_summed, down_summed = (
        lax.psum_scatter(qkv_grad, "dp", scatter_dimension=0, tiled=True),
        lax.psum_scatter(out_weight_grad, "dp", scatter_dimension=0, tiled=True),
        lax.psum_scatter(up_grad, "dp", scatter_dimension=0, tiled=True),
        lax.psum_scatter(down_grad, "dp", scatter_dimension=0, tiled=True),
    )
    mix_in_summed, mix_out_summed, static_summed, gain_summed, gain_mlp_summed = lax.psum(
        (mix_in_rows_grad, mix_out_grad, mix_static_grad, stream_gain_grad, gain_mlp_grad), "dp"
    )
    return (
        output_cols,
        history_grad,
        mix_in_summed,
        mix_out_summed,
        static_summed,
        gain_summed,
        qkv_summed,
        out_weight_summed,
        gain_mlp_summed,
        up_summed,
        down_summed,
    )


def solution(mesh):
    in_specs = (
        P(None, "dp", "stream"),
        P(),
        P(),
        P(),
        P(None, "stream"),
        P(None, None, "stream"),
        P(None, "stream"),
        P(),
        P(None, "stream"),
        P(None, "stream"),
        P("dp", "stream"),
        P("dp"),
        P(),
    )
    out_specs = (
        P("dp", "stream"),
        P(None, "dp", "stream"),
        P("stream", None),
        P(),
        P(),
        P(None, "stream"),
        P("dp", None, "stream"),
        P("dp", "stream"),
        P(),
        P("dp", "stream"),
        P("dp", "stream"),
    )
    return jax.shard_map(local, mesh=mesh, in_specs=in_specs, out_specs=out_specs, check_vma=False)
```

profile of v0, /device:TPU:0, one launch (start us, length us, event | category | flops | bytes accessed | tf_op | source)
XLA Modules:
  0.0 2251.5 jit_solution(6929410303746302613)
XLA Ops:
  7.2 2.5 convolution_bitcast_fusion.1
  12.1 13.4 psum.119
  25.5 23.0 %all-reduce.13.cloned.1.call-done = f32[1024,44]{0,1:T(8,128)} async-done(((f32[1024,44]{0,1:T(8,128)}), f32[1024,44]{0,1:T(8,128)}) %all-reduce.13.cloned.1.call-update) | async-done | bytes 180240 | tf_op jit(solution)/shard_map/psum | solution.py:163
  53.5 6.1 fusion.62
  59.8 2.1 copy-done.3
  61.9 3.3 fusion.60
  65.3 3.3 fusion.61
  70.0 17.8 all-reduce.4
  88.5 4.4 multiply_convert_fusion.3
  93.7 215.7 %all-gather.3.cloned.1.call-done = bf16[3,1024,2048]{2,1,0:T(8,128)(2,1)} async-done(((bf16[3,1024,512]{2,1,0:T(8,128)(2,1)}), bf16[3,1024,2048]{2,1,0:T(8,128)(2,1)}) %all-gather.3.cloned.1.call-update) | async-done | bytes 12582928 | tf_op jit(solution)/shard_map/all_gather | solution.py:190
  309.4 11.5 convolution_convert_fusion
  326.8 2.4 fusion.10
  330.1 3.6 fusion.133
  333.9 5.8 fusion.216
  339.8 5.1 fusion.66
  347.4 286.6 %all-reduce.15.cloned.1.call-done = f32[1024,2048]{1,0:T(8,128)} async-done(((f32[1024,2048]{1,0:T(8,128)}), f32[1024,2048]{1,0:T(8,128)}) %all-reduce.15.cloned.1.call-update) | async-done | bytes 8388624 | tf_op jit(solution)/shard_map/psum | solution.py:203
  634.0 3.8 reduce_sum.567
  637.9 4.6 multiply_reduce_fusion.3
  644.4 31.8 %multiply_convert_fusion.1 = (bf16[1024,2048]{1,0:T(8,128)(2,1)}, f32[1024,2048]{1,0:T(8,128)}, f32[1024,2048]{1,0:T(8,128)}) fusion(bf16[2048,2048]{1,0:T(8,128)(2,1)} %param.33, f32[1024,2048]{1,0:T(8,128)S(1)} %copy-done.4, f32[2048]{0:T(1024)S(1)} %copy-done.136, f32[1024]{0:T(1024)S(1)} %add_rsqrt_fusion.1, f32[1024]{0:T(1024)S(1)} %broadcast_multiply_fusion.6), kind=kOutput, calls=%fused_computation.14 | convolution fusion | flops 8734638080 | bytes 37765120 | tf_op jit(solution)/shard_map/dot_general | solution.py:208
  676.2 39.1 %all-gather.5.cloned.1.call-done = bf16[1024,2048]{1,0:T(8,128)(2,1)} async-done(((bf16[1024,512]{1,0:T(8,128)(2,1)}), bf16[1024,2048]{1,0:T(8,128)(2,1)}) %all-gather.5.cloned.1.call-update) | async-done | bytes 4194320 | tf_op jit(solution)/shard_map/all_gather | solution.py:220
  715.4 18.8 add_convert_fusion
  736.1 13.4 fusion.218
  749.6 289.4 %all-reduce.17.cloned.1.call-done = f32[1024,2048]{1,0:T(8,128)} async-done(((f32[1024,2048]{1,0:T(8,128)}), f32[1024,2048]{1,0:T(8,128)}) %all-reduce.17.cloned.1.call-update) | async-done | bytes 8388624 | tf_op jit(solution)/shard_map/psum | solution.py:227
  1039.1 8.2 multiply_reduce_fusion
  1048.5 5.6 multiply_add_fusion
  1054.1 2.4 fusion.113
  1057.4 2.8 fusion.219
  1060.7 2.1 fusion.117
  1062.8 9.6 fusion.130
  1072.4 8.6 fusion.122
  1081.1 4.7 fusion.220
  1085.8 6.6 fusion.98
  1093.9 2.0 copy.74
  1095.9 18.1 fusion.126
  1114.1 23.9 %fusion.99 = bf16[1024,4,128]{0,2,1:T(8,128)(2,1)} fusion(f32[512,4,128]{0,2,1:T(8,128)} %fusion.122, bf16[512,4,128]{0,2,1:T(8,128)(2,1)S(1)} %bitcast.400, f32[4,512,1024]{2,1,0:T(8,128)} %fusion.220, f32[4,512,1024]{2,1,0:T(8,128)} %copy-done.12, f32[4,512]{1,0:T(4,128)S(1)} %log_add_fusion, pred[512,1024]{1,0:T(8,128)(4,1)S(1)} %copy-done.24), kind=kOutput, calls=%fused_computation.202 | convolution fusion | flops 560991232 | bytes 19931136 | tf_op jit(solution)/shard_map/while/body/eval_jaxpr/hqk,qhd->khd/dot_general | solution.py:128
  1140.8 15.3 fusion.157
  1156.2 14.6 fusion.217
  1170.8 14.3 convolution_bitcast_fusion
  1185.1 5.5 convert_reduce_fusion
  1190.6 13.2 convert_bitcast_fusion.1
  1203.9 4.6 fusion.67
  1210.5 359.1 %reduce-scatter.9.cloned.1.call-done = f32[3,1024,512]{2,1,0:T(8,128)} async-done(((f32[3,1024,2048]{2,1,0:T(8,128)}), f32[3,1024,512]{2,1,0:T(8,128)}) %reduce-scatter.9.cloned.1.call-update) | async-done | bytes 6291472 | tf_op jit(solution)/shard_map/reduce_scatter | solution.py:250
  1569.8 12.2 multiply_reduce_fusion.6
  1585.5 10.7 multiply_reduce_fusion.17
  1598.1 7.8 fusion.102
  1606.6 16.6 fusion.206
  1623.3 15.2 fusion.44
  1638.6 80.3 %reduce-scatter.7.cloned.1.call-done = f32[1024,512]{1,0:T(8,128)} async-done(((f32[1024,2048]{1,0:T(8,128)}), f32[1024,512]{1,0:T(8,128)}) %reduce-scatter.7.cloned.1.call-update) | async-done | bytes 2097168 | tf_op jit(solution)/shard_map/reduce_scatter | solution.py:211
  1718.9 3.5 add_convert_fusion.11
  1722.5 93.1 %reduce-scatter.11.cloned.1.call-done = f32[256,3,512]{0,2,1:T(8,128)} async-done(((f32[2048,3,512]{0,2,1:T(8,128)}), f32[256,3,512]{0,2,1:T(8,128)}) %reduce-scatter.11.cloned.1.call-update) | async-done | bytes 1572880 | tf_op jit(solution)/shard_map/reduce_scatter | solution.py:311
  1815.6 3.0 copy.83
  1818.6 34.9 %all-reduce.21.cloned.1.call-done = (f32[3,1024]{1,0:T(4,128)}, f32[3,1024]{1,0:T(4,128)}, f32[1024,1,11]{0,1,2:T(1,128)}, f32[1024,11]{0,1:T(8,128)}) async-done(((f32[3,1024]{1,0:T(4,128)}, f32[3,1024]{1,0:T(4,128)}, f32[1024,1,11]{0,1,2:T(1,128)}, f32[1024,11]{0,1:T(8,128)}), (f32[3,1024]{1,0:T(4,128)}, f32[3,1024]{1,0:T(4,128)}, f32[1024,1,11]{0,1,2:T(1,128)}, ...) | async-done | bytes 114704 | tf_op jit(solution)/shard_map/psum | solution.py:263
  1854.9 5.6 subtract_multiply_fusion.1
  1860.6 4.7 fusion.136
  1865.3 3.4 fusion.138
  1868.8 2.6 fusion.140
  1884.7 8.1 all-reduce.23.cloned.1.call-done
  1894.6 2.5 convolution_bitcast_fusion.2
  1897.1 5.8 fusion.121
  1903.3 23.6 %all-reduce.2 = (f32[44,44]{1,0:T(8,128)}, f32[4,11]{0,1:T(8,128)S(1)}, f32[3,512]{1,0:T(4,128)}, f32[2048]{0:T(1024)}) all-reduce(f32[44,44]{1,0:T(8,128)S(1)} %fusion.168, f32[4,11]{0,1:T(8,128)S(1)} %get-tuple-element.237, f32[3,512]{1,0:T(4,128)S(1)} %copy-done.135, ...), channel_id=1, replica_groups=mesh['dp'=8,'stream'=4] {'dp'}, use_global_device_ids=true, to_apply=%region_76.77 | all-reduce | flops 5564 | bytes 44512 | tf_op jit(solution)/shard_map/psum | solution.py:316
  1927.5 20.5 reduce-scatter.13.cloned.1.call-done
  1948.1 120.0 %reduce-scatter.15.cloned.1.call-done = f32[256,2048]{1,0:T(8,128)} async-done(((f32[2048,2048]{1,0:T(8,128)}), f32[256,2048]{1,0:T(8,128)}) %reduce-scatter.15.cloned.1.call-update) | async-done | bytes 2097168 | tf_op jit(solution)/shard_map/reduce_scatter | solution.py:313
  2068.1 120.1 %reduce-scatter.17.cloned.1.call-done = f32[256,2048]{1,0:T(8,128)} async-done(((f32[2048,2048]{1,0:T(8,128)}), f32[256,2048]{1,0:T(8,128)}) %reduce-scatter.17.cloned.1.call-update) | async-done | bytes 2097168 | tf_op jit(solution)/shard_map/reduce_scatter | solution.py:314
  2188.2 55.0 %all-reduce.19.cloned.1.call-done = f32[512,44]{0,1:T(8,128)} async-done(((f32[512,44]{0,1:T(8,128)}), f32[512,44]{0,1:T(8,128)}) %all-reduce.19.cloned.1.call-update) | async-done | bytes 90128 | tf_op jit(solution)/shard_map/psum | solution.py:316
  (413 shorter events, 55.5 us)
Async XLA Ops:
  7.2 326.7 %copy-start = (bf16[2048,512]{1,0:T(8,128)(2,1)S(1)}, bf16[2048,512]{1,0:T(8,128)(2,1)}, u32[]{:S(2)}) copy-start(bf16[2048,512]{1,0:T(8,128)(2,1)} %param.31) | copy-start | bytes 6291460
  7.2 41.3 %all-reduce.13.cloned.1.call-start = ((), (), s32[]{:S(2)}) async-start(), calls=%async_computation.6 | async-start | bytes 393216 | tf_op jit(solution)/shard_map/psum | solution.py:163
  9.8 299.7 %all-gather.3.cloned.1.call-start = ((), (), s32[]{:S(2)}) async-start(), calls=%async_computation.7 | async-start | bytes 15728640 | tf_op jit(solution)/shard_map/all_gather | solution.py:190
  25.5 23.0 %copy-start.132 = (f32[1024]{0:T(1024)}, f32[1024]{0:T(1024)S(1)}, u32[]{:S(2)}) copy-start(f32[1024]{0:T(1024)S(1)} %psum.119) | copy-start | bytes 12292
  25.5 24.3 %copy-start.54 = (f32[1024]{0:T(1024)}, f32[1024]{0:T(1024)S(1)}, u32[]{:S(2)}) copy-start(f32[1024]{0:T(1024)S(1)} %add_rsqrt_fusion.2) | copy-start | bytes 12292
  52.6 287.1 %copy-start.58 = (f32[1024,1,1]{0,2,1:T(1,128)}, f32[1024,1,1]{0,2,1:T(1,128)S(1)}, u32[]{:S(2)}) copy-start(f32[1024,1,1]{0,2,1:T(1,128)S(1)} %get-tuple-element.276) | copy-start | bytes 12292
  52.6 287.1 %copy-start.64 = (f32[1024,1,1]{0,2,1:T(1,128)}, f32[1024,1,1]{0,2,1:T(1,128)S(1)}, u32[]{:S(2)}) copy-start(f32[1024,1,1]{0,2,1:T(1,128)S(1)} %get-tuple-element.277) | copy-start | bytes 12292
  52.6 287.1 %copy-start.70 = (f32[1024,1,1]{0,2,1:T(1,128)}, f32[1024,1,1]{0,2,1:T(1,128)S(1)}, u32[]{:S(2)}) copy-start(f32[1024,1,1]{0,2,1:T(1,128)S(1)} %get-tuple-element.278) | copy-start | bytes 12292
  52.6 287.1 %copy-start.76 = (f32[1024,1,1]{0,2,1:T(1,128)}, f32[1024,1,1]{0,2,1:T(1,128)S(1)}, u32[]{:S(2)}) copy-start(f32[1024,1,1]{0,2,1:T(1,128)S(1)} %get-tuple-element.279) | copy-start | bytes 12292
  52.6 287.1 %copy-start.80 = (f32[1024,1,1]{0,2,1:T(1,128)}, f32[1024,1,1]{0,2,1:T(1,128)S(1)}, u32[]{:S(2)}) copy-start(f32[1024,1,1]{0,2,1:T(1,128)S(1)} %get-tuple-element.280) | copy-start | bytes 12292
  52.6 287.1 %copy-start.90 = (f32[1024,1,1]{0,2,1:T(1,128)}, f32[1024,1,1]{0,2,1:T(1,128)S(1)}, u32[]{:S(2)}) copy-start(f32[1024,1,1]{0,2,1:T(1,128)S(1)} %get-tuple-element.281) | copy-start | bytes 12292
  52.6 287.1 %copy-start.100 = (f32[1024,1,1]{0,2,1:T(1,128)}, f32[1024,1,1]{0,2,1:T(1,128)S(1)}, u32[]{:S(2)}) copy-start(f32[1024,1,1]{0,2,1:T(1,128)S(1)} %get-tuple-element.282) | copy-start | bytes 12292
  53.3 11.9 copy-start.86
  53.4 11.9 copy-start.96
  53.4 11.9 copy-start.106
  53.4 11.9 copy-start.110
  53.4 11.9 copy-start.112
  53.4 11.9 copy-start.114
  53.4 11.9 copy-start.116
  53.4 11.9 copy-start.120
  53.4 11.9 copy-start.124
  53.4 11.9 copy-start.130
  68.7 19.8 copy-start.52
  93.0 541.1 %all-reduce.15.cloned.1.call-start = ((), (), s32[]{:S(2)}) async-start(), calls=%async_computation.8 | async-start | bytes 16777216 | tf_op jit(solution)/shard_map/psum | solution.py:203
  93.3 230.1 %copy-start.30 = (pred[512,512]{0,1:T(8,128)(4,1)}, pred[512,512]{0,1:T(8,128)(4,1)S(1)}, u32[]{:S(2)}) copy-start(pred[512,512]{0,1:T(8,128)(4,1)S(1)} %iota_compare_fusion.1) | copy-start | bytes 786436
  93.7 235.6 %copy-start.23 = (pred[512,1024]{1,0:T(8,128)(4,1)}, pred[512,1024]{1,0:T(8,128)(4,1)S(1)}, u32[]{:S(2)}) copy-start(pred[512,1024]{1,0:T(8,128)(4,1)S(1)} %iota_compare_fusion) | copy-start | bytes 1572868
  344.9 370.5 %all-gather.5.cloned.1.call-start = ((), (), s32[]{:S(2)}) async-start(), calls=%async_computation.10 | async-start | bytes 5242880 | tf_op jit(solution)/shard_map/all_gather | solution.py:220
  345.5 693.6 %all-reduce.17.cloned.1.call-start = ((), (), s32[]{:S(2)}) async-start(), calls=%async_computation.11 | async-start | bytes 16777216 | tf_op jit(solution)/shard_map/psum | solution.py:227
  749.5 820.1 %reduce-scatter.9.cloned.1.call-start = ((), (), s32[]{:S(2)}) async-start(), calls=%async_computation.12 | async-start | bytes 31457280 | tf_op jit(solution)/shard_map/reduce_scatter | solution.py:250
  1095.9 18.2 copy-start.33
  1114.1 26.7 %copy-start.47 = (bf16[1,512,512]{2,1,0:T(8,128)(2,1)S(1)}, bf16[1,512,512]{2,1,0:T(8,128)(2,1)}, u32[]{:S(2)}) copy-start(bf16[1,512,512]{2,1,0:T(8,128)(2,1)} %copy.74) | copy-start | bytes 1572868
  1156.1 562.8 %reduce-scatter.7.cloned.1.call-start = ((), (), s32[]{:S(2)}) async-start(), calls=%async_computation.9 | async-start | bytes 10485760 | tf_op jit(solution)/shard_map/reduce_scatter | solution.py:211
  1170.7 644.8 %reduce-scatter.11.cloned.1.call-start = ((), (), s32[]{:S(2)}) async-start(), calls=%async_computation.14 | async-start | bytes 14155776 | tf_op jit(solution)/shard_map/reduce_scatter | solution.py:311
  1185.1 668.4 %all-reduce.21.cloned.1.call-start = ((), (), s32[]{:S(2)}) async-start(), calls=%async_computation.18 | async-start | bytes 286720 | tf_op jit(solution)/shard_map/psum | solution.py:263
  1185.1 18.7 slice-start.3
  1190.6 13.2 slice-start.4
  1190.6 13.2 slice-start.5
  1203.9 365.8 %copy-start.7 = (f32[1,1024,512]{2,1,0:T(8,128)S(1)}, f32[1,1024,512]{2,1,0:T(8,128)}, u32[]{:S(2)}) copy-start(f32[1,1024,512]{2,1,0:T(8,128)} %copy-done.6) | copy-start | bytes 6291460
  1203.9 365.8 %copy-start.46 = (f32[3,1024]{1,0:T(4,128)S(1)}, f32[3,1024]{1,0:T(4,128)}, u32[]{:S(2)}) copy-start(f32[3,1024]{1,0:T(4,128)} %copy-done.45) | copy-start | bytes 36868
  1203.9 365.8 %copy-start.49 = (f32[3,1024]{1,0:T(4,128)S(1)}, f32[3,1024]{1,0:T(4,128)}, u32[]{:S(2)}) copy-start(f32[3,1024]{1,0:T(4,128)} %copy-done.48) | copy-start | bytes 36868
  1203.9 365.8 %copy-start.53 = (f32[3,512]{1,0:T(4,128)S(1)}, f32[3,512]{1,0:T(4,128)}, u32[]{:S(2)}) copy-start(f32[3,512]{1,0:T(4,128)} %param.29) | copy-start | bytes 18436
  1569.7 12.3 slice-start.8
  1569.7 12.3 copy-start.9
  1569.7 12.3 copy-start.11
  1569.7 12.3 slice-start.9
  1569.7 12.3 copy-start.14
  1569.7 12.8 copy-start.15
  1569.7 13.4 copy-start.16
  1569.7 14.0 copy-start.19
  1569.8 14.6 copy-start.20
  1569.8 15.2 copy-start.21
  1569.8 15.8 copy-start.22
  1585.5 12.6 copy-start.44
  1596.6 296.2 %all-reduce.23.cloned.1.call-start = ((), (), s32[]{:S(2)}) async-start(), calls=%async_computation.19 | async-start | bytes 720896 | tf_op jit(solution)/shard_map/psum | solution.py:263
  1598.1 350.0 %reduce-scatter.13.cloned.1.call-start = ((), (), s32[]{:S(2)}) async-start(), calls=%async_computation.15 | async-start | bytes 4718592 | tf_op jit(solution)/shard_map/reduce_scatter | solution.py:312
  1605.9 462.1 %reduce-scatter.15.cloned.1.call-start = ((), (), s32[]{:S(2)}) async-start(), calls=%async_computation.16 | async-start | bytes 18874368 | tf_op jit(solution)/shard_map/reduce_scatter | solution.py:313
  1623.3 564.9 %reduce-scatter.17.cloned.1.call-start = ((), (), s32[]{:S(2)}) async-start(), calls=%async_computation.17 | async-start | bytes 18874368 | tf_op jit(solution)/shard_map/reduce_scatter | solution.py:314
  1638.5 604.6 %all-reduce.19.cloned.1.call-start = ((), (), s32[]{:S(2)}) async-start(), calls=%async_computation.13 | async-start | bytes 196608 | tf_op jit(solution)/shard_map/psum | solution.py:316
  1860.5 22.2 copy-start.2
  1882.8 11.4 copy-start.40
  1882.8 11.4 copy-start.42
  1882.8 11.7 copy-start.133
  1884.7 12.4 copy-start.139
  1897.1 347.6 %copy-start.1 = (bf16[2048,512]{1,0:T(8,128)(2,1)S(1)}, bf16[2048,512]{1,0:T(8,128)(2,1)}, u32[]{:S(2)}) copy-start(bf16[2048,512]{1,0:T(8,128)(2,1)} %param.31) | copy-start | bytes 6291460
  (104 other events, 487.6 us)
Sparse Core Ops, SparseCore 0:
  10.9 37.5 all-reduce.12
  93.1 216.2 all-gather.2
  345.0 288.9 all-reduce.14
  635.5 79.7 all-gather.4
  749.7 289.3 all-reduce.16
  1156.2 413.3 reduce-scatter.8
  1572.6 146.2 reduce-scatter.6
  1722.4 93.1 reduce-scatter.10
  1818.7 34.6 all-reduce.20
  1855.8 36.9 all-reduce.22
  1897.1 50.9 reduce-scatter.12
  1952.1 115.9 reduce-scatter.14
  2072.2 115.9 reduce-scatter.16
  2191.7 51.4 all-reduce.18
where the time goes:
time: 2260 us; the launch traced here: 2250 us
  waiting for transfers between devices  1750 us (77%)
  matrix products  265 us (12%)
  other arithmetic  134 us (6%)
  blocking collectives  54.9 us (2%)
  local copies, waits for them, and re-layouts  33.4 us (1%)
    reduce_scatter x1, waiting for transfers between devices, local(): lax.psum_scatter(norm_part, 'stream', scatter_dimension=2, tiled=True)  359 us
    psum x1, waiting for transfers between devices, local(): d_normed_mlp = lax.psum(times_transpose(d_hpre, up_weight), 'stream')  289 us
    psum x1, waiting for transfers between devices, local(): residual = lax.psum(branch_part, 'stream')  287 us
    all_gather x1, waiting for transfers between devices, local(): normed = lax.all_gather(normed_cols, 'stream', axis=2, tiled=True)  216 us
    reduce_scatter x1, waiting for transfers between devices, local(): lax.psum_scatter(down_grad, 'dp', scatter_dimension=0, tiled=True)  120 us
    reduce_scatter x1, waiting for transfers between devices, local(): lax.psum_scatter(up_grad, 'dp', scatter_dimension=0, tiled=True)  120 us
    reduce_scatter x1, waiting for transfers between devices, local(): lax.psum_scatter(qkv_grad, 'dp', scatter_dimension=0, tiled=True)  93.1 us
    reduce_scatter x1, waiting for transfers between devices, local(): lax.psum_scatter(mlp_part, 'stream', scatter_dimension=1, tiled=True)  80.3 us
  transfers between devices with their start and end apart: 14, of which 14 were waited for; matrix products, arithmetic and copies ran while one was open for 9% of the time, Pallas kernels for 0%

commit v1 on v0

v1 whole, which is shorter than its diff:
```python
import functools
import math

import jax
import jax.numpy as jnp
from jax import lax
from jax.experimental import pallas as pl
from jax.experimental.pallas import tpu as pltpu
from jax.sharding import PartitionSpec as P

HEAD_DIM = 128
SEQ = 1024
CHUNKS = 2
SUB = 256

HIGH = lax.Precision.HIGHEST
EPS_NORM = 1e-05
EPS_MIX = 1e-06
COT_SCALE = 0.4
F32 = jnp.float32
BF16 = jnp.bfloat16


def gelu_both(values):
    cdf = 0.5 * (1.0 + lax.erf(values * math.sqrt(0.5)))
    density = jnp.exp(-0.5 * jnp.square(values)) * (1.0 / math.sqrt(2.0 * math.pi))
    return values * cdf, cdf + values * density


def dot_tt(former, latter, dims, precision=None):
    return lax.dot_general(
        former, latter, (dims, ((), ())), precision=precision, preferred_element_type=F32
    )


def contract_rows(former, latter):
    return dot_tt(former, latter, ((0,), (0,)))


def times_transpose(former, latter):
    return dot_tt(former, latter, ((1,), (1,)))


def line_gather(piece, member):
    n = lax.axis_size("stream")
    from_low, from_high = [piece], [piece]
    for step in range(1, n):
        up = [(i, i + 1) for i in range(step - 1, n - 1)]
        down = [(i, i - 1) for i in range(1, n - step + 1)]
        from_low.append(lax.ppermute(from_low[-1], "stream", up))
        from_high.append(lax.ppermute(from_high[-1], "stream", down))
    slots = []
    for slot in range(n):
        value = piece
        for at in range(n):
            if at > slot:
                value = jnp.where(member == at, from_low[at - slot], value)
            elif at < slot:
                value = jnp.where(member == at, from_high[slot - at], value)
        slots.append(value)
    return jnp.concatenate(slots, axis=-1)


def line_scatter(block):
    n = lax.axis_size("stream")
    parts = {}

    def part(idx):
        if idx not in parts:
            parts[idx] = block(idx)
        return parts[idx]

    up = down = None
    for step in range(n - 1):
        up_value, down_value = part(n - 1 - step), part(1 + step)
        if up is not None:
            if n - 1 - step == 1 + step:
                up_value = down_value = up_value + up.astype(F32) + down.astype(F32)
            else:
                up_value = up_value + up.astype(F32)
                down_value = down_value + down.astype(F32)
        up = lax.ppermute(up_value.astype(BF16), "stream", [(i, i + 1) for i in range(step + 1)])
        down = lax.ppermute(
            down_value.astype(BF16), "stream", [(i, i - 1) for i in range(n - 1 - step, n)]
        )
    return part(0) + up.astype(F32) + down.astype(F32)


def butterfly(value, axis, merge=jnp.add):
    n = lax.axis_size(axis)
    span = 1
    while span < n:
        other = lax.ppermute(value, axis, [(i, i ^ span) for i in range(n)])
        value = merge(value, other)
        span *= 2
    return value


def merge_moments(width):
    def start(value):
        state = {"count": width}

        def merge(mine, other):
            half = mine.shape[0] // 2
            gap = mine[:half] - other[:half]
            mean = 0.5 * (mine[:half] + other[:half])
            square = mine[half:] + other[half:] + jnp.square(gap) * (0.5 * state["count"])
            state["count"] *= 2
            return jnp.concatenate([mean, square], axis=0)

        return butterfly(value, "stream", merge)

    return start


def attend_forward_kernel(chunk, q_ref, *refs):
    k_refs, v_refs = refs[: chunk + 1], refs[chunk + 1 : 2 * chunk + 2]
    o_ref, lse_ref = refs[2 * chunk + 2 :]
    rows = q_ref.shape[0]
    keys = jnp.concatenate([ref[...] for ref in k_refs], axis=0)
    values = jnp.concatenate([ref[...] for ref in v_refs], axis=0)
    for sub in range(rows // SUB):
        count = chunk * rows + (sub + 1) * SUB
        span = pl.ds(sub * SUB, SUB)
        scores = times_transpose(keys[:count], q_ref[span, :]) * HEAD_DIM ** (-0.5)
        allowed = lax.broadcasted_iota(jnp.int32, (SUB, SUB), 0) <= lax.broadcasted_iota(
            jnp.int32, (SUB, SUB), 1
        )
        tail = jnp.where(allowed, scores[count - SUB :], -1e30)
        scores = jnp.concatenate([scores[: count - SUB], tail], axis=0) if count > SUB else tail
        top = jnp.max(scores, axis=0, keepdims=True)
        weights = jnp.exp(scores - top)
        total = jnp.sum(weights, axis=0, keepdims=True)
        probs = (weights * (1.0 / total)).astype(BF16)
        lse_ref[0, :, span] = top + jnp.log(total)
        out = contract_rows(values[:count], probs)
        o_ref[span, :] = out.T.astype(BF16)


def attend_forward(queries, keys, values):
    rows, width = queries.shape
    heads = width // HEAD_DIM
    chunk = len(keys) - 1
    spec = pl.BlockSpec((rows, HEAD_DIM), lambda h: (0, h))
    return pl.pallas_call(
        functools.partial(attend_forward_kernel, chunk),
        grid=(heads,),
        in_specs=[spec] * (2 * chunk + 3),
        out_specs=[spec, pl.BlockSpec((1, 1, rows), lambda h: (h, 0, 0))],
        out_shape=[
            jax.ShapeDtypeStruct((rows, width), BF16),
            jax.ShapeDtypeStruct((heads, 1, rows), F32),
        ],
        compiler_params=pltpu.CompilerParams(vmem_limit_bytes=48 * 2**20),
        name="attend_forward",
    )(queries, *keys, *values)


def attend_backward_kernel(chunk, last, q_ref, do_ref, lse_ref, *refs):
    n = chunk + 1
    k_refs, v_refs, refs = refs[:n], refs[n : 2 * n], refs[2 * n :]
    if not last:
        dk_in, dv_in, refs = refs[:n], refs[n : 2 * n], refs[2 * n :]
    dq_ref, dk_refs, dv_refs, (dk_acc, dv_acc) = refs[0], refs[1 : 1 + n], refs[1 + n : 1 + 2 * n], refs[1 + 2 * n :]
    rows = q_ref.shape[0]
    keys = jnp.concatenate([ref[...] for ref in k_refs], axis=0)
    values = jnp.concatenate([ref[...] for ref in v_refs], axis=0)
    if last:
        dk_acc[...] = jnp.zeros_like(dk_acc)
        dv_acc[...] = jnp.zeros_like(dv_acc)
    else:
        for i in range(n):
            dk_acc[pl.ds(i * rows, rows), :] = dk_in[i][...]
            dv_acc[pl.ds(i * rows, rows), :] = dv_in[i][...]
    scale = HEAD_DIM ** (-0.5)
    for sub in range(rows // SUB):
        count = chunk * rows + (sub + 1) * SUB
        span = pl.ds(sub * SUB, SUB)
        query, grad = q_ref[span, :], do_ref[span, :]
        scores = times_transpose(keys[:count], query) * scale
        probs = jnp.exp(scores - lse_ref[0, :, span])
        allowed = lax.broadcasted_iota(jnp.int32, (SUB, SUB), 0) <= lax.broadcasted_iota(
            jnp.int32, (SUB, SUB), 1
        )
        tail = jnp.where(allowed, probs[count - SUB :], 0.0)
        probs = jnp.concatenate([probs[: count - SUB], tail], axis=0) if count > SUB else tail
        prob_grad = times_transpose(values[:count], grad)
        row_dot = jnp.sum(probs * prob_grad, axis=0, keepdims=True)
        score_grad = (probs * (prob_grad - row_dot)).astype(BF16)
        dq_ref[span, :] = (contract_rows(keys[:count], score_grad) * scale).T.astype(BF16)
        dk_acc[pl.ds(0, count), :] += jnp.dot(score_grad, query, preferred_element_type=F32) * scale
        dv_acc[pl.ds(0, count), :] += jnp.dot(
            probs.astype(BF16), grad, preferred_element_type=F32
        )
    for i in range(n):
        dk_refs[i][...] = dk_acc[pl.ds(i * rows, rows), :].astype(dk_refs[i].dtype)
        dv_refs[i][...] = dv_acc[pl.ds(i * rows, rows), :].astype(dv_refs[i].dtype)


def attend_backward(queries, grad, lse, keys, values, sums):
    rows, width = queries.shape
    heads = width // HEAD_DIM
    chunk = len(keys) - 1
    n = chunk + 1
    spec = pl.BlockSpec((rows, HEAD_DIM), lambda h: (0, h))
    kinds = [F32] * chunk + [BF16]
    dk_dv = [jax.ShapeDtypeStruct((rows, width), kind) for kind in kinds]
    carried = [] if sums is None else [*sums[0], *sums[1]]
    outs = pl.pallas_call(
        functools.partial(attend_backward_kernel, chunk, sums is None),
        grid=(heads,),
        in_specs=[spec, spec, pl.BlockSpec((1, 1, rows), lambda h: (h, 0, 0))]
        + [spec] * (2 * n + len(carried)),
        out_specs=[spec] * (1 + 2 * n),
        out_shape=[jax.ShapeDtypeStruct((rows, width), BF16), *dk_dv, *dk_dv],
        scratch_shapes=[pltpu.VMEM((n * rows, HEAD_DIM), F32)] * 2,
        compiler_params=pltpu.CompilerParams(vmem_limit_bytes=48 * 2**20),
        name="attend_backward",
    )(queries, grad, lse, *keys, *values, *carried)
    return outs[0], outs[1 : 1 + n], outs[1 + n :]


def local(
    history,
    mix_in,
    mix_out,
    mix_static,
    stream_gain,
    qkv_weight,
    out_weight,
    mlp_gain,
    up_weight,
    down_weight,
    out_grad,
    seq_group,
    group_weight,
):
    n_stream = lax.axis_size("stream")
    member = lax.axis_index("stream")
    n_hist, tokens, width = history.shape
    assert tokens == SEQ
    full_width = width * n_stream
    rows = tokens // CHUNKS
    order = list(reversed(range(CHUNKS)))
    spans = [slice(c * rows, (c + 1) * rows) for c in range(CHUNKS)]
    first_col = member * width

    def rows_of(weight, idx):
        begin = lax.rem(member + idx, n_stream) * width
        return lax.dynamic_slice_in_dim(weight, begin, width, 0)

    moments_of = merge_moments(width)

    def moments(parts):
        means = jnp.stack([jnp.mean(part, axis=1) for part in parts])
        squares = jnp.stack(
            [jnp.sum(jnp.square(part - mean[:, None]), axis=1) for part, mean in zip(parts, means)]
        )
        both = moments_of(jnp.concatenate([means, squares], axis=0))
        count = len(parts)
        inv = lax.rsqrt(both[count:] / full_width + EPS_NORM)
        return [both[i][:, None] for i in range(count)], [inv[i][:, None] for i in range(count)]

    qkv_slices = [qkv_weight[:, s, :] for s in range(3)]
    mix_in_rows = lax.dynamic_slice_in_dim(mix_in, first_col, width, 0)
    mix_out_float = mix_out.astype(F32)
    mlp_gain_cols = lax.dynamic_slice_in_dim(mlp_gain, first_col, width, 0)

    group_pick = (
        seq_group[:, None] == jnp.arange(group_weight.shape[0], dtype=jnp.int32)[None, :]
    ).astype(F32)
    seq_weight = jnp.sum(group_pick * group_weight.astype(F32)[None, :]) * COT_SCALE
    cot_cols = out_grad.astype(F32) * seq_weight
    cot_low_cols = cot_cols.astype(BF16)

    scale_t, raw_t, pre_t, act_t, slope_t, coef_t, coef = {}, {}, {}, {}, {}, {}, {}
    for c in order:
        last = history[n_hist - 1, spans[c]]
        square_part = jnp.sum(jnp.square(last.astype(F32)), axis=1)[None]
        raw_part = dot_tt(mix_in_rows, last, ((0,), (1,)))
        both = butterfly(jnp.concatenate([raw_part, square_part], axis=0), "stream")
        raw_t[c] = both[:-1]
        scale_t[c] = lax.rsqrt(both[-1:] / full_width + EPS_MIX)
        pre_t[c] = scale_t[c] * raw_t[c]
        act_t[c], slope_t[c] = gelu_both(pre_t[c])
        coef_t[c] = dot_tt(mix_out_float, act_t[c], ((0,), (0,)), HIGH) + mix_static.reshape(-1, 1)
        coef[c] = coef_t[c].T

    streams, hat, inv_std, normed = {}, {}, {}, {}
    for c in order:
        mixed = []
        for s in range(4):
            total = coef[c][:, s * n_hist][:, None] * history[0, spans[c]].astype(F32)
            for j in range(1, n_hist):
                total = total + coef[c][:, s * n_hist + j][:, None] * history[j, spans[c]].astype(F32)
            mixed.append(total)
        streams[c] = mixed
        mean, inv_std[c] = moments(mixed[:3])
        hat[c] = [(mixed[s] - mean[s]) * inv_std[c][s] for s in range(3)]
        cols = jnp.stack([(hat[c][s] * stream_gain[s][None, :]).astype(BF16) for s in range(3)])
        normed[c] = line_gather(cols, member)

    cot_low = {c: line_gather(cot_low_cols[spans[c]], member) for c in order}

    proj = {
        c: [
            jnp.dot(normed[c][s], qkv_slices[s], preferred_element_type=F32).astype(BF16)
            for s in range(3)
        ]
        for c in order
    }
    query = {c: proj[c][0] for c in order}
    key = {c: proj[c][1] for c in order}
    value = {c: proj[c][2] for c in order}

    heads_out, lse, residual, hat_mlp, inv_mlp, normed_mlp = {}, {}, {}, {}, {}, {}
    for c in order:
        heads_out[c], lse[c] = attend_forward(
            query[c], [key[i] for i in range(c + 1)], [value[i] for i in range(c + 1)]
        )
        branch = line_scatter(lambda idx: times_transpose(heads_out[c], rows_of(out_weight, idx)))
        residual[c] = streams[c][3] + branch
        (mean,), (inv_mlp[c],) = moments([residual[c]])
        hat_mlp[c] = (residual[c] - mean) * inv_mlp[c]
        normed_mlp[c] = line_gather((hat_mlp[c] * mlp_gain_cols[None, :]).astype(BF16), member)

    hidden, d_hpre, d_normed_mlp = {}, {}, {}
    for c in order:
        d_hidden = jnp.dot(cot_low[c], down_weight, preferred_element_type=F32)
        hidden_pre = jnp.dot(normed_mlp[c], up_weight, preferred_element_type=F32)
        act, slope = gelu_both(hidden_pre)
        hidden[c] = act.astype(BF16)
        d_hpre[c] = (d_hidden * slope).astype(BF16)
        d_normed_mlp[c] = line_scatter(
            lambda idx: times_transpose(d_hpre[c], rows_of(up_weight, idx))
        )

    resid_grad, d_branch, d_heads = {}, {}, {}
    gain_part = 0.0
    for c in order:
        gain_part = gain_part + jnp.sum(d_normed_mlp[c] * hat_mlp[c], axis=0)
        scaled = d_normed_mlp[c] * mlp_gain_cols[None, :]
        sums = butterfly(
            jnp.stack([jnp.sum(scaled, axis=1), jnp.sum(scaled * hat_mlp[c], axis=1)]), "stream"
        )
        sums = sums / full_width
        resid_grad[c] = cot_cols[spans[c]] + inv_mlp[c] * (
            scaled - sums[0][:, None] - hat_mlp[c] * sums[1][:, None]
        )
        d_branch[c] = line_gather(resid_grad[c].astype(BF16), member)
        d_heads[c] = jnp.dot(d_branch[c], out_weight, preferred_element_type=F32).astype(BF16)
    d_proj = {}
    carried = None
    for c in order:
        dq, dk, dv = attend_backward(
            query[c],
            d_heads[c],
            lse[c],
            [key[i] for i in range(c + 1)],
            [value[i] for i in range(c + 1)],
            carried,
        )
        carried = (dk[:c], dv[:c])
        d_proj[c] = [dq, dk[c], dv[c]]

    d_normed = {}
    for c in order:
        d_normed[c] = [
            line_scatter(lambda idx: times_transpose(d_proj[c][s], rows_of(qkv_slices[s], idx)))
            for s in range(3)
        ]

    output = {}
    for c in order:
        output[c] = (
            residual[c]
            + line_scatter(lambda idx: times_transpose(hidden[c], rows_of(down_weight, idx)))
        ).astype(BF16)
    output_cols = jnp.concatenate([output[c] for c in range(CHUNKS)], axis=0)

    def whole(parts, axis=0):
        return jnp.concatenate([parts[c] for c in range(CHUNKS)], axis=axis)

    def weight_grad(former, latter):
        part = contract_rows(whole(former), whole(latter)).astype(BF16)
        return lax.psum_scatter(part, "dp", scatter_dimension=0, tiled=True).astype(F32)

    down_grad = weight_grad(cot_low, hidden)
    up_grad = weight_grad(normed_mlp, d_hpre)
    out_weight_grad = weight_grad(d_branch, heads_out)
    qkv_part = jnp.concatenate(
        [
            contract_rows(
                whole({c: normed[c][s] for c in order}), whole({c: d_proj[c][s] for c in order})
            ).astype(BF16)
            for s in range(3)
        ],
        axis=1,
    )
    qkv_grad = lax.psum_scatter(qkv_part, "dp", scatter_dimension=0, tiled=True).astype(F32)
    qkv_grad = qkv_grad.reshape(qkv_grad.shape[0], 3, width)

    placed = jnp.where(
        jnp.arange(n_stream)[:, None] == member, gain_part[None, :], jnp.zeros((n_stream, width), F32)
    )
    gain_mlp_grad = butterfly(butterfly(placed, "stream"), "dp").reshape(full_width)

    gain_grad = [0.0] * 3
    static_part = 0.0
    mix_out_part = 0.0
    mix_in_part = 0.0
    history_grad = []
    for c in order:
        layers = [history[j, spans[c]].astype(F32) for j in range(n_hist)]
        plain = jnp.stack([jnp.sum(layer, axis=1) for layer in layers])
        hat_dot = [jnp.stack([jnp.sum(hat[c][s] * layer, axis=1) for layer in layers]) for s in range(3)]
        resid_dot = jnp.stack([jnp.sum(resid_grad[c] * layer, axis=1) for layer in layers])
        early = butterfly(jnp.concatenate([plain, *hat_dot, resid_dot], axis=0), "stream")
        plain = early[:n_hist]
        hat_dot = [early[(s + 1) * n_hist : (s + 2) * n_hist] for s in range(3)]
        resid_dot = early[4 * n_hist :]

        grad_norm = [d_normed[c][s] * stream_gain[s][None, :] for s in range(3)]
        for s in range(3):
            gain_grad[s] = gain_grad[s] + jnp.sum(d_normed[c][s] * hat[c][s], axis=0)
        grad_sum = jnp.stack([jnp.sum(g, axis=1) for g in grad_norm])
        grad_hat = jnp.stack([jnp.sum(g * h, axis=1) for g, h in zip(grad_norm, hat[c])])
        grad_dot = [
            jnp.stack([jnp.sum(g * layer, axis=1) for layer in layers]) for g in grad_norm
        ]
        late = butterfly(jnp.concatenate([grad_sum, grad_hat, *grad_dot], axis=0), "stream")
        mean_grad = late[:3] / full_width
        mean_hat = late[3:6] / full_width
        grad_dot = [late[6 + s * n_hist : 6 + (s + 1) * n_hist] for s in range(3)]
        d_coef = jnp.concatenate(
            [
                inv_std[c][s].T
                * (grad_dot[s] - mean_grad[s][None] * plain - mean_hat[s][None] * hat_dot[s])
                for s in range(3)
            ]
            + [resid_dot],
            axis=0,
        )
        d_streams = [
            inv_std[c][s]
            * (grad_norm[s] - mean_grad[s][:, None] - hat[c][s] * mean_hat[s][:, None])
            for s in range(3)
        ] + [resid_grad[c]]
        static_part = static_part + jnp.sum(d_coef, axis=1)
        mix_out_part = mix_out_part + dot_tt(act_t[c], d_coef, ((1,), (1,)), HIGH)
        d_pre = dot_tt(mix_out_float, d_coef, ((1,), (0,)), HIGH) * slope_t[c]
        d_raw = d_pre * scale_t[c]
        last = layers[n_hist - 1]
        mix_in_part = mix_in_part + dot_tt(d_raw, last, ((1,), (0,)), HIGH)
        scale_term = (
            scale_t[c] * scale_t[c] * scale_t[c] / full_width
            * jnp.sum(d_pre * raw_t[c], axis=0, keepdims=True)
        ).T
        mix_back = dot_tt(d_raw, mix_in_rows.astype(F32), ((0,), (1,)), HIGH) - scale_term * last
        grads = []
        for j in range(n_hist):
            total = coef[c][:, 3 * n_hist + j][:, None] * d_streams[3]
            for s in range(3):
                total = total + coef[c][:, s * n_hist + j][:, None] * d_streams[s]
            if j == n_hist - 1:
                total = total + mix_back
            grads.append(total.astype(BF16))
        history_grad.append(jnp.stack(grads))
    history_grad = jnp.concatenate(list(reversed(history_grad)), axis=1)

    stream_gain_grad = butterfly(jnp.stack(gain_grad), "dp")
    small = jnp.concatenate(
        [mix_in_part, mix_out_part, static_part[:, None]], axis=1
    )
    small = butterfly(small, "dp")
    mixh = mix_in.shape[1]
    mix_in_grad = small[:, :width].T
    mix_out_grad = small[:, width : width + 4 * n_hist]
    static_grad = small[:, width + 4 * n_hist].reshape(4, n_hist)
    return (
        output_cols,
        history_grad,
        mix_in_grad,
        mix_out_grad,
        static_grad,
        stream_gain_grad,
        qkv_grad,
        out_weight_grad,
        gain_mlp_grad,
        up_grad,
        down_grad,
    )


def solution(mesh):
    in_specs = (
        P(None, "dp", "stream"),
        P(),
        P(),
        P(),
        P(None, "stream"),
        P(None, None, "stream"),
        P(None, "stream"),
        P(),
        P(None, "stream"),
        P(None, "stream"),
        P("dp", "stream"),
        P("dp"),
        P(),
    )
    out_specs = (
        P("dp", "stream"),
        P(None, "dp", "stream"),
        P("stream", None),
        P(),
        P(),
        P(None, "stream"),
        P("dp", None, "stream"),
        P("dp", "stream"),
        P(),
        P("dp", "stream"),
        P("dp", "stream"),
    )
    return jax.shard_map(local, mesh=mesh, in_specs=in_specs, out_specs=out_specs, check_vma=False)
```

time: 2260 us -> 1330 us (0.59)
  waiting for transfers between devices: 1750 us -> 393 us
  starting transfers between devices: 0.76 us -> 338 us
  local copies, waits for them, and re-layouts: 33.4 us -> 123 us
  blocking collectives: 54.9 us -> 0 us
  other arithmetic: 134 us -> 163 us
  Pallas kernels: 0 us -> 26.1 us
    reduce_scatter x6 -> x4, waiting for transfers between devices: 793 us -> 0.01 us  [the longest x3 0.01 us: weight_grad(): lax.psum_scatter(part, 'dp', scatter_dimension=0, tiled=True).astype(F32)]
    psum x6 -> x0, waiting for transfers between devices: 697 us -> none  [the longest x1 289 us: local(): d_normed_mlp = lax.psum(times_transpose(d_hpre, up_weight), 'stream')]
    ppermute x0 -> x155, waiting for transfers between devices: none -> 393 us  [the longest x24 219 us: line_gather(): from_high.append(lax.ppermute(from_high[-1], 'stream', down))]
    ppermute x0 -> x155, starting transfers between devices: none -> 338 us  [the longest x36 146 us: line_scatter(): lax.ppermute(up_value.astype(BF16), 'stream', [(i, i + 1) for i in range(...]
    all_gather x2 -> x0, waiting for transfers between devices: 255 us -> none  [the longest x1 216 us: local(): normed = lax.all_gather(normed_cols, 'stream', axis=2, tiled=True)]
    unnamed x331 -> x819, local copies, waits for them, and re-layouts: 21.6 us -> 80 us
    psum x3 -> x0, blocking collectives: 54.9 us -> none  [the longest x1 23.6 us: local(): lax.psum((mix_in_rows_grad, mix_out_grad, mix_static_grad, stream_gain_gr...]
    pallas_call x0 -> x4, Pallas kernels: none -> 26.1 us  [the longest x2 14.5 us: attend_backward(): pl.pallas_call(functools.partial(attend_backward_kernel, chunk, sums is N...]
  transfers between devices with their start and end apart: 14 -> 159, of which waited for: 14 -> 59; matrix products, arithmetic and copies ran while one was open for 9% -> 36% of each run, Pallas kernels for 0% -> 2%
where the time goes in v1:
time: 1330 us; the launch traced here: 1310 us
  waiting for transfers between devices  393 us (30%)
  starting transfers between devices  338 us (25%)
  matrix products  245 us (18%)
  other arithmetic  163 us (12%)
  local copies, waits for them, and re-layouts  123 us (9%)
  Pallas kernels  26.1 us (2%)
  between operations  23.5 us (2%)
    ppermute x24, waiting for transfers between devices, line_gather(): from_high.append(lax.ppermute(from_high[-1], 'stream', down))  219 us
    dot_general x66, matrix products, dot_tt(): lax.dot_general(former, latter, (dims, ((), ())), precision=precision, pr...  190 us
    ppermute x36, starting transfers between devices, line_scatter(): lax.ppermute(up_value.astype(BF16), 'stream', [(i, i + 1) for i in range(...  146 us
    ppermute x36, waiting for transfers between devices, line_scatter(): lax.ppermute(up_value.astype(BF16), 'stream', [(i, i + 1) for i in range(...  102 us
    unnamed x819, local copies, waits for them, and re-layouts  80 us
    ppermute x35, starting transfers between devices, butterfly(): other = lax.ppermute(value, axis, [(i, i ^ span) for i in range(n)])  68.4 us
    ppermute x24, starting transfers between devices, line_gather(): from_low.append(lax.ppermute(from_low[-1], 'stream', up))  51 us
    ppermute x36, starting transfers between devices, line_scatter(): lax.ppermute(down_value.astype(BF16), 'stream', [(i, i - 1) for i in rang...  41.2 us
  transfers between devices with their start and end apart: 159, of which 59 were waited for; matrix products, arithmetic and copies ran while one was open for 36% of the time, Pallas kernels for 2%

profile of v1, /device:TPU:0, one launch (start us, length us, event | category | flops | bytes accessed | tf_op | source)
XLA Modules:
  0.0 1313.1 jit_solution(5894145324228105250)
XLA Ops:
  15.3 7.4 fusion.1064
  73.0 6.3 collective-permute-done.1
  129.2 5.8 collective-permute-start.34
  136.3 23.7 %collective-permute-done.7 = bf16[3,512,512]{1,2,0:T(8,128)(2,1)S(1)} collective-permute-done((bf16[3,512,512]{1,2,0:T(8,128)(2,1)S(1)}, bf16[3,512,512]{1,2,0:T(8,128)(2,1)S(1)}, u32[]{:S(2)}, u32[]{:S(2)}) %collective-permute-start.7) | collective-permute-done | bytes 1572896 | tf_op jit(solution)/shard_map/ppermute | solution.py:51
  164.3 22.0 %collective-permute-done.34 = bf16[3,512,512]{1,2,0:T(8,128)(2,1)} collective-permute-done((bf16[3,512,512]{1,2,0:T(8,128)(2,1)S(1)}, bf16[3,512,512]{1,2,0:T(8,128)(2,1)}, u32[]{:S(2)}, u32[]{:S(2)}) %collective-permute-start.34) | collective-permute-done | bytes 1572896 | tf_op jit(solution)/shard_map/ppermute | solution.py:50
  188.0 5.8 collective-permute-done.37
  195.1 32.4 %collective-permute-done.8 = bf16[3,512,512]{1,2,0:T(8,128)(2,1)} collective-permute-done((bf16[3,512,512]{1,2,0:T(8,128)(2,1)S(1)}, bf16[3,512,512]{1,2,0:T(8,128)(2,1)}, u32[]{:S(2)}, u32[]{:S(2)}) %collective-permute-start.8) | collective-permute-done | bytes 1572896 | tf_op jit(solution)/shard_map/ppermute | solution.py:51
  239.5 6.5 collective-permute-start.60
  248.1 13.2 %collective-permute-done.38 = bf16[3,512,512]{1,2,0:T(8,128)(2,1)} collective-permute-done((bf16[3,512,512]{1,2,0:T(8,128)(2,1)}, bf16[3,512,512]{1,2,0:T(8,128)(2,1)}, u32[]{:S(2)}, u32[]{:S(2)}) %collective-permute-start.38) | collective-permute-done | bytes 1572896 | tf_op jit(solution)/shard_map/ppermute | solution.py:51
  262.5 32.4 %collective-permute-done.9 = bf16[3,512,512]{1,2,0:T(8,128)(2,1)} collective-permute-done((bf16[3,512,512]{1,2,0:T(8,128)(2,1)}, bf16[3,512,512]{1,2,0:T(8,128)(2,1)}, u32[]{:S(2)}, u32[]{:S(2)}) %collective-permute-start.9) | collective-permute-done | bytes 1572896 | tf_op jit(solution)/shard_map/ppermute | solution.py:51
  318.7 6.7 collective-permute-done.39
  333.1 7.2 attend_forward.3
  346.1 15.8 %collective-permute-start.40 = (bf16[512,512]{0,1:T(8,128)(2,1)S(1)}, bf16[512,512]{0,1:T(8,128)(2,1)S(1)}, u32[]{:S(2)}, u32[]{:S(2)}) collective-permute-start(bf16[512,512]{0,1:T(8,128)(2,1)S(1)} %get-tuple-element.498), channel_id=1, source_target_pairs={{0,1},{4,5},{8,9},{12,13},{16,17},{20,21},{24,25},{28,29}} | collective-permute-start | bytes 1572872 | tf_op jit(solution)/shard_map/ppermute | solution.py:82
  362.2 5.5 collective-permute-start.13
  379.2 6.3 collective-permute-done.13
  388.0 10.3 collective-permute-start.16
  401.8 7.0 collective-permute-start.17
  412.9 11.9 collective-permute-done.17
  433.7 9.6 collective-permute-done.21
  444.8 9.7 collective-permute-done.45
  457.7 14.7 %collective-permute-done.22 = bf16[512,512]{0,1:T(8,128)(2,1)S(1)} collective-permute-done((bf16[512,512]{0,1:T(8,128)(2,1)S(1)}, bf16[512,512]{0,1:T(8,128)(2,1)S(1)}, u32[]{:S(2)}, u32[]{:S(2)}) %collective-permute-start.22) | collective-permute-done | bytes 524320 | tf_op jit(solution)/shard_map/ppermute | solution.py:51
  484.0 11.2 multiply_convert_fusion.3
  504.4 8.6 multiply_convert_fusion.1
  526.7 6.9 collective-permute-done.66
  550.9 5.2 collective-permute-done.68
  575.4 7.1 collective-permute-start.48
  589.7 9.6 collective-permute-done.51
  601.3 9.2 collective-permute-done.84
  615.3 6.5 collective-permute-done.52
  623.1 5.1 collective-permute-done.85
  628.6 5.3 collective-permute-done.53
  634.2 11.2 multiply_convert_fusion.2
  656.1 11.0 multiply_convert_fusion
  679.0 6.9 collective-permute-done.86
  703.2 5.1 collective-permute-done.88
  737.7 6.1 collective-permute-start.94
  745.8 6.5 collective-permute-done.77
  754.2 9.2 collective-permute-done.97
  765.5 9.2 collective-permute-done.78
  776.7 5.9 collective-permute-done.98
  788.6 5.2 collective-permute-done.99
  795.5 25.4 %fusion.64 = bf16[2048,512]{1,0:T(8,128)(2,1)} fusion(bf16[512,512]{0,1:T(8,128)(2,1)S(1)} %get-tuple-element.334, bf16[512,512]{0,1:T(8,128)(2,1)S(1)} %get-tuple-element.333, bf16[512,512]{0,1:T(8,128)(2,1)S(1)} %get-tuple-element.332, bf16[512,512]{0,1:T(8,128)(2,1)S(1)} %get-tuple-element.331, bf16[512,512]{0,1:T(8,128)(2,1)S(1)} %get-tuple-element.330, ...), kind=kOutput, calls=%fused_computation.104 | convolution fusion | flops 2184183808 | bytes 7340032 | tf_op jit(solution)/shard_map/dot_general | solution.py:31
  821.0 17.7 %convolution_convert_fusion = bf16[2048,2048]{1,0:T(8,128)(2,1)} fusion(bf16[512,512]{0,1:T(8,128)(2,1)} %copy-done.229, bf16[512,512]{0,1:T(8,128)(2,1)} %copy-done.228, bf16[512,512]{0,1:T(8,128)(2,1)} %copy-done.227, bf16[512,512]{0,1:T(8,128)(2,1)} %copy-done.226, bf16[512,512]{0,1:T(8,128)(2,1)} %copy-done.195, bf16[512,512]{0,1:T(8,128)(2,1)} %copy-done.194, ...), kind=kOutput, calls=%fused_computation.1 | convolution fusion | flops 8636071936 | bytes 16777216 | tf_op jit(solution)/shard_map/dot_general | solution.py:31
  850.1 5.9 fusion.1066
  860.0 7.1 slice_bitcast_fusion.2
  867.3 35.7 %convolution_convert_fusion.1 = bf16[2048,2048]{1,0:T(8,128)(2,1)} fusion(bf16[512,512]{0,1:T(8,128)(2,1)S(1)} %copy-done.225, bf16[512,512]{0,1:T(8,128)(2,1)S(1)} %copy-done.223, bf16[512,512]{0,1:T(8,128)(2,1)S(1)} %copy-done.221, bf16[512,512]{0,1:T(8,128)(2,1)S(1)} %copy-done.219, bf16[512,512]{0,1:T(8,128)(2,1)S(1)} %copy-done.190, ...), kind=kOutput, calls=%fused_computation.2 | convolution fusion | flops 8636071936 | bytes 16777216 | tf_op jit(solution)/shard_map/dot_general | solution.py:31
  915.9 9.2 attend_backward.2
  926.3 5.3 attend_backward.3
  959.0 5.3 fusion.73
  964.3 6.1 fusion.70
  970.4 5.5 fusion.67
  1004.0 5.6 collective-permute-done.112
  1038.1 5.2 collective-permute-done.124
  1044.2 5.2 collective-permute-start.114
  1060.6 5.2 collective-permute-done.130
  1071.8 5.2 collective-permute-done.114
  1078.6 5.3 collective-permute-start.125
  1100.8 8.1 collective-permute-start.131
  1113.2 5.8 collective-permute-start.133
  1173.0 6.0 collective-permute-start.142
  1181.4 5.8 collective-permute-start.140
  1192.2 5.9 pad_maximum_fusion.3
  1269.4 8.2 pad_maximum_fusion
  1277.6 16.4 %copy.295 = bf16[11,1024,512]{2,1,0:T(8,128)(2,1)} copy(bf16[11,1024,512]{1,2,0:T(8,128)(2,1)} %pad_maximum_fusion) | data formatting | bytes 23068672
  (1394 shorter events, 667.3 us)
Async XLA Ops:
  7.2 1288.9 %reduce-scatter.7.cloned.1.call-start = ((), (), s32[]{:S(2)}) async-start(), calls=%async_computation.5 | async-start | bytes 2359296 | tf_op jit(solution)/shard_map/reduce_scatter | solution.py:386
  12.3 56.1 %collective-permute-start = (f32[45,512]{1,0:T(8,128)}, f32[45,512]{1,0:T(8,128)}, u32[]{:S(2)}, u32[]{:S(2)}) collective-permute-start(f32[45,512]{1,0:T(8,128)} %pad_maximum_fusion.8), channel_id=1, source_target_pairs={{0,1},{1,0},{2,3},{3,2},{4,5},{5,4},{6,7},{7,6},{8,9},{9,8},{10,11... | collective-permute-start | bytes 276488 | tf_op jit(solution)/shard_map/ppermute | solution.py:93
  25.5 46.5 %collective-permute-start.30 = (f32[45,512]{1,0:T(8,128)S(1)}, f32[45,512]{1,0:T(8,128)S(1)}, u32[]{:S(2)}, u32[]{:S(2)}) collective-permute-start(f32[45,512]{1,0:T(8,128)S(1)} %pad_maximum_fusion.9), channel_id=1, source_target_pairs={{0,1},{1,0},{2,3},{3,2},{4,5},{5,4},{6,7},{7,6},{8,9},{9,8},{10,11... | collective-permute-start | bytes 276488 | tf_op jit(solution)/shard_map/ppermute | solution.py:93
  118.6 43.8 %collective-permute-start.4 = (bf16[3,512,512]{1,2,0:T(8,128)(2,1)S(1)}, bf16[3,512,512]{1,2,0:T(8,128)(2,1)S(1)}, u32[]{:S(2)}, u32[]{:S(2)}) collective-permute-start(bf16[3,512,512]{1,2,0:T(8,128)(2,1)S(1)} %pad_maximum_fusion.4), channel_id=1, source_target_pairs={{0,1},{1,2},{2,3},{4,5},{5,6},{6,7},{8,9},{9,10},{10,11},{12,13},{... | collective-permute-start | bytes 4718600 | tf_op jit(solution)/shard_map/ppermute | solution.py:50
  120.8 39.2 %collective-permute-start.7 = (bf16[3,512,512]{1,2,0:T(8,128)(2,1)S(1)}, bf16[3,512,512]{1,2,0:T(8,128)(2,1)S(1)}, u32[]{:S(2)}, u32[]{:S(2)}) collective-permute-start(bf16[3,512,512]{1,2,0:T(8,128)(2,1)S(1)} %pad_maximum_fusion.4), channel_id=1, source_target_pairs={{1,0},{2,1},{3,2},{5,4},{6,5},{7,6},{9,8},{10,9},{11,10},{13,12},{... | collective-permute-start | bytes 4718600 | tf_op jit(solution)/shard_map/ppermute | solution.py:51
  129.2 57.0 %collective-permute-start.34 = (bf16[3,512,512]{1,2,0:T(8,128)(2,1)S(1)}, bf16[3,512,512]{1,2,0:T(8,128)(2,1)}, u32[]{:S(2)}, u32[]{:S(2)}) collective-permute-start(bf16[3,512,512]{1,2,0:T(8,128)(2,1)S(1)} %pad_maximum_fusion.5), channel_id=1, source_target_pairs={{0,1},{1,2},{2,3},{4,5},{5,6},{6,7},{8,9},{9,10},{10,11},{12,13},{... | collective-permute-start | bytes 4718600 | tf_op jit(solution)/shard_map/ppermute | solution.py:50
  135.0 58.8 %collective-permute-start.37 = (bf16[3,512,512]{1,2,0:T(8,128)(2,1)S(1)}, bf16[3,512,512]{1,2,0:T(8,128)(2,1)}, u32[]{:S(2)}, u32[]{:S(2)}) collective-permute-start(bf16[3,512,512]{1,2,0:T(8,128)(2,1)S(1)} %pad_maximum_fusion.5), channel_id=1, source_target_pairs={{1,0},{2,1},{3,2},{5,4},{6,5},{7,6},{9,8},{10,9},{11,10},{13,12},{... | collective-permute-start | bytes 4718600 | tf_op jit(solution)/shard_map/ppermute | solution.py:51
  161.1 66.4 %collective-permute-start.8 = (bf16[3,512,512]{1,2,0:T(8,128)(2,1)S(1)}, bf16[3,512,512]{1,2,0:T(8,128)(2,1)}, u32[]{:S(2)}, u32[]{:S(2)}) collective-permute-start(bf16[3,512,512]{1,2,0:T(8,128)(2,1)S(1)} %collective-permute-done.7), channel_id=1, source_target_pairs={{1,0},{2,1},{5,4},{6,5},{9,8},{10,9},{13,12},{14,13},{17,16},{18,1... | collective-permute-start | bytes 4718600 | tf_op jit(solution)/shard_map/ppermute | solution.py:51
  162.5 66.4 %collective-permute-start.5 = (bf16[3,512,512]{1,2,0:T(8,128)(2,1)S(1)}, bf16[3,512,512]{1,2,0:T(8,128)(2,1)}, u32[]{:S(2)}, u32[]{:S(2)}) collective-permute-start(bf16[3,512,512]{1,2,0:T(8,128)(2,1)S(1)} %collective-permute-done.4), channel_id=1, source_target_pairs={{1,2},{2,3},{5,6},{6,7},{9,10},{10,11},{13,14},{14,15},{17,18},{18... | collective-permute-start | bytes 4718600 | tf_op jit(solution)/shard_map/ppermute | solution.py:50
  186.2 59.9 %collective-permute-start.35 = (bf16[3,512,512]{1,2,0:T(8,128)(2,1)}, bf16[3,512,512]{1,2,0:T(8,128)(2,1)}, u32[]{:S(2)}, u32[]{:S(2)}) collective-permute-start(bf16[3,512,512]{1,2,0:T(8,128)(2,1)} %collective-permute-done.34), channel_id=1, source_target_pairs={{1,2},{2,3},{5,6},{6,7},{9,10},{10,11},{13,14},{14,15},{17,18},{18... | collective-permute-start | bytes 4718600 | tf_op jit(solution)/shard_map/ppermute | solution.py:50
  193.8 67.4 %collective-permute-start.38 = (bf16[3,512,512]{1,2,0:T(8,128)(2,1)}, bf16[3,512,512]{1,2,0:T(8,128)(2,1)}, u32[]{:S(2)}, u32[]{:S(2)}) collective-permute-start(bf16[3,512,512]{1,2,0:T(8,128)(2,1)} %collective-permute-done.37), channel_id=1, source_target_pairs={{1,0},{2,1},{5,4},{6,5},{9,8},{10,9},{13,12},{14,13},{17,16},{18,1... | collective-permute-start | bytes 4718600 | tf_op jit(solution)/shard_map/ppermute | solution.py:51
  227.5 67.4 %collective-permute-start.9 = (bf16[3,512,512]{1,2,0:T(8,128)(2,1)}, bf16[3,512,512]{1,2,0:T(8,128)(2,1)}, u32[]{:S(2)}, u32[]{:S(2)}) collective-permute-start(bf16[3,512,512]{1,2,0:T(8,128)(2,1)} %collective-permute-done.8), channel_id=1, source_target_pairs={{1,0},{5,4},{9,8},{13,12},{17,16},{21,20},{25,24},{29,28}} | collective-permute-start | bytes 4718600 | tf_op jit(solution)/shard_map/ppermute | solution.py:51
  228.8 68.4 %collective-permute-start.6 = (bf16[3,512,512]{1,2,0:T(8,128)(2,1)}, bf16[3,512,512]{1,2,0:T(8,128)(2,1)}, u32[]{:S(2)}, u32[]{:S(2)}) collective-permute-start(bf16[3,512,512]{1,2,0:T(8,128)(2,1)} %collective-permute-done.5), channel_id=1, source_target_pairs={{2,3},{6,7},{10,11},{14,15},{18,19},{22,23},{26,27},{30,31}} | collective-permute-start | bytes 4718600 | tf_op jit(solution)/shard_map/ppermute | solution.py:50
  239.5 159.5 %collective-permute-start.60 = (bf16[512,512]{0,1:T(8,128)(2,1)}, bf16[512,512]{0,1:T(8,128)(2,1)}, u32[]{:S(2)}, u32[]{:S(2)}) collective-permute-start(bf16[512,512]{0,1:T(8,128)(2,1)} %slice.1164), channel_id=1, source_target_pairs={{0,1},{1,2},{2,3},{4,5},{5,6},{6,7},{8,9},{9,10},{10,11},{12,13},{... | collective-permute-start | bytes 1572872 | tf_op jit(solution)/shard_map/ppermute | solution.py:50
  246.1 69.4 %collective-permute-start.36 = (bf16[3,512,512]{1,2,0:T(8,128)(2,1)}, bf16[3,512,512]{1,2,0:T(8,128)(2,1)}, u32[]{:S(2)}, u32[]{:S(2)}) collective-permute-start(bf16[3,512,512]{1,2,0:T(8,128)(2,1)} %collective-permute-done.35), channel_id=1, source_target_pairs={{2,3},{6,7},{10,11},{14,15},{18,19},{22,23},{26,27},{30,31}} | collective-permute-start | bytes 4718600 | tf_op jit(solution)/shard_map/ppermute | solution.py:50
  261.2 64.2 %collective-permute-start.39 = (bf16[3,512,512]{1,2,0:T(8,128)(2,1)}, bf16[3,512,512]{1,2,0:T(8,128)(2,1)}, u32[]{:S(2)}, u32[]{:S(2)}) collective-permute-start(bf16[3,512,512]{1,2,0:T(8,128)(2,1)} %collective-permute-done.38), channel_id=1, source_target_pairs={{1,0},{5,4},{9,8},{13,12},{17,16},{21,20},{25,24},{29,28}} | collective-permute-start | bytes 4718600 | tf_op jit(solution)/shard_map/ppermute | solution.py:51
  310.2 30.1 %collective-permute-start.11 = (bf16[512,512]{0,1:T(8,128)(2,1)}, bf16[512,512]{0,1:T(8,128)(2,1)}, u32[]{:S(2)}, u32[]{:S(2)}) collective-permute-start(bf16[512,512]{0,1:T(8,128)(2,1)} %get-tuple-element.500), channel_id=1, source_target_pairs={{3,2},{7,6},{11,10},{15,14},{19,18},{23,22},{27,26},{31,30}} | collective-permute-start | bytes 1572872 | tf_op jit(solution)/shard_map/ppermute | solution.py:83
  313.3 27.0 %collective-permute-start.10 = (bf16[512,512]{0,1:T(8,128)(2,1)}, bf16[512,512]{0,1:T(8,128)(2,1)}, u32[]{:S(2)}, u32[]{:S(2)}) collective-permute-start(bf16[512,512]{0,1:T(8,128)(2,1)} %get-tuple-element.502), channel_id=1, source_target_pairs={{0,1},{4,5},{8,9},{12,13},{16,17},{20,21},{24,25},{28,29}} | collective-permute-start | bytes 1572872 | tf_op jit(solution)/shard_map/ppermute | solution.py:82
  344.2 25.5 %collective-permute-start.41 = (bf16[512,512]{0,1:T(8,128)(2,1)S(1)}, bf16[512,512]{0,1:T(8,128)(2,1)S(1)}, u32[]{:S(2)}, u32[]{:S(2)}) collective-permute-start(bf16[512,512]{0,1:T(8,128)(2,1)S(1)} %get-tuple-element.496), channel_id=1, source_target_pairs={{3,2},{7,6},{11,10},{15,14},{19,18},{23,22},{27,26},{31,30}} | collective-permute-start | bytes 1572872 | tf_op jit(solution)/shard_map/ppermute | solution.py:83
  346.1 28.2 %collective-permute-start.40 = (bf16[512,512]{0,1:T(8,128)(2,1)S(1)}, bf16[512,512]{0,1:T(8,128)(2,1)S(1)}, u32[]{:S(2)}, u32[]{:S(2)}) collective-permute-start(bf16[512,512]{0,1:T(8,128)(2,1)S(1)} %get-tuple-element.498), channel_id=1, source_target_pairs={{0,1},{4,5},{8,9},{12,13},{16,17},{20,21},{24,25},{28,29}} | collective-permute-start | bytes 1572872 | tf_op jit(solution)/shard_map/ppermute | solution.py:82
  369.7 30.0 %collective-permute-start.63 = (bf16[512,512]{0,1:T(8,128)(2,1)}, bf16[512,512]{0,1:T(8,128)(2,1)S(1)}, u32[]{:S(2)}, u32[]{:S(2)}) collective-permute-start(bf16[512,512]{0,1:T(8,128)(2,1)} %slice.1164), channel_id=1, source_target_pairs={{1,0},{2,1},{3,2},{5,4},{6,5},{7,6},{9,8},{10,9},{11,10},{13,12},{... | collective-permute-start | bytes 1572872 | tf_op jit(solution)/shard_map/ppermute | solution.py:51
  374.8 33.9 %collective-permute-start.42 = (bf16[512,512]{0,1:T(8,128)(2,1)S(1)}, bf16[512,512]{0,1:T(8,128)(2,1)S(1)}, u32[]{:S(2)}, u32[]{:S(2)}) collective-permute-start(bf16[512,512]{0,1:T(8,128)(2,1)S(1)} %add_convert_fusion.50), channel_id=1, source_target_pairs={{0,1},{1,2},{4,5},{5,6},{8,9},{9,10},{12,13},{13,14},{16,17},{17,1... | collective-permute-start | bytes 1572872 | tf_op jit(solution)/shard_map/ppermute | solution.py:82
  399.0 28.8 %collective-permute-start.61 = (bf16[512,512]{0,1:T(8,128)(2,1)}, bf16[512,512]{0,1:T(8,128)(2,1)S(1)}, u32[]{:S(2)}, u32[]{:S(2)}) collective-permute-start(bf16[512,512]{0,1:T(8,128)(2,1)} %collective-permute-done.60), channel_id=1, source_target_pairs={{1,2},{2,3},{5,6},{6,7},{9,10},{10,11},{13,14},{14,15},{17,18},{18... | collective-permute-start | bytes 1572872 | tf_op jit(solution)/shard_map/ppermute | solution.py:50
  399.7 30.0 %collective-permute-start.64 = (bf16[512,512]{0,1:T(8,128)(2,1)S(1)}, bf16[512,512]{0,1:T(8,128)(2,1)S(1)}, u32[]{:S(2)}, u32[]{:S(2)}) collective-permute-start(bf16[512,512]{0,1:T(8,128)(2,1)S(1)} %collective-permute-done.63), channel_id=1, source_target_pairs={{1,0},{2,1},{5,4},{6,5},{9,8},{10,9},{13,12},{14,13},{17,16},{18,1... | collective-permute-start | bytes 1572872 | tf_op jit(solution)/shard_map/ppermute | solution.py:51
  401.0 25.3 %collective-permute-start.44 = (bf16[512,512]{0,1:T(8,128)(2,1)S(1)}, bf16[512,512]{0,1:T(8,128)(2,1)S(1)}, u32[]{:S(2)}, u32[]{:S(2)}) collective-permute-start(bf16[512,512]{0,1:T(8,128)(2,1)S(1)} %add_convert_fusion.50), channel_id=1, source_target_pairs={{2,1},{3,2},{6,5},{7,6},{10,9},{11,10},{14,13},{15,14},{18,17},{19... | collective-permute-start | bytes 1572872 | tf_op jit(solution)/shard_map/ppermute | solution.py:83
  427.8 26.7 %collective-permute-start.45 = (bf16[512,512]{0,1:T(8,128)(2,1)S(1)}, bf16[512,512]{0,1:T(8,128)(2,1)S(1)}, u32[]{:S(2)}, u32[]{:S(2)}) collective-permute-start(bf16[512,512]{0,1:T(8,128)(2,1)S(1)} %add_convert_fusion.48), channel_id=1, source_target_pairs={{1,0},{2,1},{3,2},{5,4},{6,5},{7,6},{9,8},{10,9},{11,10},{13,12},{... | collective-permute-start | bytes 1572872 | tf_op jit(solution)/shard_map/ppermute | solution.py:83
  429.7 44.1 %collective-permute-start.62 = (bf16[512,512]{0,1:T(8,128)(2,1)S(1)}, bf16[512,512]{0,1:T(8,128)(2,1)S(1)}, u32[]{:S(2)}, u32[]{:S(2)}) collective-permute-start(bf16[512,512]{0,1:T(8,128)(2,1)S(1)} %collective-permute-done.61), channel_id=1, source_target_pairs={{2,3},{6,7},{10,11},{14,15},{18,19},{22,23},{26,27},{30,31}} | collective-permute-start | bytes 1572872 | tf_op jit(solution)/shard_map/ppermute | solution.py:50
  430.4 43.4 %collective-permute-start.65 = (bf16[512,512]{0,1:T(8,128)(2,1)S(1)}, bf16[512,512]{0,1:T(8,128)(2,1)S(1)}, u32[]{:S(2)}, u32[]{:S(2)}) collective-permute-start(bf16[512,512]{0,1:T(8,128)(2,1)S(1)} %collective-permute-done.64), channel_id=1, source_target_pairs={{1,0},{5,4},{9,8},{13,12},{17,16},{21,20},{25,24},{29,28}} | collective-permute-start | bytes 1572872 | tf_op jit(solution)/shard_map/ppermute | solution.py:51
  443.2 29.2 %collective-permute-start.22 = (bf16[512,512]{0,1:T(8,128)(2,1)S(1)}, bf16[512,512]{0,1:T(8,128)(2,1)S(1)}, u32[]{:S(2)}, u32[]{:S(2)}) collective-permute-start(bf16[512,512]{0,1:T(8,128)(2,1)S(1)} %collective-permute-done.21), channel_id=1, source_target_pairs={{1,0},{2,1},{5,4},{6,5},{9,8},{10,9},{13,12},{14,13},{17,16},{18,1... | collective-permute-start | bytes 1572872 | tf_op jit(solution)/shard_map/ppermute | solution.py:51
  475.1 108.7 %collective-permute-start.80 = (bf16[512,512]{0,1:T(8,128)(2,1)S(1)}, bf16[512,512]{0,1:T(8,128)(2,1)S(1)}, u32[]{:S(2)}, u32[]{:S(2)}) collective-permute-start(bf16[512,512]{0,1:T(8,128)(2,1)S(1)} %get-tuple-element.344), channel_id=1, source_target_pairs={{0,1},{1,2},{2,3},{4,5},{5,6},{6,7},{8,9},{9,10},{10,11},{12,13},{... | collective-permute-start | bytes 1572872 | tf_op jit(solution)/shard_map/ppermute | solution.py:50
  479.8 46.2 %collective-permute-start.47 = (f32[2,512]{1,0:T(2,128)S(1)}, f32[2,512]{1,0:T(2,128)S(1)}, u32[]{:S(2)}, u32[]{:S(2)}) collective-permute-start(f32[2,512]{1,0:T(2,128)S(1)} %pad_maximum_fusion.20), channel_id=1, source_target_pairs={{0,2},{1,3},{2,0},{3,1},{4,6},{5,7},{6,4},{7,5},{8,10},{9,11},{10,... | collective-permute-start | bytes 12296 | tf_op jit(solution)/shard_map/ppermute | solution.py:93
  585.1 25.5 %collective-permute-start.84 = (bf16[512,512]{0,1:T(8,128)(2,1)S(1)}, bf16[512,512]{0,1:T(8,128)(2,1)S(1)}, u32[]{:S(2)}, u32[]{:S(2)}) collective-permute-start(bf16[512,512]{0,1:T(8,128)(2,1)S(1)} %collective-permute-done.83), channel_id=1, source_target_pairs={{1,0},{2,1},{5,4},{6,5},{9,8},{10,9},{13,12},{14,13},{17,16},{18,1... | collective-permute-start | bytes 1572872 | tf_op jit(solution)/shard_map/ppermute | solution.py:51
  589.0 25.6 %collective-permute-start.49 = (bf16[512,512]{0,1:T(8,128)(2,1)S(1)}, bf16[512,512]{0,1:T(8,128)(2,1)S(1)}, u32[]{:S(2)}, u32[]{:S(2)}) collective-permute-start(bf16[512,512]{0,1:T(8,128)(2,1)S(1)} %collective-permute-done.48), channel_id=1, source_target_pairs={{1,2},{2,3},{5,6},{6,7},{9,10},{10,11},{13,14},{14,15},{17,18},{18... | collective-permute-start | bytes 1572872 | tf_op jit(solution)/shard_map/ppermute | solution.py:50
  628.5 49.7 %collective-permute-start.73 = (f32[2,512]{1,0:T(2,128)S(1)}, f32[2,512]{1,0:T(2,128)S(1)}, u32[]{:S(2)}, u32[]{:S(2)}) collective-permute-start(f32[2,512]{1,0:T(2,128)S(1)} %fusion.1034), channel_id=1, source_target_pairs={{0,2},{1,3},{2,0},{3,1},{4,6},{5,7},{6,4},{7,5},{8,10},{9,11},{10,... | collective-permute-start | bytes 12296 | tf_op jit(solution)/shard_map/ppermute | solution.py:93
  820.9 477.0 %reduce-scatter.11.cloned.1.call-start = ((), (), s32[]{:S(2)}) async-start(), calls=%async_computation.7 | async-start | bytes 9437184 | tf_op jit(solution)/shard_map/reduce_scatter | solution.py:386
  838.7 462.0 %reduce-scatter.9.cloned.1.call-start = ((), (), s32[]{:S(2)}) async-start(), calls=%async_computation.6 | async-start | bytes 9437184 | tf_op jit(solution)/shard_map/reduce_scatter | solution.py:386
  867.2 35.9 %collective-permute-start.152 = (f32[4,512]{1,0:T(4,128)S(1)}, f32[4,512]{1,0:T(4,128)S(1)}, u32[]{:S(2)}, u32[]{:S(2)}) collective-permute-start(f32[4,512]{1,0:T(4,128)S(1)} %fusion.1166), channel_id=1, source_target_pairs={{0,4},{4,0},{8,12},{12,8},{16,20},{20,16},{24,28},{28,24},{1,5},{5... | collective-permute-start | bytes 24584 | tf_op jit(solution)/shard_map/ppermute | solution.py:93
  903.0 400.5 %reduce-scatter.5.cloned.1.call-start = ((), (), s32[]{:S(2)}) async-start(), calls=%async_computation.4 | async-start | bytes 7077888 | tf_op jit(solution)/shard_map/reduce_scatter | solution.py:400
  948.2 28.7 %collective-permute-start.101 = (bf16[512,512]{0,1:T(8,128)(2,1)}, bf16[512,512]{0,1:T(8,128)(2,1)}, u32[]{:S(2)}, u32[]{:S(2)}) collective-permute-start(bf16[512,512]{0,1:T(8,128)(2,1)} %get-tuple-element.538), channel_id=1, source_target_pairs={{3,2},{7,6},{11,10},{15,14},{19,18},{23,22},{27,26},{31,30}} | collective-permute-start | bytes 1572872 | tf_op jit(solution)/shard_map/ppermute | solution.py:83
  949.7 28.1 %collective-permute-start.100 = (bf16[512,512]{0,1:T(8,128)(2,1)}, bf16[512,512]{0,1:T(8,128)(2,1)}, u32[]{:S(2)}, u32[]{:S(2)}) collective-permute-start(bf16[512,512]{0,1:T(8,128)(2,1)} %get-tuple-element.540), channel_id=1, source_target_pairs={{0,1},{4,5},{8,9},{12,13},{16,17},{20,21},{24,25},{28,29}} | collective-permute-start | bytes 1572872 | tf_op jit(solution)/shard_map/ppermute | solution.py:82
  953.0 28.0 %collective-permute-start.123 = (bf16[512,512]{0,1:T(8,128)(2,1)}, bf16[512,512]{0,1:T(8,128)(2,1)}, u32[]{:S(2)}, u32[]{:S(2)}) collective-permute-start(bf16[512,512]{0,1:T(8,128)(2,1)} %get-tuple-element.524), channel_id=1, source_target_pairs={{3,2},{7,6},{11,10},{15,14},{19,18},{23,22},{27,26},{31,30}} | collective-permute-start | bytes 1572872 | tf_op jit(solution)/shard_map/ppermute | solution.py:83
  954.4 27.2 %collective-permute-start.122 = (bf16[512,512]{0,1:T(8,128)(2,1)}, bf16[512,512]{0,1:T(8,128)(2,1)}, u32[]{:S(2)}, u32[]{:S(2)}) collective-permute-start(bf16[512,512]{0,1:T(8,128)(2,1)} %get-tuple-element.526), channel_id=1, source_target_pairs={{0,1},{4,5},{8,9},{12,13},{16,17},{20,21},{24,25},{28,29}} | collective-permute-start | bytes 1572872 | tf_op jit(solution)/shard_map/ppermute | solution.py:82
  956.5 30.7 %collective-permute-start.106 = (bf16[512,512]{0,1:T(8,128)(2,1)}, bf16[512,512]{0,1:T(8,128)(2,1)}, u32[]{:S(2)}, u32[]{:S(2)}) collective-permute-start(bf16[512,512]{0,1:T(8,128)(2,1)} %get-tuple-element.544), channel_id=1, source_target_pairs={{0,1},{4,5},{8,9},{12,13},{16,17},{20,21},{24,25},{28,29}} | collective-permute-start | bytes 1572872 | tf_op jit(solution)/shard_map/ppermute | solution.py:82
  981.7 27.9 %collective-permute-start.112 = (bf16[512,512]{0,1:T(8,128)(2,1)S(1)}, bf16[512,512]{0,1:T(8,128)(2,1)S(1)}, u32[]{:S(2)}, u32[]{:S(2)}) collective-permute-start(bf16[512,512]{0,1:T(8,128)(2,1)S(1)} %copy-done.210), channel_id=1, source_target_pairs={{0,1},{4,5},{8,9},{12,13},{16,17},{20,21},{24,25},{28,29}} | collective-permute-start | bytes 1572872 | tf_op jit(solution)/shard_map/ppermute | solution.py:82
  987.9 32.9 %collective-permute-start.134 = (bf16[512,512]{0,1:T(8,128)(2,1)S(1)}, bf16[512,512]{0,1:T(8,128)(2,1)S(1)}, u32[]{:S(2)}, u32[]{:S(2)}) collective-permute-start(bf16[512,512]{0,1:T(8,128)(2,1)S(1)} %copy-done.208), channel_id=1, source_target_pairs={{0,1},{4,5},{8,9},{12,13},{16,17},{20,21},{24,25},{28,29}} | collective-permute-start | bytes 1572872 | tf_op jit(solution)/shard_map/ppermute | solution.py:82
  999.0 33.0 %collective-permute-start.102 = (bf16[512,512]{0,1:T(8,128)(2,1)S(1)}, bf16[512,512]{0,1:T(8,128)(2,1)S(1)}, u32[]{:S(2)}, u32[]{:S(2)}) collective-permute-start(bf16[512,512]{0,1:T(8,128)(2,1)S(1)} %add_convert_fusion.37), channel_id=1, source_target_pairs={{0,1},{1,2},{4,5},{5,6},{8,9},{9,10},{12,13},{13,14},{16,17},{17,1... | collective-permute-start | bytes 1572872 | tf_op jit(solution)/shard_map/ppermute | solution.py:82
  1010.3 33.0 %collective-permute-start.124 = (bf16[512,512]{0,1:T(8,128)(2,1)S(1)}, bf16[512,512]{0,1:T(8,128)(2,1)S(1)}, u32[]{:S(2)}, u32[]{:S(2)}) collective-permute-start(bf16[512,512]{0,1:T(8,128)(2,1)S(1)} %add_convert_fusion.18), channel_id=1, source_target_pairs={{0,1},{1,2},{4,5},{5,6},{8,9},{9,10},{12,13},{13,14},{16,17},{17,1... | collective-permute-start | bytes 1572872 | tf_op jit(solution)/shard_map/ppermute | solution.py:82
  1021.5 33.0 %collective-permute-start.108 = (bf16[512,512]{0,1:T(8,128)(2,1)S(1)}, bf16[512,512]{0,1:T(8,128)(2,1)S(1)}, u32[]{:S(2)}, u32[]{:S(2)}) collective-permute-start(bf16[512,512]{0,1:T(8,128)(2,1)S(1)} %add_convert_fusion.34), channel_id=1, source_target_pairs={{0,1},{1,2},{4,5},{5,6},{8,9},{9,10},{12,13},{13,14},{16,17},{17,1... | collective-permute-start | bytes 1572872 | tf_op jit(solution)/shard_map/ppermute | solution.py:82
  1032.9 32.8 %collective-permute-start.130 = (bf16[512,512]{0,1:T(8,128)(2,1)S(1)}, bf16[512,512]{0,1:T(8,128)(2,1)S(1)}, u32[]{:S(2)}, u32[]{:S(2)}) collective-permute-start(bf16[512,512]{0,1:T(8,128)(2,1)S(1)} %add_convert_fusion.15), channel_id=1, source_target_pairs={{0,1},{1,2},{4,5},{5,6},{8,9},{9,10},{12,13},{13,14},{16,17},{17,1... | collective-permute-start | bytes 1572872 | tf_op jit(solution)/shard_map/ppermute | solution.py:82
  1044.2 32.8 %collective-permute-start.114 = (bf16[512,512]{0,1:T(8,128)(2,1)S(1)}, bf16[512,512]{0,1:T(8,128)(2,1)S(1)}, u32[]{:S(2)}, u32[]{:S(2)}) collective-permute-start(bf16[512,512]{0,1:T(8,128)(2,1)S(1)} %add_convert_fusion.31), channel_id=1, source_target_pairs={{0,1},{1,2},{4,5},{5,6},{8,9},{9,10},{12,13},{13,14},{16,17},{17,1... | collective-permute-start | bytes 1572872 | tf_op jit(solution)/shard_map/ppermute | solution.py:82
  1055.4 32.8 %collective-permute-start.136 = (bf16[512,512]{0,1:T(8,128)(2,1)S(1)}, bf16[512,512]{0,1:T(8,128)(2,1)S(1)}, u32[]{:S(2)}, u32[]{:S(2)}) collective-permute-start(bf16[512,512]{0,1:T(8,128)(2,1)S(1)} %add_convert_fusion.12), channel_id=1, source_target_pairs={{0,1},{1,2},{4,5},{5,6},{8,9},{9,10},{12,13},{13,14},{16,17},{17,1... | collective-permute-start | bytes 1572872 | tf_op jit(solution)/shard_map/ppermute | solution.py:82
  1066.6 32.8 %collective-permute-start.103 = (bf16[512,512]{0,1:T(8,128)(2,1)S(1)}, bf16[512,512]{0,1:T(8,128)(2,1)S(1)}, u32[]{:S(2)}, u32[]{:S(2)}) collective-permute-start(bf16[512,512]{0,1:T(8,128)(2,1)S(1)} %add_convert_fusion.36), channel_id=1, source_target_pairs={{0,1},{1,2},{2,3},{4,5},{5,6},{6,7},{8,9},{9,10},{10,11},{12,13},{... | collective-permute-start | bytes 1572872 | tf_op jit(solution)/shard_map/ppermute | solution.py:82
  1078.6 34.6 %collective-permute-start.125 = (bf16[512,512]{0,1:T(8,128)(2,1)S(1)}, bf16[512,512]{0,1:T(8,128)(2,1)S(1)}, u32[]{:S(2)}, u32[]{:S(2)}) collective-permute-start(bf16[512,512]{0,1:T(8,128)(2,1)S(1)} %add_convert_fusion.17), channel_id=1, source_target_pairs={{0,1},{1,2},{2,3},{4,5},{5,6},{6,7},{8,9},{9,10},{10,11},{12,13},{... | collective-permute-start | bytes 1572872 | tf_op jit(solution)/shard_map/ppermute | solution.py:82
  1088.2 30.8 %collective-permute-start.127 = (bf16[512,512]{0,1:T(8,128)(2,1)S(1)}, bf16[512,512]{0,1:T(8,128)(2,1)S(1)}, u32[]{:S(2)}, u32[]{:S(2)}) collective-permute-start(bf16[512,512]{0,1:T(8,128)(2,1)S(1)} %add_convert_fusion.16), channel_id=1, source_target_pairs={{1,0},{2,1},{3,2},{5,4},{6,5},{7,6},{9,8},{10,9},{11,10},{13,12},{... | collective-permute-start | bytes 1572872 | tf_op jit(solution)/shard_map/ppermute | solution.py:83
  1089.7 38.2 %collective-permute-start.109 = (bf16[512,512]{0,1:T(8,128)(2,1)S(1)}, bf16[512,512]{0,1:T(8,128)(2,1)S(1)}, u32[]{:S(2)}, u32[]{:S(2)}) collective-permute-start(bf16[512,512]{0,1:T(8,128)(2,1)S(1)} %add_convert_fusion.33), channel_id=1, source_target_pairs={{0,1},{1,2},{2,3},{4,5},{5,6},{6,7},{8,9},{9,10},{10,11},{12,13},{... | collective-permute-start | bytes 1572872 | tf_op jit(solution)/shard_map/ppermute | solution.py:82
  1099.5 29.9 %collective-permute-start.111 = (bf16[512,512]{0,1:T(8,128)(2,1)S(1)}, bf16[512,512]{0,1:T(8,128)(2,1)S(1)}, u32[]{:S(2)}, u32[]{:S(2)}) collective-permute-start(bf16[512,512]{0,1:T(8,128)(2,1)S(1)} %add_convert_fusion.32), channel_id=1, source_target_pairs={{1,0},{2,1},{3,2},{5,4},{6,5},{7,6},{9,8},{10,9},{11,10},{13,12},{... | collective-permute-start | bytes 1572872 | tf_op jit(solution)/shard_map/ppermute | solution.py:83
  1100.8 37.5 %collective-permute-start.131 = (bf16[512,512]{0,1:T(8,128)(2,1)S(1)}, bf16[512,512]{0,1:T(8,128)(2,1)S(1)}, u32[]{:S(2)}, u32[]{:S(2)}) collective-permute-start(bf16[512,512]{0,1:T(8,128)(2,1)S(1)} %add_convert_fusion.14), channel_id=1, source_target_pairs={{0,1},{1,2},{2,3},{4,5},{5,6},{6,7},{8,9},{9,10},{10,11},{12,13},{... | collective-permute-start | bytes 1572872 | tf_op jit(solution)/shard_map/ppermute | solution.py:82
  1113.2 26.4 %collective-permute-start.133 = (bf16[512,512]{0,1:T(8,128)(2,1)S(1)}, bf16[512,512]{0,1:T(8,128)(2,1)S(1)}, u32[]{:S(2)}, u32[]{:S(2)}) collective-permute-start(bf16[512,512]{0,1:T(8,128)(2,1)S(1)} %add_convert_fusion.13), channel_id=1, source_target_pairs={{1,0},{2,1},{3,2},{5,4},{6,5},{7,6},{9,8},{10,9},{11,10},{13,12},{... | collective-permute-start | bytes 1572872 | tf_op jit(solution)/shard_map/ppermute | solution.py:83
  1119.0 25.4 %collective-permute-start.115 = (bf16[512,512]{0,1:T(8,128)(2,1)S(1)}, bf16[512,512]{0,1:T(8,128)(2,1)S(1)}, u32[]{:S(2)}, u32[]{:S(2)}) collective-permute-start(bf16[512,512]{0,1:T(8,128)(2,1)S(1)} %add_convert_fusion.30), channel_id=1, source_target_pairs={{0,1},{1,2},{2,3},{4,5},{5,6},{6,7},{8,9},{9,10},{10,11},{12,13},{... | collective-permute-start | bytes 1572872 | tf_op jit(solution)/shard_map/ppermute | solution.py:82
  1163.1 39.9 %collective-permute-start.120 = (f32[55,512]{1,0:T(8,128)S(1)}, f32[55,512]{1,0:T(8,128)}, u32[]{:S(2)}, u32[]{:S(2)}) collective-permute-start(f32[55,512]{1,0:T(8,128)S(1)} %concatenate.142), channel_id=1, source_target_pairs={{0,1},{1,0},{2,3},{3,2},{4,5},{5,4},{6,7},{7,6},{8,9},{9,8},{10,11... | collective-permute-start | bytes 337928 | tf_op jit(solution)/shard_map/ppermute | solution.py:93
  1173.0 33.9 %collective-permute-start.142 = (f32[55,512]{1,0:T(8,128)S(1)}, f32[55,512]{1,0:T(8,128)}, u32[]{:S(2)}, u32[]{:S(2)}) collective-permute-start(f32[55,512]{1,0:T(8,128)S(1)} %concatenate.145), channel_id=1, source_target_pairs={{0,1},{1,0},{2,3},{3,2},{4,5},{5,4},{6,7},{7,6},{8,9},{9,8},{10,11... | collective-permute-start | bytes 337928 | tf_op jit(solution)/shard_map/ppermute | solution.py:93
  1204.0 42.9 %collective-permute-start.121 = (f32[55,512]{1,0:T(8,128)S(1)}, f32[55,512]{1,0:T(8,128)S(1)}, u32[]{:S(2)}, u32[]{:S(2)}) collective-permute-start(f32[55,512]{1,0:T(8,128)S(1)} %add.1537), channel_id=1, source_target_pairs={{0,2},{1,3},{2,0},{3,1},{4,6},{5,7},{6,4},{7,5},{8,10},{9,11},{10,... | collective-permute-start | bytes 337928 | tf_op jit(solution)/shard_map/ppermute | solution.py:93
  1207.9 39.1 %collective-permute-start.143 = (f32[55,512]{1,0:T(8,128)S(1)}, f32[55,512]{1,0:T(8,128)S(1)}, u32[]{:S(2)}, u32[]{:S(2)}) collective-permute-start(f32[55,512]{1,0:T(8,128)S(1)} %add.1594), channel_id=1, source_target_pairs={{0,2},{1,3},{2,0},{3,1},{4,6},{5,7},{6,4},{7,5},{8,10},{9,11},{10,... | collective-permute-start | bytes 337928 | tf_op jit(solution)/shard_map/ppermute | solution.py:93
  1267.9 26.1 %collective-permute-start.146 = (f32[44,557]{1,0:T(8,128)S(1)}, f32[44,557]{1,0:T(8,128)S(1)}, u32[]{:S(2)}, u32[]{:S(2)}) collective-permute-start(f32[44,557]{1,0:T(8,128)S(1)} %add.1603), channel_id=1, source_target_pairs={{0,16},{4,20},{8,24},{12,28},{16,0},{20,4},{24,8},{28,12},{1,17},{... | collective-permute-start | bytes 294104 | tf_op jit(solution)/shard_map/ppermute | solution.py:93
  (491 other events, 10702.8 us)
Sparse Core Ops, SparseCore 0:
  821.0 39.3 reduce-scatter.6
  864.3 71.4 reduce-scatter.10
  939.3 71.2 reduce-scatter.8
  1198.2 59.9 reduce-scatter.4

commit v2 on v1

v2 whole, which is shorter than its diff:
```python
import functools
import math

import jax
import jax.numpy as jnp
from jax import lax
from jax.experimental import pallas as pl
from jax.experimental.pallas import tpu as pltpu
from jax.sharding import PartitionSpec as P

HEAD_DIM = 128
SEQ = 1024
CHUNKS = 2
SUB = 256

HIGH = lax.Precision.HIGHEST
EPS_NORM = 1e-05
EPS_MIX = 1e-06
COT_SCALE = 0.4
F32 = jnp.float32
BF16 = jnp.bfloat16


def gelu_both(values):
    cdf = 0.5 * (1.0 + lax.erf(values * math.sqrt(0.5)))
    density = jnp.exp(-0.5 * jnp.square(values)) * (1.0 / math.sqrt(2.0 * math.pi))
    return values * cdf, cdf + values * density


def dot_tt(former, latter, dims, precision=None):
    return lax.dot_general(
        former, latter, (dims, ((), ())), precision=precision, preferred_element_type=F32
    )


def contract_rows(former, latter):
    return dot_tt(former, latter, ((0,), (0,)))


def times_transpose(former, latter):
    return dot_tt(former, latter, ((1,), (1,)))


def after(value, *others):
    return lax.optimization_barrier((value, *others))[0]


class Order:
    def __init__(self):
        self.tick = ()

    def hold(self, value):
        return after(value, *self.tick) if self.tick else value

    def did(self, *outs):
        self.tick = (*self.tick, *outs)

    def send(self, *chains):
        items = [chain.items() for chain in chains]
        flat = [value for chain_items in items for value, _, _ in chain_items]
        held = lax.optimization_barrier((*flat, *self.tick))[: len(flat)]
        self.tick = tuple(held)
        at = 0
        for chain, chain_items in zip(chains, items):
            got = []
            for _, axis, perm in chain_items:
                got.append(lax.ppermute(held[at], axis, perm))
                at += 1
            chain.take(got)


class LineGather:
    def __init__(self, piece, member):
        self.piece, self.member = piece, member
        self.low, self.high = [piece], [piece]

    def items(self):
        n, step = lax.axis_size("stream"), len(self.low)
        return [
            (self.low[-1], "stream", [(i, i + 1) for i in range(step - 1, n - 1)]),
            (self.high[-1], "stream", [(i, i - 1) for i in range(1, n - step + 1)]),
        ]

    def take(self, got):
        self.low.append(got[0])
        self.high.append(got[1])

    def value(self):
        n, member = lax.axis_size("stream"), self.member
        slots = []
        for slot in range(n):
            value = self.piece
            for at in range(n):
                if at > slot:
                    value = jnp.where(member == at, self.low[at - slot], value)
                elif at < slot:
                    value = jnp.where(member == at, self.high[slot - at], value)
            slots.append(value)
        return jnp.concatenate(slots, axis=-1)


class LineScatter:
    def __init__(self, order, block):
        self.order, self.block = order, block
        self.parts, self.came, self.step = {}, None, 0

    def part(self, idx):
        if idx not in self.parts:
            self.parts[idx] = self.block(idx, lambda value: value)
        return self.parts[idx]

    def items(self):
        n, step = lax.axis_size("stream"), self.step
        up_idx, down_idx = n - 1 - step, 1 + step
        up_value, down_value = self.part(up_idx), self.part(down_idx)
        if self.came is not None:
            up, down = [got.astype(F32) for got in self.came]
            if up_idx == down_idx:
                up_value = down_value = up_value + up + down
            else:
                up_value, down_value = up_value + up, down_value + down
        return [
            (up_value.astype(BF16), "stream", [(i, i + 1) for i in range(step + 1)]),
            (down_value.astype(BF16), "stream", [(i, i - 1) for i in range(n - 1 - step, n)]),
        ]

    def take(self, got):
        self.came = got
        self.step += 1

    def prepare(self):
        n, step = lax.axis_size("stream"), self.step
        for idx in {n - 1 - step, (1 + step) % n}:
            if idx not in self.parts:
                self.parts[idx] = self.block(idx, self.order.hold)
                self.order.did(self.parts[idx])

    def pieces(self):
        return self.part(0), *self.came

    def value(self):
        own, up, down = self.pieces()
        return own + up.astype(F32) + down.astype(F32)


class Butterfly:
    def __init__(self, value, axes=("stream",), merge=jnp.add):
        self.now, self.merge = value, merge
        self.turns = [(axis, 1 << i) for axis in axes for i in range(lax.axis_size(axis).bit_length() - 1)]
        assert all(lax.axis_size(axis) & (lax.axis_size(axis) - 1) == 0 for axis in axes)

    def items(self):
        axis, span = self.turns[0]
        return [(self.now, axis, [(i, i ^ span) for i in range(lax.axis_size(axis))])]

    def take(self, got):
        self.turns = self.turns[1:]
        self.now = self.merge(self.now, got[0])

    def value(self):
        assert not self.turns
        return self.now


def moments_merger(width, half):
    count = [width]

    def merge(mine, other):
        row = lax.broadcasted_iota(jnp.int32, mine.shape, 0)
        total = mine + other
        gap = jnp.roll(mine - other, half, axis=0)
        square = total + jnp.square(gap) * (0.5 * count[0])
        count[0] *= 2
        return jnp.where(row < half, 0.5 * total, square)

    return merge


def attend_forward_kernel(chunk, q_ref, *refs):
    k_refs, v_refs = refs[: chunk + 1], refs[chunk + 1 : 2 * chunk + 2]
    o_ref, lse_ref = refs[2 * chunk + 2 :]
    rows = q_ref.shape[0]
    keys = jnp.concatenate([ref[...] for ref in k_refs], axis=0)
    values = jnp.concatenate([ref[...] for ref in v_refs], axis=0)
    for sub in range(rows // SUB):
        count = chunk * rows + (sub + 1) * SUB
        span = pl.ds(sub * SUB, SUB)
        scores = times_transpose(keys[:count], q_ref[span, :]) * HEAD_DIM ** (-0.5)
        allowed = lax.broadcasted_iota(jnp.int32, (SUB, SUB), 0) <= lax.broadcasted_iota(
            jnp.int32, (SUB, SUB), 1
        )
        tail = jnp.where(allowed, scores[count - SUB :], -1e30)
        scores = jnp.concatenate([scores[: count - SUB], tail], axis=0) if count > SUB else tail
        top = jnp.max(scores, axis=0, keepdims=True)
        weights = jnp.exp(scores - top)
        total = jnp.sum(weights, axis=0, keepdims=True)
        probs = (weights * (1.0 / total)).astype(BF16)
        lse_ref[0, :, span] = top + jnp.log(total)
        out = contract_rows(values[:count], probs)
        o_ref[span, :] = out.T.astype(BF16)


def attend_forward(queries, keys, values):
    rows, width = queries.shape
    heads = width // HEAD_DIM
    chunk = len(keys) - 1
    spec = pl.BlockSpec((rows, HEAD_DIM), lambda h: (0, h))
    return pl.pallas_call(
        functools.partial(attend_forward_kernel, chunk),
        grid=(heads,),
        in_specs=[spec] * (2 * chunk + 3),
        out_specs=[spec, pl.BlockSpec((1, 1, rows), lambda h: (h, 0, 0))],
        out_shape=[
            jax.ShapeDtypeStruct((rows, width), BF16),
            jax.ShapeDtypeStruct((heads, 1, rows), F32),
        ],
        compiler_params=pltpu.CompilerParams(vmem_limit_bytes=48 * 2**20),
        name="attend_forward",
    )(queries, *keys, *values)


def attend_backward_kernel(chunk, q_ref, do_ref, lse_ref, *refs):
    n = chunk + 1
    k_refs, v_refs, refs = refs[:n], refs[n : 2 * n], refs[2 * n :]
    dk_in, dv_in, refs = refs[:chunk], refs[chunk : 2 * chunk], refs[2 * chunk :]
    dq_ref, dk_refs, dv_refs, (dk_acc, dv_acc) = refs[0], refs[1 : 1 + n], refs[1 + n : 1 + 2 * n], refs[1 + 2 * n :]
    rows = q_ref.shape[0]
    keys = jnp.concatenate([ref[...] for ref in k_refs], axis=0)
    values = jnp.concatenate([ref[...] for ref in v_refs], axis=0)
    for i in range(n):
        here = pl.ds(i * rows, rows)
        dk_acc[here, :] = dk_in[i][...] if i < chunk else jnp.zeros((rows, HEAD_DIM), F32)
        dv_acc[here, :] = dv_in[i][...] if i < chunk else jnp.zeros((rows, HEAD_DIM), F32)
    scale = HEAD_DIM ** (-0.5)
    for sub in range(rows // SUB):
        count = chunk * rows + (sub + 1) * SUB
        span = pl.ds(sub * SUB, SUB)
        query, grad = q_ref[span, :], do_ref[span, :]
        scores = times_transpose(keys[:count], query) * scale
        probs = jnp.exp(scores - lse_ref[0, :, span])
        allowed = lax.broadcasted_iota(jnp.int32, (SUB, SUB), 0) <= lax.broadcasted_iota(
            jnp.int32, (SUB, SUB), 1
        )
        tail = jnp.where(allowed, probs[count - SUB :], 0.0)
        probs = jnp.concatenate([probs[: count - SUB], tail], axis=0) if count > SUB else tail
        prob_grad = times_transpose(values[:count], grad)
        row_dot = jnp.sum(probs * prob_grad, axis=0, keepdims=True)
        score_grad = (probs * (prob_grad - row_dot)).astype(BF16)
        dq_ref[span, :] = (contract_rows(keys[:count], score_grad) * scale).T.astype(BF16)
        dk_acc[pl.ds(0, count), :] += jnp.dot(score_grad, query, preferred_element_type=F32) * scale
        dv_acc[pl.ds(0, count), :] += jnp.dot(
            probs.astype(BF16), grad, preferred_element_type=F32
        )
    for i in range(n):
        dk_refs[i][...] = dk_acc[pl.ds(i * rows, rows), :].astype(dk_refs[i].dtype)
        dv_refs[i][...] = dv_acc[pl.ds(i * rows, rows), :].astype(dv_refs[i].dtype)


def attend_backward(queries, grad, lse, keys, values, sums, final):
    rows, width = queries.shape
    heads = width // HEAD_DIM
    chunk = len(keys) - 1
    n = chunk + 1
    spec = pl.BlockSpec((rows, HEAD_DIM), lambda h: (0, h))
    dk_dv = [jax.ShapeDtypeStruct((rows, width), BF16 if final else F32)] * (2 * n)
    carried = [] if sums is None else [*sums[0], *sums[1]]
    outs = pl.pallas_call(
        functools.partial(attend_backward_kernel, chunk),
        grid=(heads,),
        in_specs=[spec, spec, pl.BlockSpec((1, 1, rows), lambda h: (h, 0, 0))]
        + [spec] * (2 * n + len(carried)),
        out_specs=[spec] * (1 + 2 * n),
        out_shape=[jax.ShapeDtypeStruct((rows, width), BF16), *dk_dv],
        scratch_shapes=[pltpu.VMEM((n * rows, HEAD_DIM), F32)] * 2,
        compiler_params=pltpu.CompilerParams(vmem_limit_bytes=48 * 2**20),
        name="attend_backward",
    )(queries, grad, lse, *keys, *values, *carried)
    return outs[0], outs[1 : 1 + n], outs[1 + n :]


GROUP = 64
TILE = 128
SLOT = 16
SCALE_ROW = 48
MEAN_ROW = 56
LANES = 128


def put_lane(acc, idx, column):
    lane = lax.broadcasted_iota(jnp.int32, acc.shape, 1)
    return jnp.where(lane == idx, column, acc)


def row_sum(values):
    return jnp.sum(values, axis=1, keepdims=True)


def spread(values, idx):
    return jnp.broadcast_to(values[:, idx : idx + 1], (values.shape[0], LANES))


def by_groups(tile, body):
    def step(i, carry):
        body(pl.ds(pl.multiple_of(i * GROUP, GROUP), GROUP))
        return carry

    lax.fori_loop(0, tile // GROUP, step, 0)


def mix_kernel(picked, hist_ref, coef_ref, *refs):
    out_refs, stat_ref, stat_acc = refs[: len(picked)], *(refs[len(picked) :] or (None, None))
    n_hist, tile, width = hist_ref.shape

    def group(span):
        coef = coef_ref[span, :]
        cols = {(s, j): spread(coef, s * n_hist + j) for s in picked for j in range(n_hist)}
        pivots, sums, squares = [], [], []
        for w in range(width // LANES):
            lanes = pl.ds(w * LANES, LANES)
            totals = [0.0] * len(picked)
            for j in range(n_hist):
                layer = hist_ref[j, span, lanes].astype(F32)
                for i, s in enumerate(picked):
                    totals[i] = totals[i] + cols[s, j] * layer
            for i, total in enumerate(totals):
                out_refs[i][span, lanes] = total
                if stat_ref is None:
                    continue
                if w == 0:
                    pivots.append(spread(total, 0))
                    sums.append(0.0)
                    squares.append(0.0)
                gap = total - pivots[i]
                sums[i] = sums[i] + gap
                squares[i] = squares[i] + jnp.square(gap)
        if stat_ref is not None:
            stats = jnp.zeros((GROUP, LANES), F32)
            for i in range(len(picked)):
                shift = row_sum(sums[i]) * (1.0 / width)
                stats = put_lane(stats, i, pivots[i] + shift)
                stats = put_lane(stats, len(picked) + i, row_sum(squares[i]) - shift * shift * width)
            stat_acc[span, :] = stats

    by_groups(tile, group)
    if stat_ref is not None:
        stat_ref[...] = stat_acc[...].T[: stat_ref.shape[0]]


def mix_streams(history, coef, chunk, picked, with_stats):
    n_hist, tokens, width = history.shape
    rows = coef.shape[0]
    base = chunk * rows // TILE
    wide = pl.BlockSpec((TILE, width), lambda i: (i, 0))
    n = len(picked)
    return pl.pallas_call(
        functools.partial(mix_kernel, picked),
        grid=(rows // TILE,),
        in_specs=[
            pl.BlockSpec((n_hist, TILE, width), lambda i: (0, base + i, 0)),
            pl.BlockSpec((TILE, 4 * n_hist), lambda i: (i, 0)),
        ],
        out_specs=[wide] * n + ([pl.BlockSpec((8, TILE), lambda i: (0, i))] if with_stats else []),
        out_shape=[jax.ShapeDtypeStruct((rows, width), F32)] * n
        + ([jax.ShapeDtypeStruct((8, rows), F32)] if with_stats else []),
        scratch_shapes=[pltpu.VMEM((TILE, LANES), F32)] if with_stats else [],
        compiler_params=pltpu.CompilerParams(vmem_limit_bytes=32 * 2**20),
        name="mix_streams",
    )(history, coef)


def hat_of(stream, stat, s):
    return (stream - spread(stat, s)) * spread(stat, 3 + s)


def early_kernel(hist_ref, x0, x1, x2, stat_ref, resid_ref, sums_ref, acc_ref):
    n_hist, tile, width = hist_ref.shape

    def group(span):
        stat = stat_ref[span, :]
        sums = jnp.zeros((GROUP, LANES), F32)
        pieces = [pl.ds(w * LANES, LANES) for w in range(width // LANES)]
        others = [[hat_of(x[span, p], stat, s) for p in pieces] for s, x in enumerate((x0, x1, x2))]
        others.append([resid_ref[span, p] for p in pieces])
        for j in range(n_hist):
            layer = [hist_ref[j, span, p].astype(F32) for p in pieces]
            sums = put_lane(sums, j, row_sum(sum(layer[1:], layer[0])))
            for s in range(4):
                terms = [x * y for x, y in zip(others[s], layer)]
                sums = put_lane(sums, (s + 1) * SLOT + j, row_sum(sum(terms[1:], terms[0])))
        acc_ref[span, :] = sums

    by_groups(tile, group)
    sums_ref[...] = acc_ref[...].T[: sums_ref.shape[0]]


def early_dots(history, streams, stat, resid_grad, chunk):
    n_hist, tokens, width = history.shape
    rows = resid_grad.shape[0]
    base = chunk * rows // TILE
    wide = pl.BlockSpec((TILE, width), lambda i: (i, 0))
    return pl.pallas_call(
        early_kernel,
        grid=(rows // TILE,),
        in_specs=[
            pl.BlockSpec((n_hist, TILE, width), lambda i: (0, base + i, 0)),
            wide,
            wide,
            wide,
            pl.BlockSpec((TILE, LANES), lambda i: (i, 0)),
            wide,
        ],
        out_specs=pl.BlockSpec((5 * SLOT, TILE), lambda i: (0, i)),
        out_shape=jax.ShapeDtypeStruct((5 * SLOT, rows), F32),
        scratch_shapes=[pltpu.VMEM((TILE, LANES), F32)],
        compiler_params=pltpu.CompilerParams(vmem_limit_bytes=32 * 2**20),
        name="early_dots",
    )(history, *streams, stat, resid_grad)


def late_kernel(hist_ref, x0, x1, x2, stat_ref, gain_ref, d0, d1, d2, *refs):
    sums_ref, gain_grad_ref, acc_ref = refs[-3:]
    n_hist, tile, width = hist_ref.shape

    @pl.when(pl.program_id(0) == 0)
    def _():
        gain_grad_ref[...] = jnp.zeros_like(gain_grad_ref)

    def group(span):
        stat = stat_ref[span, :]
        sums = jnp.zeros((GROUP, LANES), F32)
        pieces = [pl.ds(w * LANES, LANES) for w in range(width // LANES)]
        grads = []
        for s, (x, d) in enumerate(((x0, d0), (x1, d1), (x2, d2))):
            scaled, dots = [], []
            for p in pieces:
                product = d[span, p] * hat_of(x[span, p], stat, s)
                gain = gain_ref[pl.ds(s, 1), p]
                gain_grad_ref[s, :, p] += jnp.sum(product.reshape(GROUP // 8, 8, LANES), axis=0)
                scaled.append(d[span, p] * gain)
                dots.append(product * gain)
            sums = put_lane(sums, s * SLOT + n_hist, row_sum(sum(scaled[1:], scaled[0])))
            sums = put_lane(sums, s * SLOT + n_hist + 1, row_sum(sum(dots[1:], dots[0])))
            grads.append(scaled)
        for j in range(n_hist):
            layer = [hist_ref[j, span, p].astype(F32) for p in pieces]
            for s in range(3):
                terms = [x * y for x, y in zip(grads[s], layer)]
                sums = put_lane(sums, s * SLOT + j, row_sum(sum(terms[1:], terms[0])))
        acc_ref[span, :] = sums

    by_groups(tile, group)
    sums_ref[...] = acc_ref[...].T[: sums_ref.shape[0]]


def late_dots(history, streams, stat, gain, d_normed, chunk, others):
    n_hist, tokens, width = history.shape
    rows = stat.shape[0]
    base = chunk * rows // TILE
    wide = pl.BlockSpec((TILE, width), lambda i: (i, 0))
    slices = [pl.BlockSpec((None, TILE, width), lambda i, s=s: (s, i, 0)) for s in range(3)]
    return pl.pallas_call(
        late_kernel,
        grid=(rows // TILE,),
        in_specs=[
            pl.BlockSpec((n_hist, TILE, width), lambda i: (0, base + i, 0)),
            wide,
            wide,
            wide,
            pl.BlockSpec((TILE, LANES), lambda i: (i, 0)),
            pl.BlockSpec((3, width), lambda i: (0, 0)),
            *slices,
        ]
        + [pl.BlockSpec(memory_space=pl.ANY)] * len(others),
        out_specs=[
            pl.BlockSpec((3 * SLOT, TILE), lambda i: (0, i)),
            pl.BlockSpec((3, 8, width), lambda i: (0, 0, 0)),
        ],
        out_shape=[
            jax.ShapeDtypeStruct((3 * SLOT, rows), F32),
            jax.ShapeDtypeStruct((3, 8, width), F32),
        ],
        scratch_shapes=[pltpu.VMEM((TILE, LANES), F32)],
        compiler_params=pltpu.CompilerParams(vmem_limit_bytes=32 * 2**20),
        name="late_dots",
    )(history, *streams, stat, gain, d_normed, d_normed, d_normed, *others)


def layers_kernel(coef_ref, x0, x1, x2, stat_ref, gain_ref, mean_ref, d0, d1, d2, resid_ref, extra_ref, *refs):
    out_ref = refs[-1]
    n_hist, tile, width = out_ref.shape

    def group(span):
        stat, coef, means = stat_ref[span, :], coef_ref[span, :], mean_ref[span, :]
        cols = [spread(coef, i) for i in range(4 * n_hist)]
        for w in range(width // LANES):
            p = pl.ds(w * LANES, LANES)
            grads = []
            for s, (x, d) in enumerate(((x0, d0), (x1, d1), (x2, d2))):
                scaled = d[span, p] * gain_ref[pl.ds(s, 1), p]
                hat = hat_of(x[span, p], stat, s)
                grads.append(
                    spread(stat, 3 + s) * (scaled - spread(means, MEAN_ROW + s) - hat * spread(means, MEAN_ROW + 3 + s))
                )
            grads.append(resid_ref[span, p])
            for j in range(n_hist):
                total = extra_ref[span, p] if j == n_hist - 1 else 0.0
                for s in range(4):
                    total = total + cols[s * n_hist + j] * grads[s]
                out_ref[j, span, p] = total.astype(BF16)

    by_groups(tile, group)


def layer_grads(coef, streams, stat, gain, means, d_normed, resid_grad, extra, chunk, held, tokens):
    rows, width = resid_grad.shape
    n_hist = coef.shape[1] // 4
    base = chunk * rows // TILE
    wide = pl.BlockSpec((TILE, width), lambda i: (i, 0))
    slices = [pl.BlockSpec((None, TILE, width), lambda i, s=s: (s, i, 0)) for s in range(3)]
    narrow = pl.BlockSpec((TILE, LANES), lambda i: (i, 0))
    return pl.pallas_call(
        layers_kernel,
        grid=(rows // TILE,),
        in_specs=[
            pl.BlockSpec((TILE, 4 * n_hist), lambda i: (i, 0)),
            wide,
            wide,
            wide,
            narrow,
            pl.BlockSpec((3, width), lambda i: (0, 0)),
            pl.BlockSpec((TILE, LANES), lambda i: (i, 0)),
            *slices,
            wide,
            wide,
        ]
        + ([] if held is None else [pl.BlockSpec(memory_space=pl.ANY)]),
        out_specs=pl.BlockSpec((n_hist, TILE, width), lambda i: (0, base + i, 0)),
        out_shape=jax.ShapeDtypeStruct((n_hist, tokens, width), BF16),
        input_output_aliases={} if held is None else {12: 0},
        compiler_params=pltpu.CompilerParams(vmem_limit_bytes=32 * 2**20),
        name="layer_grads",
    )(coef, *streams, stat, gain, means, d_normed, d_normed, d_normed, resid_grad, extra, *([] if held is None else [held]))


def coef_kernel(full_width, n_hist, early, late, stat, act, slope, raw, scale, mix_out, mix_in, last, out_part, in_part, turned_ref, extra_ref, pack):
    rows = late.shape[1]
    mixh = act.shape[0]
    inside = lax.broadcasted_iota(jnp.int32, (SLOT, rows), 0) < n_hist
    pack[...] = jnp.zeros_like(pack)
    slots = []
    for s in range(3):
        mean = late[pl.ds(s * SLOT + n_hist, 1), :] * (1.0 / full_width)
        mean_hat = late[pl.ds(s * SLOT + n_hist + 1, 1), :] * (1.0 / full_width)
        pack[pl.ds(MEAN_ROW + s, 1), :] = mean
        pack[pl.ds(MEAN_ROW + 3 + s, 1), :] = mean_hat
        slot = inv_std(stat[pl.ds(3 + s, 1), :], full_width) * (
            late[pl.ds(s * SLOT, SLOT), :]
            - mean * early[pl.ds(0, SLOT), :]
            - mean_hat * early[pl.ds((s + 1) * SLOT, SLOT), :]
        )
        slots.append(jnp.where(inside, slot, 0.0))
    slots.append(jnp.where(inside, early[pl.ds(4 * SLOT, SLOT), :], 0.0))
    d_coef = jnp.concatenate(slots, axis=0)
    ones = jnp.ones((8, rows), F32)
    out_part[pl.ds(0, mixh), :] = dot_tt(act[...], d_coef, ((1,), (1,)), HIGH)
    out_part[pl.ds(SCALE_ROW, 8), :] = dot_tt(ones, d_coef, ((1,), (1,)), HIGH)
    d_pre = dot_tt(mix_out[...], d_coef, ((1,), (0,)), HIGH) * slope[...]
    d_raw = d_pre * scale[...]
    in_part[...] = dot_tt(d_raw, last[...].astype(F32), ((1,), (0,)), HIGH)
    pack[pl.ds(0, mixh), :] = d_raw
    pack[pl.ds(SCALE_ROW, 1), :] = (
        scale[...] * scale[...] * scale[...] * (1.0 / full_width)
        * jnp.sum(d_pre * raw[...], axis=0, keepdims=True)
    )
    turned = pack[...].T
    turned_ref[...] = turned
    back = dot_tt(turned, mix_in[...], ((1,), (1,)), HIGH)
    extra_ref[...] = back - turned[:, SCALE_ROW : SCALE_ROW + 1] * last[...].astype(F32)


def coef_grads(full_width, early, late, stat, act, slope, raw, scale, mix_out, mix_in, history, chunk):
    n_hist, tokens, width = history.shape
    rows = late.shape[1]
    mixh = act.shape[0]

    def full(array):
        return pl.BlockSpec(array.shape, lambda i: (0,) * array.ndim)

    arrays = [early, late, stat, act, slope, raw, scale, mix_out, mix_in]
    outs = [
        jax.ShapeDtypeStruct((SCALE_ROW + 8, 4 * SLOT), F32),
        jax.ShapeDtypeStruct((mixh, width), F32),
        jax.ShapeDtypeStruct((rows, LANES), F32),
        jax.ShapeDtypeStruct((rows, width), F32),
    ]
    return pl.pallas_call(
        functools.partial(coef_kernel, full_width, n_hist),
        grid=(1,),
        in_specs=[full(a) for a in arrays]
        + [pl.BlockSpec((None, rows, width), lambda i: (n_hist - 1, chunk, 0))],
        out_specs=[full(a) for a in outs],
        out_shape=outs,
        scratch_shapes=[pltpu.VMEM((LANES, rows), F32)],
        compiler_params=pltpu.CompilerParams(vmem_limit_bytes=32 * 2**20),
        name="coef_grads",
    )(*arrays, history)


def columns(rows_values):
    return jnp.concatenate([rows_values, jnp.zeros((TILE - 8, TILE), F32)], axis=0).T


def inv_std(squares, full_width):
    return lax.rsqrt(squares * (1.0 / full_width) + EPS_NORM)


def norm_kernel(full_width, x0, x1, x2, moment_ref, gain_ref, cols_ref, stat_ref):
    row = lax.broadcasted_iota(jnp.int32, (8, TILE), 0)
    moments = moment_ref[...]
    stat = columns(jnp.where(row < 3, moments, inv_std(moments, full_width)))
    stat_ref[...] = stat
    for s, x in enumerate((x0, x1, x2)):
        hat = (x[...] - stat[:, s : s + 1]) * stat[:, 3 + s : 4 + s]
        cols_ref[s] = (hat * gain_ref[pl.ds(s, 1), :]).astype(BF16)


def norm_streams(full_width, streams, moments, gain):
    rows, width = streams[0].shape
    wide = pl.BlockSpec((TILE, width), lambda i: (i, 0))
    return pl.pallas_call(
        functools.partial(norm_kernel, full_width),
        grid=(rows // TILE,),
        in_specs=[
            wide,
            wide,
            wide,
            pl.BlockSpec((8, TILE), lambda i: (0, i)),
            pl.BlockSpec((3, width), lambda i: (0, 0)),
        ],
        out_specs=[
            pl.BlockSpec((3, TILE, width), lambda i: (0, i, 0)),
            pl.BlockSpec((TILE, LANES), lambda i: (i, 0)),
        ],
        out_shape=[
            jax.ShapeDtypeStruct((3, rows, width), BF16),
            jax.ShapeDtypeStruct((rows, LANES), F32),
        ],
        compiler_params=pltpu.CompilerParams(vmem_limit_bytes=32 * 2**20),
        name="norm_streams",
    )(*streams, moments, gain)


def residual_kernel(own, up, down, base, out_ref, stat_ref):
    width = own.shape[1]
    value = base[...] + own[...] + up[...].astype(F32) + down[...].astype(F32)
    out_ref[...] = value
    pivot = value[:, :1]
    gap = value - pivot
    shift = row_sum(gap) * (1.0 / width)
    acc = put_lane(jnp.zeros((TILE, LANES), F32), 0, pivot + shift)
    acc = put_lane(acc, 1, row_sum(jnp.square(gap)) - shift * shift * width)
    stat_ref[...] = acc.T[:8]


def residual_rows(own, up, down, base):
    rows, width = own.shape
    wide = pl.BlockSpec((TILE, width), lambda i: (i, 0))
    return pl.pallas_call(
        residual_kernel,
        grid=(rows // TILE,),
        in_specs=[wide] * 4,
        out_specs=[wide, pl.BlockSpec((8, TILE), lambda i: (0, i))],
        out_shape=[
            jax.ShapeDtypeStruct((rows, width), F32),
            jax.ShapeDtypeStruct((8, rows), F32),
        ],
        compiler_params=pltpu.CompilerParams(vmem_limit_bytes=32 * 2**20),
        name="residual_rows",
    )(own, up, down, base)


def hat_kernel(full_width, x, stat_ref, gain_ref, out_ref):
    stat = columns(stat_ref[...])
    hat = (x[...] - stat[:, :1]) * inv_std(stat[:, 1:2], full_width)
    out_ref[...] = (hat * gain_ref[...]).astype(BF16)


def mlp_input(full_width, residual, stat, gain):
    rows, width = residual.shape
    wide = pl.BlockSpec((TILE, width), lambda i: (i, 0))
    return pl.pallas_call(
        functools.partial(hat_kernel, full_width),
        grid=(rows // TILE,),
        in_specs=[
            wide,
            pl.BlockSpec((8, TILE), lambda i: (0, i)),
            pl.BlockSpec((1, width), lambda i: (0, 0)),
        ],
        out_specs=wide,
        out_shape=jax.ShapeDtypeStruct((rows, width), BF16),
        compiler_params=pltpu.CompilerParams(vmem_limit_bytes=32 * 2**20),
        name="mlp_input",
    )(residual, stat, gain)


def mlp_back_kernel(full_width, own, up, down, x, stat_ref, gain_ref, out_ref, sums_ref, gain_grad_ref):
    @pl.when(pl.program_id(0) == 0)
    def _():
        gain_grad_ref[...] = jnp.zeros_like(gain_grad_ref)

    stat = columns(stat_ref[...])
    grad = own[...] + up[...].astype(F32) + down[...].astype(F32)
    out_ref[...] = grad
    product = grad * ((x[...] - stat[:, :1]) * inv_std(stat[:, 1:2], full_width))
    gain_grad_ref[...] += jnp.sum(product.reshape(TILE // 8, 8, -1), axis=0)
    acc = put_lane(jnp.zeros((TILE, LANES), F32), 0, row_sum(grad * gain_ref[...]))
    acc = put_lane(acc, 1, row_sum(product * gain_ref[...]))
    sums_ref[...] = acc.T[:8]


def mlp_back_rows(full_width, own, up, down, residual, stat, gain):
    rows, width = residual.shape
    wide = pl.BlockSpec((TILE, width), lambda i: (i, 0))
    narrow = pl.BlockSpec((8, TILE), lambda i: (0, i))
    return pl.pallas_call(
        functools.partial(mlp_back_kernel, full_width),
        grid=(rows // TILE,),
        in_specs=[wide] * 4 + [narrow, pl.BlockSpec((1, width), lambda i: (0, 0))],
        out_specs=[wide, narrow, pl.BlockSpec((8, width), lambda i: (0, 0))],
        out_shape=[
            jax.ShapeDtypeStruct((rows, width), F32),
            jax.ShapeDtypeStruct((8, rows), F32),
            jax.ShapeDtypeStruct((8, width), F32),
        ],
        compiler_params=pltpu.CompilerParams(vmem_limit_bytes=32 * 2**20),
        name="mlp_back_rows",
    )(own, up, down, residual, stat, gain)


def resid_grad_kernel(full_width, grad, x, stat_ref, sums_ref, gain_ref, cot, out_ref, low_ref):
    stat = columns(stat_ref[...])
    sums = columns(sums_ref[...]) * (1.0 / full_width)
    inv = inv_std(stat[:, 1:2], full_width)
    hat = (x[...] - stat[:, :1]) * inv
    value = cot[...] + inv * (grad[...] * gain_ref[...] - sums[:, :1] - hat * sums[:, 1:2])
    out_ref[...] = value
    low_ref[...] = value.astype(BF16)


def resid_grad_rows(full_width, grad, residual, stat, sums, gain, cot):
    rows, width = residual.shape
    wide = pl.BlockSpec((TILE, width), lambda i: (i, 0))
    narrow = pl.BlockSpec((8, TILE), lambda i: (0, i))
    return pl.pallas_call(
        functools.partial(resid_grad_kernel, full_width),
        grid=(rows // TILE,),
        in_specs=[wide, wide, narrow, narrow, pl.BlockSpec((1, width), lambda i: (0, 0)), wide],
        out_specs=[wide, wide],
        out_shape=[
            jax.ShapeDtypeStruct((rows, width), F32),
            jax.ShapeDtypeStruct((rows, width), BF16),
        ],
        compiler_params=pltpu.CompilerParams(vmem_limit_bytes=32 * 2**20),
        name="resid_grad_rows",
    )(grad, residual, stat, sums, gain, cot)


def rows_product_kernel(n, *refs):
    former, latter, out_ref, turned = refs[:n], refs[n : 2 * n], refs[-2], refs[-1]
    rows = former[0].shape[0]

    @pl.when(pl.program_id(1) == 0)
    def _():
        for c in range(n):
            turned[:, pl.ds(c * rows, rows)] = former[c][...].T

    total = 0.0
    for c in range(n):
        total = total + jnp.dot(
            turned[:, pl.ds(c * rows, rows)], latter[c][...], preferred_element_type=F32
        )
    out_ref[...] = total.astype(BF16)


def rows_product(former, latter, out_cols, first, held, others=(), slot=None):
    n = len(former)
    rows, height = former[0].shape[-2:]
    width = latter[0].shape[1]
    tile_m, tile_n = min(512, height), min(1024, width)
    begin = first // tile_n
    free = [*others] + ([] if held is None else [held])
    return pl.pallas_call(
        functools.partial(rows_product_kernel, n),
        grid=(height // tile_m, width // tile_n),
        in_specs=[
            pl.BlockSpec((rows, tile_m), lambda i, j: (0, i))
            if slot is None
            else pl.BlockSpec((None, rows, tile_m), lambda i, j: (slot, 0, i))
        ]
        * n
        + [pl.BlockSpec((rows, tile_n), lambda i, j: (0, j))] * n
        + [pl.BlockSpec(memory_space=pl.ANY)] * len(free),
        out_specs=pl.BlockSpec((tile_m, tile_n), lambda i, j: (i, begin + j)),
        out_shape=jax.ShapeDtypeStruct((height, out_cols), BF16),
        input_output_aliases={} if held is None else {2 * n + len(others): 0},
        scratch_shapes=[pltpu.VMEM((tile_m, n * rows), BF16)],
        compiler_params=pltpu.CompilerParams(vmem_limit_bytes=48 * 2**20),
        name="rows_product",
    )(*former, *latter, *free)


def local(
    history,
    mix_in,
    mix_out,
    mix_static,
    stream_gain,
    qkv_weight,
    out_weight,
    mlp_gain,
    up_weight,
    down_weight,
    out_grad,
    seq_group,
    group_weight,
):
    n_stream = lax.axis_size("stream")
    member = lax.axis_index("stream")
    n_hist, tokens, width = history.shape
    assert tokens == SEQ
    full_width = width * n_stream
    rows = tokens // CHUNKS
    both = range(CHUNKS)
    spans = [slice(c * rows, (c + 1) * rows) for c in both]
    first_col = member * width
    mixh = mix_in.shape[1]
    ff = up_weight.shape[1]
    order = Order()

    def rows_of(weight, idx):
        begin = lax.rem(member + idx, n_stream) * width
        return lax.dynamic_slice_in_dim(weight, begin, width, 0)

    def dp_sum(part):
        return lax.psum_scatter(part, "dp", scatter_dimension=0, tiled=True).astype(F32)

    mix_in_rows = lax.dynamic_slice_in_dim(mix_in, first_col, width, 0)
    mix_out_float = mix_out.astype(F32)

    raw = []
    for c in both:
        last = history[n_hist - 1, spans[c]]
        square_part = jnp.sum(jnp.square(last.astype(F32)), axis=1)[None]
        raw_part = dot_tt(mix_in_rows, last, ((0,), (1,)))
        raw.append(Butterfly(jnp.concatenate([raw_part, square_part], axis=0)))
    order.send(*raw)

    group_pick = (
        seq_group[:, None] == jnp.arange(group_weight.shape[0], dtype=jnp.int32)[None, :]
    ).astype(F32)
    seq_weight = jnp.sum(group_pick * group_weight.astype(F32)[None, :]) * COT_SCALE
    out_grad_held = order.hold(out_grad)
    cot_cols = [out_grad_held[spans[c]].astype(F32) * seq_weight for c in both]
    cot = [LineGather(cot_cols[c].astype(BF16), member) for c in both]
    order.did(cot[0].piece)
    order.send(*raw)
    order.send(cot[0])

    scale_t, raw_t, act_t, slope_t, coef = [], [], [], [], []
    for c in both:
        sums = raw[c].value()
        raw_t.append(sums[:-1])
        scale_t.append(lax.rsqrt(sums[-1:] / full_width + EPS_MIX))
        act, slope = gelu_both(scale_t[c] * raw_t[c])
        act_t.append(act)
        slope_t.append(slope)
        coef_t = dot_tt(mix_out_float, act, ((0,), (0,)), HIGH) + mix_static.reshape(-1, 1)
        coef.append(coef_t.T)

    streams, moments = [None] * 2, [None] * 2
    stat, stat_rows, normed_chain = [None] * 2, [None] * 2, [None] * 2
    resid_streams = [None] * 2

    def mix(c):
        *streams[c], sums = mix_streams(history, coef[c], c, (0, 1, 2), True)
        moments[c] = Butterfly(sums, merge=moments_merger(width, 3))

    def norm(c):
        stat_rows[c] = moments[c].value()
        cols, stat[c] = norm_streams(full_width, streams[c], stat_rows[c], stream_gain)
        normed_chain[c] = LineGather(cols, member)

    def mix_resid(c):
        (resid_streams[c],) = mix_streams(history, order.hold(coef[c]), c, (3,), False)
        order.did(resid_streams[c])

    mix(0)
    order.send(moments[0])
    coef[1] = order.hold(coef[1])
    mix(1)
    order.did(streams[1][0])
    order.send(moments[0])
    norm(0)
    order.send(normed_chain[0])
    order.send(moments[1])
    mix_resid(0)
    mix_resid(1)
    order.send(normed_chain[0])
    order.send(moments[1])
    norm(1)
    order.did(normed_chain[1].piece)
    qkv_slices = [qkv_weight[:, s, :] for s in range(3)]
    order.send(normed_chain[0])
    order.send(normed_chain[1])

    normed, query, key, value, heads_out, lse = [], [], [], [], [], []
    branch = []

    def attend(c):
        normed.append(normed_chain[c].value())
        for held, s in ((query, 0), (key, 1), (value, 2)):
            held.append(
                jnp.dot(normed[c][s], qkv_slices[s], preferred_element_type=F32).astype(BF16)
            )
        out, out_lse = attend_forward(query[c], key[: c + 1], value[: c + 1])
        heads_out.append(out)
        lse.append(out_lse)
        branch.append(
            LineScatter(
                order, lambda idx, hold: times_transpose(hold(out), rows_of(out_weight, idx))
            )
        )

    residual, resid_moments = [], []

    def end_branch(c):
        value, stats = residual_rows(*branch[c].pieces(), resid_streams[c])
        residual.append(value)
        resid_moments.append(Butterfly(stats, merge=moments_merger(width, 1)))

    mlp_gain_cols = lax.dynamic_slice_in_dim(mlp_gain, first_col, width, 0)[None, :]
    mlp_in = []

    def norm_mlp(c):
        cols = mlp_input(full_width, residual[c], resid_moments[c].value(), mlp_gain_cols)
        mlp_in.append(LineGather(cols, member))

    cot_low, d_hidden = [], []

    def down_back(c):
        cot_low.append(cot[c].value())
        d_hidden.append(
            jnp.dot(order.hold(cot_low[c]), down_weight, preferred_element_type=F32)
        )
        order.did(d_hidden[c])

    normed_mlp, hidden, d_hpre, mlp_back, mlp_out = [], [], [], [], []

    def mlp(c):
        normed_mlp.append(mlp_in[c].value())
        hidden_pre = jnp.dot(normed_mlp[c], up_weight, preferred_element_type=F32)
        act, slope = gelu_both(hidden_pre)
        act = act.astype(BF16)
        d_pre = (d_hidden[c] * slope).astype(BF16)
        hidden.append(act)
        d_hpre.append(d_pre)
        mlp_back.append(
            LineScatter(
                order, lambda idx, hold: times_transpose(hold(d_pre), rows_of(up_weight, idx))
            )
        )
        mlp_out.append(
            LineScatter(
                order, lambda idx, hold: times_transpose(hold(act), rows_of(down_weight, idx))
            )
        )

    d_normed_mlp, back_sums, mlp_gain_shares = [], [], []

    def end_mlp_back(c):
        value, sums, share = mlp_back_rows(
            full_width, *mlp_back[c].pieces(), residual[c], resid_moments[c].value(), mlp_gain_cols
        )
        d_normed_mlp.append(value)
        back_sums.append(Butterfly(sums))
        mlp_gain_shares.append(share)

    resid_grad, branch_grad = [], []

    def norm_mlp_back(c):
        value, low = resid_grad_rows(
            full_width, d_normed_mlp[c], residual[c], resid_moments[c].value(),
            back_sums[c].value(), mlp_gain_cols, cot_cols[c],
        )
        resid_grad.append(value)
        branch_grad.append(LineGather(low, member))

    d_branch, d_proj = [], []
    carried = [None]

    def attend_back(c):
        d_branch.append(branch_grad[c].value())
        d_heads = jnp.dot(d_branch[c], out_weight, preferred_element_type=F32).astype(BF16)
        d_query, dk, dv = attend_backward(
            query[c], d_heads, lse[c], key[: c + 1], value[: c + 1], carried[0], c == CHUNKS - 1
        )
        carried[0] = (dk, dv)
        d_proj.append([d_query, None, None])
        if c == CHUNKS - 1:
            for i in both:
                d_proj[i][1:] = [dk[i], dv[i]]

    attend(0)
    order.send(branch[0])
    branch[0].prepare()
    order.send(normed_chain[1])
    order.send(branch[0])
    branch[0].prepare()
    order.send(normed_chain[1])
    order.send(branch[0])
    branch[0].prepare()
    end_branch(0)
    order.send(resid_moments[0], cot[0])
    order.send(resid_moments[0])
    norm_mlp(0)
    order.send(mlp_in[0], cot[0])
    attend(1)
    order.send(branch[1], mlp_in[0])
    branch[1].prepare()
    down_back(0)
    order.send(branch[1], mlp_in[0])
    branch[1].prepare()
    order.send(branch[1], cot[1])
    branch[1].prepare()
    mlp(0)
    end_branch(1)
    order.send(resid_moments[1])
    order.did(hidden[0])
    order.send(resid_moments[1], cot[1])
    norm_mlp(1)
    order.send(mlp_in[1], mlp_back[0])
    mlp_back[0].prepare()
    order.send(cot[1])
    order.send(mlp_in[1], mlp_back[0])
    mlp_back[0].prepare()
    down_back(1)
    order.send(mlp_in[1], mlp_back[0])
    mlp_back[0].prepare()
    end_mlp_back(0)
    order.send(back_sums[0])
    mlp(1)
    order.did(hidden[1])
    order.send(back_sums[0])
    norm_mlp_back(0)
    order.send(mlp_back[1], branch_grad[0])
    mlp_back[1].prepare()
    order.send(mlp_back[1], branch_grad[0])
    mlp_back[1].prepare()
    order.send(mlp_back[1], branch_grad[0])
    mlp_back[1].prepare()
    end_mlp_back(1)
    order.send(back_sums[1])
    attend_back(0)
    order.did(d_proj[0][0])
    order.send(back_sums[1])
    norm_mlp_back(1)
    mlp_out[0].prepare()
    order.send(branch_grad[1], mlp_out[0])
    mlp_out[0].prepare()
    order.send(branch_grad[1], mlp_out[0])
    mlp_out[0].prepare()
    order.send(branch_grad[1], mlp_out[0])
    mlp_out[0].prepare()
    attend_back(1)

    def grad_chain(c):
        return LineScatter(
            order,
            lambda idx, hold: jnp.stack(
                [times_transpose(hold(d_proj[c][s]), rows_of(qkv_slices[s], idx)) for s in range(3)]
            ),
        )

    def weight_part(former, latter, out_cols, first=0, held=None):
        part = rows_product(former, latter, out_cols, first, held, order.tick)
        order.did(part)
        return part

    def early(c):
        sums = early_dots(history, streams[c], stat[c], order.hold(resid_grad[c]), c)
        order.did(sums)
        return Butterfly(sums)

    gain_part = jnp.sum(mlp_gain_shares[0] + mlp_gain_shares[1], axis=0)
    placed = jnp.where(
        jnp.arange(n_stream)[:, None] == member, gain_part[None, :], jnp.zeros((n_stream, width), F32)
    )
    gain_chain = Butterfly(placed)

    grads = [grad_chain(c) for c in both]
    order.send(grads[0])
    order.send(grads[1])
    down_part = weight_part(cot_low, hidden, ff)
    out_part = weight_part(d_branch, heads_out, width)
    down_grad, out_weight_grad = dp_sum(down_part), dp_sum(out_part)
    grads[0].prepare()
    grads[1].prepare()
    order.send(grads[0])
    up_part = weight_part(normed_mlp, d_hpre, ff)
    early_chain = [early(0)]
    up_grad = dp_sum(up_part)
    order.send(grads[1], gain_chain)
    grads[0].prepare()
    order.send(grads[0], gain_chain, early_chain[0])
    qkv_part = None
    for s in range(3):
        qkv_part = rows_product(
            [normed[c] for c in both], [d_proj[c][s] for c in both], 3 * width, s * width, qkv_part,
            order.tick, s,
        )
    order.did(qkv_part)
    qkv_grad = dp_sum(qkv_part)
    qkv_grad = qkv_grad.reshape(qkv_grad.shape[0], 3, width)
    early_chain.append(early(1))
    grads[1].prepare()
    order.send(grads[1], *early_chain)

    mix_out_wide = jnp.pad(
        mix_out_float.reshape(-1, 4, n_hist), ((0, 0), (0, 0), (0, SLOT - n_hist))
    ).reshape(-1, 4 * SLOT)
    mix_in_wide = jnp.pad(mix_in_rows.astype(F32), ((0, 0), (0, LANES - mixh)))
    d_normed, late, gain_shares, shares = [], [], [], []
    history_grad = [None]

    def late_sums(c, others):
        d_normed.append(grads[c].value())
        sums, gain_share = late_dots(
            history, streams[c], stat[c], stream_gain, d_normed[c], c, others
        )
        late.append(Butterfly(sums))
        gain_shares.append(gain_share)

    def coefs(c):
        shares.append(
            coef_grads(
                full_width, early_chain[c].value(), late[c].value(), stat_rows[c], act_t[c],
                slope_t[c], raw_t[c], scale_t[c], mix_out_wide, mix_in_wide, history, c,
            )
        )

    def layers(c):
        _, _, turned, extra = shares[c]
        history_grad[0] = layer_grads(
            coef[c], streams[c], stat[c], stream_gain, order.hold(turned), d_normed[c],
            resid_grad[c], extra, c, history_grad[0], tokens,
        )
        order.did(history_grad[0])

    mlp_out[1].prepare()
    late_sums(0, ())
    order.send(late[0], early_chain[1])
    late_sums(1, (down_grad, up_grad, out_weight_grad))
    order.send(late[0], late[1])
    order.send(late[1])
    order.send(mlp_out[1])
    mlp_out[1].prepare()
    coefs(0)
    coefs(1)
    out_share, in_share = [shares[0][i] + shares[1][i] for i in range(2)]
    gain_share = jnp.sum(gain_shares[0] + gain_shares[1], axis=1)
    out_share = jnp.pad(out_share, ((0, 0), (0, width - 4 * SLOT)))
    small = Butterfly(
        jnp.concatenate([out_share, in_share, gain_share, gain_chain.value()], axis=0), ("dp",)
    )
    order.send(small)
    layers(0)
    order.send(small, mlp_out[1])
    layers(1)
    while small.turns:
        order.send(small, *([mlp_out[1]] if mlp_out[1].step < n_stream - 1 else []))
    output_cols = jnp.concatenate(
        [(residual[c] + mlp_out[c].value()).astype(BF16) for c in both], axis=0
    )
    small = small.value()
    top = out_share.shape[0]
    by_slot = small[:top, : 4 * SLOT].reshape(-1, 4, SLOT)[:, :, :n_hist]
    return (
        output_cols,
        history_grad[0],
        small[top : top + mixh].T,
        by_slot[:mixh].reshape(mixh, 4 * n_hist),
        by_slot[SCALE_ROW],
        small[top + mixh : top + mixh + 3],
        qkv_grad,
        out_weight_grad,
        small[top + mixh + 3 :].reshape(full_width),
        up_grad,
        down_grad,
    )


def solution(mesh):
    in_specs = (
        P(None, "dp", "stream"),
        P(),
        P(),
        P(),
        P(None, "stream"),
        P(None, None, "stream"),
        P(None, "stream"),
        P(),
        P(None, "stream"),
        P(None, "stream"),
        P("dp", "stream"),
        P("dp"),
        P(),
    )
    out_specs = (
        P("dp", "stream"),
        P(None, "dp", "stream"),
        P("stream", None),
        P(),
        P(),
        P(None, "stream"),
        P("dp", None, "stream"),
        P("dp", "stream"),
        P(),
        P("dp", "stream"),
        P("dp", "stream"),
    )
    return jax.shard_map(local, mesh=mesh, in_specs=in_specs, out_specs=out_specs, check_vma=False)
```

time: 1330 us -> 1060 us (0.80)
  Pallas kernels: 26.1 us -> 161 us
  matrix products: 245 us -> 128 us
  other arithmetic: 163 us -> 68.9 us
  starting transfers between devices: 338 us -> 254 us
  local copies, waits for them, and re-layouts: 123 us -> 55.4 us
  waiting for transfers between devices: 393 us -> 363 us
    pallas_call x2 -> x30, Pallas kernels: 14.5 us -> 150 us  [the longest x6 56.3 us: rows_product(): pl.pallas_call(functools.partial(rows_product_kernel, n), grid=(height //...]
    dot_general x66 -> x52, matrix products: 190 us -> 78.3 us  [dot_tt(): lax.dot_general(former, latter, (dims, ((), ())), precision=precision, pr...]
    ppermute x155 -> x125, starting transfers between devices: 338 us -> 254 us  [send(): got.append(lax.ppermute(held[at], axis, perm))]
    reduce_sum x47 -> x2, other arithmetic: 64.9 us -> 0.05 us  [the longest x1 0.03 us: local(): gain_share = jnp.sum(gain_shares[0] + gain_shares[1], axis=1)]
    ppermute x155 -> x125, waiting for transfers between devices: 393 us -> 362 us  [send(): got.append(lax.ppermute(held[at], axis, perm))]
    unnamed x819 -> x437, local copies, waits for them, and re-layouts: 80 us -> 49.4 us
    unnamed x25 -> x7, other arithmetic: 29.2 us -> 0.01 us
    slice x22 -> x12, local copies, waits for them, and re-layouts: 14.9 us -> 1.54 us  [the longest x1 0.75 us: local(): by_slot[SCALE_ROW]]
  transfers between devices with their start and end apart: 159 -> 129, of which waited for: 59 -> 55; matrix products, arithmetic and copies ran while one was open for 36% -> 17% of each run, Pallas kernels for 2% -> 11%
where the time goes in v2:
time: 1060 us; the launch traced here: 1050 us
  waiting for transfers between devices  363 us (34%)
  starting transfers between devices  254 us (24%)
  Pallas kernels  161 us (15%)
  matrix products  128 us (12%)
  other arithmetic  68.9 us (7%)
  local copies, waits for them, and re-layouts  55.4 us (5%)
  between operations  19.8 us (2%)
    ppermute x125, waiting for transfers between devices, send(): got.append(lax.ppermute(held[at], axis, perm))  362 us
    ppermute x125, starting transfers between devices, send(): got.append(lax.ppermute(held[at], axis, perm))  254 us
    dot_general x52, matrix products, dot_tt(): lax.dot_general(former, latter, (dims, ((), ())), precision=precision, pr...  78.3 us
    pallas_call x6, Pallas kernels, rows_product(): pl.pallas_call(functools.partial(rows_product_kernel, n), grid=(height //...  56.3 us
    unnamed x437, local copies, waits for them, and re-layouts  49.4 us
  transfers between devices with their start and end apart: 129, of which 55 were waited for; matrix products, arithmetic and copies ran while one was open for 17% of the time, Pallas kernels for 11%

profile of v2, /device:TPU:0, one launch (start us, length us, event | category | flops | bytes accessed | tf_op | source)
XLA Modules:
  0.0 1051.1 jit_solution(4612359130006038151)
XLA Ops:
  23.4 7.1 collective-permute-done.4
  37.2 6.2 mix_streams.4
  44.5 6.2 mix_streams.5
  67.1 25.0 %collective-permute-done.6 = bf16[3,512,512]{2,1,0:T(8,128)(2,1)S(1)} collective-permute-done((bf16[3,512,512]{2,1,0:T(8,128)(2,1)S(1)}, bf16[3,512,512]{2,1,0:T(8,128)(2,1)S(1)}, u32[]{:S(2)}, u32[]{:S(2)}) %collective-permute-start.6) | collective-permute-done | bytes 1572896 | tf_op jit(solution)/shard_map/ppermute | solution.py:67
  92.1 5.3 collective-permute-done.7
  104.4 31.8 %collective-permute-done.10 = f32[8,512]{1,0:T(8,128)S(1)} collective-permute-done((f32[8,512]{1,0:T(8,128)S(1)}, f32[8,512]{1,0:T(8,128)S(1)}, u32[]{:S(2)}, u32[]{:S(2)}) %collective-permute-start.10) | collective-permute-done | bytes 16416 | tf_op jit(solution)/shard_map/ppermute | solution.py:67
  136.4 4.6 collective-permute-done.11
  147.5 6.8 collective-permute-start.16
  155.6 30.1 %collective-permute-done.13 = bf16[3,512,512]{2,1,0:T(8,128)(2,1)} collective-permute-done((bf16[3,512,512]{2,1,0:T(8,128)(2,1)}, bf16[3,512,512]{2,1,0:T(8,128)(2,1)}, u32[]{:S(2)}, u32[]{:S(2)}) %collective-permute-start.13) | collective-permute-done | bytes 1572896 | tf_op jit(solution)/shard_map/ppermute | solution.py:67
  197.9 4.4 attend_forward.2
  209.2 6.2 collective-permute-done.14
  220.2 5.9 collective-permute-start.18
  226.8 5.7 collective-permute-done.18
  233.7 15.2 %collective-permute-done.21 = bf16[3,512,512]{2,1,0:T(8,128)(2,1)} collective-permute-done((bf16[3,512,512]{2,1,0:T(8,128)(2,1)}, bf16[3,512,512]{2,1,0:T(8,128)(2,1)}, u32[]{:S(2)}, u32[]{:S(2)}) %collective-permute-start.21) | collective-permute-done | bytes 1572896 | tf_op jit(solution)/shard_map/ppermute | solution.py:67
  248.9 14.2 %collective-permute-start.22 = (bf16[512,512]{1,0:T(8,128)(2,1)S(1)}, bf16[512,512]{1,0:T(8,128)(2,1)S(1)}, u32[]{:S(2)}, u32[]{:S(2)}) collective-permute-start(bf16[512,512]{1,0:T(8,128)(2,1)S(1)} %add_convert_fusion.24), channel_id=1, source_target_pairs={{0,1},{1,2},{2,3},{4,5},{5,6},{6,7},{8,9},{9,10},{10,11},{12,13},{... | collective-permute-start | bytes 1572872 | tf_op jit(solution)/shard_map/ppermute | solution.py:67
  267.5 7.2 collective-permute-start.26
  277.3 32.4 %collective-permute-done.23.down = bf16[512,512]{1,0:T(8,128)(2,1)} collective-permute-done((bf16[512,512]{1,0:T(8,128)(2,1)}, bf16[512,512]{1,0:T(8,128)(2,1)}, u32[]{:S(2)}, u32[]{:S(2)}) %collective-permute-start.23) | collective-permute-done | bytes 524320 | tf_op jit(solution)/shard_map/ppermute | solution.py:67
  312.5 6.8 collective-permute-done.27
  327.0 7.7 collective-permute-done.29
  352.0 7.2 attend_forward.3
  369.8 6.0 fusion.242
  384.5 9.1 collective-permute-done.42
  394.0 6.1 collective-permute-start.44
  401.4 4.6 collective-permute-start.47
  409.3 10.2 multiply_convert_fusion.3
  439.6 4.6 collective-permute-start.54
  457.3 9.3 collective-permute-start.60
  468.2 10.2 fusion.243
  489.7 5.0 collective-permute-done.65.down
  500.8 10.2 multiply_convert_fusion.1
  542.8 6.5 collective-permute-done.72
  549.7 9.5 collective-permute-done.75
  580.2 5.1 attend_backward.2
  598.5 5.8 collective-permute-done.84
  610.0 4.5 collective-permute-done.83
  615.3 5.1 collective-permute-start.88
  629.3 8.3 collective-permute-done.87
  650.9 9.5 attend_backward.3
  674.6 16.8 %rows_product.6.refs_6_ = bf16[2048,2048]{1,0:T(8,128)(2,1)} custom-call(bf16[512,2048]{1,0:T(8,128)(2,1)S(1)} %pad_maximum_fusion.8.refs_0_, bf16[512,2048]{1,0:T(8,128)(2,1)} %copy-done.141, bf16[512,2048]{1,0:T(8,128)(2,1)} %get-tuple-element.352.refs_2_, bf16[512,2048]{1,0:T(8,128)(2,1)} %get-tuple-element.409.refs_3_, ...), custom_call_target="tpu_custom_call" | custom-call | tf_op jit(solution)/shard_map/rows_product/pallas_call | solution.py:792
  691.4 5.7 rows_product.7
  707.7 11.5 %collective-permute-done.94 = bf16[3,512,512]{2,1,0:T(8,128)(2,1)S(1)} collective-permute-done((bf16[3,512,512]{2,1,0:T(8,128)(2,1)}, bf16[3,512,512]{2,1,0:T(8,128)(2,1)S(1)}, u32[]{:S(2)}, u32[]{:S(2)}) %collective-permute-start.94) | collective-permute-done | bytes 1572896 | tf_op jit(solution)/shard_map/ppermute | solution.py:67
  721.0 16.2 %rows_product.8 = bf16[2048,2048]{1,0:T(8,128)(2,1)} custom-call(bf16[512,2048]{1,0:T(8,128)(2,1)S(1)} %pad_maximum_fusion.9.refs_0_, bf16[512,2048]{1,0:T(8,128)(2,1)S(1)} %pad_maximum_fusion.11.refs_1_, bf16[512,2048]{1,0:T(8,128)(2,1)} %copy-done.146, bf16[512,2048]{1,0:T(8,128)(2,1)} %copy-done.149, ...), custom_call_target="tpu_custom_call" | custom-call | tf_op jit(solution)/shard_map/rows_product/pallas_call | solution.py:792
  749.9 6.4 copy-done.3
  756.3 6.1 early_dots.2.refs_7_
  762.4 7.4 collective-permute-done.98
  774.0 12.7 %collective-permute-done.100 = f32[4,512]{1,0:T(4,128)S(1)} collective-permute-done((f32[4,512]{1,0:T(4,128)S(1)}, f32[4,512]{1,0:T(4,128)S(1)}, u32[]{:S(2)}, u32[]{:S(2)}) %collective-permute-start.100) | collective-permute-done | bytes 8224 | tf_op jit(solution)/shard_map/ppermute | solution.py:67
  790.9 5.8 rows_product.9.refs_8_
  796.7 6.1 rows_product.10.refs_8_
  802.8 5.8 rows_product.11
  808.6 5.6 collective-permute-start.102
  822.5 4.9 collective-permute-start.105
  827.4 5.8 copy-done.4
  834.1 6.1 early_dots.3
  840.3 7.9 collective-permute-done.102
  855.9 6.6 collective-permute-start.109
  876.6 21.0 %collective-permute-done.107 = f32[80,512]{1,0:T(8,128)S(1)} collective-permute-done((f32[80,512]{1,0:T(8,128)S(1)}, f32[80,512]{1,0:T(8,128)S(1)}, u32[]{:S(2)}, u32[]{:S(2)}) %collective-permute-start.107) | collective-permute-done | bytes 163872 | tf_op jit(solution)/shard_map/ppermute | solution.py:67
  899.6 6.1 late_dots.2
  911.9 5.4 fusion.1.d0.d1.d2
  932.2 6.1 late_dots.3
  951.9 6.7 collective-permute-done.104
  978.9 10.1 layer_grads.2.refs_0_
  996.7 5.4 collective-permute-start.90
  1002.1 10.1 layer_grads.3
  1021.6 8.7 collective-permute-start.122
  (862 shorter events, 448.8 us)
Async XLA Ops:
  7.2 903.7 %reduce-scatter.9.cloned.1.call-start = ((), (), s32[]{:S(2)}) async-start(), calls=%async_computation.6 | async-start | bytes 2359296 | tf_op jit(solution)/shard_map/reduce_scatter | solution.py:845
  57.4 34.7 %collective-permute-start.6 = (bf16[3,512,512]{2,1,0:T(8,128)(2,1)S(1)}, bf16[3,512,512]{2,1,0:T(8,128)(2,1)S(1)}, u32[]{:S(2)}, u32[]{:S(2)}) collective-permute-start(bf16[3,512,512]{2,1,0:T(8,128)(2,1)S(1)} %get-tuple-element.234), channel_id=1, source_target_pairs={{0,1},{1,2},{2,3},{4,5},{5,6},{6,7},{8,9},{9,10},{10,11},{12,13},{... | collective-permute-start | bytes 4718600 | tf_op jit(solution)/shard_map/ppermute | solution.py:67
  60.5 36.9 %collective-permute-start.7 = (bf16[3,512,512]{2,1,0:T(8,128)(2,1)S(1)}, bf16[3,512,512]{2,1,0:T(8,128)(2,1)S(1)}, u32[]{:S(2)}, u32[]{:S(2)}) collective-permute-start(bf16[3,512,512]{2,1,0:T(8,128)(2,1)S(1)} %get-tuple-element.234), channel_id=1, source_target_pairs={{1,0},{2,1},{3,2},{5,4},{6,5},{7,6},{9,8},{10,9},{11,10},{13,12},{... | collective-permute-start | bytes 4718600 | tf_op jit(solution)/shard_map/ppermute | solution.py:67
  97.3 47.0 %collective-permute-start.8 = (bf16[3,512,512]{2,1,0:T(8,128)(2,1)S(1)}, bf16[3,512,512]{2,1,0:T(8,128)(2,1)}, u32[]{:S(2)}, u32[]{:S(2)}) collective-permute-start(bf16[3,512,512]{2,1,0:T(8,128)(2,1)S(1)} %collective-permute-done.6), channel_id=1, source_target_pairs={{1,2},{2,3},{5,6},{6,7},{9,10},{10,11},{13,14},{14,15},{17,18},{18... | collective-permute-start | bytes 4718600 | tf_op jit(solution)/shard_map/ppermute | solution.py:67
  99.2 45.1 %collective-permute-start.9 = (bf16[3,512,512]{2,1,0:T(8,128)(2,1)S(1)}, bf16[3,512,512]{2,1,0:T(8,128)(2,1)}, u32[]{:S(2)}, u32[]{:S(2)}) collective-permute-start(bf16[3,512,512]{2,1,0:T(8,128)(2,1)S(1)} %collective-permute-done.7), channel_id=1, source_target_pairs={{1,0},{2,1},{5,4},{6,5},{9,8},{10,9},{13,12},{14,13},{17,16},{18,1... | collective-permute-start | bytes 4718600 | tf_op jit(solution)/shard_map/ppermute | solution.py:67
  100.5 35.8 %collective-permute-start.10 = (f32[8,512]{1,0:T(8,128)S(1)}, f32[8,512]{1,0:T(8,128)S(1)}, u32[]{:S(2)}, u32[]{:S(2)}) collective-permute-start(f32[8,512]{1,0:T(8,128)S(1)} %get-tuple-element.236), channel_id=1, source_target_pairs={{0,1},{1,0},{2,3},{3,2},{4,5},{5,4},{6,7},{7,6},{8,9},{9,8},{10,11... | collective-permute-start | bytes 49160 | tf_op jit(solution)/shard_map/ppermute | solution.py:67
  146.2 39.5 %collective-permute-start.13 = (bf16[3,512,512]{2,1,0:T(8,128)(2,1)}, bf16[3,512,512]{2,1,0:T(8,128)(2,1)}, u32[]{:S(2)}, u32[]{:S(2)}) collective-permute-start(bf16[3,512,512]{2,1,0:T(8,128)(2,1)} %collective-permute-done.9), channel_id=1, source_target_pairs={{1,0},{5,4},{9,8},{13,12},{17,16},{21,20},{25,24},{29,28}} | collective-permute-start | bytes 4718600 | tf_op jit(solution)/shard_map/ppermute | solution.py:67
  147.5 69.6 %collective-permute-start.16 = (bf16[3,512,512]{2,1,0:T(8,128)(2,1)}, bf16[3,512,512]{2,1,0:T(8,128)(2,1)}, u32[]{:S(2)}, u32[]{:S(2)}) collective-permute-start(bf16[3,512,512]{2,1,0:T(8,128)(2,1)} %copy-done.87), channel_id=1, source_target_pairs={{0,1},{1,2},{2,3},{4,5},{5,6},{6,7},{8,9},{9,10},{10,11},{12,13},{... | collective-permute-start | bytes 4718600 | tf_op jit(solution)/shard_map/ppermute | solution.py:67
  154.3 62.8 %collective-permute-start.17 = (bf16[3,512,512]{2,1,0:T(8,128)(2,1)}, bf16[3,512,512]{2,1,0:T(8,128)(2,1)}, u32[]{:S(2)}, u32[]{:S(2)}) collective-permute-start(bf16[3,512,512]{2,1,0:T(8,128)(2,1)} %copy-done.87), channel_id=1, source_target_pairs={{1,0},{2,1},{3,2},{5,4},{6,5},{7,6},{9,8},{10,9},{11,10},{13,12},{... | collective-permute-start | bytes 4718600 | tf_op jit(solution)/shard_map/ppermute | solution.py:67
  217.1 16.6 %collective-permute-start.20 = (bf16[3,512,512]{2,1,0:T(8,128)(2,1)}, bf16[3,512,512]{2,1,0:T(8,128)(2,1)}, u32[]{:S(2)}, u32[]{:S(2)}) collective-permute-start(bf16[3,512,512]{2,1,0:T(8,128)(2,1)} %collective-permute-done.16), channel_id=1, source_target_pairs={{1,2},{2,3},{5,6},{6,7},{9,10},{10,11},{13,14},{14,15},{17,18},{18... | collective-permute-start | bytes 4718600 | tf_op jit(solution)/shard_map/ppermute | solution.py:67
  218.9 30.0 %collective-permute-start.21 = (bf16[3,512,512]{2,1,0:T(8,128)(2,1)}, bf16[3,512,512]{2,1,0:T(8,128)(2,1)}, u32[]{:S(2)}, u32[]{:S(2)}) collective-permute-start(bf16[3,512,512]{2,1,0:T(8,128)(2,1)} %collective-permute-done.17), channel_id=1, source_target_pairs={{1,0},{2,1},{5,4},{6,5},{9,8},{10,9},{13,12},{14,13},{17,16},{18,1... | collective-permute-start | bytes 4718600 | tf_op jit(solution)/shard_map/ppermute | solution.py:67
  248.9 25.8 %collective-permute-start.22 = (bf16[512,512]{1,0:T(8,128)(2,1)S(1)}, bf16[512,512]{1,0:T(8,128)(2,1)S(1)}, u32[]{:S(2)}, u32[]{:S(2)}) collective-permute-start(bf16[512,512]{1,0:T(8,128)(2,1)S(1)} %add_convert_fusion.24), channel_id=1, source_target_pairs={{0,1},{1,2},{2,3},{4,5},{5,6},{6,7},{8,9},{9,10},{10,11},{12,13},{... | collective-permute-start | bytes 1572872 | tf_op jit(solution)/shard_map/ppermute | solution.py:67
  263.1 79.0 %collective-permute-start.24 = (bf16[3,512,512]{2,1,0:T(8,128)(2,1)}, bf16[3,512,512]{2,1,0:T(8,128)(2,1)}, u32[]{:S(2)}, u32[]{:S(2)}) collective-permute-start(bf16[3,512,512]{2,1,0:T(8,128)(2,1)} %collective-permute-done.20), channel_id=1, source_target_pairs={{2,3},{6,7},{10,11},{14,15},{18,19},{22,23},{26,27},{30,31}} | collective-permute-start | bytes 4718600 | tf_op jit(solution)/shard_map/ppermute | solution.py:67
  264.9 78.5 %collective-permute-start.25 = (bf16[3,512,512]{2,1,0:T(8,128)(2,1)}, bf16[3,512,512]{2,1,0:T(8,128)(2,1)}, u32[]{:S(2)}, u32[]{:S(2)}) collective-permute-start(bf16[3,512,512]{2,1,0:T(8,128)(2,1)} %collective-permute-done.21), channel_id=1, source_target_pairs={{1,0},{5,4},{9,8},{13,12},{17,16},{21,20},{25,24},{29,28}} | collective-permute-start | bytes 4718600 | tf_op jit(solution)/shard_map/ppermute | solution.py:67
  266.2 43.5 %collective-permute-start.23 = (bf16[512,512]{1,0:T(8,128)(2,1)}, bf16[512,512]{1,0:T(8,128)(2,1)}, u32[]{:S(2)}, u32[]{:S(2)}) collective-permute-start(bf16[512,512]{1,0:T(8,128)(2,1)} %add_convert_fusion.23), channel_id=1, source_target_pairs={{1,0},{2,1},{3,2},{5,4},{6,5},{7,6},{9,8},{10,9},{11,10},{13,12},{... | collective-permute-start | bytes 1572872 | tf_op jit(solution)/shard_map/ppermute | solution.py:67
  267.5 45.0 %collective-permute-start.26 = (bf16[512,512]{1,0:T(8,128)(2,1)}, bf16[512,512]{1,0:T(8,128)(2,1)}, u32[]{:S(2)}, u32[]{:S(2)}) collective-permute-start(bf16[512,512]{1,0:T(8,128)(2,1)} %get-tuple-element.227), channel_id=1, source_target_pairs={{0,1},{1,2},{2,3},{4,5},{5,6},{6,7},{8,9},{9,10},{10,11},{12,13},{... | collective-permute-start | bytes 1572872 | tf_op jit(solution)/shard_map/ppermute | solution.py:67
  275.5 43.8 %collective-permute-start.27 = (bf16[512,512]{1,0:T(8,128)(2,1)}, bf16[512,512]{1,0:T(8,128)(2,1)}, u32[]{:S(2)}, u32[]{:S(2)}) collective-permute-start(bf16[512,512]{1,0:T(8,128)(2,1)} %get-tuple-element.227), channel_id=1, source_target_pairs={{1,0},{2,1},{3,2},{5,4},{6,5},{7,6},{9,8},{10,9},{11,10},{13,12},{... | collective-permute-start | bytes 1572872 | tf_op jit(solution)/shard_map/ppermute | solution.py:67
  319.3 16.4 %collective-permute-start.30 = (bf16[512,512]{1,0:T(8,128)(2,1)}, bf16[512,512]{1,0:T(8,128)(2,1)S(1)}, u32[]{:S(2)}, u32[]{:S(2)}) collective-permute-start(bf16[512,512]{1,0:T(8,128)(2,1)} %collective-permute-done.26), channel_id=1, source_target_pairs={{1,2},{2,3},{5,6},{6,7},{9,10},{10,11},{13,14},{14,15},{17,18},{18... | collective-permute-start | bytes 1572872 | tf_op jit(solution)/shard_map/ppermute | solution.py:67
  320.0 17.8 %collective-permute-start.31 = (bf16[512,512]{1,0:T(8,128)(2,1)}, bf16[512,512]{1,0:T(8,128)(2,1)S(1)}, u32[]{:S(2)}, u32[]{:S(2)}) collective-permute-start(bf16[512,512]{1,0:T(8,128)(2,1)} %collective-permute-done.27), channel_id=1, source_target_pairs={{1,0},{2,1},{5,4},{6,5},{9,8},{10,9},{13,12},{14,13},{17,16},{18,1... | collective-permute-start | bytes 1572872 | tf_op jit(solution)/shard_map/ppermute | solution.py:67
  337.8 22.3 %collective-permute-start.32 = (bf16[512,512]{1,0:T(8,128)(2,1)S(1)}, bf16[512,512]{1,0:T(8,128)(2,1)}, u32[]{:S(2)}, u32[]{:S(2)}) collective-permute-start(bf16[512,512]{1,0:T(8,128)(2,1)S(1)} %mlp_input.2), channel_id=1, source_target_pairs={{0,1},{1,2},{2,3},{4,5},{5,6},{6,7},{8,9},{9,10},{10,11},{12,13},{... | collective-permute-start | bytes 1572872 | tf_op jit(solution)/shard_map/ppermute | solution.py:67
  340.1 20.0 %collective-permute-start.33 = (bf16[512,512]{1,0:T(8,128)(2,1)S(1)}, bf16[512,512]{1,0:T(8,128)(2,1)}, u32[]{:S(2)}, u32[]{:S(2)}) collective-permute-start(bf16[512,512]{1,0:T(8,128)(2,1)S(1)} %mlp_input.2), channel_id=1, source_target_pairs={{1,0},{2,1},{3,2},{5,4},{6,5},{7,6},{9,8},{10,9},{11,10},{13,12},{... | collective-permute-start | bytes 1572872 | tf_op jit(solution)/shard_map/ppermute | solution.py:67
  341.4 24.9 %collective-permute-start.38 = (bf16[512,512]{1,0:T(8,128)(2,1)S(1)}, bf16[512,512]{1,0:T(8,128)(2,1)S(1)}, u32[]{:S(2)}, u32[]{:S(2)}) collective-permute-start(bf16[512,512]{1,0:T(8,128)(2,1)S(1)} %collective-permute-done.30), channel_id=1, source_target_pairs={{2,3},{6,7},{10,11},{14,15},{18,19},{22,23},{26,27},{30,31}} | collective-permute-start | bytes 1572872 | tf_op jit(solution)/shard_map/ppermute | solution.py:67
  342.1 25.8 %collective-permute-start.39 = (bf16[512,512]{1,0:T(8,128)(2,1)S(1)}, bf16[512,512]{1,0:T(8,128)(2,1)S(1)}, u32[]{:S(2)}, u32[]{:S(2)}) collective-permute-start(bf16[512,512]{1,0:T(8,128)(2,1)S(1)} %collective-permute-done.31), channel_id=1, source_target_pairs={{1,0},{5,4},{9,8},{13,12},{17,16},{21,20},{25,24},{29,28}} | collective-permute-start | bytes 1572872 | tf_op jit(solution)/shard_map/ppermute | solution.py:67
  360.2 15.7 %collective-permute-start.35 = (bf16[512,512]{1,0:T(8,128)(2,1)S(1)}, bf16[512,512]{1,0:T(8,128)(2,1)S(1)}, u32[]{:S(2)}, u32[]{:S(2)}) collective-permute-start(bf16[512,512]{1,0:T(8,128)(2,1)S(1)} %get-tuple-element.274), channel_id=1, source_target_pairs={{3,2},{7,6},{11,10},{15,14},{19,18},{23,22},{27,26},{31,30}} | collective-permute-start | bytes 1572872 | tf_op jit(solution)/shard_map/ppermute | solution.py:67
  382.5 23.6 %collective-permute-start.40 = (bf16[512,512]{1,0:T(8,128)(2,1)S(1)}, bf16[512,512]{1,0:T(8,128)(2,1)S(1)}, u32[]{:S(2)}, u32[]{:S(2)}) collective-permute-start(bf16[512,512]{1,0:T(8,128)(2,1)S(1)} %collective-permute-done.36), channel_id=1, source_target_pairs={{2,3},{6,7},{10,11},{14,15},{18,19},{22,23},{26,27},{30,31}} | collective-permute-start | bytes 1572872 | tf_op jit(solution)/shard_map/ppermute | solution.py:67
  383.2 24.6 %collective-permute-start.41 = (bf16[512,512]{1,0:T(8,128)(2,1)S(1)}, bf16[512,512]{1,0:T(8,128)(2,1)S(1)}, u32[]{:S(2)}, u32[]{:S(2)}) collective-permute-start(bf16[512,512]{1,0:T(8,128)(2,1)S(1)} %collective-permute-done.37), channel_id=1, source_target_pairs={{1,0},{5,4},{9,8},{13,12},{17,16},{21,20},{25,24},{29,28}} | collective-permute-start | bytes 1572872 | tf_op jit(solution)/shard_map/ppermute | solution.py:67
  394.0 26.0 %collective-permute-start.44 = (bf16[512,512]{1,0:T(8,128)(2,1)S(1)}, bf16[512,512]{1,0:T(8,128)(2,1)S(1)}, u32[]{:S(2)}, u32[]{:S(2)}) collective-permute-start(bf16[512,512]{1,0:T(8,128)(2,1)S(1)} %add_convert_fusion.21), channel_id=1, source_target_pairs={{0,1},{1,2},{2,3},{4,5},{5,6},{6,7},{8,9},{9,10},{10,11},{12,13},{... | collective-permute-start | bytes 1572872 | tf_op jit(solution)/shard_map/ppermute | solution.py:67
  400.1 19.9 %collective-permute-start.45 = (bf16[512,512]{1,0:T(8,128)(2,1)S(1)}, bf16[512,512]{1,0:T(8,128)(2,1)S(1)}, u32[]{:S(2)}, u32[]{:S(2)}) collective-permute-start(bf16[512,512]{1,0:T(8,128)(2,1)S(1)} %add_convert_fusion.20), channel_id=1, source_target_pairs={{1,0},{2,1},{3,2},{5,4},{6,5},{7,6},{9,8},{10,9},{11,10},{13,12},{... | collective-permute-start | bytes 1572872 | tf_op jit(solution)/shard_map/ppermute | solution.py:67
  401.4 26.1 %collective-permute-start.47 = (bf16[512,512]{1,0:T(8,128)(2,1)S(1)}, bf16[512,512]{1,0:T(8,128)(2,1)S(1)}, u32[]{:S(2)}, u32[]{:S(2)}) collective-permute-start(bf16[512,512]{1,0:T(8,128)(2,1)S(1)} %copy-done.150), channel_id=1, source_target_pairs={{0,1},{1,2},{2,3},{4,5},{5,6},{6,7},{8,9},{9,10},{10,11},{12,13},{... | collective-permute-start | bytes 1572872 | tf_op jit(solution)/shard_map/ppermute | solution.py:67
  406.0 21.5 %collective-permute-start.48 = (bf16[512,512]{1,0:T(8,128)(2,1)S(1)}, bf16[512,512]{1,0:T(8,128)(2,1)S(1)}, u32[]{:S(2)}, u32[]{:S(2)}) collective-permute-start(bf16[512,512]{1,0:T(8,128)(2,1)S(1)} %copy-done.150), channel_id=1, source_target_pairs={{1,0},{2,1},{3,2},{5,4},{6,5},{7,6},{9,8},{10,9},{11,10},{13,12},{... | collective-permute-start | bytes 1572872 | tf_op jit(solution)/shard_map/ppermute | solution.py:67
  450.8 15.8 %collective-permute-start.52 = (bf16[512,512]{1,0:T(8,128)(2,1)S(1)}, bf16[512,512]{1,0:T(8,128)(2,1)S(1)}, u32[]{:S(2)}, u32[]{:S(2)}) collective-permute-start(bf16[512,512]{1,0:T(8,128)(2,1)S(1)} %collective-permute-done.49), channel_id=1, source_target_pairs={{2,3},{6,7},{10,11},{14,15},{18,19},{22,23},{26,27},{30,31}} | collective-permute-start | bytes 1572872 | tf_op jit(solution)/shard_map/ppermute | solution.py:67
  451.5 16.1 %collective-permute-start.53 = (bf16[512,512]{1,0:T(8,128)(2,1)S(1)}, bf16[512,512]{1,0:T(8,128)(2,1)S(1)}, u32[]{:S(2)}, u32[]{:S(2)}) collective-permute-start(bf16[512,512]{1,0:T(8,128)(2,1)S(1)} %collective-permute-done.50), channel_id=1, source_target_pairs={{1,0},{5,4},{9,8},{13,12},{17,16},{21,20},{25,24},{29,28}} | collective-permute-start | bytes 1572872 | tf_op jit(solution)/shard_map/ppermute | solution.py:67
  455.3 23.5 %collective-permute-start.58 = (bf16[512,512]{1,0:T(8,128)(2,1)S(1)}, bf16[512,512]{1,0:T(8,128)(2,1)S(1)}, u32[]{:S(2)}, u32[]{:S(2)}) collective-permute-start(bf16[512,512]{1,0:T(8,128)(2,1)S(1)} %collective-permute-done.54), channel_id=1, source_target_pairs={{1,2},{2,3},{5,6},{6,7},{9,10},{10,11},{13,14},{14,15},{17,18},{18... | collective-permute-start | bytes 1572872 | tf_op jit(solution)/shard_map/ppermute | solution.py:67
  456.0 22.9 %collective-permute-start.59 = (bf16[512,512]{1,0:T(8,128)(2,1)S(1)}, bf16[512,512]{1,0:T(8,128)(2,1)S(1)}, u32[]{:S(2)}, u32[]{:S(2)}) collective-permute-start(bf16[512,512]{1,0:T(8,128)(2,1)S(1)} %collective-permute-done.55), channel_id=1, source_target_pairs={{1,0},{2,1},{5,4},{6,5},{9,8},{10,9},{13,12},{14,13},{17,16},{18,1... | collective-permute-start | bytes 1572872 | tf_op jit(solution)/shard_map/ppermute | solution.py:67
  457.3 21.2 %collective-permute-start.60 = (bf16[512,512]{1,0:T(8,128)(2,1)S(1)}, bf16[512,512]{1,0:T(8,128)(2,1)S(1)}, u32[]{:S(2)}, u32[]{:S(2)}) collective-permute-start(bf16[512,512]{1,0:T(8,128)(2,1)S(1)} %add_convert_fusion.19), channel_id=1, source_target_pairs={{0,1},{1,2},{4,5},{5,6},{8,9},{9,10},{12,13},{13,14},{16,17},{17,1... | collective-permute-start | bytes 1572872 | tf_op jit(solution)/shard_map/ppermute | solution.py:67
  496.1 16.2 %collective-permute-start.66 = (f32[8,512]{1,0:T(8,128)S(1)}, f32[8,512]{1,0:T(8,128)S(1)}, u32[]{:S(2)}, u32[]{:S(2)}) collective-permute-start(f32[8,512]{1,0:T(8,128)S(1)} %get-tuple-element.313), channel_id=1, source_target_pairs={{0,1},{1,0},{2,3},{3,2},{4,5},{5,4},{6,7},{7,6},{8,9},{9,8},{10,11... | collective-permute-start | bytes 49160 | tf_op jit(solution)/shard_map/ppermute | solution.py:67
  541.5 17.8 %collective-permute-start.75 = (bf16[512,512]{1,0:T(8,128)(2,1)S(1)}, bf16[512,512]{1,0:T(8,128)(2,1)S(1)}, u32[]{:S(2)}, u32[]{:S(2)}) collective-permute-start(bf16[512,512]{1,0:T(8,128)(2,1)S(1)} %collective-permute-done.71), channel_id=1, source_target_pairs={{1,0},{2,1},{5,4},{6,5},{9,8},{10,9},{13,12},{14,13},{17,16},{18,1... | collective-permute-start | bytes 1572872 | tf_op jit(solution)/shard_map/ppermute | solution.py:67
  597.2 17.2 %collective-permute-start.83 = (bf16[512,512]{1,0:T(8,128)(2,1)S(1)}, bf16[512,512]{1,0:T(8,128)(2,1)S(1)}, u32[]{:S(2)}, u32[]{:S(2)}) collective-permute-start(bf16[512,512]{1,0:T(8,128)(2,1)S(1)} %get-tuple-element.340), channel_id=1, source_target_pairs={{1,0},{2,1},{3,2},{5,4},{6,5},{7,6},{9,8},{10,9},{11,10},{13,12},{... | collective-permute-start | bytes 1572872 | tf_op jit(solution)/shard_map/ppermute | solution.py:67
  697.2 220.2 %reduce-scatter.5.cloned.1.call-start = ((), (), s32[]{:S(2)}) async-start(), calls=%async_computation.4 | async-start | bytes 9437184 | tf_op jit(solution)/shard_map/reduce_scatter | solution.py:845
  697.9 222.3 %reduce-scatter.7.cloned.1.call-start = ((), (), s32[]{:S(2)}) async-start(), calls=%async_computation.5 | async-start | bytes 9437184 | tf_op jit(solution)/shard_map/reduce_scatter | solution.py:845
  698.9 20.3 %collective-permute-start.94 = (bf16[3,512,512]{2,1,0:T(8,128)(2,1)}, bf16[3,512,512]{2,1,0:T(8,128)(2,1)S(1)}, u32[]{:S(2)}, u32[]{:S(2)}) collective-permute-start(bf16[3,512,512]{2,1,0:T(8,128)(2,1)} %fusion.3), channel_id=1, source_target_pairs={{0,1},{4,5},{8,9},{12,13},{16,17},{20,21},{24,25},{28,29}} | collective-permute-start | bytes 4718600 | tf_op jit(solution)/shard_map/ppermute | solution.py:67
  737.2 280.0 %reduce-scatter.11.cloned.1.call-start = ((), (), s32[]{:S(2)}) async-start(), calls=%async_computation.7 | async-start | bytes 7077888 | tf_op jit(solution)/shard_map/reduce_scatter | solution.py:845
  737.3 25.1 %collective-permute-start.99 = (bf16[3,512,512]{2,1,0:T(8,128)(2,1)}, bf16[3,512,512]{2,1,0:T(8,128)(2,1)S(1)}, u32[]{:S(2)}, u32[]{:S(2)}) collective-permute-start(bf16[3,512,512]{2,1,0:T(8,128)(2,1)} %fusion.4.refs_5_), channel_id=1, source_target_pairs={{3,2},{7,6},{11,10},{15,14},{19,18},{23,22},{27,26},{31,30}} | collective-permute-start | bytes 4718600 | tf_op jit(solution)/shard_map/ppermute | solution.py:67
  738.2 31.7 %collective-permute-start.98 = (bf16[3,512,512]{2,1,0:T(8,128)(2,1)}, bf16[3,512,512]{2,1,0:T(8,128)(2,1)S(1)}, u32[]{:S(2)}, u32[]{:S(2)}) collective-permute-start(bf16[3,512,512]{2,1,0:T(8,128)(2,1)} %fusion.5.refs_4_), channel_id=1, source_target_pairs={{0,1},{4,5},{8,9},{12,13},{16,17},{20,21},{24,25},{28,29}} | collective-permute-start | bytes 4718600 | tf_op jit(solution)/shard_map/ppermute | solution.py:67
  742.6 44.2 %collective-permute-start.96 = (bf16[3,512,512]{2,1,0:T(8,128)(2,1)}, bf16[3,512,512]{2,1,0:T(8,128)(2,1)S(1)}, u32[]{:S(2)}, u32[]{:S(2)}) collective-permute-start(bf16[3,512,512]{2,1,0:T(8,128)(2,1)} %add_convert_fusion.5.refs_4_.refs_5_), channel_id=1, source_target_pairs={{0,1},{1,2},{4,5},{5,6},{8,9},{9,10},{12,13},{13,14},{16,17},{17,1... | collective-permute-start | bytes 4718600 | tf_op jit(solution)/shard_map/ppermute | solution.py:67
  744.0 43.4 %collective-permute-start.97 = (bf16[3,512,512]{2,1,0:T(8,128)(2,1)}, bf16[3,512,512]{2,1,0:T(8,128)(2,1)S(1)}, u32[]{:S(2)}, u32[]{:S(2)}) collective-permute-start(bf16[3,512,512]{2,1,0:T(8,128)(2,1)} %add_convert_fusion.5.refs_4_.refs_5_), channel_id=1, source_target_pairs={{2,1},{3,2},{6,5},{7,6},{10,9},{11,10},{14,13},{15,14},{18,17},{19... | collective-permute-start | bytes 4718600 | tf_op jit(solution)/shard_map/ppermute | solution.py:67
  808.6 39.6 %collective-permute-start.102 = (bf16[3,512,512]{2,1,0:T(8,128)(2,1)}, bf16[3,512,512]{2,1,0:T(8,128)(2,1)}, u32[]{:S(2)}, u32[]{:S(2)}) collective-permute-start(bf16[3,512,512]{2,1,0:T(8,128)(2,1)} %add_convert_fusion.2), channel_id=1, source_target_pairs={{0,1},{1,2},{4,5},{5,6},{8,9},{9,10},{12,13},{13,14},{16,17},{17,1... | collective-permute-start | bytes 4718600 | tf_op jit(solution)/shard_map/ppermute | solution.py:67
  814.2 37.1 %collective-permute-start.103 = (bf16[3,512,512]{2,1,0:T(8,128)(2,1)}, bf16[3,512,512]{2,1,0:T(8,128)(2,1)}, u32[]{:S(2)}, u32[]{:S(2)}) collective-permute-start(bf16[3,512,512]{2,1,0:T(8,128)(2,1)} %add_convert_fusion.2), channel_id=1, source_target_pairs={{2,1},{3,2},{6,5},{7,6},{10,9},{11,10},{14,13},{15,14},{18,17},{19... | collective-permute-start | bytes 4718600 | tf_op jit(solution)/shard_map/ppermute | solution.py:67
  821.1 33.4 %collective-permute-start.101 = (f32[80,512]{1,0:T(8,128)S(1)}, f32[80,512]{1,0:T(8,128)S(1)}, u32[]{:S(2)}, u32[]{:S(2)}) collective-permute-start(f32[80,512]{1,0:T(8,128)S(1)} %early_dots.2.refs_7_), channel_id=1, source_target_pairs={{0,1},{1,0},{2,3},{3,2},{4,5},{5,4},{6,7},{7,6},{8,9},{9,8},{10,11... | collective-permute-start | bytes 491528 | tf_op jit(solution)/shard_map/ppermute | solution.py:67
  821.1 76.5 %collective-permute-start.106 = (bf16[3,512,512]{2,1,0:T(8,128)(2,1)}, bf16[3,512,512]{2,1,0:T(8,128)(2,1)S(1)}, u32[]{:S(2)}, u32[]{:S(2)}) collective-permute-start(bf16[3,512,512]{2,1,0:T(8,128)(2,1)} %add_convert_fusion.3.refs_5_), channel_id=1, source_target_pairs={{1,0},{2,1},{3,2},{5,4},{6,5},{7,6},{9,8},{10,9},{11,10},{13,12},{... | collective-permute-start | bytes 4718600 | tf_op jit(solution)/shard_map/ppermute | solution.py:67
  822.5 75.2 %collective-permute-start.105 = (bf16[3,512,512]{2,1,0:T(8,128)(2,1)S(1)}, bf16[3,512,512]{2,1,0:T(8,128)(2,1)S(1)}, u32[]{:S(2)}, u32[]{:S(2)}) collective-permute-start(bf16[3,512,512]{2,1,0:T(8,128)(2,1)S(1)} %copy-done.12), channel_id=1, source_target_pairs={{0,1},{1,2},{2,3},{4,5},{5,6},{6,7},{8,9},{9,10},{10,11},{12,13},{... | collective-permute-start | bytes 4718600 | tf_op jit(solution)/shard_map/ppermute | solution.py:67
  854.5 57.4 %collective-permute-start.110 = (bf16[3,512,512]{2,1,0:T(8,128)(2,1)}, bf16[3,512,512]{2,1,0:T(8,128)(2,1)}, u32[]{:S(2)}, u32[]{:S(2)}) collective-permute-start(bf16[3,512,512]{2,1,0:T(8,128)(2,1)} %add_convert_fusion), channel_id=1, source_target_pairs={{1,0},{2,1},{3,2},{5,4},{6,5},{7,6},{9,8},{10,9},{11,10},{13,12},{... | collective-permute-start | bytes 4718600 | tf_op jit(solution)/shard_map/ppermute | solution.py:67
  855.9 56.0 %collective-permute-start.109 = (bf16[3,512,512]{2,1,0:T(8,128)(2,1)}, bf16[3,512,512]{2,1,0:T(8,128)(2,1)}, u32[]{:S(2)}, u32[]{:S(2)}) collective-permute-start(bf16[3,512,512]{2,1,0:T(8,128)(2,1)} %add_convert_fusion.1), channel_id=1, source_target_pairs={{0,1},{1,2},{2,3},{4,5},{5,6},{6,7},{8,9},{9,10},{10,11},{12,13},{... | collective-permute-start | bytes 4718600 | tf_op jit(solution)/shard_map/ppermute | solution.py:67
  867.5 30.1 %collective-permute-start.107 = (f32[80,512]{1,0:T(8,128)S(1)}, f32[80,512]{1,0:T(8,128)S(1)}, u32[]{:S(2)}, u32[]{:S(2)}) collective-permute-start(f32[80,512]{1,0:T(8,128)S(1)} %early_dots.3), channel_id=1, source_target_pairs={{0,1},{1,0},{2,3},{3,2},{4,5},{5,4},{6,7},{7,6},{8,9},{9,8},{10,11... | collective-permute-start | bytes 491528 | tf_op jit(solution)/shard_map/ppermute | solution.py:67
  943.7 31.6 %collective-permute-start.118 = (bf16[512,512]{1,0:T(8,128)(2,1)}, bf16[512,512]{1,0:T(8,128)(2,1)}, u32[]{:S(2)}, u32[]{:S(2)}) collective-permute-start(bf16[512,512]{1,0:T(8,128)(2,1)} %get-tuple-element.408), channel_id=1, source_target_pairs={{3,2},{7,6},{11,10},{15,14},{19,18},{23,22},{27,26},{31,30}} | collective-permute-start | bytes 1572872 | tf_op jit(solution)/shard_map/ppermute | solution.py:67
  945.2 30.1 %collective-permute-start.117 = (bf16[512,512]{1,0:T(8,128)(2,1)}, bf16[512,512]{1,0:T(8,128)(2,1)}, u32[]{:S(2)}, u32[]{:S(2)}) collective-permute-start(bf16[512,512]{1,0:T(8,128)(2,1)} %get-tuple-element.407), channel_id=1, source_target_pairs={{0,1},{4,5},{8,9},{12,13},{16,17},{20,21},{24,25},{28,29}} | collective-permute-start | bytes 1572872 | tf_op jit(solution)/shard_map/ppermute | solution.py:67
  989.0 23.2 %collective-permute-start.120 = (bf16[512,512]{1,0:T(8,128)(2,1)S(1)}, bf16[512,512]{1,0:T(8,128)(2,1)S(1)}, u32[]{:S(2)}, u32[]{:S(2)}) collective-permute-start(bf16[512,512]{1,0:T(8,128)(2,1)S(1)} %add_convert_fusion.9), channel_id=1, source_target_pairs={{0,1},{1,2},{4,5},{5,6},{8,9},{9,10},{12,13},{13,14},{16,17},{17,1... | collective-permute-start | bytes 1572872 | tf_op jit(solution)/shard_map/ppermute | solution.py:67
  990.6 21.5 %collective-permute-start.119 = (f32[107,512]{1,0:T(8,128)S(1)}, f32[107,512]{1,0:T(8,128)S(1)}, u32[]{:S(2)}, u32[]{:S(2)}) collective-permute-start(f32[107,512]{1,0:T(8,128)S(1)} %fusion.220), channel_id=1, source_target_pairs={{0,8},{4,12},{8,0},{12,4},{16,24},{20,28},{24,16},{28,20},{1,9},{5... | collective-permute-start | bytes 657416 | tf_op jit(solution)/shard_map/ppermute | solution.py:67
  992.4 20.8 %collective-permute-start.121 = (bf16[512,512]{1,0:T(8,128)(2,1)S(1)}, bf16[512,512]{1,0:T(8,128)(2,1)S(1)}, u32[]{:S(2)}, u32[]{:S(2)}) collective-permute-start(bf16[512,512]{1,0:T(8,128)(2,1)S(1)} %add_convert_fusion.9), channel_id=1, source_target_pairs={{2,1},{3,2},{6,5},{7,6},{10,9},{11,10},{14,13},{15,14},{18,17},{19... | collective-permute-start | bytes 1572872 | tf_op jit(solution)/shard_map/ppermute | solution.py:67
  995.4 20.7 %collective-permute-start.91 = (bf16[512,512]{1,0:T(8,128)(2,1)S(1)}, bf16[512,512]{1,0:T(8,128)(2,1)S(1)}, u32[]{:S(2)}, u32[]{:S(2)}) collective-permute-start(bf16[512,512]{1,0:T(8,128)(2,1)S(1)} %copy-done.189), channel_id=1, source_target_pairs={{1,0},{2,1},{3,2},{5,4},{6,5},{7,6},{9,8},{10,9},{11,10},{13,12},{... | collective-permute-start | bytes 1572872 | tf_op jit(solution)/shard_map/ppermute | solution.py:67
  996.7 19.4 %collective-permute-start.90 = (bf16[512,512]{1,0:T(8,128)(2,1)S(1)}, bf16[512,512]{1,0:T(8,128)(2,1)S(1)}, u32[]{:S(2)}, u32[]{:S(2)}) collective-permute-start(bf16[512,512]{1,0:T(8,128)(2,1)S(1)} %copy-done.188), channel_id=1, source_target_pairs={{0,1},{1,2},{2,3},{4,5},{5,6},{6,7},{8,9},{9,10},{10,11},{12,13},{... | collective-permute-start | bytes 1572872 | tf_op jit(solution)/shard_map/ppermute | solution.py:67
  1014.5 15.8 %collective-permute-start.124 = (f32[107,512]{1,0:T(8,128)S(1)}, f32[107,512]{1,0:T(8,128)}, u32[]{:S(2)}, u32[]{:S(2)}) collective-permute-start(f32[107,512]{1,0:T(8,128)S(1)} %add.511), channel_id=1, source_target_pairs={{0,16},{4,20},{8,24},{12,28},{16,0},{20,4},{24,8},{28,12},{1,17},{... | collective-permute-start | bytes 657416 | tf_op jit(solution)/shard_map/ppermute | solution.py:67
  1020.3 18.7 %collective-permute-start.123 = (bf16[512,512]{1,0:T(8,128)(2,1)}, bf16[512,512]{1,0:T(8,128)(2,1)}, u32[]{:S(2)}, u32[]{:S(2)}) collective-permute-start(bf16[512,512]{1,0:T(8,128)(2,1)} %add_convert_fusion.7), channel_id=1, source_target_pairs={{1,0},{2,1},{3,2},{5,4},{6,5},{7,6},{9,8},{10,9},{11,10},{13,12},{... | collective-permute-start | bytes 1572872 | tf_op jit(solution)/shard_map/ppermute | solution.py:67
  1021.6 18.6 %collective-permute-start.122 = (bf16[512,512]{1,0:T(8,128)(2,1)}, bf16[512,512]{1,0:T(8,128)(2,1)}, u32[]{:S(2)}, u32[]{:S(2)}) collective-permute-start(bf16[512,512]{1,0:T(8,128)(2,1)} %add_convert_fusion.8), channel_id=1, source_target_pairs={{0,1},{1,2},{2,3},{4,5},{5,6},{6,7},{8,9},{9,10},{10,11},{12,13},{... | collective-permute-start | bytes 1572872 | tf_op jit(solution)/shard_map/ppermute | solution.py:67
  (280 other events, 4166.8 us)
Sparse Core Ops, SparseCore 0:
  697.3 39.4 reduce-scatter.8
  741.2 71.2 reduce-scatter.4
  816.0 71.2 reduce-scatter.6
  890.9 61.7 reduce-scatter.10

commit v3 on v2

--- a/solution.py
+++ b/solution.py
@@ -141,6 +141,28 @@
     def value(self):
         own, up, down = self.pieces()
         return own + up.astype(F32) + down.astype(F32)
+
+
+class ProductScatter(LineScatter):
+    def __init__(self, order, member, lhs, weight):
+        super().__init__(order, None)
+        self.args = (member, lhs, weight)
+
+    def items(self):
+        n, step = lax.axis_size("stream"), self.step
+        up_turn, down_turn = n - 1 - step, 1 + step
+        turns = (up_turn,) if up_turn == down_turn else (up_turn, down_turn)
+        values = send_values(*self.args, turns, self.came)
+        return [
+            (values[0], "stream", [(i, i + 1) for i in range(step + 1)]),
+            (values[-1], "stream", [(i, i - 1) for i in range(n - 1 - step, n)]),
+        ]
+
+    def own(self):
+        member, lhs, weight = self.args
+        (value,) = send_values(member, [self.order.hold(lhs[0]), *lhs[1:]], weight, (0,), None, F32)
+        self.order.did(value)
+        return value
 
 
 class Butterfly:
@@ -278,7 +300,8 @@
     return outs[0], outs[1 : 1 + n], outs[1 + n :]
 
 
-GROUP = 64
+GROUP = 128
+VMEM_MOST = 60 * 2**20
 TILE = 128
 SLOT = 16
 SCALE_ROW = 48
@@ -348,7 +371,7 @@
 
 def mix_streams(history, coef, chunk, picked, with_stats):
     n_hist, tokens, width = history.shape
-    rows = coef.shape[0]
+    rows = tokens // CHUNKS
     base = chunk * rows // TILE
     wide = pl.BlockSpec((TILE, width), lambda i: (i, 0))
     n = len(picked)
@@ -357,13 +380,13 @@
         grid=(rows // TILE,),
         in_specs=[
             pl.BlockSpec((n_hist, TILE, width), lambda i: (0, base + i, 0)),
-            pl.BlockSpec((TILE, 4 * n_hist), lambda i: (i, 0)),
+            pl.BlockSpec((TILE, 4 * n_hist), lambda i: (base + i, 0)),
         ],
         out_specs=[wide] * n + ([pl.BlockSpec((8, TILE), lambda i: (0, i))] if with_stats else []),
         out_shape=[jax.ShapeDtypeStruct((rows, width), F32)] * n
         + ([jax.ShapeDtypeStruct((8, rows), F32)] if with_stats else []),
         scratch_shapes=[pltpu.VMEM((TILE, LANES), F32)] if with_stats else [],
-        compiler_params=pltpu.CompilerParams(vmem_limit_bytes=32 * 2**20),
+        compiler_params=pltpu.CompilerParams(vmem_limit_bytes=VMEM_MOST),
         name="mix_streams",
     )(history, coef)
 
@@ -372,7 +395,7 @@
     return (stream - spread(stat, s)) * spread(stat, 3 + s)
 
 
-def early_kernel(hist_ref, x0, x1, x2, stat_ref, resid_ref, sums_ref, acc_ref):
+def early_kernel(hist_ref, x0, x1, x2, stat_ref, sums_ref, acc_ref):
     n_hist, tile, width = hist_ref.shape
 
     def group(span):
@@ -380,11 +403,10 @@
         sums = jnp.zeros((GROUP, LANES), F32)
         pieces = [pl.ds(w * LANES, LANES) for w in range(width // LANES)]
         others = [[hat_of(x[span, p], stat, s) for p in pieces] for s, x in enumerate((x0, x1, x2))]
-        others.append([resid_ref[span, p] for p in pieces])
         for j in range(n_hist):
             layer = [hist_ref[j, span, p].astype(F32) for p in pieces]
             sums = put_lane(sums, j, row_sum(sum(layer[1:], layer[0])))
-            for s in range(4):
+            for s in range(3):
                 terms = [x * y for x, y in zip(others[s], layer)]
                 sums = put_lane(sums, (s + 1) * SLOT + j, row_sum(sum(terms[1:], terms[0])))
         acc_ref[span, :] = sums
@@ -393,9 +415,9 @@
     sums_ref[...] = acc_ref[...].T[: sums_ref.shape[0]]
 
 
-def early_dots(history, streams, stat, resid_grad, chunk):
+def early_dots(history, streams, stat, chunk):
     n_hist, tokens, width = history.shape
-    rows = resid_grad.shape[0]
+    rows = stat.shape[0]
     base = chunk * rows // TILE
     wide = pl.BlockSpec((TILE, width), lambda i: (i, 0))
     return pl.pallas_call(
@@ -407,18 +429,17 @@
             wide,
             wide,
             pl.BlockSpec((TILE, LANES), lambda i: (i, 0)),
-            wide,
         ],
-        out_specs=pl.BlockSpec((5 * SLOT, TILE), lambda i: (0, i)),
-        out_shape=jax.ShapeDtypeStruct((5 * SLOT, rows), F32),
+        out_specs=pl.BlockSpec((4 * SLOT, TILE), lambda i: (0, i)),
+        out_shape=jax.ShapeDtypeStruct((4 * SLOT, rows), F32),
         scratch_shapes=[pltpu.VMEM((TILE, LANES), F32)],
-        compiler_params=pltpu.CompilerParams(vmem_limit_bytes=32 * 2**20),
+        compiler_params=pltpu.CompilerParams(vmem_limit_bytes=VMEM_MOST),
         name="early_dots",
-    )(history, *streams, stat, resid_grad)
-
-
-def late_kernel(hist_ref, x0, x1, x2, stat_ref, gain_ref, d0, d1, d2, *refs):
-    sums_ref, gain_grad_ref, acc_ref = refs[-3:]
+    )(history, *streams, stat)
+
+
+def late_kernel(hist_ref, x0, x1, x2, stat_ref, gain_ref, resid_ref, own, up, down, g0, g1, g2, sums_ref, gain_grad_ref, acc_ref):
+    grad_refs = (g0, g1, g2)
     n_hist, tile, width = hist_ref.shape
 
     @pl.when(pl.program_id(0) == 0)
@@ -430,20 +451,23 @@
         sums = jnp.zeros((GROUP, LANES), F32)
         pieces = [pl.ds(w * LANES, LANES) for w in range(width // LANES)]
         grads = []
-        for s, (x, d) in enumerate(((x0, d0), (x1, d1), (x2, d2))):
+        for s, x in enumerate((x0, x1, x2)):
             scaled, dots = [], []
             for p in pieces:
-                product = d[span, p] * hat_of(x[span, p], stat, s)
+                d = own[s, span, p] + up[s, span, p].astype(F32) + down[s, span, p].astype(F32)
+                product = d * hat_of(x[span, p], stat, s)
                 gain = gain_ref[pl.ds(s, 1), p]
                 gain_grad_ref[s, :, p] += jnp.sum(product.reshape(GROUP // 8, 8, LANES), axis=0)
-                scaled.append(d[span, p] * gain)
+                scaled.append(d * gain)
                 dots.append(product * gain)
+                grad_refs[s][span, p] = scaled[-1]
             sums = put_lane(sums, s * SLOT + n_hist, row_sum(sum(scaled[1:], scaled[0])))
             sums = put_lane(sums, s * SLOT + n_hist + 1, row_sum(sum(dots[1:], dots[0])))
             grads.append(scaled)
+        grads.append([resid_ref[span, p] for p in pieces])
         for j in range(n_hist):
             layer = [hist_ref[j, span, p].astype(F32) for p in pieces]
-            for s in range(3):
+            for s in range(4):
                 terms = [x * y for x, y in zip(grads[s], layer)]
                 sums = put_lane(sums, s * SLOT + j, row_sum(sum(terms[1:], terms[0])))
         acc_ref[span, :] = sums
@@ -452,12 +476,12 @@
     sums_ref[...] = acc_ref[...].T[: sums_ref.shape[0]]
 
 
-def late_dots(history, streams, stat, gain, d_normed, chunk, others):
+def late_dots(history, streams, stat, gain, resid_grad, own, came, chunk):
     n_hist, tokens, width = history.shape
     rows = stat.shape[0]
     base = chunk * rows // TILE
     wide = pl.BlockSpec((TILE, width), lambda i: (i, 0))
-    slices = [pl.BlockSpec((None, TILE, width), lambda i, s=s: (s, i, 0)) for s in range(3)]
+    three = pl.BlockSpec((3, TILE, width), lambda i: (0, i, 0))
     return pl.pallas_call(
         late_kernel,
         grid=(rows // TILE,),
@@ -468,24 +492,30 @@
             wide,
             pl.BlockSpec((TILE, LANES), lambda i: (i, 0)),
             pl.BlockSpec((3, width), lambda i: (0, 0)),
-            *slices,
-        ]
-        + [pl.BlockSpec(memory_space=pl.ANY)] * len(others),
+            wide,
+            three,
+            three,
+            three,
+        ],
         out_specs=[
-            pl.BlockSpec((3 * SLOT, TILE), lambda i: (0, i)),
+            wide,
+            wide,
+            wide,
+            pl.BlockSpec((4 * SLOT, TILE), lambda i: (0, i)),
             pl.BlockSpec((3, 8, width), lambda i: (0, 0, 0)),
         ],
-        out_shape=[
-            jax.ShapeDtypeStruct((3 * SLOT, rows), F32),
+        out_shape=[jax.ShapeDtypeStruct((rows, width), F32)] * 3
+        + [
+            jax.ShapeDtypeStruct((4 * SLOT, rows), F32),
             jax.ShapeDtypeStruct((3, 8, width), F32),
         ],
         scratch_shapes=[pltpu.VMEM((TILE, LANES), F32)],
-        compiler_params=pltpu.CompilerParams(vmem_limit_bytes=32 * 2**20),
+        compiler_params=pltpu.CompilerParams(vmem_limit_bytes=VMEM_MOST),
         name="late_dots",
-    )(history, *streams, stat, gain, d_normed, d_normed, d_normed, *others)
-
-
-def layers_kernel(coef_ref, x0, x1, x2, stat_ref, gain_ref, mean_ref, d0, d1, d2, resid_ref, extra_ref, *refs):
+    )(history, *streams, stat, gain, resid_grad, own, *came)
+
+
+def layers_kernel(coef_ref, x0, x1, x2, stat_ref, mean_ref, d0, d1, d2, resid_ref, extra_ref, *refs):
     out_ref = refs[-1]
     n_hist, tile, width = out_ref.shape
 
@@ -496,10 +526,9 @@
             p = pl.ds(w * LANES, LANES)
             grads = []
             for s, (x, d) in enumerate(((x0, d0), (x1, d1), (x2, d2))):
-                scaled = d[span, p] * gain_ref[pl.ds(s, 1), p]
                 hat = hat_of(x[span, p], stat, s)
                 grads.append(
-                    spread(stat, 3 + s) * (scaled - spread(means, MEAN_ROW + s) - hat * spread(means, MEAN_ROW + 3 + s))
+                    spread(stat, 3 + s) * (d[span, p] - spread(means, MEAN_ROW + s) - hat * spread(means, MEAN_ROW + 3 + s))
                 )
             grads.append(resid_ref[span, p])
             for j in range(n_hist):
@@ -511,35 +540,36 @@
     by_groups(tile, group)
 
 
-def layer_grads(coef, streams, stat, gain, means, d_normed, resid_grad, extra, chunk, held, tokens):
+def layer_grads(coef, streams, stat, means, scaled, resid_grad, extra, chunk, held, tokens, others):
     rows, width = resid_grad.shape
     n_hist = coef.shape[1] // 4
     base = chunk * rows // TILE
     wide = pl.BlockSpec((TILE, width), lambda i: (i, 0))
-    slices = [pl.BlockSpec((None, TILE, width), lambda i, s=s: (s, i, 0)) for s in range(3)]
     narrow = pl.BlockSpec((TILE, LANES), lambda i: (i, 0))
+    free = [*others] + ([] if held is None else [held])
     return pl.pallas_call(
         layers_kernel,
         grid=(rows // TILE,),
         in_specs=[
-            pl.BlockSpec((TILE, 4 * n_hist), lambda i: (i, 0)),
+            pl.BlockSpec((TILE, 4 * n_hist), lambda i: (base + i, 0)),
             wide,
             wide,
             wide,
             narrow,
-            pl.BlockSpec((3, width), lambda i: (0, 0)),
-            pl.BlockSpec((TILE, LANES), lambda i: (i, 0)),
-            *slices,
+            narrow,
+            wide,
+            wide,
+            wide,
             wide,
             wide,
         ]
-        + ([] if held is None else [pl.BlockSpec(memory_space=pl.ANY)]),
+        + [pl.BlockSpec(memory_space=pl.ANY)] * len(free),
         out_specs=pl.BlockSpec((n_hist, TILE, width), lambda i: (0, base + i, 0)),
         out_shape=jax.ShapeDtypeStruct((n_hist, tokens, width), BF16),
-        input_output_aliases={} if held is None else {12: 0},
+        input_output_aliases={} if held is None else {11 + len(others): 0},
         compiler_params=pltpu.CompilerParams(vmem_limit_bytes=32 * 2**20),
         name="layer_grads",
-    )(coef, *streams, stat, gain, means, d_normed, d_normed, d_normed, resid_grad, extra, *([] if held is None else [held]))
+    )(coef, *streams, stat, means, *scaled, resid_grad, extra, *free)
 
 
 def coef_kernel(full_width, n_hist, early, late, stat, act, slope, raw, scale, mix_out, mix_in, last, out_part, in_part, turned_ref, extra_ref, pack):
@@ -559,7 +589,7 @@
             - mean_hat * early[pl.ds((s + 1) * SLOT, SLOT), :]
         )
         slots.append(jnp.where(inside, slot, 0.0))
-    slots.append(jnp.where(inside, early[pl.ds(4 * SLOT, SLOT), :], 0.0))
+    slots.append(jnp.where(inside, late[pl.ds(3 * SLOT, SLOT), :], 0.0))
     d_coef = jnp.concatenate(slots, axis=0)
     ones = jnp.ones((8, rows), F32)
     out_part[pl.ds(0, mixh), :] = dot_tt(act[...], d_coef, ((1,), (1,)), HIGH)
@@ -578,13 +608,16 @@
     extra_ref[...] = back - turned[:, SCALE_ROW : SCALE_ROW + 1] * last[...].astype(F32)
 
 
-def coef_grads(full_width, early, late, stat, act, slope, raw, scale, mix_out, mix_in, history, chunk):
-    n_hist, tokens, width = history.shape
+def coef_grads(full_width, n_hist, early, late, stat, act, slope, raw, scale, mix_out, mix_in, last, chunk):
+    width = last.shape[1]
     rows = late.shape[1]
     mixh = act.shape[0]
 
     def full(array):
         return pl.BlockSpec(array.shape, lambda i: (0,) * array.ndim)
+
+    def part(array):
+        return pl.BlockSpec((array.shape[0], rows), lambda i: (0, chunk))
 
     arrays = [early, late, stat, act, slope, raw, scale, mix_out, mix_in]
     outs = [
@@ -596,14 +629,57 @@
     return pl.pallas_call(
         functools.partial(coef_kernel, full_width, n_hist),
         grid=(1,),
-        in_specs=[full(a) for a in arrays]
-        + [pl.BlockSpec((None, rows, width), lambda i: (n_hist - 1, chunk, 0))],
+        in_specs=[part(early)]
+        + [full(a) for a in arrays[1:3]]
+        + [part(a) for a in arrays[3:7]]
+        + [full(a) for a in arrays[7:]]
+        + [pl.BlockSpec((rows, width), lambda i: (chunk, 0))],
         out_specs=[full(a) for a in outs],
         out_shape=outs,
         scratch_shapes=[pltpu.VMEM((LANES, rows), F32)],
         compiler_params=pltpu.CompilerParams(vmem_limit_bytes=32 * 2**20),
         name="coef_grads",
-    )(*arrays, history)
+    )(*arrays, last)
+
+
+def send_kernel(count, turns, has_came, member_ref, *refs):
+    lhs, refs = refs[:count], refs[count:]
+    weights, refs = refs[: len(turns)], refs[len(turns) :]
+    came, outs = (refs[:2], refs[2:]) if has_came else ((), refs)
+    for k in range(len(turns)):
+        for s in range(count):
+            value = times_transpose(lhs[s][...], weights[k][s])
+            if has_came:
+                for got in came if len(turns) == 1 else (came[k],):
+                    value = value + got[s].astype(F32)
+            outs[k][s] = value.astype(outs[k].dtype)
+
+
+def send_values(member, lhs, weight, turns, came, kind=BF16):
+    n = lax.axis_size("stream")
+    count = len(lhs)
+    rows, depth = lhs[0].shape
+    width = weight.shape[1] // n
+    tile = 256
+    piece = pl.BlockSpec((count, tile, width), lambda i, m: (0, i, 0))
+
+    def block(turn):
+        return pl.BlockSpec((count, width, depth), lambda i, m: (0, lax.rem(m[0] + turn, n), 0))
+
+    return pl.pallas_call(
+        functools.partial(send_kernel, count, turns, came is not None),
+        grid_spec=pltpu.PrefetchScalarGridSpec(
+            num_scalar_prefetch=1,
+            grid=(rows // tile,),
+            in_specs=[pl.BlockSpec((tile, depth), lambda i, m: (i, 0))] * count
+            + [block(turn) for turn in turns]
+            + ([] if came is None else [piece] * 2),
+            out_specs=[piece] * len(turns),
+        ),
+        out_shape=[jax.ShapeDtypeStruct((count, rows, width), kind)] * len(turns),
+        compiler_params=pltpu.CompilerParams(vmem_limit_bytes=48 * 2**20),
+        name="send_values",
+    )(member, *lhs, *([weight] * len(turns)), *(came or ()))
 
 
 def columns(rows_values):
@@ -614,14 +690,18 @@
     return lax.rsqrt(squares * (1.0 / full_width) + EPS_NORM)
 
 
-def norm_kernel(full_width, x0, x1, x2, moment_ref, gain_ref, cols_ref, stat_ref):
+def norm_kernel(full_width, x0, x1, x2, moment_ref, gain_ref, qk_ref, v_ref, stat_ref):
     row = lax.broadcasted_iota(jnp.int32, (8, TILE), 0)
     moments = moment_ref[...]
     stat = columns(jnp.where(row < 3, moments, inv_std(moments, full_width)))
     stat_ref[...] = stat
     for s, x in enumerate((x0, x1, x2)):
         hat = (x[...] - stat[:, s : s + 1]) * stat[:, 3 + s : 4 + s]
-        cols_ref[s] = (hat * gain_ref[pl.ds(s, 1), :]).astype(BF16)
+        value = (hat * gain_ref[pl.ds(s, 1), :]).astype(BF16)
+        if s < 2:
+            qk_ref[s] = value
+        else:
+            v_ref[...] = value
 
 
 def norm_streams(full_width, streams, moments, gain):
@@ -638,11 +718,13 @@
             pl.BlockSpec((3, width), lambda i: (0, 0)),
         ],
         out_specs=[
-            pl.BlockSpec((3, TILE, width), lambda i: (0, i, 0)),
+            pl.BlockSpec((2, TILE, width), lambda i: (0, i, 0)),
+            wide,
             pl.BlockSpec((TILE, LANES), lambda i: (i, 0)),
         ],
         out_shape=[
-            jax.ShapeDtypeStruct((3, rows, width), BF16),
+            jax.ShapeDtypeStruct((2, rows, width), BF16),
+            jax.ShapeDtypeStruct((rows, width), BF16),
             jax.ShapeDtypeStruct((rows, LANES), F32),
         ],
         compiler_params=pltpu.CompilerParams(vmem_limit_bytes=32 * 2**20),
@@ -650,60 +732,141 @@
     )(*streams, moments, gain)
 
 
-def residual_kernel(own, up, down, base, out_ref, stat_ref):
+def residual_kernel(member_ref, own, up, down, base, out_ref, low_ref, stat_ref):
     width = own.shape[1]
     value = base[...] + own[...] + up[...].astype(F32) + down[...].astype(F32)
     out_ref[...] = value
     pivot = value[:, :1]
     gap = value - pivot
     shift = row_sum(gap) * (1.0 / width)
-    acc = put_lane(jnp.zeros((TILE, LANES), F32), 0, pivot + shift)
-    acc = put_lane(acc, 1, row_sum(jnp.square(gap)) - shift * shift * width)
+    low_ref[...] = (gap - shift).astype(BF16)
+    acc = put_lane(jnp.zeros((TILE, LANES), F32), member_ref[0], pivot + shift)
+    square = row_sum(jnp.square(gap)) - shift * shift * width
+    acc = put_lane(acc, 4 + member_ref[0], square)
     stat_ref[...] = acc.T[:8]
 
 
-def residual_rows(own, up, down, base):
+def residual_rows(member, own, up, down, base):
     rows, width = own.shape
-    wide = pl.BlockSpec((TILE, width), lambda i: (i, 0))
+    assert lax.axis_size("stream") == 4
+    wide = pl.BlockSpec((TILE, width), lambda i, m: (i, 0))
     return pl.pallas_call(
         residual_kernel,
-        grid=(rows // TILE,),
-        in_specs=[wide] * 4,
-        out_specs=[wide, pl.BlockSpec((8, TILE), lambda i: (0, i))],
+        grid_spec=pltpu.PrefetchScalarGridSpec(
+            num_scalar_prefetch=1,
+            grid=(rows // TILE,),
+            in_specs=[wide] * 4,
+            out_specs=[wide, wide, pl.BlockSpec((8, TILE), lambda i, m: (0, i))],
+        ),
         out_shape=[
             jax.ShapeDtypeStruct((rows, width), F32),
+            jax.ShapeDtypeStruct((rows, width), BF16),
             jax.ShapeDtypeStruct((8, rows), F32),
         ],
         compiler_params=pltpu.CompilerParams(vmem_limit_bytes=32 * 2**20),
         name="residual_rows",
-    )(own, up, down, base)
-
-
-def hat_kernel(full_width, x, stat_ref, gain_ref, out_ref):
-    stat = columns(stat_ref[...])
-    hat = (x[...] - stat[:, :1]) * inv_std(stat[:, 1:2], full_width)
-    out_ref[...] = (hat * gain_ref[...]).astype(BF16)
-
-
-def mlp_input(full_width, residual, stat, gain):
-    rows, width = residual.shape
-    wide = pl.BlockSpec((TILE, width), lambda i: (i, 0))
+    )(member, own, up, down, base)
+
+
+def by_member(member_ref, pieces, store):
+    n = (len(pieces) + 1) // 2
+    low, high = (None, *pieces[1:n]), (None, *pieces[n:])
+    for at in range(n):
+
+        @pl.when(member_ref[0] == at)
+        def _():
+            for slot in range(n):
+                if slot == at:
+                    store(slot, pieces[0])
+                elif slot < at:
+                    store(slot, low[at - slot])
+                else:
+                    store(slot, high[slot - at])
+
+
+def normed_kernel(full_width, member_ref, *refs):
+    pieces, (stat_ref, gain_ref, out_ref, moment_ref) = refs[:-4], refs[-4:]
+    n = (len(pieces) + 1) // 2
+    width = pieces[0].shape[1]
+    stat = stat_ref[...]
+    mean = jnp.sum(stat[:n], axis=0, keepdims=True) * (1.0 / n)
+    gaps = stat[:n] - mean
+    square = jnp.sum(stat[n:], axis=0, keepdims=True) + width * jnp.sum(
+        jnp.square(gaps), axis=0, keepdims=True
+    )
+    moment_ref[...] = jnp.concatenate([mean, square, jnp.zeros((6, TILE), F32)], axis=0)
+    table = columns(
+        jnp.concatenate([gaps, inv_std(square, full_width), jnp.zeros((3, TILE), F32)], axis=0)
+    )
+
+    def store(slot, ref):
+        cols = pl.ds(slot * width, width)
+        hat = (ref[...].astype(F32) + table[:, slot : slot + 1]) * table[:, n : n + 1]
+        out_ref[:, cols] = (hat * gain_ref[:, cols]).astype(BF16)
+
+    by_member(member_ref, pieces, store)
+
+
+def normed_rows(full_width, member, chain, stat, gain):
+    pieces = [chain.piece, *chain.low[1:], *chain.high[1:]]
+    rows, width = chain.piece.shape
+    wide = pl.BlockSpec((TILE, width), lambda i, m: (i, 0))
+    narrow = pl.BlockSpec((8, TILE), lambda i, m: (0, i))
     return pl.pallas_call(
-        functools.partial(hat_kernel, full_width),
-        grid=(rows // TILE,),
-        in_specs=[
-            wide,
-            pl.BlockSpec((8, TILE), lambda i: (0, i)),
-            pl.BlockSpec((1, width), lambda i: (0, 0)),
+        functools.partial(normed_kernel, full_width),
+        grid_spec=pltpu.PrefetchScalarGridSpec(
+            num_scalar_prefetch=1,
+            grid=(rows // TILE,),
+            in_specs=[wide] * len(pieces)
+            + [narrow, pl.BlockSpec((1, full_width), lambda i, m: (0, 0))],
+            out_specs=[pl.BlockSpec((TILE, full_width), lambda i, m: (i, 0)), narrow],
+        ),
+        out_shape=[
+            jax.ShapeDtypeStruct((rows, full_width), BF16),
+            jax.ShapeDtypeStruct((8, rows), F32),
         ],
-        out_specs=wide,
-        out_shape=jax.ShapeDtypeStruct((rows, width), BF16),
         compiler_params=pltpu.CompilerParams(vmem_limit_bytes=32 * 2**20),
-        name="mlp_input",
-    )(residual, stat, gain)
-
-
-def mlp_back_kernel(full_width, own, up, down, x, stat_ref, gain_ref, out_ref, sums_ref, gain_grad_ref):
+        name="normed_rows",
+    )(member, *pieces, stat, gain)
+
+
+def branch_kernel(full_width, member_ref, *refs):
+    pieces, (stat_ref, sums_ref, normed_ref, gain_ref, out_ref) = refs[:-5], refs[-5:]
+    width = pieces[0].shape[1]
+    inv = inv_std(columns(stat_ref[...])[:, 1:2], full_width)
+    sums = columns(sums_ref[...]) * (1.0 / full_width)
+    mean, slope = inv * sums[:, :1], inv * sums[:, 1:2]
+
+    def store(slot, ref):
+        cols = pl.ds(slot * width, width)
+        hat = normed_ref[:, cols].astype(F32) / gain_ref[:, cols]
+        out_ref[:, cols] = (ref[...].astype(F32) - mean - hat * slope).astype(BF16)
+
+    by_member(member_ref, pieces, store)
+
+
+def branch_rows(full_width, member, chain, stat, sums, normed, gain):
+    pieces = [chain.piece, *chain.low[1:], *chain.high[1:]]
+    rows, width = chain.piece.shape
+    wide = pl.BlockSpec((TILE, width), lambda i, m: (i, 0))
+    narrow = pl.BlockSpec((8, TILE), lambda i, m: (0, i))
+    whole = pl.BlockSpec((TILE, full_width), lambda i, m: (i, 0))
+    return pl.pallas_call(
+        functools.partial(branch_kernel, full_width),
+        grid_spec=pltpu.PrefetchScalarGridSpec(
+            num_scalar_prefetch=1,
+            grid=(rows // TILE,),
+            in_specs=[wide] * len(pieces)
+            + [narrow, narrow, whole, pl.BlockSpec((1, full_width), lambda i, m: (0, 0))],
+            out_specs=whole,
+        ),
+        out_shape=jax.ShapeDtypeStruct((rows, full_width), BF16),
+        compiler_params=pltpu.CompilerParams(vmem_limit_bytes=32 * 2**20),
+        name="branch_rows",
+    )(member, *pieces, stat, sums, normed, gain)
+
+
+def mlp_back_kernel(full_width, own, up, down, x, stat_ref, gain_ref, cot, out_ref, low_ref, sums_ref, gain_grad_ref):
     @pl.when(pl.program_id(0) == 0)
     def _():
         gain_grad_ref[...] = jnp.zeros_like(gain_grad_ref)
@@ -711,40 +874,42 @@
     stat = columns(stat_ref[...])
     grad = own[...] + up[...].astype(F32) + down[...].astype(F32)
     out_ref[...] = grad
-    product = grad * ((x[...] - stat[:, :1]) * inv_std(stat[:, 1:2], full_width))
+    inv = inv_std(stat[:, 1:2], full_width)
+    product = grad * ((x[...] - stat[:, :1]) * inv)
+    low_ref[...] = (cot[...] + inv * (grad * gain_ref[...])).astype(BF16)
     gain_grad_ref[...] += jnp.sum(product.reshape(TILE // 8, 8, -1), axis=0)
     acc = put_lane(jnp.zeros((TILE, LANES), F32), 0, row_sum(grad * gain_ref[...]))
     acc = put_lane(acc, 1, row_sum(product * gain_ref[...]))
     sums_ref[...] = acc.T[:8]
 
 
-def mlp_back_rows(full_width, own, up, down, residual, stat, gain):
+def mlp_back_rows(full_width, own, up, down, residual, stat, gain, cot):
     rows, width = residual.shape
     wide = pl.BlockSpec((TILE, width), lambda i: (i, 0))
     narrow = pl.BlockSpec((8, TILE), lambda i: (0, i))
     return pl.pallas_call(
         functools.partial(mlp_back_kernel, full_width),
         grid=(rows // TILE,),
-        in_specs=[wide] * 4 + [narrow, pl.BlockSpec((1, width), lambda i: (0, 0))],
-        out_specs=[wide, narrow, pl.BlockSpec((8, width), lambda i: (0, 0))],
+        in_specs=[wide] * 4 + [narrow, pl.BlockSpec((1, width), lambda i: (0, 0)), wide],
+        out_specs=[wide, wide, narrow, pl.BlockSpec((8, width), lambda i: (0, 0))],
         out_shape=[
             jax.ShapeDtypeStruct((rows, width), F32),
+            jax.ShapeDtypeStruct((rows, width), BF16),
             jax.ShapeDtypeStruct((8, rows), F32),
             jax.ShapeDtypeStruct((8, width), F32),
         ],
         compiler_params=pltpu.CompilerParams(vmem_limit_bytes=32 * 2**20),
         name="mlp_back_rows",
-    )(own, up, down, residual, stat, gain)
-
-
-def resid_grad_kernel(full_width, grad, x, stat_ref, sums_ref, gain_ref, cot, out_ref, low_ref):
+    )(own, up, down, residual, stat, gain, cot)
+
+
+def resid_grad_kernel(full_width, grad, x, stat_ref, sums_ref, gain_ref, cot, out_ref):
     stat = columns(stat_ref[...])
     sums = columns(sums_ref[...]) * (1.0 / full_width)
     inv = inv_std(stat[:, 1:2], full_width)
     hat = (x[...] - stat[:, :1]) * inv
     value = cot[...] + inv * (grad[...] * gain_ref[...] - sums[:, :1] - hat * sums[:, 1:2])
     out_ref[...] = value
-    low_ref[...] = value.astype(BF16)
 
 
 def resid_grad_rows(full_width, grad, residual, stat, sums, gain, cot):
@@ -755,39 +920,33 @@
         functools.partial(resid_grad_kernel, full_width),
         grid=(rows // TILE,),
         in_specs=[wide, wide, narrow, narrow, pl.BlockSpec((1, width), lambda i: (0, 0)), wide],
-        out_specs=[wide, wide],
-        out_shape=[
-            jax.ShapeDtypeStruct((rows, width), F32),
-            jax.ShapeDtypeStruct((rows, width), BF16),
-        ],
+        out_specs=wide,
+        out_shape=jax.ShapeDtypeStruct((rows, width), F32),
         compiler_params=pltpu.CompilerParams(vmem_limit_bytes=32 * 2**20),
         name="resid_grad_rows",
     )(grad, residual, stat, sums, gain, cot)
 
 
 def rows_product_kernel(n, *refs):
-    former, latter, out_ref, turned = refs[:n], refs[n : 2 * n], refs[-2], refs[-1]
-    rows = former[0].shape[0]
-
-    @pl.when(pl.program_id(1) == 0)
-    def _():
-        for c in range(n):
-            turned[:, pl.ds(c * rows, rows)] = former[c][...].T
-
+    former, latter, out_ref = refs[:n], refs[n : 2 * n], refs[-1]
     total = 0.0
     for c in range(n):
-        total = total + jnp.dot(
-            turned[:, pl.ds(c * rows, rows)], latter[c][...], preferred_element_type=F32
-        )
+        total = total + contract_rows(former[c][...], latter[c][...])
     out_ref[...] = total.astype(BF16)
 
 
-def rows_product(former, latter, out_cols, first, held, others=(), slot=None):
+def rows_product(former, latter, out_cols, first, held, others=(), slot=None, half=None):
     n = len(former)
     rows, height = former[0].shape[-2:]
     width = latter[0].shape[1]
-    tile_m, tile_n = min(512, height), min(1024, width)
+    skip = 0
+    if half is not None:
+        width //= 2
+        out_cols //= 2
+    tile_m, tile_n = min(512, height), min(2048, width)
     begin = first // tile_n
+    if half:
+        skip = width // tile_n
     free = [*others] + ([] if held is None else [held])
     return pl.pallas_call(
         functools.partial(rows_product_kernel, n),
@@ -798,12 +957,11 @@
             else pl.BlockSpec((None, rows, tile_m), lambda i, j: (slot, 0, i))
         ]
         * n
-        + [pl.BlockSpec((rows, tile_n), lambda i, j: (0, j))] * n
+        + [pl.BlockSpec((rows, tile_n), lambda i, j: (0, skip + j))] * n
         + [pl.BlockSpec(memory_space=pl.ANY)] * len(free),
         out_specs=pl.BlockSpec((tile_m, tile_n), lambda i, j: (i, begin + j)),
         out_shape=jax.ShapeDtypeStruct((height, out_cols), BF16),
         input_output_aliases={} if held is None else {2 * n + len(others): 0},
-        scratch_shapes=[pltpu.VMEM((tile_m, n * rows), BF16)],
         compiler_params=pltpu.CompilerParams(vmem_limit_bytes=48 * 2**20),
         name="rows_product",
     )(*former, *latter, *free)
@@ -847,13 +1005,15 @@
     mix_in_rows = lax.dynamic_slice_in_dim(mix_in, first_col, width, 0)
     mix_out_float = mix_out.astype(F32)
 
-    raw = []
-    for c in both:
-        last = history[n_hist - 1, spans[c]]
-        square_part = jnp.sum(jnp.square(last.astype(F32)), axis=1)[None]
-        raw_part = dot_tt(mix_in_rows, last, ((0,), (1,)))
-        raw.append(Butterfly(jnp.concatenate([raw_part, square_part], axis=0)))
-    order.send(*raw)
+    last = history[n_hist - 1]
+    square_part = jnp.sum(jnp.square(last.astype(F32)), axis=1)[None]
+    raw_part = dot_tt(mix_in_rows, last, ((0,), (1,)))
+    raw = Butterfly(jnp.concatenate([raw_part, square_part], axis=0))
+    order.send(raw)
+
+    here = member.astype(jnp.int32).reshape(1)
+    qkv_rows = jnp.transpose(order.hold(qkv_weight), (1, 0, 2))
+    order.did(qkv_rows)
 
     group_pick = (
         seq_group[:, None] == jnp.arange(group_weight.shape[0], dtype=jnp.int32)[None, :]
@@ -862,66 +1022,66 @@
     out_grad_held = order.hold(out_grad)
     cot_cols = [out_grad_held[spans[c]].astype(F32) * seq_weight for c in both]
     cot = [LineGather(cot_cols[c].astype(BF16), member) for c in both]
-    order.did(cot[0].piece)
-    order.send(*raw)
+    order.did(cot[0].piece, cot[1].piece)
+    order.send(raw)
     order.send(cot[0])
 
-    scale_t, raw_t, act_t, slope_t, coef = [], [], [], [], []
-    for c in both:
-        sums = raw[c].value()
-        raw_t.append(sums[:-1])
-        scale_t.append(lax.rsqrt(sums[-1:] / full_width + EPS_MIX))
-        act, slope = gelu_both(scale_t[c] * raw_t[c])
-        act_t.append(act)
-        slope_t.append(slope)
-        coef_t = dot_tt(mix_out_float, act, ((0,), (0,)), HIGH) + mix_static.reshape(-1, 1)
-        coef.append(coef_t.T)
+    sums = raw.value()
+    raw_t = sums[:-1]
+    scale_t = lax.rsqrt(sums[-1:] / full_width + EPS_MIX)
+    act_t, slope_t = gelu_both(scale_t * raw_t)
+    coef = (dot_tt(mix_out_float, act_t, ((0,), (0,)), HIGH) + mix_static.reshape(-1, 1)).T
 
     streams, moments = [None] * 2, [None] * 2
     stat, stat_rows, normed_chain = [None] * 2, [None] * 2, [None] * 2
-    resid_streams = [None] * 2
+    resid_streams, early_chain = [None] * 2, []
 
     def mix(c):
-        *streams[c], sums = mix_streams(history, coef[c], c, (0, 1, 2), True)
+        *streams[c], sums = mix_streams(history, coef, c, (0, 1, 2), True)
         moments[c] = Butterfly(sums, merge=moments_merger(width, 3))
 
     def norm(c):
         stat_rows[c] = moments[c].value()
-        cols, stat[c] = norm_streams(full_width, streams[c], stat_rows[c], stream_gain)
-        normed_chain[c] = LineGather(cols, member)
+        pair, single, stat[c] = norm_streams(full_width, streams[c], stat_rows[c], stream_gain)
+        normed_chain[c] = [LineGather(pair, member), LineGather(single, member)]
+
+    def early(c):
+        sums = early_dots(history, [order.hold(streams[c][0]), *streams[c][1:]], stat[c], c)
+        order.did(sums)
+        early_chain.append(Butterfly(sums))
 
     def mix_resid(c):
-        (resid_streams[c],) = mix_streams(history, order.hold(coef[c]), c, (3,), False)
+        (resid_streams[c],) = mix_streams(history, order.hold(coef), c, (3,), False)
         order.did(resid_streams[c])
 
     mix(0)
-    order.send(moments[0])
-    coef[1] = order.hold(coef[1])
     mix(1)
-    order.did(streams[1][0])
-    order.send(moments[0])
+    order.send(*moments)
+    order.send(*moments)
     norm(0)
-    order.send(normed_chain[0])
-    order.send(moments[1])
+    order.send(normed_chain[0][0])
+    order.send(normed_chain[0][1])
+    norm(1)
+    order.did(normed_chain[1][0].piece)
     mix_resid(0)
+    order.send(normed_chain[0][0])
+    order.send(normed_chain[0][1])
+    early(0)
+    order.send(normed_chain[0][0])
+    order.send(normed_chain[0][1])
     mix_resid(1)
-    order.send(normed_chain[0])
-    order.send(moments[1])
-    norm(1)
-    order.did(normed_chain[1].piece)
-    qkv_slices = [qkv_weight[:, s, :] for s in range(3)]
-    order.send(normed_chain[0])
-    order.send(normed_chain[1])
+    order.send(normed_chain[1][0])
+    order.send(normed_chain[1][1])
 
     normed, query, key, value, heads_out, lse = [], [], [], [], [], []
     branch = []
 
+    def project(c):
+        normed.append([chain.value() for chain in normed_chain[c]])
+        for held, s, full in ((query, 0, normed[c][0][0]), (key, 1, normed[c][0][1]), (value, 2, normed[c][1])):
+            held.append(jnp.dot(full, qkv_rows[s], preferred_element_type=F32).astype(BF16))
+
     def attend(c):
-        normed.append(normed_chain[c].value())
-        for held, s in ((query, 0), (key, 1), (value, 2)):
-            held.append(
-                jnp.dot(normed[c][s], qkv_slices[s], preferred_element_type=F32).astype(BF16)
-            )
         out, out_lse = attend_forward(query[c], key[: c + 1], value[: c + 1])
         heads_out.append(out)
         lse.append(out_lse)
@@ -932,18 +1092,15 @@
         )
 
     residual, resid_moments = [], []
+    mlp_gain_cols = lax.dynamic_slice_in_dim(mlp_gain, first_col, width, 0)[None, :]
+    mlp_in, mlp_moments = [], []
+    normed_mlp, hidden, d_hpre, mlp_back, mlp_out = [], [], [], [], []
 
     def end_branch(c):
-        value, stats = residual_rows(*branch[c].pieces(), resid_streams[c])
+        value, low, stats = residual_rows(here, *branch[c].pieces(), resid_streams[c])
         residual.append(value)
-        resid_moments.append(Butterfly(stats, merge=moments_merger(width, 1)))
-
-    mlp_gain_cols = lax.dynamic_slice_in_dim(mlp_gain, first_col, width, 0)[None, :]
-    mlp_in = []
-
-    def norm_mlp(c):
-        cols = mlp_input(full_width, residual[c], resid_moments[c].value(), mlp_gain_cols)
-        mlp_in.append(LineGather(cols, member))
+        resid_moments.append(Butterfly(stats))
+        mlp_in.append(LineGather(low, member))
 
     cot_low, d_hidden = [], []
 
@@ -954,10 +1111,12 @@
         )
         order.did(d_hidden[c])
 
-    normed_mlp, hidden, d_hpre, mlp_back, mlp_out = [], [], [], [], []
-
     def mlp(c):
-        normed_mlp.append(mlp_in[c].value())
+        full, moments_all = normed_rows(
+            full_width, here, mlp_in[c], resid_moments[c].value(), mlp_gain[None, :]
+        )
+        normed_mlp.append(full)
+        mlp_moments.append(moments_all)
         hidden_pre = jnp.dot(normed_mlp[c], up_weight, preferred_element_type=F32)
         act, slope = gelu_both(hidden_pre)
         act = act.astype(BF16)
@@ -975,31 +1134,40 @@
             )
         )
 
+    def weight_part(former, latter, out_cols, others):
+        return rows_product(former, latter, out_cols, 0, None, others)
+
     d_normed_mlp, back_sums, mlp_gain_shares = [], [], []
 
+    resid_grad, branch_grad = [], []
+
     def end_mlp_back(c):
-        value, sums, share = mlp_back_rows(
-            full_width, *mlp_back[c].pieces(), residual[c], resid_moments[c].value(), mlp_gain_cols
+        value, low, sums, share = mlp_back_rows(
+            full_width, *mlp_back[c].pieces(), residual[c], mlp_moments[c], mlp_gain_cols,
+            cot_cols[c],
         )
         d_normed_mlp.append(value)
         back_sums.append(Butterfly(sums))
         mlp_gain_shares.append(share)
-
-    resid_grad, branch_grad = [], []
-
-    def norm_mlp_back(c):
-        value, low = resid_grad_rows(
-            full_width, d_normed_mlp[c], residual[c], resid_moments[c].value(),
-            back_sums[c].value(), mlp_gain_cols, cot_cols[c],
-        )
-        resid_grad.append(value)
         branch_grad.append(LineGather(low, member))
 
     d_branch, d_proj = [], []
     carried = [None]
 
     def attend_back(c):
-        d_branch.append(branch_grad[c].value())
+        sums = back_sums[c].value()
+        d_branch.append(
+            branch_rows(
+                full_width, here, branch_grad[c], mlp_moments[c], sums, normed_mlp[c],
+                mlp_gain[None, :],
+            )
+        )
+        resid_grad.append(
+            resid_grad_rows(
+                full_width, d_normed_mlp[c], residual[c], mlp_moments[c], sums, mlp_gain_cols,
+                cot_cols[c],
+            )
+        )
         d_heads = jnp.dot(d_branch[c], out_weight, preferred_element_type=F32).astype(BF16)
         d_query, dk, dv = attend_backward(
             query[c], d_heads, lse[c], key[: c + 1], value[: c + 1], carried[0], c == CHUNKS - 1
@@ -1010,120 +1178,101 @@
             for i in both:
                 d_proj[i][1:] = [dk[i], dv[i]]
 
+    project(0)
     attend(0)
     order.send(branch[0])
     branch[0].prepare()
-    order.send(normed_chain[1])
+    order.send(normed_chain[1][0])
     order.send(branch[0])
     branch[0].prepare()
-    order.send(normed_chain[1])
+    order.send(normed_chain[1][1])
+    early(1)
     order.send(branch[0])
     branch[0].prepare()
+    order.send(normed_chain[1][0])
+    order.send(normed_chain[1][1])
     end_branch(0)
     order.send(resid_moments[0], cot[0])
+    project(1)
     order.send(resid_moments[0])
-    norm_mlp(0)
-    order.send(mlp_in[0], cot[0])
+    order.send(cot[0])
     attend(1)
     order.send(branch[1], mlp_in[0])
     branch[1].prepare()
     down_back(0)
     order.send(branch[1], mlp_in[0])
     branch[1].prepare()
-    order.send(branch[1], cot[1])
+    order.send(branch[1], mlp_in[0])
     branch[1].prepare()
+    order.send(cot[1])
+    end_branch(1)
+    order.send(mlp_in[1], resid_moments[1])
     mlp(0)
-    end_branch(1)
-    order.send(resid_moments[1])
-    order.did(hidden[0])
-    order.send(resid_moments[1], cot[1])
-    norm_mlp(1)
-    order.send(mlp_in[1], mlp_back[0])
+    order.send(cot[1])
+    order.send(mlp_in[1], mlp_back[0], resid_moments[1])
     mlp_back[0].prepare()
     order.send(cot[1])
     order.send(mlp_in[1], mlp_back[0])
     mlp_back[0].prepare()
     down_back(1)
-    order.send(mlp_in[1], mlp_back[0])
+    order.send(mlp_back[0])
     mlp_back[0].prepare()
+    mlp(1)
     end_mlp_back(0)
-    order.send(back_sums[0])
-    mlp(1)
-    order.did(hidden[1])
-    order.send(back_sums[0])
-    norm_mlp_back(0)
     order.send(mlp_back[1], branch_grad[0])
     mlp_back[1].prepare()
-    order.send(mlp_back[1], branch_grad[0])
+    order.send(mlp_back[1], branch_grad[0], back_sums[0])
     mlp_back[1].prepare()
-    order.send(mlp_back[1], branch_grad[0])
+    order.send(mlp_back[1], branch_grad[0], back_sums[0])
     mlp_back[1].prepare()
     end_mlp_back(1)
-    order.send(back_sums[1])
-    attend_back(0)
-    order.did(d_proj[0][0])
-    order.send(back_sums[1])
-    norm_mlp_back(1)
     mlp_out[0].prepare()
     order.send(branch_grad[1], mlp_out[0])
     mlp_out[0].prepare()
-    order.send(branch_grad[1], mlp_out[0])
+    attend_back(0)
+    order.send(branch_grad[1], mlp_out[0], back_sums[1])
+    chain = branch_grad[1]
+    chain.low[-1], chain.high[-1], d_proj[0][0] = lax.optimization_barrier(
+        (chain.low[-1], chain.high[-1], d_proj[0][0])
+    )
     mlp_out[0].prepare()
-    order.send(branch_grad[1], mlp_out[0])
+    order.send(branch_grad[1], mlp_out[0], back_sums[1])
     mlp_out[0].prepare()
+    mlp_out[1].prepare()
     attend_back(1)
-
-    def grad_chain(c):
-        return LineScatter(
-            order,
-            lambda idx, hold: jnp.stack(
-                [times_transpose(hold(d_proj[c][s]), rows_of(qkv_slices[s], idx)) for s in range(3)]
-            ),
-        )
-
-    def weight_part(former, latter, out_cols, first=0, held=None):
-        part = rows_product(former, latter, out_cols, first, held, order.tick)
-        order.did(part)
-        return part
-
-    def early(c):
-        sums = early_dots(history, streams[c], stat[c], order.hold(resid_grad[c]), c)
-        order.did(sums)
-        return Butterfly(sums)
-
-    gain_part = jnp.sum(mlp_gain_shares[0] + mlp_gain_shares[1], axis=0)
-    placed = jnp.where(
-        jnp.arange(n_stream)[:, None] == member, gain_part[None, :], jnp.zeros((n_stream, width), F32)
-    )
-    gain_chain = Butterfly(placed)
-
-    grads = [grad_chain(c) for c in both]
-    order.send(grads[0])
-    order.send(grads[1])
-    down_part = weight_part(cot_low, hidden, ff)
-    out_part = weight_part(d_branch, heads_out, width)
-    down_grad, out_weight_grad = dp_sum(down_part), dp_sum(out_part)
-    grads[0].prepare()
-    grads[1].prepare()
-    order.send(grads[0])
-    up_part = weight_part(normed_mlp, d_hpre, ff)
-    early_chain = [early(0)]
-    up_grad = dp_sum(up_part)
-    order.send(grads[1], gain_chain)
-    grads[0].prepare()
-    order.send(grads[0], gain_chain, early_chain[0])
+    order.send(mlp_out[1])
+    mlp_out[1].prepare()
+
+    grads = [ProductScatter(order, here, d_proj[c], qkv_rows) for c in both]
+    own = [None] * 2
+    early_one = Butterfly(jnp.concatenate([chain.now for chain in early_chain], axis=1))
+    order.send(*grads, early_one)
+    out_part = weight_part(d_branch, heads_out, width, grads[0].came)
+    down_part = weight_part(cot_low, hidden, ff, grads[1].came)
+    order.send(*grads, early_one)
+    up_part = weight_part(normed_mlp, d_hpre, ff, grads[0].came)
     qkv_part = None
     for s in range(3):
         qkv_part = rows_product(
-            [normed[c] for c in both], [d_proj[c][s] for c in both], 3 * width, s * width, qkv_part,
-            order.tick, s,
-        )
-    order.did(qkv_part)
-    qkv_grad = dp_sum(qkv_part)
-    qkv_grad = qkv_grad.reshape(qkv_grad.shape[0], 3, width)
-    early_chain.append(early(1))
-    grads[1].prepare()
-    order.send(grads[1], *early_chain)
+            [normed[c][s // 2] for c in both], [d_proj[c][s] for c in both], 3 * width, s * width,
+            qkv_part, grads[1].came, s if s < 2 else None,
+        )
+    order.send(*grads)
+    down_grad = dp_sum(down_part)
+    own = [grads[c].own() for c in both]
+    up_grad, out_weight_grad = [dp_sum(part) for part in (up_part, out_part)]
+    qkv_sum = lax.psum_scatter(qkv_part, "dp", scatter_dimension=0, tiled=True)
+    qkv_grad = jnp.stack(
+        [qkv_sum[:, s * width : (s + 1) * width] for s in range(3)], axis=1
+    ).astype(F32)
+    gain_part = jnp.sum(mlp_gain_shares[0] + mlp_gain_shares[1], axis=0)
+    gain_chain = Butterfly(
+        jnp.where(
+            jnp.arange(n_stream)[:, None] == member,
+            gain_part[None, :],
+            jnp.zeros((n_stream, width), F32),
+        )
+    )
 
     mix_out_wide = jnp.pad(
         mix_out_float.reshape(-1, 4, n_hist), ((0, 0), (0, 0), (0, SLOT - n_hist))
@@ -1132,39 +1281,39 @@
     d_normed, late, gain_shares, shares = [], [], [], []
     history_grad = [None]
 
-    def late_sums(c, others):
-        d_normed.append(grads[c].value())
-        sums, gain_share = late_dots(
-            history, streams[c], stat[c], stream_gain, d_normed[c], c, others
-        )
+    def late_sums(c):
+        *scaled, sums, gain_share = late_dots(
+            history, streams[c], stat[c], stream_gain, resid_grad[c], own[c], grads[c].came, c
+        )
+        d_normed.append(scaled)
         late.append(Butterfly(sums))
         gain_shares.append(gain_share)
 
     def coefs(c):
         shares.append(
             coef_grads(
-                full_width, early_chain[c].value(), late[c].value(), stat_rows[c], act_t[c],
-                slope_t[c], raw_t[c], scale_t[c], mix_out_wide, mix_in_wide, history, c,
+                full_width, n_hist, early_one.value(), late[c].value(), stat_rows[c], act_t,
+                slope_t, raw_t, scale_t, mix_out_wide, mix_in_wide, last, c,
             )
         )
 
-    def layers(c):
+    def layers(c, others):
         _, _, turned, extra = shares[c]
         history_grad[0] = layer_grads(
-            coef[c], streams[c], stat[c], stream_gain, order.hold(turned), d_normed[c],
-            resid_grad[c], extra, c, history_grad[0], tokens,
+            coef, streams[c], stat[c], turned, d_normed[c], resid_grad[c], extra, c,
+            history_grad[0], tokens, others,
         )
         order.did(history_grad[0])
 
-    mlp_out[1].prepare()
-    late_sums(0, ())
-    order.send(late[0], early_chain[1])
-    late_sums(1, (down_grad, up_grad, out_weight_grad))
-    order.send(late[0], late[1])
-    order.send(late[1])
+    late_sums(0)
+    order.did(qkv_part)
+    order.send(late[0], gain_chain)
     order.send(mlp_out[1])
     mlp_out[1].prepare()
+    late_sums(1)
+    order.send(late[0], late[1], gain_chain)
     coefs(0)
+    order.send(late[1])
     coefs(1)
     out_share, in_share = [shares[0][i] + shares[1][i] for i in range(2)]
     gain_share = jnp.sum(gain_shares[0] + gain_shares[1], axis=1)
@@ -1172,12 +1321,12 @@
     small = Butterfly(
         jnp.concatenate([out_share, in_share, gain_share, gain_chain.value()], axis=0), ("dp",)
     )
+    layers(0, (small.now,))
     order.send(small)
-    layers(0)
-    order.send(small, mlp_out[1])
-    layers(1)
+    order.send(mlp_out[1])
+    layers(1, ())
     while small.turns:
-        order.send(small, *([mlp_out[1]] if mlp_out[1].step < n_stream - 1 else []))
+        order.send(small)
     output_cols = jnp.concatenate(
         [(residual[c] + mlp_out[c].value()).astype(BF16) for c in both], axis=0
     )

time: 1060 us -> 1040 us (0.981)
  Pallas kernels: 161 us -> 214 us
  waiting for transfers between devices: 363 us -> 315 us
  starting transfers between devices: 254 us -> 281 us
  matrix products: 128 us -> 105 us
  other arithmetic: 68.9 us -> 50.1 us
    ppermute x125 -> x133, waiting for transfers between devices: 362 us -> 315 us  [send(): got.append(lax.ppermute(held[at], axis, perm))]
    pallas_call x4 -> x14, Pallas kernels: 5.74 us -> 45.1 us  [the longest x8 34.2 us: send_values(): pl.pallas_call(functools.partial(send_kernel, count, turns, came is not N...]
    ppermute x125 -> x133, starting transfers between devices: 254 us -> 280 us  [send(): got.append(lax.ppermute(held[at], axis, perm))]
    dot_general x52 -> x26, matrix products: 78.3 us -> 59.5 us  [dot_tt(): lax.dot_general(former, latter, (dims, ((), ())), precision=precision, pr...]
    unnamed x437 -> x394, local copies, waits for them, and re-layouts: 49.4 us -> 38.5 us
  transfers between devices with their start and end apart: 129 -> 137, of which waited for: 55 -> 49; matrix products, arithmetic and copies ran while one was open for 17% -> 15% of each run, Pallas kernels for 11% -> 19%
where the time goes in v3:
time: 1040 us; the launch traced here: 1030 us
  waiting for transfers between devices  315 us (30%)
  starting transfers between devices  281 us (27%)
  Pallas kernels  214 us (21%)
  matrix products  105 us (10%)
  other arithmetic  50.1 us (5%)
  local copies, waits for them, and re-layouts  47.2 us (5%)
  between operations  19 us (2%)
    ppermute x133, waiting for transfers between devices, send(): got.append(lax.ppermute(held[at], axis, perm))  315 us
    ppermute x133, starting transfers between devices, send(): got.append(lax.ppermute(held[at], axis, perm))  280 us
    dot_general x26, matrix products, dot_tt(): lax.dot_general(former, latter, (dims, ((), ())), precision=precision, pr...  59.5 us
    pallas_call x6, Pallas kernels, rows_product(): pl.pallas_call(functools.partial(rows_product_kernel, n), grid=(height //...  50.7 us
    unnamed x394, local copies, waits for them, and re-layouts  38.5 us
    pallas_call x8, Pallas kernels, send_values(): pl.pallas_call(functools.partial(send_kernel, count, turns, came is not N...  34.2 us
    pallas_call x4, Pallas kernels, mix_streams(): pl.pallas_call(functools.partial(mix_kernel, picked), grid=(rows // TILE,...  24.4 us
  transfers between devices with their start and end apart: 137, of which 49 were waited for; matrix products, arithmetic and copies ran while one was open for 15% of the time, Pallas kernels for 19%

profile of v3, /device:TPU:0, one launch (start us, length us, event | category | flops | bytes accessed | tf_op | source)
XLA Modules:
  0.0 1031.7 jit_solution(7557826243964350711)
XLA Ops:
  24.9 7.7 collective-permute-done.1
  35.4 7.2 mix_streams.5
  42.6 7.3 mix_streams.4
  74.0 5.4 collective-permute-start.10
  89.4 5.8 collective-permute-done.5
  95.3 5.5 collective-permute-done.6
  103.7 8.3 collective-permute-done.11
  114.7 7.2 early_dots.2
  121.9 12.5 %collective-permute-done.9 = bf16[2,512,512]{2,1,0:T(8,128)(2,1)} collective-permute-done((bf16[2,512,512]{2,1,0:T(8,128)(2,1)}, bf16[2,512,512]{2,1,0:T(8,128)(2,1)}, u32[]{:S(2)}, u32[]{:S(2)}) %collective-permute-start.9) | collective-permute-done | bytes 1048608 | tf_op jit(solution)/shard_map/ppermute | solution.py:67
  134.5 7.4 collective-permute-done.15
  147.6 5.0 mix_streams.7.base
  152.5 7.3 collective-permute-start.20
  167.9 14.9 %collective-permute-done.13 = bf16[2,512,512]{2,1,0:T(8,128)(2,1)} collective-permute-done((bf16[2,512,512]{2,1,0:T(8,128)(2,1)}, bf16[2,512,512]{2,1,0:T(8,128)(2,1)}, u32[]{:S(2)}, u32[]{:S(2)}) %collective-permute-start.13) | collective-permute-done | bytes 1048608 | tf_op jit(solution)/shard_map/ppermute | solution.py:67
  202.9 6.8 collective-permute-done.18
  212.8 5.8 collective-permute-start.22
  227.3 7.2 early_dots.3
  237.3 6.3 collective-permute-start.26
  252.4 10.1 collective-permute-done.27.down
  263.3 12.1 %collective-permute-start.36 = (bf16[512,512]{1,0:T(8,128)(2,1)}, bf16[512,512]{1,0:T(8,128)(2,1)}, u32[]{:S(2)}, u32[]{:S(2)}) collective-permute-start(bf16[512,512]{1,0:T(8,128)(2,1)} %get-tuple-element.250), channel_id=1, source_target_pairs={{0,1},{1,2},{2,3},{4,5},{5,6},{6,7},{8,9},{9,10},{10,11},{12,13},{... | collective-permute-start | bytes 1572872 | tf_op jit(solution)/shard_map/ppermute | solution.py:67
  281.8 10.2 collective-permute-done.37
  299.4 22.5 %collective-permute-done.40 = f32[8,512]{1,0:T(8,128)S(1)} collective-permute-done((f32[8,512]{1,0:T(8,128)S(1)}, f32[8,512]{1,0:T(8,128)S(1)}, u32[]{:S(2)}, u32[]{:S(2)}) %collective-permute-start.40) | collective-permute-done | bytes 16416 | tf_op jit(solution)/shard_map/ppermute | solution.py:67
  332.6 7.0 collective-permute-done.31
  346.3 7.2 attend_forward.3
  364.3 6.0 fusion.119
  378.4 9.6 collective-permute-done.48
  388.4 7.9 collective-permute-done.50.refs_5_
  396.3 5.6 collective-permute-start.56
  424.0 5.3 collective-permute-done.52.refs_6_
  432.4 8.6 multiply_convert_fusion.3
  457.7 5.2 collective-permute-done.66.refs_5_
  474.2 7.6 fusion.120
  482.2 7.7 collective-permute-start.74
  493.3 10.1 multiply_convert_fusion.1
  529.0 5.2 collective-permute-done.78.refs_1_
  547.4 14.8 %collective-permute-done.83.refs_5_ = bf16[512,512]{1,0:T(8,128)(2,1)S(1)} collective-permute-done((bf16[512,512]{1,0:T(8,128)(2,1)S(1)}, bf16[512,512]{1,0:T(8,128)(2,1)S(1)}, u32[]{:S(2)}, u32[]{:S(2)}) %collective-permute-start.83) | collective-permute-done | bytes 524320 | tf_op jit(solution)/shard_map/ppermute | solution.py:67
  581.7 5.4 collective-permute-start.89
  606.4 5.4 collective-permute-start.96
  616.3 5.1 attend_backward.2
  655.4 9.4 attend_backward.3
  664.9 5.0 send_values.8
  670.0 5.3 send_values.9
  685.4 15.6 %collective-permute-done.106.refs_4_ = bf16[3,512,512]{2,1,0:T(8,128)(2,1)S(1)} collective-permute-done((bf16[3,512,512]{2,1,0:T(8,128)(2,1)S(1)}, bf16[3,512,512]{2,1,0:T(8,128)(2,1)S(1)}, u32[]{:S(2)}, u32[]{:S(2)}) %collective-permute-start.106) | collective-permute-done | bytes 1572896 | tf_op jit(solution)/shard_map/ppermute | solution.py:67
  701.0 5.7 rows_product.9
  712.1 22.8 %collective-permute-done.110 = f32[64,1024]{1,0:T(8,128)S(1)} collective-permute-done((f32[64,1024]{1,0:T(8,128)}, f32[64,1024]{1,0:T(8,128)S(1)}, u32[]{:S(2)}, u32[]{:S(2)}) %collective-permute-start.110) | collective-permute-done | bytes 262176 | tf_op jit(solution)/shard_map/ppermute | solution.py:67
  754.0 15.2 %collective-permute-done.113.refs_5_.refs_4_ = bf16[3,512,512]{2,1,0:T(8,128)(2,1)S(1)} collective-permute-done((bf16[3,512,512]{2,1,0:T(8,128)(2,1)S(1)}, bf16[3,512,512]{2,1,0:T(8,128)(2,1)S(1)}, u32[]{:S(2)}, u32[]{:S(2)}) %collective-permute-start.113) | collective-permute-done | bytes 1572896 | tf_op jit(solution)/shard_map/ppermute | solution.py:67
  769.3 6.6 rows_product.6.refs_6_
  775.8 5.9 rows_product.7.refs_6_
  781.7 5.8 rows_product.8
  789.1 13.4 %rows_product.11 = bf16[2048,2048]{1,0:T(8,128)(2,1)} custom-call(bf16[512,2048]{1,0:T(8,128)(2,1)S(1)} %copy-done.59, bf16[512,2048]{1,0:T(8,128)(2,1)} %copy-done.137, bf16[512,2048]{1,0:T(8,128)(2,1)} %copy-done.142, bf16[512,2048]{1,0:T(8,128)(2,1)} %get-tuple-element.402.refs_3_, bf16[3,512,512]{2,1,0:T(8,128)(2,1)} %collective-permute-done.108.refs_4_, ...), custom_call_target="tpu_custom_call" | custom-call | tf_op jit(solution)/shard_map/rows_product/pallas_call | solution.py:951
  802.6 5.8 collective-permute-start.111
  809.1 20.6 %collective-permute-done.111.refs_5_.refs_4_ = bf16[3,512,512]{2,1,0:T(8,128)(2,1)S(1)} collective-permute-done((bf16[3,512,512]{2,1,0:T(8,128)(2,1)}, bf16[3,512,512]{2,1,0:T(8,128)(2,1)S(1)}, u32[]{:S(2)}, u32[]{:S(2)}) %collective-permute-start.111) | collective-permute-done | bytes 1572896 | tf_op jit(solution)/shard_map/ppermute | solution.py:67
  829.7 13.4 %rows_product.10 = bf16[2048,2048]{1,0:T(8,128)(2,1)} custom-call(bf16[512,2048]{1,0:T(8,128)(2,1)S(1)} %copy-done.54, bf16[512,2048]{1,0:T(8,128)(2,1)} %copy-done.55, bf16[512,2048]{1,0:T(8,128)(2,1)} %copy-done.139, bf16[512,2048]{1,0:T(8,128)(2,1)} %copy-done.144, bf16[3,512,512]{2,1,0:T(8,128)(2,1)S(1)} %collective-permute-done.111.refs_5_.refs_4_, ...), custom_call_target="tpu_custom_call" | custom-call | tf_op jit(solution)/shard_map/rows_product/pallas_call | solution.py:951
  846.8 5.8 send_values.12
  852.6 5.7 send_values.13
  858.3 7.6 collective-permute-start.115
  867.2 5.7 collective-permute-start.121
  895.7 10.4 %late_dots.2 = (f32[512,512]{1,0:T(8,128)}, f32[512,512]{1,0:T(8,128)}, f32[512,512]{1,0:T(8,128)}, f32[64,512]{1,0:T(8,128)}, f32[3,8,512]{2,1,0:T(8,128)}) custom-call(bf16[11,1024,512]{2,1,0:T(8,128)(2,1)} %hist_ref.15, f32[512,512]{1,0:T(8,128)} %get-tuple-element.270.x0, f32[512,512]{1,0:T(8,128)} %get-tuple-element.245.x1, ...), custom_call_target="tpu_custom_call" | custom-call | tf_op jit(solution)/shard_map/late_dots/pallas_call | solution.py:485
  913.3 6.3 collective-permute-done.121.up
  919.6 7.6 collective-permute-start.117
  927.2 10.3 late_dots.3
  940.7 5.4 fusion.6
  952.3 7.0 collective-permute-done.127
  969.7 9.4 layer_grads.2.refs_0_
  979.3 9.5 layer_grads.3
  (785 shorter events, 465.4 us)
Async XLA Ops:
  7.2 990.5 %reduce-scatter.7.cloned.1.call-start = ((), (), s32[]{:S(2)}) async-start(), calls=%async_computation.5 | async-start | bytes 2359296 | tf_op jit(solution)/shard_map/reduce_scatter | solution.py:1003
  68.8 26.5 %collective-permute-start.5 = (bf16[2,512,512]{2,1,0:T(8,128)(2,1)S(1)}, bf16[2,512,512]{2,1,0:T(8,128)(2,1)}, u32[]{:S(2)}, u32[]{:S(2)}) collective-permute-start(bf16[2,512,512]{2,1,0:T(8,128)(2,1)S(1)} %get-tuple-element.257), channel_id=1, source_target_pairs={{0,1},{1,2},{2,3},{4,5},{5,6},{6,7},{8,9},{9,10},{10,11},{12,13},{... | collective-permute-start | bytes 3145736 | tf_op jit(solution)/shard_map/ppermute | solution.py:67
  72.7 28.1 %collective-permute-start.6 = (bf16[2,512,512]{2,1,0:T(8,128)(2,1)S(1)}, bf16[2,512,512]{2,1,0:T(8,128)(2,1)}, u32[]{:S(2)}, u32[]{:S(2)}) collective-permute-start(bf16[2,512,512]{2,1,0:T(8,128)(2,1)S(1)} %get-tuple-element.257), channel_id=1, source_target_pairs={{1,0},{2,1},{3,2},{5,4},{6,5},{7,6},{9,8},{10,9},{11,10},{13,12},{... | collective-permute-start | bytes 3145736 | tf_op jit(solution)/shard_map/ppermute | solution.py:67
  74.0 29.8 %collective-permute-start.10 = (bf16[512,512]{1,0:T(8,128)(2,1)S(1)}, bf16[512,512]{1,0:T(8,128)(2,1)}, u32[]{:S(2)}, u32[]{:S(2)}) collective-permute-start(bf16[512,512]{1,0:T(8,128)(2,1)S(1)} %get-tuple-element.260), channel_id=1, source_target_pairs={{0,1},{1,2},{2,3},{4,5},{5,6},{6,7},{8,9},{9,10},{10,11},{12,13},{... | collective-permute-start | bytes 1572872 | tf_op jit(solution)/shard_map/ppermute | solution.py:67
  79.3 32.7 %collective-permute-start.11 = (bf16[512,512]{1,0:T(8,128)(2,1)S(1)}, bf16[512,512]{1,0:T(8,128)(2,1)}, u32[]{:S(2)}, u32[]{:S(2)}) collective-permute-start(bf16[512,512]{1,0:T(8,128)(2,1)S(1)} %get-tuple-element.260), channel_id=1, source_target_pairs={{1,0},{2,1},{3,2},{5,4},{6,5},{7,6},{9,8},{10,9},{11,10},{13,12},{... | collective-permute-start | bytes 1572872 | tf_op jit(solution)/shard_map/ppermute | solution.py:67
  100.8 21.2 %collective-permute-start.8 = (bf16[2,512,512]{2,1,0:T(8,128)(2,1)}, bf16[2,512,512]{2,1,0:T(8,128)(2,1)}, u32[]{:S(2)}, u32[]{:S(2)}) collective-permute-start(bf16[2,512,512]{2,1,0:T(8,128)(2,1)} %collective-permute-done.5), channel_id=1, source_target_pairs={{1,2},{2,3},{5,6},{6,7},{9,10},{10,11},{13,14},{14,15},{17,18},{18... | collective-permute-start | bytes 3145736 | tf_op jit(solution)/shard_map/ppermute | solution.py:67
  102.4 32.0 %collective-permute-start.9 = (bf16[2,512,512]{2,1,0:T(8,128)(2,1)}, bf16[2,512,512]{2,1,0:T(8,128)(2,1)}, u32[]{:S(2)}, u32[]{:S(2)}) collective-permute-start(bf16[2,512,512]{2,1,0:T(8,128)(2,1)} %collective-permute-done.6), channel_id=1, source_target_pairs={{1,0},{2,1},{5,4},{6,5},{9,8},{10,9},{13,12},{14,13},{17,16},{18,1... | collective-permute-start | bytes 3145736 | tf_op jit(solution)/shard_map/ppermute | solution.py:67
  112.0 22.5 %collective-permute-start.14 = (bf16[512,512]{1,0:T(8,128)(2,1)}, bf16[512,512]{1,0:T(8,128)(2,1)}, u32[]{:S(2)}, u32[]{:S(2)}) collective-permute-start(bf16[512,512]{1,0:T(8,128)(2,1)} %collective-permute-done.10), channel_id=1, source_target_pairs={{1,2},{2,3},{5,6},{6,7},{9,10},{10,11},{13,14},{14,15},{17,18},{18... | collective-permute-start | bytes 1572872 | tf_op jit(solution)/shard_map/ppermute | solution.py:67
  113.4 28.4 %collective-permute-start.15 = (bf16[512,512]{1,0:T(8,128)(2,1)}, bf16[512,512]{1,0:T(8,128)(2,1)}, u32[]{:S(2)}, u32[]{:S(2)}) collective-permute-start(bf16[512,512]{1,0:T(8,128)(2,1)} %collective-permute-done.11), channel_id=1, source_target_pairs={{1,0},{2,1},{5,4},{6,5},{9,8},{10,9},{13,12},{14,13},{17,16},{18,1... | collective-permute-start | bytes 1572872 | tf_op jit(solution)/shard_map/ppermute | solution.py:67
  144.6 23.3 %collective-permute-start.12 = (bf16[2,512,512]{2,1,0:T(8,128)(2,1)}, bf16[2,512,512]{2,1,0:T(8,128)(2,1)}, u32[]{:S(2)}, u32[]{:S(2)}) collective-permute-start(bf16[2,512,512]{2,1,0:T(8,128)(2,1)} %collective-permute-done.8), channel_id=1, source_target_pairs={{2,3},{6,7},{10,11},{14,15},{18,19},{22,23},{26,27},{30,31}} | collective-permute-start | bytes 3145736 | tf_op jit(solution)/shard_map/ppermute | solution.py:67
  146.3 36.6 %collective-permute-start.13 = (bf16[2,512,512]{2,1,0:T(8,128)(2,1)}, bf16[2,512,512]{2,1,0:T(8,128)(2,1)}, u32[]{:S(2)}, u32[]{:S(2)}) collective-permute-start(bf16[2,512,512]{2,1,0:T(8,128)(2,1)} %collective-permute-done.9), channel_id=1, source_target_pairs={{1,0},{5,4},{9,8},{13,12},{17,16},{21,20},{25,24},{29,28}} | collective-permute-start | bytes 3145736 | tf_op jit(solution)/shard_map/ppermute | solution.py:67
  152.5 60.2 %collective-permute-start.20 = (bf16[2,512,512]{2,1,0:T(8,128)(2,1)}, bf16[2,512,512]{2,1,0:T(8,128)(2,1)}, u32[]{:S(2)}, u32[]{:S(2)}) collective-permute-start(bf16[2,512,512]{2,1,0:T(8,128)(2,1)} %get-tuple-element.280), channel_id=1, source_target_pairs={{0,1},{1,2},{2,3},{4,5},{5,6},{6,7},{8,9},{9,10},{10,11},{12,13},{... | collective-permute-start | bytes 3145736 | tf_op jit(solution)/shard_map/ppermute | solution.py:67
  159.8 53.0 %collective-permute-start.21 = (bf16[2,512,512]{2,1,0:T(8,128)(2,1)}, bf16[2,512,512]{2,1,0:T(8,128)(2,1)}, u32[]{:S(2)}, u32[]{:S(2)}) collective-permute-start(bf16[2,512,512]{2,1,0:T(8,128)(2,1)} %get-tuple-element.280), channel_id=1, source_target_pairs={{1,0},{2,1},{3,2},{5,4},{6,5},{7,6},{9,8},{10,9},{11,10},{13,12},{... | collective-permute-start | bytes 3145736 | tf_op jit(solution)/shard_map/ppermute | solution.py:67
  200.8 20.9 %collective-permute-start.24 = (bf16[512,512]{1,0:T(8,128)(2,1)}, bf16[512,512]{1,0:T(8,128)(2,1)}, u32[]{:S(2)}, u32[]{:S(2)}) collective-permute-start(bf16[512,512]{1,0:T(8,128)(2,1)} %copy-done.106), channel_id=1, source_target_pairs={{0,1},{1,2},{2,3},{4,5},{5,6},{6,7},{8,9},{9,10},{10,11},{12,13},{... | collective-permute-start | bytes 1572872 | tf_op jit(solution)/shard_map/ppermute | solution.py:67
  212.8 21.7 %collective-permute-start.22 = (bf16[512,512]{1,0:T(8,128)(2,1)S(1)}, bf16[512,512]{1,0:T(8,128)(2,1)}, u32[]{:S(2)}, u32[]{:S(2)}) collective-permute-start(bf16[512,512]{1,0:T(8,128)(2,1)S(1)} %add_convert_fusion.19), channel_id=1, source_target_pairs={{0,1},{1,2},{4,5},{5,6},{8,9},{9,10},{12,13},{13,14},{16,17},{17,1... | collective-permute-start | bytes 1572872 | tf_op jit(solution)/shard_map/ppermute | solution.py:67
  220.1 55.3 %collective-permute-start.28 = (bf16[2,512,512]{2,1,0:T(8,128)(2,1)}, bf16[2,512,512]{2,1,0:T(8,128)(2,1)}, u32[]{:S(2)}, u32[]{:S(2)}) collective-permute-start(bf16[2,512,512]{2,1,0:T(8,128)(2,1)} %collective-permute-done.20), channel_id=1, source_target_pairs={{1,2},{2,3},{5,6},{6,7},{9,10},{10,11},{13,14},{14,15},{17,18},{18... | collective-permute-start | bytes 3145736 | tf_op jit(solution)/shard_map/ppermute | solution.py:67
  221.7 57.7 %collective-permute-start.29 = (bf16[2,512,512]{2,1,0:T(8,128)(2,1)}, bf16[2,512,512]{2,1,0:T(8,128)(2,1)}, u32[]{:S(2)}, u32[]{:S(2)}) collective-permute-start(bf16[2,512,512]{2,1,0:T(8,128)(2,1)} %collective-permute-done.21), channel_id=1, source_target_pairs={{1,0},{2,1},{5,4},{6,5},{9,8},{10,9},{13,12},{14,13},{17,16},{18,1... | collective-permute-start | bytes 3145736 | tf_op jit(solution)/shard_map/ppermute | solution.py:67
  245.0 34.5 %collective-permute-start.32 = (bf16[512,512]{1,0:T(8,128)(2,1)}, bf16[512,512]{1,0:T(8,128)(2,1)}, u32[]{:S(2)}, u32[]{:S(2)}) collective-permute-start(bf16[512,512]{1,0:T(8,128)(2,1)} %collective-permute-done.24), channel_id=1, source_target_pairs={{1,2},{2,3},{5,6},{6,7},{9,10},{10,11},{13,14},{14,15},{17,18},{18... | collective-permute-start | bytes 1572872 | tf_op jit(solution)/shard_map/ppermute | solution.py:67
  251.1 28.3 %collective-permute-start.33 = (bf16[512,512]{1,0:T(8,128)(2,1)}, bf16[512,512]{1,0:T(8,128)(2,1)}, u32[]{:S(2)}, u32[]{:S(2)}) collective-permute-start(bf16[512,512]{1,0:T(8,128)(2,1)} %collective-permute-done.25), channel_id=1, source_target_pairs={{1,0},{2,1},{5,4},{6,5},{9,8},{10,9},{13,12},{14,13},{17,16},{18,1... | collective-permute-start | bytes 1572872 | tf_op jit(solution)/shard_map/ppermute | solution.py:67
  291.9 30.7 %collective-permute-start.38 = (bf16[512,512]{1,0:T(8,128)(2,1)}, bf16[512,512]{1,0:T(8,128)(2,1)}, u32[]{:S(2)}, u32[]{:S(2)}) collective-permute-start(bf16[512,512]{1,0:T(8,128)(2,1)} %collective-permute-done.36), channel_id=1, source_target_pairs={{1,2},{2,3},{5,6},{6,7},{9,10},{10,11},{13,14},{14,15},{17,18},{18... | collective-permute-start | bytes 1572872 | tf_op jit(solution)/shard_map/ppermute | solution.py:67
  293.4 30.6 %collective-permute-start.39 = (bf16[512,512]{1,0:T(8,128)(2,1)}, bf16[512,512]{1,0:T(8,128)(2,1)}, u32[]{:S(2)}, u32[]{:S(2)}) collective-permute-start(bf16[512,512]{1,0:T(8,128)(2,1)} %collective-permute-done.37), channel_id=1, source_target_pairs={{1,0},{2,1},{5,4},{6,5},{9,8},{10,9},{13,12},{14,13},{17,16},{18,1... | collective-permute-start | bytes 1572872 | tf_op jit(solution)/shard_map/ppermute | solution.py:67
  294.7 30.8 %collective-permute-start.34 = (bf16[512,512]{1,0:T(8,128)(2,1)}, bf16[512,512]{1,0:T(8,128)(2,1)S(1)}, u32[]{:S(2)}, u32[]{:S(2)}) collective-permute-start(bf16[512,512]{1,0:T(8,128)(2,1)} %collective-permute-done.32), channel_id=1, source_target_pairs={{2,3},{6,7},{10,11},{14,15},{18,19},{22,23},{26,27},{30,31}} | collective-permute-start | bytes 1572872 | tf_op jit(solution)/shard_map/ppermute | solution.py:67
  295.4 31.6 %collective-permute-start.35 = (bf16[512,512]{1,0:T(8,128)(2,1)}, bf16[512,512]{1,0:T(8,128)(2,1)S(1)}, u32[]{:S(2)}, u32[]{:S(2)}) collective-permute-start(bf16[512,512]{1,0:T(8,128)(2,1)} %collective-permute-done.33), channel_id=1, source_target_pairs={{1,0},{5,4},{9,8},{13,12},{17,16},{21,20},{25,24},{29,28}} | collective-permute-start | bytes 1572872 | tf_op jit(solution)/shard_map/ppermute | solution.py:67
  296.7 25.3 %collective-permute-start.40 = (f32[8,512]{1,0:T(8,128)S(1)}, f32[8,512]{1,0:T(8,128)S(1)}, u32[]{:S(2)}, u32[]{:S(2)}) collective-permute-start(f32[8,512]{1,0:T(8,128)S(1)} %get-tuple-element.307), channel_id=1, source_target_pairs={{0,1},{1,0},{2,3},{3,2},{4,5},{5,4},{6,7},{7,6},{8,9},{9,8},{10,11... | collective-permute-start | bytes 49160 | tf_op jit(solution)/shard_map/ppermute | solution.py:67
  324.0 33.2 %collective-permute-start.45 = (bf16[512,512]{1,0:T(8,128)(2,1)}, bf16[512,512]{1,0:T(8,128)(2,1)}, u32[]{:S(2)}, u32[]{:S(2)}) collective-permute-start(bf16[512,512]{1,0:T(8,128)(2,1)} %collective-permute-done.38), channel_id=1, source_target_pairs={{2,3},{6,7},{10,11},{14,15},{18,19},{22,23},{26,27},{30,31}} | collective-permute-start | bytes 1572872 | tf_op jit(solution)/shard_map/ppermute | solution.py:67
  325.5 31.7 %collective-permute-start.46 = (bf16[512,512]{1,0:T(8,128)(2,1)}, bf16[512,512]{1,0:T(8,128)(2,1)}, u32[]{:S(2)}, u32[]{:S(2)}) collective-permute-start(bf16[512,512]{1,0:T(8,128)(2,1)} %collective-permute-done.39), channel_id=1, source_target_pairs={{1,0},{5,4},{9,8},{13,12},{17,16},{21,20},{25,24},{29,28}} | collective-permute-start | bytes 1572872 | tf_op jit(solution)/shard_map/ppermute | solution.py:67
  377.1 19.2 %collective-permute-start.50 = (bf16[512,512]{1,0:T(8,128)(2,1)S(1)}, bf16[512,512]{1,0:T(8,128)(2,1)S(1)}, u32[]{:S(2)}, u32[]{:S(2)}) collective-permute-start(bf16[512,512]{1,0:T(8,128)(2,1)S(1)} %collective-permute-done.44.refs_4_), channel_id=1, source_target_pairs={{1,0},{2,1},{5,4},{6,5},{9,8},{10,9},{13,12},{14,13},{17,16},{18,1... | collective-permute-start | bytes 1572872 | tf_op jit(solution)/shard_map/ppermute | solution.py:67
  417.6 26.1 %collective-permute-start.62 = (f32[8,512]{1,0:T(8,128)S(1)}, f32[8,512]{1,0:T(8,128)S(1)}, u32[]{:S(2)}, u32[]{:S(2)}) collective-permute-start(f32[8,512]{1,0:T(8,128)S(1)} %get-tuple-element.333), channel_id=1, source_target_pairs={{0,1},{1,0},{2,3},{3,2},{4,5},{5,4},{6,7},{7,6},{8,9},{9,8},{10,11... | collective-permute-start | bytes 49160 | tf_op jit(solution)/shard_map/ppermute | solution.py:67
  419.4 24.3 %collective-permute-start.60 = (bf16[512,512]{1,0:T(8,128)(2,1)S(1)}, bf16[512,512]{1,0:T(8,128)(2,1)S(1)}, u32[]{:S(2)}, u32[]{:S(2)}) collective-permute-start(bf16[512,512]{1,0:T(8,128)(2,1)S(1)} %get-tuple-element.332.refs_0_), channel_id=1, source_target_pairs={{0,1},{1,2},{2,3},{4,5},{5,6},{6,7},{8,9},{9,10},{10,11},{12,13},{... | collective-permute-start | bytes 1572872 | tf_op jit(solution)/shard_map/ppermute | solution.py:67
  422.0 21.7 %collective-permute-start.61 = (bf16[512,512]{1,0:T(8,128)(2,1)S(1)}, bf16[512,512]{1,0:T(8,128)(2,1)S(1)}, u32[]{:S(2)}, u32[]{:S(2)}) collective-permute-start(bf16[512,512]{1,0:T(8,128)(2,1)S(1)} %get-tuple-element.332.refs_0_), channel_id=1, source_target_pairs={{1,0},{2,1},{3,2},{5,4},{6,5},{7,6},{9,8},{10,9},{11,10},{13,12},{... | collective-permute-start | bytes 1572872 | tf_op jit(solution)/shard_map/ppermute | solution.py:67
  423.3 25.8 %collective-permute-start.58 = (bf16[512,512]{1,0:T(8,128)(2,1)S(1)}, bf16[512,512]{1,0:T(8,128)(2,1)S(1)}, u32[]{:S(2)}, u32[]{:S(2)}) collective-permute-start(bf16[512,512]{1,0:T(8,128)(2,1)S(1)} %collective-permute-done.54), channel_id=1, source_target_pairs={{1,2},{2,3},{5,6},{6,7},{9,10},{10,11},{13,14},{14,15},{17,18},{18... | collective-permute-start | bytes 1572872 | tf_op jit(solution)/shard_map/ppermute | solution.py:67
  429.3 22.8 %collective-permute-start.59 = (bf16[512,512]{1,0:T(8,128)(2,1)S(1)}, bf16[512,512]{1,0:T(8,128)(2,1)S(1)}, u32[]{:S(2)}, u32[]{:S(2)}) collective-permute-start(bf16[512,512]{1,0:T(8,128)(2,1)S(1)} %collective-permute-done.55), channel_id=1, source_target_pairs={{1,0},{2,1},{5,4},{6,5},{9,8},{10,9},{13,12},{14,13},{17,16},{18,1... | collective-permute-start | bytes 1572872 | tf_op jit(solution)/shard_map/ppermute | solution.py:67
  462.9 28.8 %collective-permute-start.69 = (bf16[512,512]{1,0:T(8,128)(2,1)S(1)}, bf16[512,512]{1,0:T(8,128)(2,1)S(1)}, u32[]{:S(2)}, u32[]{:S(2)}) collective-permute-start(bf16[512,512]{1,0:T(8,128)(2,1)S(1)} %collective-permute-done.65.refs_2_), channel_id=1, source_target_pairs={{2,3},{6,7},{10,11},{14,15},{18,19},{22,23},{26,27},{30,31}} | collective-permute-start | bytes 1572872 | tf_op jit(solution)/shard_map/ppermute | solution.py:67
  463.5 28.1 %collective-permute-start.70 = (bf16[512,512]{1,0:T(8,128)(2,1)S(1)}, bf16[512,512]{1,0:T(8,128)(2,1)S(1)}, u32[]{:S(2)}, u32[]{:S(2)}) collective-permute-start(bf16[512,512]{1,0:T(8,128)(2,1)S(1)} %collective-permute-done.66.refs_5_), channel_id=1, source_target_pairs={{1,0},{5,4},{9,8},{13,12},{17,16},{21,20},{25,24},{29,28}} | collective-permute-start | bytes 1572872 | tf_op jit(solution)/shard_map/ppermute | solution.py:67
  482.2 30.9 %collective-permute-start.74 = (bf16[512,512]{1,0:T(8,128)(2,1)S(1)}, bf16[512,512]{1,0:T(8,128)(2,1)S(1)}, u32[]{:S(2)}, u32[]{:S(2)}) collective-permute-start(bf16[512,512]{1,0:T(8,128)(2,1)S(1)} %add_convert_fusion.12), channel_id=1, source_target_pairs={{0,1},{1,2},{2,3},{4,5},{5,6},{6,7},{8,9},{9,10},{10,11},{12,13},{... | collective-permute-start | bytes 1572872 | tf_op jit(solution)/shard_map/ppermute | solution.py:67
  490.0 23.2 %collective-permute-start.75 = (bf16[512,512]{1,0:T(8,128)(2,1)S(1)}, bf16[512,512]{1,0:T(8,128)(2,1)S(1)}, u32[]{:S(2)}, u32[]{:S(2)}) collective-permute-start(bf16[512,512]{1,0:T(8,128)(2,1)S(1)} %add_convert_fusion.11), channel_id=1, source_target_pairs={{1,0},{2,1},{3,2},{5,4},{6,5},{7,6},{9,8},{10,9},{11,10},{13,12},{... | collective-permute-start | bytes 1572872 | tf_op jit(solution)/shard_map/ppermute | solution.py:67
  590.4 21.3 %collective-permute-start.93 = (bf16[512,512]{1,0:T(8,128)(2,1)S(1)}, bf16[512,512]{1,0:T(8,128)(2,1)S(1)}, u32[]{:S(2)}, u32[]{:S(2)}) collective-permute-start(bf16[512,512]{1,0:T(8,128)(2,1)S(1)} %collective-permute-done.82.refs_2_), channel_id=1, source_target_pairs={{2,3},{6,7},{10,11},{14,15},{18,19},{22,23},{26,27},{30,31}} | collective-permute-start | bytes 1572872 | tf_op jit(solution)/shard_map/ppermute | solution.py:67
  625.8 24.3 %collective-permute-start.105 = (f32[8,512]{1,0:T(8,128)S(1)}, f32[8,512]{1,0:T(8,128)S(1)}, u32[]{:S(2)}, u32[]{:S(2)}) collective-permute-start(f32[8,512]{1,0:T(8,128)S(1)} %add.356), channel_id=1, source_target_pairs={{0,2},{1,3},{2,0},{3,1},{4,6},{5,7},{6,4},{7,5},{8,10},{9,11},{10,... | collective-permute-start | bytes 49160 | tf_op jit(solution)/shard_map/ppermute | solution.py:67
  630.0 20.1 %collective-permute-start.103 = (bf16[512,512]{1,0:T(8,128)(2,1)S(1)}, bf16[512,512]{1,0:T(8,128)(2,1)S(1)}, u32[]{:S(2)}, u32[]{:S(2)}) collective-permute-start(bf16[512,512]{1,0:T(8,128)(2,1)S(1)} %collective-permute-done.91.refs_2_), channel_id=1, source_target_pairs={{2,3},{6,7},{10,11},{14,15},{18,19},{22,23},{26,27},{30,31}} | collective-permute-start | bytes 1572872 | tf_op jit(solution)/shard_map/ppermute | solution.py:67
  630.7 19.4 %collective-permute-start.104 = (bf16[512,512]{1,0:T(8,128)(2,1)}, bf16[512,512]{1,0:T(8,128)(2,1)S(1)}, u32[]{:S(2)}, u32[]{:S(2)}) collective-permute-start(bf16[512,512]{1,0:T(8,128)(2,1)} %collective-permute-done.92.refs_5_), channel_id=1, source_target_pairs={{1,0},{5,4},{9,8},{13,12},{17,16},{21,20},{25,24},{29,28}} | collective-permute-start | bytes 1572872 | tf_op jit(solution)/shard_map/ppermute | solution.py:67
  644.0 31.3 %collective-permute-start.101 = (bf16[512,512]{1,0:T(8,128)(2,1)S(1)}, bf16[512,512]{1,0:T(8,128)(2,1)S(1)}, u32[]{:S(2)}, u32[]{:S(2)}) collective-permute-start(bf16[512,512]{1,0:T(8,128)(2,1)S(1)} %get-tuple-element.400), channel_id=1, source_target_pairs={{0,1},{4,5},{8,9},{12,13},{16,17},{20,21},{24,25},{28,29}} | collective-permute-start | bytes 1572872 | tf_op jit(solution)/shard_map/ppermute | solution.py:67
  648.6 26.7 %collective-permute-start.102 = (bf16[512,512]{1,0:T(8,128)(2,1)S(1)}, bf16[512,512]{1,0:T(8,128)(2,1)S(1)}, u32[]{:S(2)}, u32[]{:S(2)}) collective-permute-start(bf16[512,512]{1,0:T(8,128)(2,1)S(1)} %get-tuple-element.401), channel_id=1, source_target_pairs={{3,2},{7,6},{11,10},{15,14},{19,18},{23,22},{27,26},{31,30}} | collective-permute-start | bytes 1572872 | tf_op jit(solution)/shard_map/ppermute | solution.py:67
  679.0 22.0 %collective-permute-start.106 = (bf16[3,512,512]{2,1,0:T(8,128)(2,1)S(1)}, bf16[3,512,512]{2,1,0:T(8,128)(2,1)S(1)}, u32[]{:S(2)}, u32[]{:S(2)}) collective-permute-start(bf16[3,512,512]{2,1,0:T(8,128)(2,1)S(1)} %get-tuple-element.417), channel_id=1, source_target_pairs={{0,1},{4,5},{8,9},{12,13},{16,17},{20,21},{24,25},{28,29}} | collective-permute-start | bytes 4718600 | tf_op jit(solution)/shard_map/ppermute | solution.py:67
  680.4 20.6 %collective-permute-start.107 = (bf16[3,512,512]{2,1,0:T(8,128)(2,1)S(1)}, bf16[3,512,512]{2,1,0:T(8,128)(2,1)S(1)}, u32[]{:S(2)}, u32[]{:S(2)}) collective-permute-start(bf16[3,512,512]{2,1,0:T(8,128)(2,1)S(1)} %get-tuple-element.418), channel_id=1, source_target_pairs={{3,2},{7,6},{11,10},{15,14},{19,18},{23,22},{27,26},{31,30}} | collective-permute-start | bytes 4718600 | tf_op jit(solution)/shard_map/ppermute | solution.py:67
  681.2 61.2 %collective-permute-start.108 = (bf16[3,512,512]{2,1,0:T(8,128)(2,1)}, bf16[3,512,512]{2,1,0:T(8,128)(2,1)}, u32[]{:S(2)}, u32[]{:S(2)}) collective-permute-start(bf16[3,512,512]{2,1,0:T(8,128)(2,1)} %get-tuple-element.419), channel_id=1, source_target_pairs={{0,1},{4,5},{8,9},{12,13},{16,17},{20,21},{24,25},{28,29}} | collective-permute-start | bytes 4718600 | tf_op jit(solution)/shard_map/ppermute | solution.py:67
  683.7 58.8 %collective-permute-start.109 = (bf16[3,512,512]{2,1,0:T(8,128)(2,1)}, bf16[3,512,512]{2,1,0:T(8,128)(2,1)}, u32[]{:S(2)}, u32[]{:S(2)}) collective-permute-start(bf16[3,512,512]{2,1,0:T(8,128)(2,1)} %get-tuple-element.420), channel_id=1, source_target_pairs={{3,2},{7,6},{11,10},{15,14},{19,18},{23,22},{27,26},{31,30}} | collective-permute-start | bytes 4718600 | tf_op jit(solution)/shard_map/ppermute | solution.py:67
  709.0 307.7 %reduce-scatter.5.cloned.1.call-start = ((), (), s32[]{:S(2)}) async-start(), calls=%async_computation.4 | async-start | bytes 7077888 | tf_op jit(solution)/shard_map/reduce_scatter | solution.py:1264
  709.5 25.4 %collective-permute-start.110 = (f32[64,1024]{1,0:T(8,128)}, f32[64,1024]{1,0:T(8,128)S(1)}, u32[]{:S(2)}, u32[]{:S(2)}) collective-permute-start(f32[64,1024]{1,0:T(8,128)} %pad_maximum_fusion.7), channel_id=1, source_target_pairs={{0,1},{1,0},{2,3},{3,2},{4,5},{5,4},{6,7},{7,6},{8,9},{9,8},{10,11... | collective-permute-start | bytes 786440 | tf_op jit(solution)/shard_map/ppermute | solution.py:67
  746.0 23.3 %collective-permute-start.113 = (bf16[3,512,512]{2,1,0:T(8,128)(2,1)S(1)}, bf16[3,512,512]{2,1,0:T(8,128)(2,1)S(1)}, u32[]{:S(2)}, u32[]{:S(2)}) collective-permute-start(bf16[3,512,512]{2,1,0:T(8,128)(2,1)S(1)} %send_values.11), channel_id=1, source_target_pairs={{0,1},{1,2},{4,5},{5,6},{8,9},{9,10},{12,13},{13,14},{16,17},{17,1... | collective-permute-start | bytes 4718600 | tf_op jit(solution)/shard_map/ppermute | solution.py:67
  787.5 231.7 %reduce-scatter.11.cloned.1.call-start = ((), (), s32[]{:S(2)}) async-start(), calls=%async_computation.7 | async-start | bytes 9437184 | tf_op jit(solution)/shard_map/reduce_scatter | solution.py:1003
  802.5 219.6 %reduce-scatter.9.cloned.1.call-start = ((), (), s32[]{:S(2)}) async-start(), calls=%async_computation.6 | async-start | bytes 9437184 | tf_op jit(solution)/shard_map/reduce_scatter | solution.py:1003
  802.6 27.2 %collective-permute-start.111 = (bf16[3,512,512]{2,1,0:T(8,128)(2,1)}, bf16[3,512,512]{2,1,0:T(8,128)(2,1)S(1)}, u32[]{:S(2)}, u32[]{:S(2)}) collective-permute-start(bf16[3,512,512]{2,1,0:T(8,128)(2,1)} %copy-done.81), channel_id=1, source_target_pairs={{0,1},{1,2},{4,5},{5,6},{8,9},{9,10},{12,13},{13,14},{16,17},{17,1... | collective-permute-start | bytes 4718600 | tf_op jit(solution)/shard_map/ppermute | solution.py:67
  808.3 21.4 %collective-permute-start.112 = (bf16[3,512,512]{2,1,0:T(8,128)(2,1)}, bf16[3,512,512]{2,1,0:T(8,128)(2,1)S(1)}, u32[]{:S(2)}, u32[]{:S(2)}) collective-permute-start(bf16[3,512,512]{2,1,0:T(8,128)(2,1)} %copy-done.81), channel_id=1, source_target_pairs={{2,1},{3,2},{6,5},{7,6},{10,9},{11,10},{14,13},{15,14},{18,17},{19... | collective-permute-start | bytes 4718600 | tf_op jit(solution)/shard_map/ppermute | solution.py:67
  858.3 37.5 %collective-permute-start.115 = (bf16[3,512,512]{2,1,0:T(8,128)(2,1)}, bf16[3,512,512]{2,1,0:T(8,128)(2,1)}, u32[]{:S(2)}, u32[]{:S(2)}) collective-permute-start(bf16[3,512,512]{2,1,0:T(8,128)(2,1)} %get-tuple-element.431), channel_id=1, source_target_pairs={{0,1},{1,2},{2,3},{4,5},{5,6},{6,7},{8,9},{9,10},{10,11},{12,13},{... | collective-permute-start | bytes 4718600 | tf_op jit(solution)/shard_map/ppermute | solution.py:67
  865.9 29.8 %collective-permute-start.116 = (bf16[3,512,512]{2,1,0:T(8,128)(2,1)}, bf16[3,512,512]{2,1,0:T(8,128)(2,1)}, u32[]{:S(2)}, u32[]{:S(2)}) collective-permute-start(bf16[3,512,512]{2,1,0:T(8,128)(2,1)} %get-tuple-element.432), channel_id=1, source_target_pairs={{1,0},{2,1},{3,2},{5,4},{6,5},{7,6},{9,8},{10,9},{11,10},{13,12},{... | collective-permute-start | bytes 4718600 | tf_op jit(solution)/shard_map/ppermute | solution.py:67
  867.2 52.4 %collective-permute-start.121 = (bf16[3,512,512]{2,1,0:T(8,128)(2,1)}, bf16[3,512,512]{2,1,0:T(8,128)(2,1)}, u32[]{:S(2)}, u32[]{:S(2)}) collective-permute-start(bf16[3,512,512]{2,1,0:T(8,128)(2,1)} %get-tuple-element.433), channel_id=1, source_target_pairs={{0,1},{1,2},{2,3},{4,5},{5,6},{6,7},{8,9},{9,10},{10,11},{12,13},{... | collective-permute-start | bytes 4718600 | tf_op jit(solution)/shard_map/ppermute | solution.py:67
  872.9 54.3 %collective-permute-start.122 = (bf16[3,512,512]{2,1,0:T(8,128)(2,1)}, bf16[3,512,512]{2,1,0:T(8,128)(2,1)}, u32[]{:S(2)}, u32[]{:S(2)}) collective-permute-start(bf16[3,512,512]{2,1,0:T(8,128)(2,1)} %get-tuple-element.434), channel_id=1, source_target_pairs={{1,0},{2,1},{3,2},{5,4},{6,5},{7,6},{9,8},{10,9},{11,10},{13,12},{... | collective-permute-start | bytes 4718600 | tf_op jit(solution)/shard_map/ppermute | solution.py:67
  906.2 31.4 %collective-permute-start.123 = (f32[4,512]{1,0:T(4,128)S(1)}, f32[4,512]{1,0:T(4,128)S(1)}, u32[]{:S(2)}, u32[]{:S(2)}) collective-permute-start(f32[4,512]{1,0:T(4,128)S(1)} %broadcast_select_fusion), channel_id=1, source_target_pairs={{0,1},{1,0},{2,3},{3,2},{4,5},{5,4},{6,7},{7,6},{8,9},{9,8},{10,11... | collective-permute-start | bytes 24584 | tf_op jit(solution)/shard_map/ppermute | solution.py:67
  912.4 36.0 %collective-permute-start.119 = (f32[64,1024]{1,0:T(8,128)S(1)}, f32[64,1024]{1,0:T(8,128)S(1)}, u32[]{:S(2)}, u32[]{:S(2)}) collective-permute-start(f32[64,1024]{1,0:T(8,128)S(1)} %copy-done.166), channel_id=1, source_target_pairs={{0,2},{1,3},{2,0},{3,1},{4,6},{5,7},{6,4},{7,5},{8,10},{9,11},{10,... | collective-permute-start | bytes 786440 | tf_op jit(solution)/shard_map/ppermute | solution.py:67
  912.4 25.2 %collective-permute-start.120 = (f32[64,512]{1,0:T(8,128)S(1)}, f32[64,512]{1,0:T(8,128)S(1)}, u32[]{:S(2)}, u32[]{:S(2)}) collective-permute-start(f32[64,512]{1,0:T(8,128)S(1)} %copy-done.174), channel_id=1, source_target_pairs={{0,1},{1,0},{2,3},{3,2},{4,5},{5,4},{6,7},{7,6},{8,9},{9,8},{10,11... | collective-permute-start | bytes 393224 | tf_op jit(solution)/shard_map/ppermute | solution.py:67
  919.6 69.1 %collective-permute-start.117 = (bf16[512,512]{1,0:T(8,128)(2,1)}, bf16[512,512]{1,0:T(8,128)(2,1)S(1)}, u32[]{:S(2)}, u32[]{:S(2)}) collective-permute-start(bf16[512,512]{1,0:T(8,128)(2,1)} %add_convert_fusion.3), channel_id=1, source_target_pairs={{0,1},{1,2},{4,5},{5,6},{8,9},{9,10},{12,13},{13,14},{16,17},{17,1... | collective-permute-start | bytes 1572872 | tf_op jit(solution)/shard_map/ppermute | solution.py:67
  946.1 51.2 %collective-permute-start.99 = (bf16[512,512]{1,0:T(8,128)(2,1)S(1)}, bf16[512,512]{1,0:T(8,128)(2,1)S(1)}, u32[]{:S(2)}, u32[]{:S(2)}) collective-permute-start(bf16[512,512]{1,0:T(8,128)(2,1)S(1)} %copy-done.171), channel_id=1, source_target_pairs={{0,1},{1,2},{2,3},{4,5},{5,6},{6,7},{8,9},{9,10},{10,11},{12,13},{... | collective-permute-start | bytes 1572872 | tf_op jit(solution)/shard_map/ppermute | solution.py:67
  948.4 41.2 %collective-permute-start.118 = (bf16[512,512]{1,0:T(8,128)(2,1)}, bf16[512,512]{1,0:T(8,128)(2,1)S(1)}, u32[]{:S(2)}, u32[]{:S(2)}) collective-permute-start(bf16[512,512]{1,0:T(8,128)(2,1)} %add_convert_fusion.3), channel_id=1, source_target_pairs={{2,1},{3,2},{6,5},{7,6},{10,9},{11,10},{14,13},{15,14},{18,17},{19... | collective-permute-start | bytes 1572872 | tf_op jit(solution)/shard_map/ppermute | solution.py:67
  962.1 35.1 %collective-permute-start.100 = (bf16[512,512]{1,0:T(8,128)(2,1)S(1)}, bf16[512,512]{1,0:T(8,128)(2,1)S(1)}, u32[]{:S(2)}, u32[]{:S(2)}) collective-permute-start(bf16[512,512]{1,0:T(8,128)(2,1)S(1)} %copy-done.172), channel_id=1, source_target_pairs={{1,0},{2,1},{3,2},{5,4},{6,5},{7,6},{9,8},{10,9},{11,10},{13,12},{... | collective-permute-start | bytes 1572872 | tf_op jit(solution)/shard_map/ppermute | solution.py:67
  (267 other events, 5474.2 us)
Sparse Core Ops, SparseCore 0:
  709.2 41.3 reduce-scatter.6
  787.7 63.0 reduce-scatter.4
  854.2 71.2 reduce-scatter.10
  929.2 71.4 reduce-scatter.8

commit v4 on v3

--- a/solution.py
+++ b/solution.py
@@ -11,7 +11,7 @@
 HEAD_DIM = 128
 SEQ = 1024
 CHUNKS = 2
-SUB = 256
+SUB = 512
 
 HIGH = lax.Precision.HIGHEST
 EPS_NORM = 1e-05
@@ -943,7 +943,7 @@
     if half is not None:
         width //= 2
         out_cols //= 2
-    tile_m, tile_n = min(512, height), min(2048, width)
+    tile_m, tile_n = min(512 if width > 512 else 1024, height), min(2048, width)
     begin = first // tile_n
     if half:
         skip = width // tile_n
@@ -1221,7 +1221,12 @@
     end_mlp_back(0)
     order.send(mlp_back[1], branch_grad[0])
     mlp_back[1].prepare()
+    down_part = weight_part(cot_low, hidden, ff, mlp_back[1].came)
     order.send(mlp_back[1], branch_grad[0], back_sums[0])
+    up_came, down_came = mlp_back[1].came
+    up_came, down_part = lax.optimization_barrier((up_came, down_part))
+    mlp_back[1].came = [up_came, down_came]
+    down_sum = lax.psum_scatter(down_part, "dp", scatter_dimension=0, tiled=True)
     mlp_back[1].prepare()
     order.send(mlp_back[1], branch_grad[0], back_sums[0])
     mlp_back[1].prepare()
@@ -1247,8 +1252,7 @@
     own = [None] * 2
     early_one = Butterfly(jnp.concatenate([chain.now for chain in early_chain], axis=1))
     order.send(*grads, early_one)
-    out_part = weight_part(d_branch, heads_out, width, grads[0].came)
-    down_part = weight_part(cot_low, hidden, ff, grads[1].came)
+    out_part = weight_part(d_branch, heads_out, width, (*grads[0].came, down_sum))
     order.send(*grads, early_one)
     up_part = weight_part(normed_mlp, d_hpre, ff, grads[0].came)
     qkv_part = None
@@ -1258,7 +1262,7 @@
             qkv_part, grads[1].came, s if s < 2 else None,
         )
     order.send(*grads)
-    down_grad = dp_sum(down_part)
+    down_grad = down_sum.astype(F32)
     own = [grads[c].own() for c in both]
     up_grad, out_weight_grad = [dp_sum(part) for part in (up_part, out_part)]
     qkv_sum = lax.psum_scatter(qkv_part, "dp", scatter_dimension=0, tiled=True)
@@ -1321,9 +1325,9 @@
     small = Butterfly(
         jnp.concatenate([out_share, in_share, gain_share, gain_chain.value()], axis=0), ("dp",)
     )
-    layers(0, (small.now,))
     order.send(small)
     order.send(mlp_out[1])
+    layers(0, (small.now,))
     layers(1, ())
     while small.turns:
         order.send(small)

time: 1040 us -> 1040 us (level)
    unnamed x394 -> x403, local copies, waits for them, and re-layouts: 38.5 us -> 47 us
  transfers between devices with their start and end apart: 137 -> 137, of which waited for: 49 -> 45; matrix products, arithmetic and copies ran while one was open for 15% -> 16% of each run, Pallas kernels for 19% -> 18%
where the time goes in v4:
time: 1040 us; the launch traced here: 1030 us
  waiting for transfers between devices  318 us (31%)
  starting transfers between devices  278 us (27%)
  Pallas kernels  205 us (20%)
  matrix products  105 us (10%)
  local copies, waits for them, and re-layouts  55.6 us (5%)
  other arithmetic  45.1 us (4%)
  between operations  19.1 us (2%)
    ppermute x133, waiting for transfers between devices, send(): got.append(lax.ppermute(held[at], axis, perm))  318 us
    ppermute x133, starting transfers between devices, send(): got.append(lax.ppermute(held[at], axis, perm))  278 us
    dot_general x26, matrix products, dot_tt(): lax.dot_general(former, latter, (dims, ((), ())), precision=precision, pr...  54.1 us
    pallas_call x6, Pallas kernels, rows_product(): pl.pallas_call(functools.partial(rows_product_kernel, n), grid=(height //...  48.5 us
    unnamed x403, local copies, waits for them, and re-layouts  47 us
    pallas_call x8, Pallas kernels, send_values(): pl.pallas_call(functools.partial(send_kernel, count, turns, came is not N...  33.4 us
    pallas_call x4, Pallas kernels, mix_streams(): pl.pallas_call(functools.partial(mix_kernel, picked), grid=(rows // TILE,...  24.4 us
    pallas_call x2, Pallas kernels, late_dots(): pl.pallas_call(late_kernel, grid=(rows // TILE,), in_specs=[pl.BlockSpec(...  20.9 us
  transfers between devices with their start and end apart: 137, of which 45 were waited for; matrix products, arithmetic and copies ran while one was open for 16% of the time, Pallas kernels for 18%

profile of v4, /device:TPU:0, one launch (start us, length us, event | category | flops | bytes accessed | tf_op | source)
XLA Modules:
  0.0 1026.0 jit_solution(7150543187907157251)
XLA Ops:
  24.9 7.7 collective-permute-done.1
  35.4 7.2 mix_streams.5
  42.6 7.2 mix_streams.4
  73.9 5.4 collective-permute-start.10
  84.5 5.0 mix_streams.6.base
  89.4 5.8 collective-permute-done.5
  95.3 5.5 collective-permute-done.6
  103.7 8.2 collective-permute-done.11
  114.8 7.2 early_dots.2
  121.9 12.5 %collective-permute-done.9 = bf16[2,512,512]{2,1,0:T(8,128)(2,1)} collective-permute-done((bf16[2,512,512]{2,1,0:T(8,128)(2,1)}, bf16[2,512,512]{2,1,0:T(8,128)(2,1)}, u32[]{:S(2)}, u32[]{:S(2)}) %collective-permute-start.9) | collective-permute-done | bytes 1048608 | tf_op jit(solution)/shard_map/ppermute | solution.py:67
  134.5 7.4 collective-permute-done.15
  147.5 5.0 mix_streams.7.base
  152.5 7.3 collective-permute-start.20
  167.6 15.2 %collective-permute-done.13 = bf16[2,512,512]{2,1,0:T(8,128)(2,1)} collective-permute-done((bf16[2,512,512]{2,1,0:T(8,128)(2,1)}, bf16[2,512,512]{2,1,0:T(8,128)(2,1)}, u32[]{:S(2)}, u32[]{:S(2)}) %collective-permute-start.13) | collective-permute-done | bytes 1048608 | tf_op jit(solution)/shard_map/ppermute | solution.py:67
  201.9 6.7 collective-permute-done.18
  211.6 5.8 collective-permute-start.22
  226.1 7.2 early_dots.3
  236.1 6.3 collective-permute-start.26
  251.2 9.9 collective-permute-done.27.down
  261.9 12.3 %collective-permute-start.36 = (bf16[512,512]{1,0:T(8,128)(2,1)}, bf16[512,512]{1,0:T(8,128)(2,1)}, u32[]{:S(2)}, u32[]{:S(2)}) collective-permute-start(bf16[512,512]{1,0:T(8,128)(2,1)} %get-tuple-element.252), channel_id=1, source_target_pairs={{0,1},{1,2},{2,3},{4,5},{5,6},{6,7},{8,9},{9,10},{10,11},{12,13},{... | collective-permute-start | bytes 1572872 | tf_op jit(solution)/shard_map/ppermute | solution.py:67
  280.4 9.9 collective-permute-done.37
  297.1 22.5 %collective-permute-done.40 = f32[8,512]{1,0:T(8,128)S(1)} collective-permute-done((f32[8,512]{1,0:T(8,128)S(1)}, f32[8,512]{1,0:T(8,128)S(1)}, u32[]{:S(2)}, u32[]{:S(2)}) %collective-permute-start.40) | collective-permute-done | bytes 16416 | tf_op jit(solution)/shard_map/ppermute | solution.py:67
  331.2 6.0 collective-permute-done.31
  344.0 5.3 attend_forward.3
  362.3 9.5 fusion.119
  378.9 9.6 collective-permute-done.48
  388.9 7.9 collective-permute-done.50.refs_5_
  396.8 5.8 collective-permute-start.56
  432.3 9.4 multiply_convert_fusion.3
  472.1 9.4 fusion.120
  481.9 6.4 collective-permute-start.74
  491.4 9.5 multiply_convert_fusion.1
  509.3 5.1 collective-permute-start.76
  529.5 5.2 collective-permute-start.80
  534.6 13.3 %rows_product.6 = bf16[2048,2048]{1,0:T(8,128)(2,1)} custom-call(bf16[512,2048]{1,0:T(8,128)(2,1)S(1)} %pad_maximum_fusion.4.refs_0_, bf16[512,2048]{1,0:T(8,128)(2,1)S(1)} %pad_maximum_fusion.5.refs_1_, bf16[512,2048]{1,0:T(8,128)(2,1)} %get-tuple-element.400.refs_2_, bf16[512,2048]{1,0:T(8,128)(2,1)} %get-tuple-element.405.refs_3_, ...), custom_call_target="tpu_custom_call" | custom-call | tf_op jit(solution)/shard_map/rows_product/pallas_call | solution.py:951
  557.5 9.3 collective-permute-done.83.refs_5_
  566.8 5.2 collective-permute-start.85
  582.9 5.3 collective-permute-done.86.down
  607.3 6.5 collective-permute-start.96
  620.5 5.0 attend_backward.2
  657.5 8.8 attend_backward.3
  666.3 5.0 send_values.8
  685.2 56.1 %collective-permute-done.110 = f32[64,1024]{1,0:T(8,128)S(1)} collective-permute-done((f32[64,1024]{1,0:T(8,128)S(1)}, f32[64,1024]{1,0:T(8,128)S(1)}, u32[]{:S(2)}, u32[]{:S(2)}) %collective-permute-start.110) | collective-permute-done | bytes 262176 | tf_op jit(solution)/shard_map/ppermute | solution.py:67
  758.0 14.7 %collective-permute-done.113.refs_5_.refs_4_ = bf16[3,512,512]{2,1,0:T(8,128)(2,1)S(1)} collective-permute-done((bf16[3,512,512]{2,1,0:T(8,128)(2,1)S(1)}, bf16[3,512,512]{2,1,0:T(8,128)(2,1)S(1)}, u32[]{:S(2)}, u32[]{:S(2)}) %collective-permute-start.113) | collective-permute-done | bytes 1572896 | tf_op jit(solution)/shard_map/ppermute | solution.py:67
  772.7 6.3 rows_product.7.refs_6_
  778.9 5.2 rows_product.8.refs_6_
  784.1 5.3 rows_product.9
  793.7 5.1 rows_product.10
  798.9 7.4 collective-permute-start.111
  807.1 17.4 %collective-permute-done.111.refs_5_.refs_4_ = bf16[3,512,512]{2,1,0:T(8,128)(2,1)S(1)} collective-permute-done((bf16[3,512,512]{2,1,0:T(8,128)(2,1)}, bf16[3,512,512]{2,1,0:T(8,128)(2,1)S(1)}, u32[]{:S(2)}, u32[]{:S(2)}) %collective-permute-start.111) | collective-permute-done | bytes 1572896 | tf_op jit(solution)/shard_map/ppermute | solution.py:67
  824.5 13.5 %rows_product.11 = bf16[2048,2048]{1,0:T(8,128)(2,1)} custom-call(bf16[512,2048]{1,0:T(8,128)(2,1)S(1)} %copy-done.51, bf16[512,2048]{1,0:T(8,128)(2,1)} %copy-done.52, bf16[512,2048]{1,0:T(8,128)(2,1)} %copy-done.145, bf16[512,2048]{1,0:T(8,128)(2,1)} %copy-done.147, bf16[3,512,512]{2,1,0:T(8,128)(2,1)S(1)} %collective-permute-done.111.refs_5_.refs_4_, ...), custom_call_target="tpu_custom_call" | custom-call | tf_op jit(solution)/shard_map/rows_product/pallas_call | solution.py:951
  841.6 5.8 send_values.12
  847.4 5.7 send_values.13
  853.1 7.6 collective-permute-start.115
  862.0 5.8 collective-permute-start.121
  890.5 10.3 late_dots.2
  907.4 7.0 collective-permute-done.121.up
  914.5 7.7 collective-permute-start.117
  922.2 10.6 %late_dots.3 = (f32[512,512]{1,0:T(8,128)}, f32[512,512]{1,0:T(8,128)}, f32[512,512]{1,0:T(8,128)}, f32[64,512]{1,0:T(8,128)}, f32[3,8,512]{2,1,0:T(8,128)}) custom-call(bf16[11,1024,512]{2,1,0:T(8,128)(2,1)} %hist_ref.15, f32[512,512]{1,0:T(8,128)} %get-tuple-element.294.x0, f32[512,512]{1,0:T(8,128)} %get-tuple-element.264.x1, ...), custom_call_target="tpu_custom_call" | custom-call | tf_op jit(solution)/shard_map/late_dots/pallas_call | solution.py:485
  945.4 7.0 collective-permute-done.127
  967.6 8.7 layer_grads.2
  976.4 5.8 copy.48.refs_0_
  983.7 9.4 layer_grads.3
  994.9 5.7 collective-permute-done.131
  (792 shorter events, 444.5 us)
Async XLA Ops:
  7.2 782.3 %reduce-scatter.7.cloned.1.call-start = ((), (), s32[]{:S(2)}) async-start(), calls=%async_computation.5 | async-start | bytes 9437184 | tf_op jit(solution)/shard_map/reduce_scatter | solution.py:1229
  68.8 26.5 %collective-permute-start.5 = (bf16[2,512,512]{2,1,0:T(8,128)(2,1)S(1)}, bf16[2,512,512]{2,1,0:T(8,128)(2,1)}, u32[]{:S(2)}, u32[]{:S(2)}) collective-permute-start(bf16[2,512,512]{2,1,0:T(8,128)(2,1)S(1)} %get-tuple-element.259), channel_id=1, source_target_pairs={{0,1},{1,2},{2,3},{4,5},{5,6},{6,7},{8,9},{9,10},{10,11},{12,13},{... | collective-permute-start | bytes 3145736 | tf_op jit(solution)/shard_map/ppermute | solution.py:67
  72.7 28.1 %collective-permute-start.6 = (bf16[2,512,512]{2,1,0:T(8,128)(2,1)S(1)}, bf16[2,512,512]{2,1,0:T(8,128)(2,1)}, u32[]{:S(2)}, u32[]{:S(2)}) collective-permute-start(bf16[2,512,512]{2,1,0:T(8,128)(2,1)S(1)} %get-tuple-element.259), channel_id=1, source_target_pairs={{1,0},{2,1},{3,2},{5,4},{6,5},{7,6},{9,8},{10,9},{11,10},{13,12},{... | collective-permute-start | bytes 3145736 | tf_op jit(solution)/shard_map/ppermute | solution.py:67
  73.9 29.8 %collective-permute-start.10 = (bf16[512,512]{1,0:T(8,128)(2,1)S(1)}, bf16[512,512]{1,0:T(8,128)(2,1)}, u32[]{:S(2)}, u32[]{:S(2)}) collective-permute-start(bf16[512,512]{1,0:T(8,128)(2,1)S(1)} %get-tuple-element.262), channel_id=1, source_target_pairs={{0,1},{1,2},{2,3},{4,5},{5,6},{6,7},{8,9},{9,10},{10,11},{12,13},{... | collective-permute-start | bytes 1572872 | tf_op jit(solution)/shard_map/ppermute | solution.py:67
  79.3 32.7 %collective-permute-start.11 = (bf16[512,512]{1,0:T(8,128)(2,1)S(1)}, bf16[512,512]{1,0:T(8,128)(2,1)}, u32[]{:S(2)}, u32[]{:S(2)}) collective-permute-start(bf16[512,512]{1,0:T(8,128)(2,1)S(1)} %get-tuple-element.262), channel_id=1, source_target_pairs={{1,0},{2,1},{3,2},{5,4},{6,5},{7,6},{9,8},{10,9},{11,10},{13,12},{... | collective-permute-start | bytes 1572872 | tf_op jit(solution)/shard_map/ppermute | solution.py:67
  100.7 21.2 %collective-permute-start.8 = (bf16[2,512,512]{2,1,0:T(8,128)(2,1)}, bf16[2,512,512]{2,1,0:T(8,128)(2,1)}, u32[]{:S(2)}, u32[]{:S(2)}) collective-permute-start(bf16[2,512,512]{2,1,0:T(8,128)(2,1)} %collective-permute-done.5), channel_id=1, source_target_pairs={{1,2},{2,3},{5,6},{6,7},{9,10},{10,11},{13,14},{14,15},{17,18},{18... | collective-permute-start | bytes 3145736 | tf_op jit(solution)/shard_map/ppermute | solution.py:67
  102.4 32.0 %collective-permute-start.9 = (bf16[2,512,512]{2,1,0:T(8,128)(2,1)}, bf16[2,512,512]{2,1,0:T(8,128)(2,1)}, u32[]{:S(2)}, u32[]{:S(2)}) collective-permute-start(bf16[2,512,512]{2,1,0:T(8,128)(2,1)} %collective-permute-done.6), channel_id=1, source_target_pairs={{1,0},{2,1},{5,4},{6,5},{9,8},{10,9},{13,12},{14,13},{17,16},{18,1... | collective-permute-start | bytes 3145736 | tf_op jit(solution)/shard_map/ppermute | solution.py:67
  112.0 22.5 %collective-permute-start.14 = (bf16[512,512]{1,0:T(8,128)(2,1)}, bf16[512,512]{1,0:T(8,128)(2,1)}, u32[]{:S(2)}, u32[]{:S(2)}) collective-permute-start(bf16[512,512]{1,0:T(8,128)(2,1)} %collective-permute-done.10), channel_id=1, source_target_pairs={{1,2},{2,3},{5,6},{6,7},{9,10},{10,11},{13,14},{14,15},{17,18},{18... | collective-permute-start | bytes 1572872 | tf_op jit(solution)/shard_map/ppermute | solution.py:67
  113.5 28.3 %collective-permute-start.15 = (bf16[512,512]{1,0:T(8,128)(2,1)}, bf16[512,512]{1,0:T(8,128)(2,1)}, u32[]{:S(2)}, u32[]{:S(2)}) collective-permute-start(bf16[512,512]{1,0:T(8,128)(2,1)} %collective-permute-done.11), channel_id=1, source_target_pairs={{1,0},{2,1},{5,4},{6,5},{9,8},{10,9},{13,12},{14,13},{17,16},{18,1... | collective-permute-start | bytes 1572872 | tf_op jit(solution)/shard_map/ppermute | solution.py:67
  144.5 23.1 %collective-permute-start.12 = (bf16[2,512,512]{2,1,0:T(8,128)(2,1)}, bf16[2,512,512]{2,1,0:T(8,128)(2,1)}, u32[]{:S(2)}, u32[]{:S(2)}) collective-permute-start(bf16[2,512,512]{2,1,0:T(8,128)(2,1)} %collective-permute-done.8), channel_id=1, source_target_pairs={{2,3},{6,7},{10,11},{14,15},{18,19},{22,23},{26,27},{30,31}} | collective-permute-start | bytes 3145736 | tf_op jit(solution)/shard_map/ppermute | solution.py:67
  146.2 36.6 %collective-permute-start.13 = (bf16[2,512,512]{2,1,0:T(8,128)(2,1)}, bf16[2,512,512]{2,1,0:T(8,128)(2,1)}, u32[]{:S(2)}, u32[]{:S(2)}) collective-permute-start(bf16[2,512,512]{2,1,0:T(8,128)(2,1)} %collective-permute-done.9), channel_id=1, source_target_pairs={{1,0},{5,4},{9,8},{13,12},{17,16},{21,20},{25,24},{29,28}} | collective-permute-start | bytes 3145736 | tf_op jit(solution)/shard_map/ppermute | solution.py:67
  152.5 59.1 %collective-permute-start.20 = (bf16[2,512,512]{2,1,0:T(8,128)(2,1)}, bf16[2,512,512]{2,1,0:T(8,128)(2,1)}, u32[]{:S(2)}, u32[]{:S(2)}) collective-permute-start(bf16[2,512,512]{2,1,0:T(8,128)(2,1)} %get-tuple-element.282), channel_id=1, source_target_pairs={{0,1},{1,2},{2,3},{4,5},{5,6},{6,7},{8,9},{9,10},{10,11},{12,13},{... | collective-permute-start | bytes 3145736 | tf_op jit(solution)/shard_map/ppermute | solution.py:67
  159.7 51.8 %collective-permute-start.21 = (bf16[2,512,512]{2,1,0:T(8,128)(2,1)}, bf16[2,512,512]{2,1,0:T(8,128)(2,1)}, u32[]{:S(2)}, u32[]{:S(2)}) collective-permute-start(bf16[2,512,512]{2,1,0:T(8,128)(2,1)} %get-tuple-element.282), channel_id=1, source_target_pairs={{1,0},{2,1},{3,2},{5,4},{6,5},{7,6},{9,8},{10,9},{11,10},{13,12},{... | collective-permute-start | bytes 3145736 | tf_op jit(solution)/shard_map/ppermute | solution.py:67
  199.8 20.8 %collective-permute-start.24 = (bf16[512,512]{1,0:T(8,128)(2,1)}, bf16[512,512]{1,0:T(8,128)(2,1)}, u32[]{:S(2)}, u32[]{:S(2)}) collective-permute-start(bf16[512,512]{1,0:T(8,128)(2,1)} %copy-done.110), channel_id=1, source_target_pairs={{0,1},{1,2},{2,3},{4,5},{5,6},{6,7},{8,9},{9,10},{10,11},{12,13},{... | collective-permute-start | bytes 1572872 | tf_op jit(solution)/shard_map/ppermute | solution.py:67
  211.6 21.7 %collective-permute-start.22 = (bf16[512,512]{1,0:T(8,128)(2,1)S(1)}, bf16[512,512]{1,0:T(8,128)(2,1)}, u32[]{:S(2)}, u32[]{:S(2)}) collective-permute-start(bf16[512,512]{1,0:T(8,128)(2,1)S(1)} %add_convert_fusion.19), channel_id=1, source_target_pairs={{0,1},{1,2},{4,5},{5,6},{8,9},{9,10},{12,13},{13,14},{16,17},{17,1... | collective-permute-start | bytes 1572872 | tf_op jit(solution)/shard_map/ppermute | solution.py:67
  218.9 55.3 %collective-permute-start.28 = (bf16[2,512,512]{2,1,0:T(8,128)(2,1)}, bf16[2,512,512]{2,1,0:T(8,128)(2,1)}, u32[]{:S(2)}, u32[]{:S(2)}) collective-permute-start(bf16[2,512,512]{2,1,0:T(8,128)(2,1)} %collective-permute-done.20), channel_id=1, source_target_pairs={{1,2},{2,3},{5,6},{6,7},{9,10},{10,11},{13,14},{14,15},{17,18},{18... | collective-permute-start | bytes 3145736 | tf_op jit(solution)/shard_map/ppermute | solution.py:67
  220.6 57.7 %collective-permute-start.29 = (bf16[2,512,512]{2,1,0:T(8,128)(2,1)}, bf16[2,512,512]{2,1,0:T(8,128)(2,1)}, u32[]{:S(2)}, u32[]{:S(2)}) collective-permute-start(bf16[2,512,512]{2,1,0:T(8,128)(2,1)} %collective-permute-done.21), channel_id=1, source_target_pairs={{1,0},{2,1},{5,4},{6,5},{9,8},{10,9},{13,12},{14,13},{17,16},{18,1... | collective-permute-start | bytes 3145736 | tf_op jit(solution)/shard_map/ppermute | solution.py:67
  243.8 34.5 %collective-permute-start.32 = (bf16[512,512]{1,0:T(8,128)(2,1)}, bf16[512,512]{1,0:T(8,128)(2,1)}, u32[]{:S(2)}, u32[]{:S(2)}) collective-permute-start(bf16[512,512]{1,0:T(8,128)(2,1)} %collective-permute-done.24), channel_id=1, source_target_pairs={{1,2},{2,3},{5,6},{6,7},{9,10},{10,11},{13,14},{14,15},{17,18},{18... | collective-permute-start | bytes 1572872 | tf_op jit(solution)/shard_map/ppermute | solution.py:67
  249.9 28.4 %collective-permute-start.33 = (bf16[512,512]{1,0:T(8,128)(2,1)}, bf16[512,512]{1,0:T(8,128)(2,1)}, u32[]{:S(2)}, u32[]{:S(2)}) collective-permute-start(bf16[512,512]{1,0:T(8,128)(2,1)} %collective-permute-done.25), channel_id=1, source_target_pairs={{1,0},{2,1},{5,4},{6,5},{9,8},{10,9},{13,12},{14,13},{17,16},{18,1... | collective-permute-start | bytes 1572872 | tf_op jit(solution)/shard_map/ppermute | solution.py:67
  290.3 30.0 %collective-permute-start.38 = (bf16[512,512]{1,0:T(8,128)(2,1)}, bf16[512,512]{1,0:T(8,128)(2,1)S(1)}, u32[]{:S(2)}, u32[]{:S(2)}) collective-permute-start(bf16[512,512]{1,0:T(8,128)(2,1)} %collective-permute-done.36), channel_id=1, source_target_pairs={{1,2},{2,3},{5,6},{6,7},{9,10},{10,11},{13,14},{14,15},{17,18},{18... | collective-permute-start | bytes 1572872 | tf_op jit(solution)/shard_map/ppermute | solution.py:67
  291.0 31.2 %collective-permute-start.39 = (bf16[512,512]{1,0:T(8,128)(2,1)}, bf16[512,512]{1,0:T(8,128)(2,1)}, u32[]{:S(2)}, u32[]{:S(2)}) collective-permute-start(bf16[512,512]{1,0:T(8,128)(2,1)} %collective-permute-done.37), channel_id=1, source_target_pairs={{1,0},{2,1},{5,4},{6,5},{9,8},{10,9},{13,12},{14,13},{17,16},{18,1... | collective-permute-start | bytes 1572872 | tf_op jit(solution)/shard_map/ppermute | solution.py:67
  292.3 31.4 %collective-permute-start.34 = (bf16[512,512]{1,0:T(8,128)(2,1)}, bf16[512,512]{1,0:T(8,128)(2,1)S(1)}, u32[]{:S(2)}, u32[]{:S(2)}) collective-permute-start(bf16[512,512]{1,0:T(8,128)(2,1)} %collective-permute-done.32), channel_id=1, source_target_pairs={{2,3},{6,7},{10,11},{14,15},{18,19},{22,23},{26,27},{30,31}} | collective-permute-start | bytes 1572872 | tf_op jit(solution)/shard_map/ppermute | solution.py:67
  293.0 32.5 %collective-permute-start.35 = (bf16[512,512]{1,0:T(8,128)(2,1)}, bf16[512,512]{1,0:T(8,128)(2,1)S(1)}, u32[]{:S(2)}, u32[]{:S(2)}) collective-permute-start(bf16[512,512]{1,0:T(8,128)(2,1)} %collective-permute-done.33), channel_id=1, source_target_pairs={{1,0},{5,4},{9,8},{13,12},{17,16},{21,20},{25,24},{29,28}} | collective-permute-start | bytes 1572872 | tf_op jit(solution)/shard_map/ppermute | solution.py:67
  294.3 25.3 %collective-permute-start.40 = (f32[8,512]{1,0:T(8,128)S(1)}, f32[8,512]{1,0:T(8,128)S(1)}, u32[]{:S(2)}, u32[]{:S(2)}) collective-permute-start(f32[8,512]{1,0:T(8,128)S(1)} %get-tuple-element.309), channel_id=1, source_target_pairs={{0,1},{1,0},{2,3},{3,2},{4,5},{5,4},{6,7},{7,6},{8,9},{9,8},{10,11... | collective-permute-start | bytes 49160 | tf_op jit(solution)/shard_map/ppermute | solution.py:67
  322.2 30.4 %collective-permute-start.45 = (bf16[512,512]{1,0:T(8,128)(2,1)S(1)}, bf16[512,512]{1,0:T(8,128)(2,1)}, u32[]{:S(2)}, u32[]{:S(2)}) collective-permute-start(bf16[512,512]{1,0:T(8,128)(2,1)S(1)} %collective-permute-done.38), channel_id=1, source_target_pairs={{2,3},{6,7},{10,11},{14,15},{18,19},{22,23},{26,27},{30,31}} | collective-permute-start | bytes 1572872 | tf_op jit(solution)/shard_map/ppermute | solution.py:67
  323.7 29.0 %collective-permute-start.46 = (bf16[512,512]{1,0:T(8,128)(2,1)}, bf16[512,512]{1,0:T(8,128)(2,1)}, u32[]{:S(2)}, u32[]{:S(2)}) collective-permute-start(bf16[512,512]{1,0:T(8,128)(2,1)} %collective-permute-done.39), channel_id=1, source_target_pairs={{1,0},{5,4},{9,8},{13,12},{17,16},{21,20},{25,24},{29,28}} | collective-permute-start | bytes 1572872 | tf_op jit(solution)/shard_map/ppermute | solution.py:67
  418.4 25.9 %collective-permute-start.62 = (f32[8,512]{1,0:T(8,128)S(1)}, f32[8,512]{1,0:T(8,128)S(1)}, u32[]{:S(2)}, u32[]{:S(2)}) collective-permute-start(f32[8,512]{1,0:T(8,128)S(1)} %get-tuple-element.335), channel_id=1, source_target_pairs={{0,1},{1,0},{2,3},{3,2},{4,5},{5,4},{6,7},{7,6},{8,9},{9,8},{10,11... | collective-permute-start | bytes 49160 | tf_op jit(solution)/shard_map/ppermute | solution.py:67
  420.4 24.0 %collective-permute-start.60 = (bf16[512,512]{1,0:T(8,128)(2,1)S(1)}, bf16[512,512]{1,0:T(8,128)(2,1)S(1)}, u32[]{:S(2)}, u32[]{:S(2)}) collective-permute-start(bf16[512,512]{1,0:T(8,128)(2,1)S(1)} %get-tuple-element.334.refs_0_), channel_id=1, source_target_pairs={{0,1},{1,2},{2,3},{4,5},{5,6},{6,7},{8,9},{9,10},{10,11},{12,13},{... | collective-permute-start | bytes 1572872 | tf_op jit(solution)/shard_map/ppermute | solution.py:67
  422.8 21.6 %collective-permute-start.61 = (bf16[512,512]{1,0:T(8,128)(2,1)S(1)}, bf16[512,512]{1,0:T(8,128)(2,1)S(1)}, u32[]{:S(2)}, u32[]{:S(2)}) collective-permute-start(bf16[512,512]{1,0:T(8,128)(2,1)S(1)} %get-tuple-element.334.refs_0_), channel_id=1, source_target_pairs={{1,0},{2,1},{3,2},{5,4},{6,5},{7,6},{9,8},{10,9},{11,10},{13,12},{... | collective-permute-start | bytes 1572872 | tf_op jit(solution)/shard_map/ppermute | solution.py:67
  424.1 25.8 %collective-permute-start.58 = (bf16[512,512]{1,0:T(8,128)(2,1)S(1)}, bf16[512,512]{1,0:T(8,128)(2,1)S(1)}, u32[]{:S(2)}, u32[]{:S(2)}) collective-permute-start(bf16[512,512]{1,0:T(8,128)(2,1)S(1)} %collective-permute-done.54), channel_id=1, source_target_pairs={{1,2},{2,3},{5,6},{6,7},{9,10},{10,11},{13,14},{14,15},{17,18},{18... | collective-permute-start | bytes 1572872 | tf_op jit(solution)/shard_map/ppermute | solution.py:67
  429.2 22.8 %collective-permute-start.59 = (bf16[512,512]{1,0:T(8,128)(2,1)S(1)}, bf16[512,512]{1,0:T(8,128)(2,1)S(1)}, u32[]{:S(2)}, u32[]{:S(2)}) collective-permute-start(bf16[512,512]{1,0:T(8,128)(2,1)S(1)} %collective-permute-done.55), channel_id=1, source_target_pairs={{1,0},{2,1},{5,4},{6,5},{9,8},{10,9},{13,12},{14,13},{17,16},{18,1... | collective-permute-start | bytes 1572872 | tf_op jit(solution)/shard_map/ppermute | solution.py:67
  463.5 26.3 %collective-permute-start.69 = (bf16[512,512]{1,0:T(8,128)(2,1)S(1)}, bf16[512,512]{1,0:T(8,128)(2,1)S(1)}, u32[]{:S(2)}, u32[]{:S(2)}) collective-permute-start(bf16[512,512]{1,0:T(8,128)(2,1)S(1)} %collective-permute-done.65.refs_2_), channel_id=1, source_target_pairs={{2,3},{6,7},{10,11},{14,15},{18,19},{22,23},{26,27},{30,31}} | collective-permute-start | bytes 1572872 | tf_op jit(solution)/shard_map/ppermute | solution.py:67
  464.2 25.6 %collective-permute-start.70 = (bf16[512,512]{1,0:T(8,128)(2,1)S(1)}, bf16[512,512]{1,0:T(8,128)(2,1)S(1)}, u32[]{:S(2)}, u32[]{:S(2)}) collective-permute-start(bf16[512,512]{1,0:T(8,128)(2,1)S(1)} %collective-permute-done.66.refs_5_), channel_id=1, source_target_pairs={{1,0},{5,4},{9,8},{13,12},{17,16},{21,20},{25,24},{29,28}} | collective-permute-start | bytes 1572872 | tf_op jit(solution)/shard_map/ppermute | solution.py:67
  481.9 24.8 %collective-permute-start.74 = (bf16[512,512]{1,0:T(8,128)(2,1)S(1)}, bf16[512,512]{1,0:T(8,128)(2,1)S(1)}, u32[]{:S(2)}, u32[]{:S(2)}) collective-permute-start(bf16[512,512]{1,0:T(8,128)(2,1)S(1)} %add_convert_fusion.12), channel_id=1, source_target_pairs={{0,1},{1,2},{2,3},{4,5},{5,6},{6,7},{8,9},{9,10},{10,11},{12,13},{... | collective-permute-start | bytes 1572872 | tf_op jit(solution)/shard_map/ppermute | solution.py:67
  548.0 464.2 %reduce-scatter.5.cloned.1.call-start = ((), (), s32[]{:S(2)}) async-start(), calls=%async_computation.4 | async-start | bytes 7077888 | tf_op jit(solution)/shard_map/reduce_scatter | solution.py:1268
  605.3 20.3 %collective-permute-start.91 = (bf16[512,512]{1,0:T(8,128)(2,1)S(1)}, bf16[512,512]{1,0:T(8,128)(2,1)S(1)}, u32[]{:S(2)}, u32[]{:S(2)}) collective-permute-start(bf16[512,512]{1,0:T(8,128)(2,1)S(1)} %collective-permute-done.87.refs_1_), channel_id=1, source_target_pairs={{1,2},{2,3},{5,6},{6,7},{9,10},{10,11},{13,14},{14,15},{17,18},{18... | collective-permute-start | bytes 1572872 | tf_op jit(solution)/shard_map/ppermute | solution.py:67
  606.0 19.6 %collective-permute-start.92 = (bf16[512,512]{1,0:T(8,128)(2,1)S(1)}, bf16[512,512]{1,0:T(8,128)(2,1)S(1)}, u32[]{:S(2)}, u32[]{:S(2)}) collective-permute-start(bf16[512,512]{1,0:T(8,128)(2,1)S(1)} %collective-permute-done.88.refs_4_), channel_id=1, source_target_pairs={{1,0},{2,1},{5,4},{6,5},{9,8},{10,9},{13,12},{14,13},{17,16},{18,1... | collective-permute-start | bytes 1572872 | tf_op jit(solution)/shard_map/ppermute | solution.py:67
  627.8 25.6 %collective-permute-start.105 = (f32[8,512]{1,0:T(8,128)S(1)}, f32[8,512]{1,0:T(8,128)S(1)}, u32[]{:S(2)}, u32[]{:S(2)}) collective-permute-start(f32[8,512]{1,0:T(8,128)S(1)} %add.356), channel_id=1, source_target_pairs={{0,2},{1,3},{2,0},{3,1},{4,6},{5,7},{6,4},{7,5},{8,10},{9,11},{10,... | collective-permute-start | bytes 49160 | tf_op jit(solution)/shard_map/ppermute | solution.py:67
  632.3 21.0 %collective-permute-start.103 = (bf16[512,512]{1,0:T(8,128)(2,1)S(1)}, bf16[512,512]{1,0:T(8,128)(2,1)S(1)}, u32[]{:S(2)}, u32[]{:S(2)}) collective-permute-start(bf16[512,512]{1,0:T(8,128)(2,1)S(1)} %collective-permute-done.91.refs_2_), channel_id=1, source_target_pairs={{2,3},{6,7},{10,11},{14,15},{18,19},{22,23},{26,27},{30,31}} | collective-permute-start | bytes 1572872 | tf_op jit(solution)/shard_map/ppermute | solution.py:67
  633.0 20.4 %collective-permute-start.104 = (bf16[512,512]{1,0:T(8,128)(2,1)S(1)}, bf16[512,512]{1,0:T(8,128)(2,1)S(1)}, u32[]{:S(2)}, u32[]{:S(2)}) collective-permute-start(bf16[512,512]{1,0:T(8,128)(2,1)S(1)} %collective-permute-done.92.refs_5_), channel_id=1, source_target_pairs={{1,0},{5,4},{9,8},{13,12},{17,16},{21,20},{25,24},{29,28}} | collective-permute-start | bytes 1572872 | tf_op jit(solution)/shard_map/ppermute | solution.py:67
  646.6 29.0 %collective-permute-start.101 = (bf16[512,512]{1,0:T(8,128)(2,1)}, bf16[512,512]{1,0:T(8,128)(2,1)S(1)}, u32[]{:S(2)}, u32[]{:S(2)}) collective-permute-start(bf16[512,512]{1,0:T(8,128)(2,1)} %get-tuple-element.403), channel_id=1, source_target_pairs={{0,1},{4,5},{8,9},{12,13},{16,17},{20,21},{24,25},{28,29}} | collective-permute-start | bytes 1572872 | tf_op jit(solution)/shard_map/ppermute | solution.py:67
  651.2 24.4 %collective-permute-start.102 = (bf16[512,512]{1,0:T(8,128)(2,1)S(1)}, bf16[512,512]{1,0:T(8,128)(2,1)}, u32[]{:S(2)}, u32[]{:S(2)}) collective-permute-start(bf16[512,512]{1,0:T(8,128)(2,1)S(1)} %get-tuple-element.404), channel_id=1, source_target_pairs={{3,2},{7,6},{11,10},{15,14},{19,18},{23,22},{27,26},{31,30}} | collective-permute-start | bytes 1572872 | tf_op jit(solution)/shard_map/ppermute | solution.py:67
  679.5 62.5 %collective-permute-start.106 = (bf16[3,512,512]{2,1,0:T(8,128)(2,1)S(1)}, bf16[3,512,512]{2,1,0:T(8,128)(2,1)S(1)}, u32[]{:S(2)}, u32[]{:S(2)}) collective-permute-start(bf16[3,512,512]{2,1,0:T(8,128)(2,1)S(1)} %get-tuple-element.420), channel_id=1, source_target_pairs={{0,1},{4,5},{8,9},{12,13},{16,17},{20,21},{24,25},{28,29}} | collective-permute-start | bytes 4718600 | tf_op jit(solution)/shard_map/ppermute | solution.py:67
  680.9 61.1 %collective-permute-start.107 = (bf16[3,512,512]{2,1,0:T(8,128)(2,1)S(1)}, bf16[3,512,512]{2,1,0:T(8,128)(2,1)S(1)}, u32[]{:S(2)}, u32[]{:S(2)}) collective-permute-start(bf16[3,512,512]{2,1,0:T(8,128)(2,1)S(1)} %get-tuple-element.421), channel_id=1, source_target_pairs={{3,2},{7,6},{11,10},{15,14},{19,18},{23,22},{27,26},{31,30}} | collective-permute-start | bytes 4718600 | tf_op jit(solution)/shard_map/ppermute | solution.py:67
  681.7 64.8 %collective-permute-start.108 = (bf16[3,512,512]{2,1,0:T(8,128)(2,1)S(1)}, bf16[3,512,512]{2,1,0:T(8,128)(2,1)S(1)}, u32[]{:S(2)}, u32[]{:S(2)}) collective-permute-start(bf16[3,512,512]{2,1,0:T(8,128)(2,1)S(1)} %get-tuple-element.422), channel_id=1, source_target_pairs={{0,1},{4,5},{8,9},{12,13},{16,17},{20,21},{24,25},{28,29}} | collective-permute-start | bytes 4718600 | tf_op jit(solution)/shard_map/ppermute | solution.py:67
  683.1 63.4 %collective-permute-start.109 = (bf16[3,512,512]{2,1,0:T(8,128)(2,1)S(1)}, bf16[3,512,512]{2,1,0:T(8,128)(2,1)}, u32[]{:S(2)}, u32[]{:S(2)}) collective-permute-start(bf16[3,512,512]{2,1,0:T(8,128)(2,1)S(1)} %get-tuple-element.423), channel_id=1, source_target_pairs={{3,2},{7,6},{11,10},{15,14},{19,18},{23,22},{27,26},{31,30}} | collective-permute-start | bytes 4718600 | tf_op jit(solution)/shard_map/ppermute | solution.py:67
  685.1 56.2 %collective-permute-start.110 = (f32[64,1024]{1,0:T(8,128)S(1)}, f32[64,1024]{1,0:T(8,128)S(1)}, u32[]{:S(2)}, u32[]{:S(2)}) collective-permute-start(f32[64,1024]{1,0:T(8,128)S(1)} %copy-done.181), channel_id=1, source_target_pairs={{0,1},{1,0},{2,3},{3,2},{4,5},{5,4},{6,7},{7,6},{8,9},{9,8},{10,11... | collective-permute-start | bytes 786440 | tf_op jit(solution)/shard_map/ppermute | solution.py:67
  750.3 22.3 %collective-permute-start.113 = (bf16[3,512,512]{2,1,0:T(8,128)(2,1)S(1)}, bf16[3,512,512]{2,1,0:T(8,128)(2,1)S(1)}, u32[]{:S(2)}, u32[]{:S(2)}) collective-permute-start(bf16[3,512,512]{2,1,0:T(8,128)(2,1)S(1)} %send_values.11), channel_id=1, source_target_pairs={{0,1},{1,2},{4,5},{5,6},{8,9},{9,10},{12,13},{13,14},{16,17},{17,1... | collective-permute-start | bytes 4718600 | tf_op jit(solution)/shard_map/ppermute | solution.py:67
  789.4 225.3 %reduce-scatter.9.cloned.1.call-start = ((), (), s32[]{:S(2)}) async-start(), calls=%async_computation.6 | async-start | bytes 2359296 | tf_op jit(solution)/shard_map/reduce_scatter | solution.py:1003
  798.9 217.6 %reduce-scatter.11.cloned.1.call-start = ((), (), s32[]{:S(2)}) async-start(), calls=%async_computation.7 | async-start | bytes 9437184 | tf_op jit(solution)/shard_map/reduce_scatter | solution.py:1003
  798.9 25.6 %collective-permute-start.111 = (bf16[3,512,512]{2,1,0:T(8,128)(2,1)}, bf16[3,512,512]{2,1,0:T(8,128)(2,1)S(1)}, u32[]{:S(2)}, u32[]{:S(2)}) collective-permute-start(bf16[3,512,512]{2,1,0:T(8,128)(2,1)} %copy-done.85), channel_id=1, source_target_pairs={{0,1},{1,2},{4,5},{5,6},{8,9},{9,10},{12,13},{13,14},{16,17},{17,1... | collective-permute-start | bytes 4718600 | tf_op jit(solution)/shard_map/ppermute | solution.py:67
  853.1 37.3 %collective-permute-start.115 = (bf16[3,512,512]{2,1,0:T(8,128)(2,1)}, bf16[3,512,512]{2,1,0:T(8,128)(2,1)}, u32[]{:S(2)}, u32[]{:S(2)}) collective-permute-start(bf16[3,512,512]{2,1,0:T(8,128)(2,1)} %get-tuple-element.434), channel_id=1, source_target_pairs={{0,1},{1,2},{2,3},{4,5},{5,6},{6,7},{8,9},{9,10},{10,11},{12,13},{... | collective-permute-start | bytes 4718600 | tf_op jit(solution)/shard_map/ppermute | solution.py:67
  860.7 29.7 %collective-permute-start.116 = (bf16[3,512,512]{2,1,0:T(8,128)(2,1)}, bf16[3,512,512]{2,1,0:T(8,128)(2,1)}, u32[]{:S(2)}, u32[]{:S(2)}) collective-permute-start(bf16[3,512,512]{2,1,0:T(8,128)(2,1)} %get-tuple-element.435), channel_id=1, source_target_pairs={{1,0},{2,1},{3,2},{5,4},{6,5},{7,6},{9,8},{10,9},{11,10},{13,12},{... | collective-permute-start | bytes 4718600 | tf_op jit(solution)/shard_map/ppermute | solution.py:67
  862.0 52.5 %collective-permute-start.121 = (bf16[3,512,512]{2,1,0:T(8,128)(2,1)}, bf16[3,512,512]{2,1,0:T(8,128)(2,1)}, u32[]{:S(2)}, u32[]{:S(2)}) collective-permute-start(bf16[3,512,512]{2,1,0:T(8,128)(2,1)} %get-tuple-element.436), channel_id=1, source_target_pairs={{0,1},{1,2},{2,3},{4,5},{5,6},{6,7},{8,9},{9,10},{10,11},{12,13},{... | collective-permute-start | bytes 4718600 | tf_op jit(solution)/shard_map/ppermute | solution.py:67
  867.8 54.4 %collective-permute-start.122 = (bf16[3,512,512]{2,1,0:T(8,128)(2,1)}, bf16[3,512,512]{2,1,0:T(8,128)(2,1)}, u32[]{:S(2)}, u32[]{:S(2)}) collective-permute-start(bf16[3,512,512]{2,1,0:T(8,128)(2,1)} %get-tuple-element.437), channel_id=1, source_target_pairs={{1,0},{2,1},{3,2},{5,4},{6,5},{7,6},{9,8},{10,9},{11,10},{13,12},{... | collective-permute-start | bytes 4718600 | tf_op jit(solution)/shard_map/ppermute | solution.py:67
  900.7 32.2 %collective-permute-start.123 = (f32[4,512]{1,0:T(4,128)S(1)}, f32[4,512]{1,0:T(4,128)S(1)}, u32[]{:S(2)}, u32[]{:S(2)}) collective-permute-start(f32[4,512]{1,0:T(4,128)S(1)} %broadcast_select_fusion), channel_id=1, source_target_pairs={{0,1},{1,0},{2,3},{3,2},{4,5},{5,4},{6,7},{7,6},{8,9},{9,8},{10,11... | collective-permute-start | bytes 24584 | tf_op jit(solution)/shard_map/ppermute | solution.py:67
  907.3 34.2 %collective-permute-start.119 = (f32[64,1024]{1,0:T(8,128)S(1)}, f32[64,1024]{1,0:T(8,128)S(1)}, u32[]{:S(2)}, u32[]{:S(2)}) collective-permute-start(f32[64,1024]{1,0:T(8,128)S(1)} %copy-done.173), channel_id=1, source_target_pairs={{0,2},{1,3},{2,0},{3,1},{4,6},{5,7},{6,4},{7,5},{8,10},{9,11},{10,... | collective-permute-start | bytes 786440 | tf_op jit(solution)/shard_map/ppermute | solution.py:67
  907.3 25.6 %collective-permute-start.120 = (f32[64,512]{1,0:T(8,128)S(1)}, f32[64,512]{1,0:T(8,128)S(1)}, u32[]{:S(2)}, u32[]{:S(2)}) collective-permute-start(f32[64,512]{1,0:T(8,128)S(1)} %copy-done.182), channel_id=1, source_target_pairs={{0,1},{1,0},{2,3},{3,2},{4,5},{5,4},{6,7},{7,6},{8,9},{9,8},{10,11... | collective-permute-start | bytes 393224 | tf_op jit(solution)/shard_map/ppermute | solution.py:67
  914.5 47.3 %collective-permute-start.117 = (bf16[512,512]{1,0:T(8,128)(2,1)}, bf16[512,512]{1,0:T(8,128)(2,1)S(1)}, u32[]{:S(2)}, u32[]{:S(2)}) collective-permute-start(bf16[512,512]{1,0:T(8,128)(2,1)} %add_convert_fusion.3), channel_id=1, source_target_pairs={{0,1},{1,2},{4,5},{5,6},{8,9},{9,10},{12,13},{13,14},{16,17},{17,1... | collective-permute-start | bytes 1572872 | tf_op jit(solution)/shard_map/ppermute | solution.py:67
  939.5 55.0 %collective-permute-start.99 = (bf16[512,512]{1,0:T(8,128)(2,1)S(1)}, bf16[512,512]{1,0:T(8,128)(2,1)S(1)}, u32[]{:S(2)}, u32[]{:S(2)}) collective-permute-start(bf16[512,512]{1,0:T(8,128)(2,1)S(1)} %copy-done.178), channel_id=1, source_target_pairs={{0,1},{1,2},{2,3},{4,5},{5,6},{6,7},{8,9},{9,10},{10,11},{12,13},{... | collective-permute-start | bytes 1572872 | tf_op jit(solution)/shard_map/ppermute | solution.py:67
  941.5 20.5 %collective-permute-start.118 = (bf16[512,512]{1,0:T(8,128)(2,1)}, bf16[512,512]{1,0:T(8,128)(2,1)S(1)}, u32[]{:S(2)}, u32[]{:S(2)}) collective-permute-start(bf16[512,512]{1,0:T(8,128)(2,1)} %add_convert_fusion.3), channel_id=1, source_target_pairs={{2,1},{3,2},{6,5},{7,6},{10,9},{11,10},{14,13},{15,14},{18,17},{19... | collective-permute-start | bytes 1572872 | tf_op jit(solution)/shard_map/ppermute | solution.py:67
  955.2 39.3 %collective-permute-start.100 = (bf16[512,512]{1,0:T(8,128)(2,1)S(1)}, bf16[512,512]{1,0:T(8,128)(2,1)S(1)}, u32[]{:S(2)}, u32[]{:S(2)}) collective-permute-start(bf16[512,512]{1,0:T(8,128)(2,1)S(1)} %copy-done.179), channel_id=1, source_target_pairs={{1,0},{2,1},{3,2},{5,4},{6,5},{7,6},{9,8},{10,9},{11,10},{13,12},{... | collective-permute-start | bytes 1572872 | tf_op jit(solution)/shard_map/ppermute | solution.py:67
  962.2 39.9 %collective-permute-start.128 = (bf16[512,512]{1,0:T(8,128)(2,1)S(1)}, bf16[512,512]{1,0:T(8,128)(2,1)S(1)}, u32[]{:S(2)}, u32[]{:S(2)}) collective-permute-start(bf16[512,512]{1,0:T(8,128)(2,1)S(1)} %add_convert_fusion.2), channel_id=1, source_target_pairs={{0,1},{1,2},{2,3},{4,5},{5,6},{6,7},{8,9},{9,10},{10,11},{12,13},{... | collective-permute-start | bytes 1572872 | tf_op jit(solution)/shard_map/ppermute | solution.py:67
  966.0 36.1 %collective-permute-start.129 = (bf16[512,512]{1,0:T(8,128)(2,1)S(1)}, bf16[512,512]{1,0:T(8,128)(2,1)S(1)}, u32[]{:S(2)}, u32[]{:S(2)}) collective-permute-start(bf16[512,512]{1,0:T(8,128)(2,1)S(1)} %add_convert_fusion.1), channel_id=1, source_target_pairs={{1,0},{2,1},{3,2},{5,4},{6,5},{7,6},{9,8},{10,9},{11,10},{13,12},{... | collective-permute-start | bytes 1572872 | tf_op jit(solution)/shard_map/ppermute | solution.py:67
  (271 other events, 4622.7 us)
Sparse Core Ops, SparseCore 0:
  548.1 71.9 reduce-scatter.6
  789.5 64.2 reduce-scatter.4
  857.6 41.1 reduce-scatter.8
  902.6 71.3 reduce-scatter.10

commit v5 on v4

--- a/solution.py
+++ b/solution.py
@@ -1253,8 +1253,8 @@
     early_one = Butterfly(jnp.concatenate([chain.now for chain in early_chain], axis=1))
     order.send(*grads, early_one)
     out_part = weight_part(d_branch, heads_out, width, (*grads[0].came, down_sum))
+    up_part = weight_part(normed_mlp, d_hpre, ff, grads[0].came)
     order.send(*grads, early_one)
-    up_part = weight_part(normed_mlp, d_hpre, ff, grads[0].came)
     qkv_part = None
     for s in range(3):
         qkv_part = rows_product(

time: 1040 us -> 1050 us (level)
    unnamed x403 -> x413, local copies, waits for them, and re-layouts: 47 us -> 48.6 us
  transfers between devices with their start and end apart: 137 -> 137, of which waited for: 45 -> 47; matrix products, arithmetic and copies ran while one was open for 16% -> 15% of each run, Pallas kernels for 18% -> 18%
where the time goes in v5:
time: 1050 us; the launch traced here: 1040 us
  waiting for transfers between devices  327 us (31%)
  starting transfers between devices  281 us (27%)
  Pallas kernels  209 us (20%)
  matrix products  103 us (10%)
  local copies, waits for them, and re-layouts  57.3 us (5%)
  other arithmetic  45.2 us (4%)
  between operations  19.2 us (2%)
    ppermute x133, waiting for transfers between devices, send(): got.append(lax.ppermute(held[at], axis, perm))  327 us
    ppermute x133, starting transfers between devices, send(): got.append(lax.ppermute(held[at], axis, perm))  281 us
    dot_general x26, matrix products, dot_tt(): lax.dot_general(former, latter, (dims, ((), ())), precision=precision, pr...  55.4 us
    pallas_call x6, Pallas kernels, rows_product(): pl.pallas_call(functools.partial(rows_product_kernel, n), grid=(height //...  49.2 us
    unnamed x413, local copies, waits for them, and re-layouts  48.6 us
    pallas_call x8, Pallas kernels, send_values(): pl.pallas_call(functools.partial(send_kernel, count, turns, came is not N...  33.9 us
    pallas_call x4, Pallas kernels, mix_streams(): pl.pallas_call(functools.partial(mix_kernel, picked), grid=(rows // TILE,...  24.4 us
    pallas_call x2, Pallas kernels, late_dots(): pl.pallas_call(late_kernel, grid=(rows // TILE,), in_specs=[pl.BlockSpec(...  21.6 us
  transfers between devices with their start and end apart: 137, of which 47 were waited for; matrix products, arithmetic and copies ran while one was open for 15% of the time, Pallas kernels for 18%

profile of v5, /device:TPU:0, one launch (start us, length us, event | category | flops | bytes accessed | tf_op | source)
XLA Modules:
  0.0 1041.9 jit_solution(15982996224994359752)
XLA Ops:
  24.7 7.7 collective-permute-done.1
  34.6 7.2 mix_streams.5
  41.8 7.2 mix_streams.4
  74.1 5.4 collective-permute-start.10
  84.7 4.9 mix_streams.6.base
  89.6 6.2 collective-permute-done.5
  95.8 5.4 collective-permute-done.6
  104.1 8.3 collective-permute-done.11
  114.4 7.2 early_dots.2
  121.6 13.3 %collective-permute-done.9 = bf16[2,512,512]{2,1,0:T(8,128)(2,1)} collective-permute-done((bf16[2,512,512]{2,1,0:T(8,128)(2,1)}, bf16[2,512,512]{2,1,0:T(8,128)(2,1)}, u32[]{:S(2)}, u32[]{:S(2)}) %collective-permute-start.9) | collective-permute-done | bytes 1048608 | tf_op jit(solution)/shard_map/ppermute | solution.py:67
  134.9 7.3 collective-permute-done.15
  147.8 5.0 mix_streams.7.base
  152.8 7.3 collective-permute-start.20
  167.7 15.2 %collective-permute-done.13 = bf16[2,512,512]{2,1,0:T(8,128)(2,1)} collective-permute-done((bf16[2,512,512]{2,1,0:T(8,128)(2,1)}, bf16[2,512,512]{2,1,0:T(8,128)(2,1)}, u32[]{:S(2)}, u32[]{:S(2)}) %collective-permute-start.13) | collective-permute-done | bytes 1048608 | tf_op jit(solution)/shard_map/ppermute | solution.py:67
  202.2 6.8 collective-permute-done.18
  212.1 5.8 collective-permute-start.22
  226.6 7.2 early_dots.3
  236.6 6.3 collective-permute-start.26
  251.7 10.1 collective-permute-done.27.down
  262.5 12.2 %collective-permute-start.36 = (bf16[512,512]{1,0:T(8,128)(2,1)}, bf16[512,512]{1,0:T(8,128)(2,1)}, u32[]{:S(2)}, u32[]{:S(2)}) collective-permute-start(bf16[512,512]{1,0:T(8,128)(2,1)} %get-tuple-element.252), channel_id=1, source_target_pairs={{0,1},{1,2},{2,3},{4,5},{5,6},{6,7},{8,9},{9,10},{10,11},{12,13},{... | collective-permute-start | bytes 1572872 | tf_op jit(solution)/shard_map/ppermute | solution.py:67
  280.9 9.8 collective-permute-done.37
  297.5 22.5 %collective-permute-done.40 = f32[8,512]{1,0:T(8,128)S(1)} collective-permute-done((f32[8,512]{1,0:T(8,128)S(1)}, f32[8,512]{1,0:T(8,128)S(1)}, u32[]{:S(2)}, u32[]{:S(2)}) %collective-permute-start.40) | collective-permute-done | bytes 16416 | tf_op jit(solution)/shard_map/ppermute | solution.py:67
  331.5 6.1 collective-permute-done.31
  344.4 5.3 attend_forward.3
  362.3 6.0 fusion.119
  376.4 9.6 collective-permute-done.48
  386.4 7.8 collective-permute-done.50.refs_5_
  394.3 7.7 collective-permute-start.56
  411.8 6.5 collective-permute-done.57.down
  433.3 9.5 multiply_convert_fusion.3
  473.1 9.4 fusion.120
  482.8 7.2 collective-permute-start.74
  493.2 9.5 multiply_convert_fusion.1
  510.3 5.2 collective-permute-start.76
  529.6 7.8 collective-permute-start.80
  537.5 13.3 %rows_product.6 = bf16[2048,2048]{1,0:T(8,128)(2,1)} custom-call(bf16[512,2048]{1,0:T(8,128)(2,1)S(1)} %pad_maximum_fusion.4.refs_0_, bf16[512,2048]{1,0:T(8,128)(2,1)S(1)} %pad_maximum_fusion.5.refs_1_, bf16[512,2048]{1,0:T(8,128)(2,1)} %get-tuple-element.400.refs_2_, bf16[512,2048]{1,0:T(8,128)(2,1)} %get-tuple-element.405.refs_3_, ...), custom_call_target="tpu_custom_call" | custom-call | tf_op jit(solution)/shard_map/rows_product/pallas_call | solution.py:951
  560.5 9.7 collective-permute-done.83.refs_5_
  570.1 5.1 collective-permute-start.85
  586.1 5.4 collective-permute-done.86.down
  612.1 6.2 collective-permute-start.96
  627.0 5.0 attend_backward.2
  663.8 8.8 attend_backward.3
  672.6 5.1 send_values.8
  690.7 55.6 %collective-permute-done.110 = f32[64,1024]{1,0:T(8,128)S(1)} collective-permute-done((f32[64,1024]{1,0:T(8,128)S(1)}, f32[64,1024]{1,0:T(8,128)S(1)}, u32[]{:S(2)}, u32[]{:S(2)}) %collective-permute-start.110) | collective-permute-done | bytes 262176 | tf_op jit(solution)/shard_map/ppermute | solution.py:67
  765.4 13.7 %collective-permute-done.113.refs_5_.refs_4_ = bf16[3,512,512]{2,1,0:T(8,128)(2,1)S(1)} collective-permute-done((bf16[3,512,512]{2,1,0:T(8,128)(2,1)S(1)}, bf16[3,512,512]{2,1,0:T(8,128)(2,1)S(1)}, u32[]{:S(2)}, u32[]{:S(2)}) %collective-permute-start.113) | collective-permute-done | bytes 1572896 | tf_op jit(solution)/shard_map/ppermute | solution.py:67
  779.2 6.3 rows_product.7.refs_6_
  785.5 5.3 rows_product.8.refs_6_
  790.8 5.2 rows_product.9
  801.2 5.1 rows_product.10
  808.3 14.0 %rows_product.11 = bf16[2048,2048]{1,0:T(8,128)(2,1)} custom-call(bf16[512,2048]{1,0:T(8,128)(2,1)S(1)} %copy-done.55, bf16[512,2048]{1,0:T(8,128)(2,1)} %copy-done.56, bf16[512,2048]{1,0:T(8,128)(2,1)} %copy-done.139, bf16[512,2048]{1,0:T(8,128)(2,1)} %copy-done.142, bf16[3,512,512]{2,1,0:T(8,128)(2,1)S(1)} %copy-done.18, bf16[3,512,512]{2,1,0:T(8,128)(2,1)S(1)} %copy-done.20), custom_call_target="tpu_custom_call" | custom-call | tf_op jit(solution)/shard_map/rows_product/pallas_call | solution.py:951
  822.3 7.3 collective-permute-start.111
  830.4 5.8 send_values.13
  836.2 28.5 %collective-permute-done.111.refs_5_ = bf16[3,512,512]{2,1,0:T(8,128)(2,1)S(1)} collective-permute-done((bf16[3,512,512]{2,1,0:T(8,128)(2,1)}, bf16[3,512,512]{2,1,0:T(8,128)(2,1)S(1)}, u32[]{:S(2)}, u32[]{:S(2)}) %collective-permute-start.111) | collective-permute-done | bytes 1572896 | tf_op jit(solution)/shard_map/ppermute | solution.py:67
  867.0 5.7 send_values.12
  872.6 6.5 collective-permute-start.115
  880.5 5.7 collective-permute-start.121
  910.2 11.3 %late_dots.2 = (f32[512,512]{1,0:T(8,128)}, f32[512,512]{1,0:T(8,128)}, f32[512,512]{1,0:T(8,128)}, f32[64,512]{1,0:T(8,128)}, f32[3,8,512]{2,1,0:T(8,128)}) custom-call(bf16[11,1024,512]{2,1,0:T(8,128)(2,1)} %hist_ref.15, f32[512,512]{1,0:T(8,128)} %get-tuple-element.272.x0, f32[512,512]{1,0:T(8,128)} %get-tuple-element.247.x1, ...), custom_call_target="tpu_custom_call" | custom-call | tf_op jit(solution)/shard_map/late_dots/pallas_call | solution.py:485
  930.5 7.8 collective-permute-start.117
  938.3 10.3 late_dots.3
  961.2 7.0 collective-permute-done.127
  983.5 8.7 layer_grads.2
  992.3 5.8 copy.48.refs_0_
  999.6 9.4 layer_grads.3
  1011.0 5.5 collective-permute-done.131
  (803 shorter events, 447.9 us)
Async XLA Ops:
  7.2 788.9 %reduce-scatter.7.cloned.1.call-start = ((), (), s32[]{:S(2)}) async-start(), calls=%async_computation.5 | async-start | bytes 9437184 | tf_op jit(solution)/shard_map/reduce_scatter | solution.py:1229
  69.0 26.8 %collective-permute-start.5 = (bf16[2,512,512]{2,1,0:T(8,128)(2,1)}, bf16[2,512,512]{2,1,0:T(8,128)(2,1)}, u32[]{:S(2)}, u32[]{:S(2)}) collective-permute-start(bf16[2,512,512]{2,1,0:T(8,128)(2,1)} %get-tuple-element.259), channel_id=1, source_target_pairs={{0,1},{1,2},{2,3},{4,5},{5,6},{6,7},{8,9},{9,10},{10,11},{12,13},{... | collective-permute-start | bytes 3145736 | tf_op jit(solution)/shard_map/ppermute | solution.py:67
  72.9 28.3 %collective-permute-start.6 = (bf16[2,512,512]{2,1,0:T(8,128)(2,1)}, bf16[2,512,512]{2,1,0:T(8,128)(2,1)}, u32[]{:S(2)}, u32[]{:S(2)}) collective-permute-start(bf16[2,512,512]{2,1,0:T(8,128)(2,1)} %get-tuple-element.259), channel_id=1, source_target_pairs={{1,0},{2,1},{3,2},{5,4},{6,5},{7,6},{9,8},{10,9},{11,10},{13,12},{... | collective-permute-start | bytes 3145736 | tf_op jit(solution)/shard_map/ppermute | solution.py:67
  74.1 29.9 %collective-permute-start.10 = (bf16[512,512]{1,0:T(8,128)(2,1)S(1)}, bf16[512,512]{1,0:T(8,128)(2,1)}, u32[]{:S(2)}, u32[]{:S(2)}) collective-permute-start(bf16[512,512]{1,0:T(8,128)(2,1)S(1)} %get-tuple-element.262), channel_id=1, source_target_pairs={{0,1},{1,2},{2,3},{4,5},{5,6},{6,7},{8,9},{9,10},{10,11},{12,13},{... | collective-permute-start | bytes 1572872 | tf_op jit(solution)/shard_map/ppermute | solution.py:67
  79.5 32.9 %collective-permute-start.11 = (bf16[512,512]{1,0:T(8,128)(2,1)S(1)}, bf16[512,512]{1,0:T(8,128)(2,1)}, u32[]{:S(2)}, u32[]{:S(2)}) collective-permute-start(bf16[512,512]{1,0:T(8,128)(2,1)S(1)} %get-tuple-element.262), channel_id=1, source_target_pairs={{1,0},{2,1},{3,2},{5,4},{6,5},{7,6},{9,8},{10,9},{11,10},{13,12},{... | collective-permute-start | bytes 1572872 | tf_op jit(solution)/shard_map/ppermute | solution.py:67
  101.2 20.4 %collective-permute-start.8 = (bf16[2,512,512]{2,1,0:T(8,128)(2,1)}, bf16[2,512,512]{2,1,0:T(8,128)(2,1)}, u32[]{:S(2)}, u32[]{:S(2)}) collective-permute-start(bf16[2,512,512]{2,1,0:T(8,128)(2,1)} %collective-permute-done.5), channel_id=1, source_target_pairs={{1,2},{2,3},{5,6},{6,7},{9,10},{10,11},{13,14},{14,15},{17,18},{18... | collective-permute-start | bytes 3145736 | tf_op jit(solution)/shard_map/ppermute | solution.py:67
  102.8 32.1 %collective-permute-start.9 = (bf16[2,512,512]{2,1,0:T(8,128)(2,1)}, bf16[2,512,512]{2,1,0:T(8,128)(2,1)}, u32[]{:S(2)}, u32[]{:S(2)}) collective-permute-start(bf16[2,512,512]{2,1,0:T(8,128)(2,1)} %collective-permute-done.6), channel_id=1, source_target_pairs={{1,0},{2,1},{5,4},{6,5},{9,8},{10,9},{13,12},{14,13},{17,16},{18,1... | collective-permute-start | bytes 3145736 | tf_op jit(solution)/shard_map/ppermute | solution.py:67
  112.4 22.5 %collective-permute-start.14 = (bf16[512,512]{1,0:T(8,128)(2,1)}, bf16[512,512]{1,0:T(8,128)(2,1)S(1)}, u32[]{:S(2)}, u32[]{:S(2)}) collective-permute-start(bf16[512,512]{1,0:T(8,128)(2,1)} %collective-permute-done.10), channel_id=1, source_target_pairs={{1,2},{2,3},{5,6},{6,7},{9,10},{10,11},{13,14},{14,15},{17,18},{18... | collective-permute-start | bytes 1572872 | tf_op jit(solution)/shard_map/ppermute | solution.py:67
  113.1 29.0 %collective-permute-start.15 = (bf16[512,512]{1,0:T(8,128)(2,1)}, bf16[512,512]{1,0:T(8,128)(2,1)S(1)}, u32[]{:S(2)}, u32[]{:S(2)}) collective-permute-start(bf16[512,512]{1,0:T(8,128)(2,1)} %collective-permute-done.11), channel_id=1, source_target_pairs={{1,0},{2,1},{5,4},{6,5},{9,8},{10,9},{13,12},{14,13},{17,16},{18,1... | collective-permute-start | bytes 1572872 | tf_op jit(solution)/shard_map/ppermute | solution.py:67
  144.9 22.9 %collective-permute-start.12 = (bf16[2,512,512]{2,1,0:T(8,128)(2,1)}, bf16[2,512,512]{2,1,0:T(8,128)(2,1)}, u32[]{:S(2)}, u32[]{:S(2)}) collective-permute-start(bf16[2,512,512]{2,1,0:T(8,128)(2,1)} %collective-permute-done.8), channel_id=1, source_target_pairs={{2,3},{6,7},{10,11},{14,15},{18,19},{22,23},{26,27},{30,31}} | collective-permute-start | bytes 3145736 | tf_op jit(solution)/shard_map/ppermute | solution.py:67
  146.5 36.4 %collective-permute-start.13 = (bf16[2,512,512]{2,1,0:T(8,128)(2,1)}, bf16[2,512,512]{2,1,0:T(8,128)(2,1)}, u32[]{:S(2)}, u32[]{:S(2)}) collective-permute-start(bf16[2,512,512]{2,1,0:T(8,128)(2,1)} %collective-permute-done.9), channel_id=1, source_target_pairs={{1,0},{5,4},{9,8},{13,12},{17,16},{21,20},{25,24},{29,28}} | collective-permute-start | bytes 3145736 | tf_op jit(solution)/shard_map/ppermute | solution.py:67
  152.8 59.2 %collective-permute-start.20 = (bf16[2,512,512]{2,1,0:T(8,128)(2,1)}, bf16[2,512,512]{2,1,0:T(8,128)(2,1)}, u32[]{:S(2)}, u32[]{:S(2)}) collective-permute-start(bf16[2,512,512]{2,1,0:T(8,128)(2,1)} %get-tuple-element.282), channel_id=1, source_target_pairs={{0,1},{1,2},{2,3},{4,5},{5,6},{6,7},{8,9},{9,10},{10,11},{12,13},{... | collective-permute-start | bytes 3145736 | tf_op jit(solution)/shard_map/ppermute | solution.py:67
  160.2 51.9 %collective-permute-start.21 = (bf16[2,512,512]{2,1,0:T(8,128)(2,1)}, bf16[2,512,512]{2,1,0:T(8,128)(2,1)}, u32[]{:S(2)}, u32[]{:S(2)}) collective-permute-start(bf16[2,512,512]{2,1,0:T(8,128)(2,1)} %get-tuple-element.282), channel_id=1, source_target_pairs={{1,0},{2,1},{3,2},{5,4},{6,5},{7,6},{9,8},{10,9},{11,10},{13,12},{... | collective-permute-start | bytes 3145736 | tf_op jit(solution)/shard_map/ppermute | solution.py:67
  200.1 20.9 %collective-permute-start.24 = (bf16[512,512]{1,0:T(8,128)(2,1)}, bf16[512,512]{1,0:T(8,128)(2,1)}, u32[]{:S(2)}, u32[]{:S(2)}) collective-permute-start(bf16[512,512]{1,0:T(8,128)(2,1)} %copy-done.102), channel_id=1, source_target_pairs={{0,1},{1,2},{2,3},{4,5},{5,6},{6,7},{8,9},{9,10},{10,11},{12,13},{... | collective-permute-start | bytes 1572872 | tf_op jit(solution)/shard_map/ppermute | solution.py:67
  212.1 21.7 %collective-permute-start.22 = (bf16[512,512]{1,0:T(8,128)(2,1)S(1)}, bf16[512,512]{1,0:T(8,128)(2,1)}, u32[]{:S(2)}, u32[]{:S(2)}) collective-permute-start(bf16[512,512]{1,0:T(8,128)(2,1)S(1)} %add_convert_fusion.19), channel_id=1, source_target_pairs={{0,1},{1,2},{4,5},{5,6},{8,9},{9,10},{12,13},{13,14},{16,17},{17,1... | collective-permute-start | bytes 1572872 | tf_op jit(solution)/shard_map/ppermute | solution.py:67
  219.3 55.4 %collective-permute-start.28 = (bf16[2,512,512]{2,1,0:T(8,128)(2,1)}, bf16[2,512,512]{2,1,0:T(8,128)(2,1)}, u32[]{:S(2)}, u32[]{:S(2)}) collective-permute-start(bf16[2,512,512]{2,1,0:T(8,128)(2,1)} %collective-permute-done.20), channel_id=1, source_target_pairs={{1,2},{2,3},{5,6},{6,7},{9,10},{10,11},{13,14},{14,15},{17,18},{18... | collective-permute-start | bytes 3145736 | tf_op jit(solution)/shard_map/ppermute | solution.py:67
  221.1 57.8 %collective-permute-start.29 = (bf16[2,512,512]{2,1,0:T(8,128)(2,1)}, bf16[2,512,512]{2,1,0:T(8,128)(2,1)}, u32[]{:S(2)}, u32[]{:S(2)}) collective-permute-start(bf16[2,512,512]{2,1,0:T(8,128)(2,1)} %collective-permute-done.21), channel_id=1, source_target_pairs={{1,0},{2,1},{5,4},{6,5},{9,8},{10,9},{13,12},{14,13},{17,16},{18,1... | collective-permute-start | bytes 3145736 | tf_op jit(solution)/shard_map/ppermute | solution.py:67
  244.3 34.6 %collective-permute-start.32 = (bf16[512,512]{1,0:T(8,128)(2,1)}, bf16[512,512]{1,0:T(8,128)(2,1)}, u32[]{:S(2)}, u32[]{:S(2)}) collective-permute-start(bf16[512,512]{1,0:T(8,128)(2,1)} %collective-permute-done.24), channel_id=1, source_target_pairs={{1,2},{2,3},{5,6},{6,7},{9,10},{10,11},{13,14},{14,15},{17,18},{18... | collective-permute-start | bytes 1572872 | tf_op jit(solution)/shard_map/ppermute | solution.py:67
  250.4 28.4 %collective-permute-start.33 = (bf16[512,512]{1,0:T(8,128)(2,1)}, bf16[512,512]{1,0:T(8,128)(2,1)}, u32[]{:S(2)}, u32[]{:S(2)}) collective-permute-start(bf16[512,512]{1,0:T(8,128)(2,1)} %collective-permute-done.25), channel_id=1, source_target_pairs={{1,0},{2,1},{5,4},{6,5},{9,8},{10,9},{13,12},{14,13},{17,16},{18,1... | collective-permute-start | bytes 1572872 | tf_op jit(solution)/shard_map/ppermute | solution.py:67
  290.8 30.0 %collective-permute-start.38 = (bf16[512,512]{1,0:T(8,128)(2,1)}, bf16[512,512]{1,0:T(8,128)(2,1)S(1)}, u32[]{:S(2)}, u32[]{:S(2)}) collective-permute-start(bf16[512,512]{1,0:T(8,128)(2,1)} %collective-permute-done.36), channel_id=1, source_target_pairs={{1,2},{2,3},{5,6},{6,7},{9,10},{10,11},{13,14},{14,15},{17,18},{18... | collective-permute-start | bytes 1572872 | tf_op jit(solution)/shard_map/ppermute | solution.py:67
  291.4 30.6 %collective-permute-start.39 = (bf16[512,512]{1,0:T(8,128)(2,1)}, bf16[512,512]{1,0:T(8,128)(2,1)S(1)}, u32[]{:S(2)}, u32[]{:S(2)}) collective-permute-start(bf16[512,512]{1,0:T(8,128)(2,1)} %collective-permute-done.37), channel_id=1, source_target_pairs={{1,0},{2,1},{5,4},{6,5},{9,8},{10,9},{13,12},{14,13},{17,16},{18,1... | collective-permute-start | bytes 1572872 | tf_op jit(solution)/shard_map/ppermute | solution.py:67
  292.7 30.8 %collective-permute-start.34 = (bf16[512,512]{1,0:T(8,128)(2,1)}, bf16[512,512]{1,0:T(8,128)(2,1)S(1)}, u32[]{:S(2)}, u32[]{:S(2)}) collective-permute-start(bf16[512,512]{1,0:T(8,128)(2,1)} %collective-permute-done.32), channel_id=1, source_target_pairs={{2,3},{6,7},{10,11},{14,15},{18,19},{22,23},{26,27},{30,31}} | collective-permute-start | bytes 1572872 | tf_op jit(solution)/shard_map/ppermute | solution.py:67
  293.5 31.9 %collective-permute-start.35 = (bf16[512,512]{1,0:T(8,128)(2,1)}, bf16[512,512]{1,0:T(8,128)(2,1)S(1)}, u32[]{:S(2)}, u32[]{:S(2)}) collective-permute-start(bf16[512,512]{1,0:T(8,128)(2,1)} %collective-permute-done.33), channel_id=1, source_target_pairs={{1,0},{5,4},{9,8},{13,12},{17,16},{21,20},{25,24},{29,28}} | collective-permute-start | bytes 1572872 | tf_op jit(solution)/shard_map/ppermute | solution.py:67
  294.8 25.2 %collective-permute-start.40 = (f32[8,512]{1,0:T(8,128)S(1)}, f32[8,512]{1,0:T(8,128)S(1)}, u32[]{:S(2)}, u32[]{:S(2)}) collective-permute-start(f32[8,512]{1,0:T(8,128)S(1)} %get-tuple-element.309), channel_id=1, source_target_pairs={{0,1},{1,0},{2,3},{3,2},{4,5},{5,4},{6,7},{7,6},{8,9},{9,8},{10,11... | collective-permute-start | bytes 49160 | tf_op jit(solution)/shard_map/ppermute | solution.py:67
  322.1 31.4 %collective-permute-start.45 = (bf16[512,512]{1,0:T(8,128)(2,1)S(1)}, bf16[512,512]{1,0:T(8,128)(2,1)}, u32[]{:S(2)}, u32[]{:S(2)}) collective-permute-start(bf16[512,512]{1,0:T(8,128)(2,1)S(1)} %collective-permute-done.38), channel_id=1, source_target_pairs={{2,3},{6,7},{10,11},{14,15},{18,19},{22,23},{26,27},{30,31}} | collective-permute-start | bytes 1572872 | tf_op jit(solution)/shard_map/ppermute | solution.py:67
  323.5 30.0 %collective-permute-start.46 = (bf16[512,512]{1,0:T(8,128)(2,1)S(1)}, bf16[512,512]{1,0:T(8,128)(2,1)}, u32[]{:S(2)}, u32[]{:S(2)}) collective-permute-start(bf16[512,512]{1,0:T(8,128)(2,1)S(1)} %collective-permute-done.39), channel_id=1, source_target_pairs={{1,0},{5,4},{9,8},{13,12},{17,16},{21,20},{25,24},{29,28}} | collective-permute-start | bytes 1572872 | tf_op jit(solution)/shard_map/ppermute | solution.py:67
  419.6 25.9 %collective-permute-start.62 = (f32[8,512]{1,0:T(8,128)S(1)}, f32[8,512]{1,0:T(8,128)S(1)}, u32[]{:S(2)}, u32[]{:S(2)}) collective-permute-start(f32[8,512]{1,0:T(8,128)S(1)} %get-tuple-element.335), channel_id=1, source_target_pairs={{0,1},{1,0},{2,3},{3,2},{4,5},{5,4},{6,7},{7,6},{8,9},{9,8},{10,11... | collective-permute-start | bytes 49160 | tf_op jit(solution)/shard_map/ppermute | solution.py:67
  421.6 24.0 %collective-permute-start.60 = (bf16[512,512]{1,0:T(8,128)(2,1)S(1)}, bf16[512,512]{1,0:T(8,128)(2,1)S(1)}, u32[]{:S(2)}, u32[]{:S(2)}) collective-permute-start(bf16[512,512]{1,0:T(8,128)(2,1)S(1)} %get-tuple-element.334.refs_0_), channel_id=1, source_target_pairs={{0,1},{1,2},{2,3},{4,5},{5,6},{6,7},{8,9},{9,10},{10,11},{12,13},{... | collective-permute-start | bytes 1572872 | tf_op jit(solution)/shard_map/ppermute | solution.py:67
  424.0 21.6 %collective-permute-start.61 = (bf16[512,512]{1,0:T(8,128)(2,1)S(1)}, bf16[512,512]{1,0:T(8,128)(2,1)S(1)}, u32[]{:S(2)}, u32[]{:S(2)}) collective-permute-start(bf16[512,512]{1,0:T(8,128)(2,1)S(1)} %get-tuple-element.334.refs_0_), channel_id=1, source_target_pairs={{1,0},{2,1},{3,2},{5,4},{6,5},{7,6},{9,8},{10,9},{11,10},{13,12},{... | collective-permute-start | bytes 1572872 | tf_op jit(solution)/shard_map/ppermute | solution.py:67
  425.3 25.8 %collective-permute-start.58 = (bf16[512,512]{1,0:T(8,128)(2,1)S(1)}, bf16[512,512]{1,0:T(8,128)(2,1)S(1)}, u32[]{:S(2)}, u32[]{:S(2)}) collective-permute-start(bf16[512,512]{1,0:T(8,128)(2,1)S(1)} %collective-permute-done.54), channel_id=1, source_target_pairs={{1,2},{2,3},{5,6},{6,7},{9,10},{10,11},{13,14},{14,15},{17,18},{18... | collective-permute-start | bytes 1572872 | tf_op jit(solution)/shard_map/ppermute | solution.py:67
  430.2 22.8 %collective-permute-start.59 = (bf16[512,512]{1,0:T(8,128)(2,1)S(1)}, bf16[512,512]{1,0:T(8,128)(2,1)S(1)}, u32[]{:S(2)}, u32[]{:S(2)}) collective-permute-start(bf16[512,512]{1,0:T(8,128)(2,1)S(1)} %collective-permute-done.55), channel_id=1, source_target_pairs={{1,0},{2,1},{5,4},{6,5},{9,8},{10,9},{13,12},{14,13},{17,16},{18,1... | collective-permute-start | bytes 1572872 | tf_op jit(solution)/shard_map/ppermute | solution.py:67
  464.7 26.8 %collective-permute-start.69 = (bf16[512,512]{1,0:T(8,128)(2,1)S(1)}, bf16[512,512]{1,0:T(8,128)(2,1)S(1)}, u32[]{:S(2)}, u32[]{:S(2)}) collective-permute-start(bf16[512,512]{1,0:T(8,128)(2,1)S(1)} %collective-permute-done.65.refs_2_), channel_id=1, source_target_pairs={{2,3},{6,7},{10,11},{14,15},{18,19},{22,23},{26,27},{30,31}} | collective-permute-start | bytes 1572872 | tf_op jit(solution)/shard_map/ppermute | solution.py:67
  465.4 26.2 %collective-permute-start.70 = (bf16[512,512]{1,0:T(8,128)(2,1)S(1)}, bf16[512,512]{1,0:T(8,128)(2,1)S(1)}, u32[]{:S(2)}, u32[]{:S(2)}) collective-permute-start(bf16[512,512]{1,0:T(8,128)(2,1)S(1)} %collective-permute-done.66.refs_5_), channel_id=1, source_target_pairs={{1,0},{5,4},{9,8},{13,12},{17,16},{21,20},{25,24},{29,28}} | collective-permute-start | bytes 1572872 | tf_op jit(solution)/shard_map/ppermute | solution.py:67
  482.8 25.9 %collective-permute-start.74 = (bf16[512,512]{1,0:T(8,128)(2,1)S(1)}, bf16[512,512]{1,0:T(8,128)(2,1)S(1)}, u32[]{:S(2)}, u32[]{:S(2)}) collective-permute-start(bf16[512,512]{1,0:T(8,128)(2,1)S(1)} %add_convert_fusion.12), channel_id=1, source_target_pairs={{0,1},{1,2},{2,3},{4,5},{5,6},{6,7},{8,9},{9,10},{10,11},{12,13},{... | collective-permute-start | bytes 1572872 | tf_op jit(solution)/shard_map/ppermute | solution.py:67
  529.6 21.1 %collective-permute-start.80 = (bf16[512,512]{1,0:T(8,128)(2,1)}, bf16[512,512]{1,0:T(8,128)(2,1)}, u32[]{:S(2)}, u32[]{:S(2)}) collective-permute-start(bf16[512,512]{1,0:T(8,128)(2,1)} %add_convert_fusion.10), channel_id=1, source_target_pairs={{0,1},{1,2},{4,5},{5,6},{8,9},{9,10},{12,13},{13,14},{16,17},{17,1... | collective-permute-start | bytes 1572872 | tf_op jit(solution)/shard_map/ppermute | solution.py:67
  550.8 477.3 %reduce-scatter.5.cloned.1.call-start = ((), (), s32[]{:S(2)}) async-start(), calls=%async_computation.4 | async-start | bytes 7077888 | tf_op jit(solution)/shard_map/reduce_scatter | solution.py:1268
  610.1 22.0 %collective-permute-start.91 = (bf16[512,512]{1,0:T(8,128)(2,1)S(1)}, bf16[512,512]{1,0:T(8,128)(2,1)S(1)}, u32[]{:S(2)}, u32[]{:S(2)}) collective-permute-start(bf16[512,512]{1,0:T(8,128)(2,1)S(1)} %collective-permute-done.87.refs_1_), channel_id=1, source_target_pairs={{1,2},{2,3},{5,6},{6,7},{9,10},{10,11},{13,14},{14,15},{17,18},{18... | collective-permute-start | bytes 1572872 | tf_op jit(solution)/shard_map/ppermute | solution.py:67
  610.8 21.3 %collective-permute-start.92 = (bf16[512,512]{1,0:T(8,128)(2,1)S(1)}, bf16[512,512]{1,0:T(8,128)(2,1)S(1)}, u32[]{:S(2)}, u32[]{:S(2)}) collective-permute-start(bf16[512,512]{1,0:T(8,128)(2,1)S(1)} %collective-permute-done.88.refs_4_), channel_id=1, source_target_pairs={{1,0},{2,1},{5,4},{6,5},{9,8},{10,9},{13,12},{14,13},{17,16},{18,1... | collective-permute-start | bytes 1572872 | tf_op jit(solution)/shard_map/ppermute | solution.py:67
  635.5 24.1 %collective-permute-start.105 = (f32[8,512]{1,0:T(8,128)S(1)}, f32[8,512]{1,0:T(8,128)S(1)}, u32[]{:S(2)}, u32[]{:S(2)}) collective-permute-start(f32[8,512]{1,0:T(8,128)S(1)} %add.356), channel_id=1, source_target_pairs={{0,2},{1,3},{2,0},{3,1},{4,6},{5,7},{6,4},{7,5},{8,10},{9,11},{10,... | collective-permute-start | bytes 49160 | tf_op jit(solution)/shard_map/ppermute | solution.py:67
  653.6 28.6 %collective-permute-start.101 = (bf16[512,512]{1,0:T(8,128)(2,1)S(1)}, bf16[512,512]{1,0:T(8,128)(2,1)S(1)}, u32[]{:S(2)}, u32[]{:S(2)}) collective-permute-start(bf16[512,512]{1,0:T(8,128)(2,1)S(1)} %get-tuple-element.403), channel_id=1, source_target_pairs={{0,1},{4,5},{8,9},{12,13},{16,17},{20,21},{24,25},{28,29}} | collective-permute-start | bytes 1572872 | tf_op jit(solution)/shard_map/ppermute | solution.py:67
  658.2 24.0 %collective-permute-start.102 = (bf16[512,512]{1,0:T(8,128)(2,1)S(1)}, bf16[512,512]{1,0:T(8,128)(2,1)S(1)}, u32[]{:S(2)}, u32[]{:S(2)}) collective-permute-start(bf16[512,512]{1,0:T(8,128)(2,1)S(1)} %get-tuple-element.404), channel_id=1, source_target_pairs={{3,2},{7,6},{11,10},{15,14},{19,18},{23,22},{27,26},{31,30}} | collective-permute-start | bytes 1572872 | tf_op jit(solution)/shard_map/ppermute | solution.py:67
  686.1 61.0 %collective-permute-start.106 = (bf16[3,512,512]{2,1,0:T(8,128)(2,1)S(1)}, bf16[3,512,512]{2,1,0:T(8,128)(2,1)S(1)}, u32[]{:S(2)}, u32[]{:S(2)}) collective-permute-start(bf16[3,512,512]{2,1,0:T(8,128)(2,1)S(1)} %get-tuple-element.420), channel_id=1, source_target_pairs={{0,1},{4,5},{8,9},{12,13},{16,17},{20,21},{24,25},{28,29}} | collective-permute-start | bytes 4718600 | tf_op jit(solution)/shard_map/ppermute | solution.py:67
  687.5 59.6 %collective-permute-start.107 = (bf16[3,512,512]{2,1,0:T(8,128)(2,1)S(1)}, bf16[3,512,512]{2,1,0:T(8,128)(2,1)S(1)}, u32[]{:S(2)}, u32[]{:S(2)}) collective-permute-start(bf16[3,512,512]{2,1,0:T(8,128)(2,1)S(1)} %get-tuple-element.421), channel_id=1, source_target_pairs={{3,2},{7,6},{11,10},{15,14},{19,18},{23,22},{27,26},{31,30}} | collective-permute-start | bytes 4718600 | tf_op jit(solution)/shard_map/ppermute | solution.py:67
  688.2 63.3 %collective-permute-start.108 = (bf16[3,512,512]{2,1,0:T(8,128)(2,1)S(1)}, bf16[3,512,512]{2,1,0:T(8,128)(2,1)S(1)}, u32[]{:S(2)}, u32[]{:S(2)}) collective-permute-start(bf16[3,512,512]{2,1,0:T(8,128)(2,1)S(1)} %get-tuple-element.422), channel_id=1, source_target_pairs={{0,1},{4,5},{8,9},{12,13},{16,17},{20,21},{24,25},{28,29}} | collective-permute-start | bytes 4718600 | tf_op jit(solution)/shard_map/ppermute | solution.py:67
  689.6 61.9 %collective-permute-start.109 = (bf16[3,512,512]{2,1,0:T(8,128)(2,1)S(1)}, bf16[3,512,512]{2,1,0:T(8,128)(2,1)S(1)}, u32[]{:S(2)}, u32[]{:S(2)}) collective-permute-start(bf16[3,512,512]{2,1,0:T(8,128)(2,1)S(1)} %get-tuple-element.423), channel_id=1, source_target_pairs={{3,2},{7,6},{11,10},{15,14},{19,18},{23,22},{27,26},{31,30}} | collective-permute-start | bytes 4718600 | tf_op jit(solution)/shard_map/ppermute | solution.py:67
  690.6 55.7 %collective-permute-start.110 = (f32[64,1024]{1,0:T(8,128)S(1)}, f32[64,1024]{1,0:T(8,128)S(1)}, u32[]{:S(2)}, u32[]{:S(2)}) collective-permute-start(f32[64,1024]{1,0:T(8,128)S(1)} %copy-done.183), channel_id=1, source_target_pairs={{0,1},{1,0},{2,3},{3,2},{4,5},{5,4},{6,7},{7,6},{8,9},{9,8},{10,11... | collective-permute-start | bytes 786440 | tf_op jit(solution)/shard_map/ppermute | solution.py:67
  756.9 22.3 %collective-permute-start.113 = (bf16[3,512,512]{2,1,0:T(8,128)(2,1)S(1)}, bf16[3,512,512]{2,1,0:T(8,128)(2,1)S(1)}, u32[]{:S(2)}, u32[]{:S(2)}) collective-permute-start(bf16[3,512,512]{2,1,0:T(8,128)(2,1)S(1)} %send_values.11), channel_id=1, source_target_pairs={{0,1},{1,2},{4,5},{5,6},{8,9},{9,10},{12,13},{13,14},{16,17},{17,1... | collective-permute-start | bytes 4718600 | tf_op jit(solution)/shard_map/ppermute | solution.py:67
  796.1 234.5 %reduce-scatter.9.cloned.1.call-start = ((), (), s32[]{:S(2)}) async-start(), calls=%async_computation.6 | async-start | bytes 2359296 | tf_op jit(solution)/shard_map/reduce_scatter | solution.py:1003
  806.3 226.0 %reduce-scatter.11.cloned.1.call-start = ((), (), s32[]{:S(2)}) async-start(), calls=%async_computation.7 | async-start | bytes 9437184 | tf_op jit(solution)/shard_map/reduce_scatter | solution.py:1003
  822.3 42.3 %collective-permute-start.111 = (bf16[3,512,512]{2,1,0:T(8,128)(2,1)}, bf16[3,512,512]{2,1,0:T(8,128)(2,1)S(1)}, u32[]{:S(2)}, u32[]{:S(2)}) collective-permute-start(bf16[3,512,512]{2,1,0:T(8,128)(2,1)} %copy-done.83), channel_id=1, source_target_pairs={{0,1},{1,2},{4,5},{5,6},{8,9},{9,10},{12,13},{13,14},{16,17},{17,1... | collective-permute-start | bytes 4718600 | tf_op jit(solution)/shard_map/ppermute | solution.py:67
  829.6 35.1 %collective-permute-start.112 = (bf16[3,512,512]{2,1,0:T(8,128)(2,1)}, bf16[3,512,512]{2,1,0:T(8,128)(2,1)S(1)}, u32[]{:S(2)}, u32[]{:S(2)}) collective-permute-start(bf16[3,512,512]{2,1,0:T(8,128)(2,1)} %copy-done.83), channel_id=1, source_target_pairs={{2,1},{3,2},{6,5},{7,6},{10,9},{11,10},{14,13},{15,14},{18,17},{19... | collective-permute-start | bytes 4718600 | tf_op jit(solution)/shard_map/ppermute | solution.py:67
  872.6 37.6 %collective-permute-start.115 = (bf16[3,512,512]{2,1,0:T(8,128)(2,1)}, bf16[3,512,512]{2,1,0:T(8,128)(2,1)}, u32[]{:S(2)}, u32[]{:S(2)}) collective-permute-start(bf16[3,512,512]{2,1,0:T(8,128)(2,1)} %get-tuple-element.434), channel_id=1, source_target_pairs={{0,1},{1,2},{2,3},{4,5},{5,6},{6,7},{8,9},{9,10},{10,11},{12,13},{... | collective-permute-start | bytes 4718600 | tf_op jit(solution)/shard_map/ppermute | solution.py:67
  879.2 31.0 %collective-permute-start.116 = (bf16[3,512,512]{2,1,0:T(8,128)(2,1)}, bf16[3,512,512]{2,1,0:T(8,128)(2,1)}, u32[]{:S(2)}, u32[]{:S(2)}) collective-permute-start(bf16[3,512,512]{2,1,0:T(8,128)(2,1)} %get-tuple-element.435), channel_id=1, source_target_pairs={{1,0},{2,1},{3,2},{5,4},{6,5},{7,6},{9,8},{10,9},{11,10},{13,12},{... | collective-permute-start | bytes 4718600 | tf_op jit(solution)/shard_map/ppermute | solution.py:67
  880.5 50.1 %collective-permute-start.121 = (bf16[3,512,512]{2,1,0:T(8,128)(2,1)}, bf16[3,512,512]{2,1,0:T(8,128)(2,1)}, u32[]{:S(2)}, u32[]{:S(2)}) collective-permute-start(bf16[3,512,512]{2,1,0:T(8,128)(2,1)} %get-tuple-element.436), channel_id=1, source_target_pairs={{0,1},{1,2},{2,3},{4,5},{5,6},{6,7},{8,9},{9,10},{10,11},{12,13},{... | collective-permute-start | bytes 4718600 | tf_op jit(solution)/shard_map/ppermute | solution.py:67
  886.2 52.2 %collective-permute-start.122 = (bf16[3,512,512]{2,1,0:T(8,128)(2,1)}, bf16[3,512,512]{2,1,0:T(8,128)(2,1)}, u32[]{:S(2)}, u32[]{:S(2)}) collective-permute-start(bf16[3,512,512]{2,1,0:T(8,128)(2,1)} %get-tuple-element.437), channel_id=1, source_target_pairs={{1,0},{2,1},{3,2},{5,4},{6,5},{7,6},{9,8},{10,9},{11,10},{13,12},{... | collective-permute-start | bytes 4718600 | tf_op jit(solution)/shard_map/ppermute | solution.py:67
  921.5 27.1 %collective-permute-start.123 = (f32[4,512]{1,0:T(4,128)S(1)}, f32[4,512]{1,0:T(4,128)S(1)}, u32[]{:S(2)}, u32[]{:S(2)}) collective-permute-start(f32[4,512]{1,0:T(4,128)S(1)} %broadcast_select_fusion), channel_id=1, source_target_pairs={{0,1},{1,0},{2,3},{3,2},{4,5},{5,4},{6,7},{7,6},{8,9},{9,8},{10,11... | collective-permute-start | bytes 24584 | tf_op jit(solution)/shard_map/ppermute | solution.py:67
  927.6 29.8 %collective-permute-start.119 = (f32[64,1024]{1,0:T(8,128)S(1)}, f32[64,1024]{1,0:T(8,128)S(1)}, u32[]{:S(2)}, u32[]{:S(2)}) collective-permute-start(f32[64,1024]{1,0:T(8,128)S(1)} %copy-done.170), channel_id=1, source_target_pairs={{0,2},{1,3},{2,0},{3,1},{4,6},{5,7},{6,4},{7,5},{8,10},{9,11},{10,... | collective-permute-start | bytes 786440 | tf_op jit(solution)/shard_map/ppermute | solution.py:67
  927.6 21.1 %collective-permute-start.120 = (f32[64,512]{1,0:T(8,128)S(1)}, f32[64,512]{1,0:T(8,128)S(1)}, u32[]{:S(2)}, u32[]{:S(2)}) collective-permute-start(f32[64,512]{1,0:T(8,128)S(1)} %copy-done.184), channel_id=1, source_target_pairs={{0,1},{1,0},{2,3},{3,2},{4,5},{5,4},{6,7},{7,6},{8,9},{9,8},{10,11... | collective-permute-start | bytes 393224 | tf_op jit(solution)/shard_map/ppermute | solution.py:67
  930.5 47.2 %collective-permute-start.117 = (bf16[512,512]{1,0:T(8,128)(2,1)}, bf16[512,512]{1,0:T(8,128)(2,1)S(1)}, u32[]{:S(2)}, u32[]{:S(2)}) collective-permute-start(bf16[512,512]{1,0:T(8,128)(2,1)} %add_convert_fusion.3), channel_id=1, source_target_pairs={{0,1},{1,2},{4,5},{5,6},{8,9},{9,10},{12,13},{13,14},{16,17},{17,1... | collective-permute-start | bytes 1572872 | tf_op jit(solution)/shard_map/ppermute | solution.py:67
  955.2 55.4 %collective-permute-start.99 = (bf16[512,512]{1,0:T(8,128)(2,1)S(1)}, bf16[512,512]{1,0:T(8,128)(2,1)S(1)}, u32[]{:S(2)}, u32[]{:S(2)}) collective-permute-start(bf16[512,512]{1,0:T(8,128)(2,1)S(1)} %copy-done.175), channel_id=1, source_target_pairs={{0,1},{1,2},{2,3},{4,5},{5,6},{6,7},{8,9},{9,10},{10,11},{12,13},{... | collective-permute-start | bytes 1572872 | tf_op jit(solution)/shard_map/ppermute | solution.py:67
  957.4 20.5 %collective-permute-start.118 = (bf16[512,512]{1,0:T(8,128)(2,1)}, bf16[512,512]{1,0:T(8,128)(2,1)S(1)}, u32[]{:S(2)}, u32[]{:S(2)}) collective-permute-start(bf16[512,512]{1,0:T(8,128)(2,1)} %add_convert_fusion.3), channel_id=1, source_target_pairs={{2,1},{3,2},{6,5},{7,6},{10,9},{11,10},{14,13},{15,14},{18,17},{19... | collective-permute-start | bytes 1572872 | tf_op jit(solution)/shard_map/ppermute | solution.py:67
  971.1 39.5 %collective-permute-start.100 = (bf16[512,512]{1,0:T(8,128)(2,1)S(1)}, bf16[512,512]{1,0:T(8,128)(2,1)S(1)}, u32[]{:S(2)}, u32[]{:S(2)}) collective-permute-start(bf16[512,512]{1,0:T(8,128)(2,1)S(1)} %copy-done.176), channel_id=1, source_target_pairs={{1,0},{2,1},{3,2},{5,4},{6,5},{7,6},{9,8},{10,9},{11,10},{13,12},{... | collective-permute-start | bytes 1572872 | tf_op jit(solution)/shard_map/ppermute | solution.py:67
  978.1 40.1 %collective-permute-start.128 = (bf16[512,512]{1,0:T(8,128)(2,1)S(1)}, bf16[512,512]{1,0:T(8,128)(2,1)S(1)}, u32[]{:S(2)}, u32[]{:S(2)}) collective-permute-start(bf16[512,512]{1,0:T(8,128)(2,1)S(1)} %add_convert_fusion.2), channel_id=1, source_target_pairs={{0,1},{1,2},{2,3},{4,5},{5,6},{6,7},{8,9},{9,10},{10,11},{12,13},{... | collective-permute-start | bytes 1572872 | tf_op jit(solution)/shard_map/ppermute | solution.py:67
  981.9 36.3 %collective-permute-start.129 = (bf16[512,512]{1,0:T(8,128)(2,1)S(1)}, bf16[512,512]{1,0:T(8,128)(2,1)S(1)}, u32[]{:S(2)}, u32[]{:S(2)}) collective-permute-start(bf16[512,512]{1,0:T(8,128)(2,1)S(1)} %add_convert_fusion.1), channel_id=1, source_target_pairs={{1,0},{2,1},{3,2},{5,4},{6,5},{7,6},{9,8},{10,9},{11,10},{13,12},{... | collective-permute-start | bytes 1572872 | tf_op jit(solution)/shard_map/ppermute | solution.py:67
  (276 other events, 4784.3 us)
Sparse Core Ops, SparseCore 0:
  550.9 72.1 reduce-scatter.6
  796.2 64.3 reduce-scatter.4
  864.4 41.1 reduce-scatter.8
  909.4 71.2 reduce-scatter.10
